TPU v7x, 32 devices: a whole 2x2x4 slice. The times are simulated.
32 devices in a mesh: lat: 8 (over z, core), lon: 4 (over y, x).
Axes of the slice: x: 2, y: 2, z: 4, core: 2. Of those that a mesh axis runs over, the one named last changes fastest.
Arguments:
- spectra: float32 [64, 2, 360, 721], P('lat', None, 'lon'), may hold values from -0.03 to 0.03
- field_slot: int32 [64], replicated, may hold values from 0 to 63, each once
- field_weight: float32 [64], replicated, may hold values from 0.3 to 3
- latents: bfloat16 [64, 1440, 512], P('lat', 'lon'), may hold values from -6 to 6
- w_hidden: bfloat16 [512, 512], replicated, may hold values from -0.25 to 0.25
- b_hidden: float32 [512], replicated, may hold values from -3 to 3
- w_out: bfloat16 [512, 64], replicated, may hold values from -0.75 to 0.75
Outputs:
- latent_grad: bfloat16 [64, 1440, 512], P('lat', 'lon')
- hidden_grad: float32 [512, 512], replicated
- bias_grad: float32 [512], replicated
- out_grad: float32 [512, 64], replicated
Inputs may be any that keep to these rules, and one draw needn't show every extreme that they name: Slot f of the spectra holds field field_slot[f]; every field stands in exactly one slot.
All inputs are finite; a program needn't handle non-finite values.
Results may differ from a plain program's by a relative error of at most 0.007.
Values sent between devices are 32-bit elements; how exact they have to be, the bound alone decides.
No kernel may reach another device: no remote copies, remote signals or barrier semaphores. Data moves between devices by JAX's collectives and lax.ppermute only.
A program may use at most 256 MiB of HBM per device.

v0:
```python
import math

import jax
import jax.numpy as jnp
from jax import lax
from jax.sharding import PartitionSpec as P

NM = 720
NLON = 1440
F = 64


step_block = 32


def band_angles(row_ids, rows_all):
    return jnp.pi * (NM // 2 - rows_all // 2 + row_ids.astype(jnp.float32)) / NM


def pair_layout(pair_ids):
    step_ids = jnp.arange(NM + 1, dtype=jnp.int32)[:, None]
    switch = (NM - pair_ids)[None, :]
    in_first = step_ids < switch
    order_ids = jnp.where(in_first, pair_ids[None, :], NM - 1 - pair_ids[None, :])
    degree_ids = jnp.where(in_first, pair_ids[None, :] + step_ids, step_ids - 1)
    restart = (step_ids == 0) | (step_ids == switch)
    return (in_first, order_ids, degree_ids, restart)


def legendre_table(pair_ids, colatitude):
    in_first, order_ids, degree_ids, restart = pair_layout(pair_ids)
    order_real = order_ids.astype(jnp.float32)
    degree_real = degree_ids.astype(jnp.float32)
    grow_coef = jnp.sqrt(
        (4.0 * degree_real * degree_real - 1.0)
        / jnp.maximum(degree_real * degree_real - order_real * order_real, 1.0)
    )
    lower_deg = degree_real - 1.0
    shrink_coef = jnp.sqrt(
        jnp.maximum(lower_deg * lower_deg - order_real * order_real, 0.0)
        / jnp.maximum(4.0 * lower_deg * lower_deg - 1.0, 1.0)
    )
    term_ids = jnp.arange(1, NM, dtype=jnp.float32)
    log_terms = jnp.log((2.0 * term_ids + 1.0) / (2.0 * term_ids))
    log_sine = jnp.log(jnp.sin(colatitude))

    def seed_for(order_set):
        order_set_real = order_set.astype(jnp.float32)
        included = term_ids[None, :] <= order_set_real[:, None]
        log_total = jnp.sum(jnp.where(included, log_terms[None, :], 0.0), axis=1)
        return jnp.exp(
            0.5 * log_total[:, None]
            - 0.5 * jnp.log(4.0 * jnp.pi)
            + order_set_real[:, None] * log_sine[None, :]
        )

    seed_first = seed_for(pair_ids)
    seed_second = seed_for(NM - 1 - pair_ids)
    cosine = jnp.cos(colatitude)[None, :]
    step_total = NM + 1
    block_total = (step_total + step_block - 1) // step_block
    padding = block_total * step_block - step_total

    def blocked(values, fill):
        padded = jnp.concatenate(
            [values, jnp.full((padding, values.shape[1]), fill, values.dtype)], axis=0
        )
        return padded.reshape(block_total, step_block, values.shape[1])

    grow_blocks = blocked(grow_coef, 0.0)
    shrink_blocks = blocked(shrink_coef, 0.0)
    restart_blocks = blocked(restart, False)
    first_blocks = blocked(in_first, True)

    def advance_block(state, block_inputs):
        previous, before_prev = state
        grow_block, shrink_block, restart_block, first_block = block_inputs
        produced = []
        for offset in range(step_block):
            seed_value = jnp.where(first_block[offset][:, None], seed_first, seed_second)
            new_value = jnp.where(
                restart_block[offset][:, None],
                seed_value,
                grow_block[offset][:, None]
                * (cosine * previous - shrink_block[offset][:, None] * before_prev),
            )
            before_prev = previous
            previous = new_value
            produced.append(new_value)
        return ((previous, before_prev), jnp.stack(produced, axis=0))

    zero_state = jnp.zeros((pair_ids.shape[0], colatitude.shape[0]), jnp.float32)
    unused_state, legendre = lax.scan(
        advance_block,
        (zero_state, zero_state),
        (grow_blocks, shrink_blocks, restart_blocks, first_blocks),
    )
    legendre = legendre.reshape(block_total * step_block, pair_ids.shape[0], colatitude.shape[0])
    return legendre[:step_total]


def spectral_coefficients(spectra, pair_ids, colatitude):
    legendre = legendre_table(pair_ids, colatitude)
    lower_half = jnp.transpose(pair_layout(pair_ids)[0]).astype(jnp.float32)
    halves = []
    for selector in (lower_half, 1.0 - lower_half):
        halves.append(
            jnp.einsum(
                "fcpk,kpi->fcpi", spectra * selector, legendre, precision=lax.Precision.HIGHEST
            )
        )
    return jnp.stack(halves, axis=3).astype(jnp.bfloat16)


def trig_table(pair_ids):
    order_ids = jnp.stack([pair_ids, NM - 1 - pair_ids], axis=1)
    column_ids = jnp.arange(NLON, dtype=jnp.int32)
    phase_ids = order_ids[:, :, None] * column_ids[None, None, :] % NLON
    phase = phase_ids.astype(jnp.float32) * (2.0 * jnp.pi / NLON)
    return jnp.stack([jnp.cos(phase), jnp.sin(phase)], axis=0).astype(jnp.bfloat16)


def local(spectra, field_slot, field_weight, latents, w_hidden, b_hidden, w_out):
    slot_count = spectra.shape[0]
    pair_count = spectra.shape[2]
    lat_rows, lon_cols, width_all = latents.shape
    lat_count = lax.axis_size("lat")
    lon_count = lax.axis_size("lon")
    rows_all = lat_rows * lat_count
    lat_index = lax.axis_index("lat")
    lon_index = lax.axis_index("lon")
    pair_ids = lon_index * pair_count + jnp.arange(pair_count, dtype=jnp.int32)
    colatitude = band_angles(jnp.arange(rows_all, dtype=jnp.int32), rows_all)
    coeffs = spectral_coefficients(spectra, pair_ids, colatitude)
    trig = trig_table(pair_ids)
    shaped = coeffs.reshape(slot_count, 2, pair_count, 2, lat_count, lat_rows)
    trig_split = trig.reshape(2, pair_count, 2, lon_count, lon_cols)
    partial_grid = jnp.einsum(
        "fcphal,cphbj->abflj", shaped, trig_split, preferred_element_type=jnp.float32
    )
    partial_grid = partial_grid.reshape(lat_count * lon_count, slot_count, lat_rows, lon_cols)
    arrived = lax.all_to_all(partial_grid, ("lat", "lon"), split_axis=0, concat_axis=0, tiled=True)
    summed = jnp.sum(arrived.reshape(lat_count, lon_count, slot_count, lat_rows, lon_cols), axis=1)
    grid_field = jnp.transpose(summed, (2, 3, 0, 1)).reshape(lat_rows, lon_cols, F)
    local_rows = lat_index * lat_rows + jnp.arange(lat_rows, dtype=jnp.int32)
    sine_rows = jnp.sin(band_angles(local_rows, rows_all))
    selector = field_slot[:, None] == jnp.arange(F, dtype=jnp.int32)[None, :]
    slot_weight = jnp.dot(
        selector.astype(jnp.float32), field_weight, precision=lax.Precision.HIGHEST
    )
    cell_count = lat_rows * lon_cols
    field_grad = (
        (grid_field * sine_rows[:, None, None] * slot_weight[None, None, :])
        .astype(jnp.bfloat16)
        .reshape(cell_count, F)
    )
    w_out_slot = jnp.dot(
        w_out, selector.astype(jnp.bfloat16).T, preferred_element_type=jnp.float32
    ).astype(jnp.bfloat16)
    flat_latents = latents.reshape(cell_count, width_all)
    preact = jnp.dot(flat_latents, w_hidden, preferred_element_type=jnp.float32) + b_hidden
    hidden = jax.nn.gelu(preact).astype(jnp.bfloat16)
    out_slot = jnp.dot(hidden.T, field_grad, preferred_element_type=jnp.float32)
    out_sum = jnp.dot(out_slot, selector.astype(jnp.float32), precision=lax.Precision.HIGHEST)
    hidden_back = jnp.dot(field_grad, w_out_slot.T, preferred_element_type=jnp.float32)
    unused_out, pullback = jax.vjp(jax.nn.gelu, preact)
    preact_back = pullback(hidden_back)[0].astype(jnp.bfloat16)
    hidden_sum = jnp.dot(flat_latents.T, preact_back, preferred_element_type=jnp.float32)
    bias_sum = jnp.sum(preact_back.astype(jnp.float32), axis=0)
    latent_grad = jnp.dot(preact_back, w_hidden.T, preferred_element_type=jnp.float32).astype(
        jnp.bfloat16
    )
    latent_grad = latent_grad.reshape(lat_rows, lon_cols, width_all)
    hidden_total, bias_total, out_total = lax.psum((hidden_sum, bias_sum, out_sum), ("lat", "lon"))
    norm_factor = math.sqrt(rows_all * NLON)
    return (
        latent_grad,
        hidden_total / norm_factor,
        bias_total / norm_factor,
        out_total / norm_factor,
    )


def solution(mesh):
    in_specs = (P("lat", None, "lon", None), P(), P(), P("lat", "lon", None), P(), P(), P())
    out_specs = (P("lat", "lon", None), P(), P(), P())
    return jax.shard_map(local, mesh=mesh, in_specs=in_specs, out_specs=out_specs, check_vma=False)
```

profile of v0, /device:TPU:0, one launch (start us, length us, event | category | flops | bytes accessed | tf_op | source)
XLA Modules:
  0.0 929.6 jit_solution(11204161307592576887)
XLA Ops:
  13.9 514.7 %while.18 = (s32[]{:T(128)}, f32[90,64]{1,0:T(8,128)S(1)}, f32[90,64]{1,0:T(8,128)S(1)}, f32[23,32,90,64]{3,2,1,0:T(8,128)}, pred[23,32,90]{2,1,0:T(8,128)(4,1)}...) while((s32[]{:T(128)}, f32[90,64]{1,0:T(8,128)S(1)}, ...), condition=%wide.region_3.4_spmd.clone.clone.clone.clone, body=%wide.region_2.3_spmd.clone.clone.clone.clone.sunk | while | flops 1860705 | bytes 8780726 | solution.py:93
  16.3 1.7 fusion.317
  38.8 1.7 fusion.317
  528.6 26.8 %slice.1028 = f32[721,90,64]{2,1,0:T(8,128)} slice(f32[736,90,64]{2,1,0:T(8,128)} %bitcast.473), slice={[0:721], [0:90], [0:64]} | slice | bytes 33223680 | tf_op jit(solution)/shard_map/slice | solution.py:99
  555.4 29.3 %copy.43 = f32[721,90,64]{0,2,1:T(8,128)} copy(f32[721,90,64]{2,1,0:T(8,128)} %slice.1028) | data formatting | bytes 33223680
  584.7 8.4 broadcast_multiply_fusion.1
  593.0 19.3 %fusion.229 = bf16[8,2,90,64]{3,0,1,2:T(8,128)(2,1)S(1)} fusion(f32[8,2,90,721]{3,1,2,0:T(2,128)} %get-tuple-element.580, f32[721,90,64]{0,2,1:T(8,128)} %copy.43), kind=kOutput, calls=%fused_computation.390 | convolution fusion | flops 797460480 | bytes 20949120 | tf_op jit(solution)/shard_map/fcpk,kpi->fcpi/dot_general | solution.py:108
  613.4 19.3 %fusion.224 = bf16[8,2,90,64]{3,0,1,2:T(8,128)(2,1)S(1)} fusion(f32[8,2,90,721]{3,1,2,0:T(2,128)} %get-tuple-element.581, f32[721,90,64]{0,2,1:T(8,128)} %copy.43), kind=kOutput, calls=%fused_computation.389 | convolution fusion | flops 797460480 | bytes 20949120 | tf_op jit(solution)/shard_map/fcpk,kpi->fcpi/dot_general | solution.py:108
  633.8 5.6 cosine_convert_fusion
  639.4 2.1 convolution_bitcast_fusion
  641.5 2.1 copy.35
  643.6 7.4 all-to-all-start
  651.5 4.3 fusion.298
  655.8 66.4 %all-to-all-done = f32[32,8,8,360]{3,2,1,0:T(8,128)} async-done(((f32[32,8,8,360]{3,2,1,0:T(8,128)}), f32[32,8,8,360]{3,2,1,0:T(8,128)}, u32[]{:S(2)}, u32[]{:S(2)}) %all-to-all-start) | async-done | bytes 2949152 | tf_op jit(solution)/shard_map/all_to_all | solution.py:142
  722.2 3.1 bitcast_reduce_fusion
  725.3 2.3 reshape.606
  727.5 4.5 fusion.213
  733.0 8.2 convert_reduce_fusion
  741.2 4.6 convolution_bitcast_fusion.1
  745.8 39.6 %psum.22 = f32[512]{0:T(512)S(1)} all-reduce(f32[512]{0:T(512)S(1)} %get-tuple-element.588), channel_id=1, replica_groups=mesh['lat'=8,'lon'=4] {'lat','lon'}, use_global_device_ids=true, to_apply=%region_7.8 | all-reduce | flops 512 | bytes 4096 | tf_op jit(solution)/shard_map/psum | solution.py:174
  786.0 5.2 convolution_convert_fusion
  791.2 126.1 %all-reduce.7.cloned.1.call-done = (f32[512,512]{0,1:T(8,128)}, f32[512,64]{0,1:T(8,128)}) async-done(((f32[512,512]{0,1:T(8,128)}, f32[512,64]{0,1:T(8,128)}), (f32[512,512]{0,1:T(8,128)}, f32[512,64]{0,1:T(8,128)})) %all-reduce.7.cloned.1.call-update) | async-done | bytes 1179664 | tf_op jit(solution)/shard_map/psum | solution.py:174
  917.2 2.3 broadcast_multiply_fusion.2
  919.6 2.6 copy.36
  (2056 shorter events, 508.0 us)
Async XLA Ops:
  7.2 644.3 %copy-start = (bf16[8,360,512]{2,1,0:T(8,128)(2,1)S(1)}, bf16[8,360,512]{2,1,0:T(8,128)(2,1)}, u32[]{:S(2)}) copy-start(bf16[8,360,512]{2,1,0:T(8,128)(2,1)} %param.12) | copy-start | bytes 8847364
  19.9 9.9 %copy-start.6 = (pred[90]{0:T(512)(128)(4,1)S(1)}, pred[90]{0:T(512)(128)(4,1)}, u32[]{:S(2)}) copy-start(pred[90]{0:T(512)(128)(4,1)} %get-tuple-element.962) | copy-start | bytes 274 | tf_op jit(solution)/shard_map/while
  19.9 9.9 %copy-start.19 = (f32[90]{0:T(128)S(1)}, f32[90]{0:T(128)}, u32[]{:S(2)}) copy-start(f32[90]{0:T(128)} %get-tuple-element.958) | copy-start | bytes 1084 | tf_op jit(solution)/shard_map/while
  42.4 9.9 %copy-start.6 = (pred[90]{0:T(512)(128)(4,1)S(1)}, pred[90]{0:T(512)(128)(4,1)}, u32[]{:S(2)}) copy-start(pred[90]{0:T(512)(128)(4,1)} %get-tuple-element.962) | copy-start | bytes 274 | tf_op jit(solution)/shard_map/while
  42.4 9.9 %copy-start.19 = (f32[90]{0:T(128)S(1)}, f32[90]{0:T(128)}, u32[]{:S(2)}) copy-start(f32[90]{0:T(128)} %get-tuple-element.958) | copy-start | bytes 1084 | tf_op jit(solution)/shard_map/while
  64.7 9.9 %copy-start.6 = (pred[90]{0:T(512)(128)(4,1)S(1)}, pred[90]{0:T(512)(128)(4,1)}, u32[]{:S(2)}) copy-start(pred[90]{0:T(512)(128)(4,1)} %get-tuple-element.962) | copy-start | bytes 274 | tf_op jit(solution)/shard_map/while
  64.8 9.9 %copy-start.19 = (f32[90]{0:T(128)S(1)}, f32[90]{0:T(128)}, u32[]{:S(2)}) copy-start(f32[90]{0:T(128)} %get-tuple-element.958) | copy-start | bytes 1084 | tf_op jit(solution)/shard_map/while
  87.1 9.9 %copy-start.6 = (pred[90]{0:T(512)(128)(4,1)S(1)}, pred[90]{0:T(512)(128)(4,1)}, u32[]{:S(2)}) copy-start(pred[90]{0:T(512)(128)(4,1)} %get-tuple-element.962) | copy-start | bytes 274 | tf_op jit(solution)/shard_map/while
  87.1 9.9 %copy-start.19 = (f32[90]{0:T(128)S(1)}, f32[90]{0:T(128)}, u32[]{:S(2)}) copy-start(f32[90]{0:T(128)} %get-tuple-element.958) | copy-start | bytes 1084 | tf_op jit(solution)/shard_map/while
  109.5 9.9 %copy-start.6 = (pred[90]{0:T(512)(128)(4,1)S(1)}, pred[90]{0:T(512)(128)(4,1)}, u32[]{:S(2)}) copy-start(pred[90]{0:T(512)(128)(4,1)} %get-tuple-element.962) | copy-start | bytes 274 | tf_op jit(solution)/shard_map/while
  109.5 9.9 %copy-start.19 = (f32[90]{0:T(128)S(1)}, f32[90]{0:T(128)}, u32[]{:S(2)}) copy-start(f32[90]{0:T(128)} %get-tuple-element.958) | copy-start | bytes 1084 | tf_op jit(solution)/shard_map/while
  132.0 9.9 %copy-start.6 = (pred[90]{0:T(512)(128)(4,1)S(1)}, pred[90]{0:T(512)(128)(4,1)}, u32[]{:S(2)}) copy-start(pred[90]{0:T(512)(128)(4,1)} %get-tuple-element.962) | copy-start | bytes 274 | tf_op jit(solution)/shard_map/while
  132.0 9.9 %copy-start.19 = (f32[90]{0:T(128)S(1)}, f32[90]{0:T(128)}, u32[]{:S(2)}) copy-start(f32[90]{0:T(128)} %get-tuple-element.958) | copy-start | bytes 1084 | tf_op jit(solution)/shard_map/while
  154.3 9.9 %copy-start.6 = (pred[90]{0:T(512)(128)(4,1)S(1)}, pred[90]{0:T(512)(128)(4,1)}, u32[]{:S(2)}) copy-start(pred[90]{0:T(512)(128)(4,1)} %get-tuple-element.962) | copy-start | bytes 274 | tf_op jit(solution)/shard_map/while
  154.3 9.9 %copy-start.19 = (f32[90]{0:T(128)S(1)}, f32[90]{0:T(128)}, u32[]{:S(2)}) copy-start(f32[90]{0:T(128)} %get-tuple-element.958) | copy-start | bytes 1084 | tf_op jit(solution)/shard_map/while
  176.7 9.9 %copy-start.6 = (pred[90]{0:T(512)(128)(4,1)S(1)}, pred[90]{0:T(512)(128)(4,1)}, u32[]{:S(2)}) copy-start(pred[90]{0:T(512)(128)(4,1)} %get-tuple-element.962) | copy-start | bytes 274 | tf_op jit(solution)/shard_map/while
  176.7 9.9 %copy-start.19 = (f32[90]{0:T(128)S(1)}, f32[90]{0:T(128)}, u32[]{:S(2)}) copy-start(f32[90]{0:T(128)} %get-tuple-element.958) | copy-start | bytes 1084 | tf_op jit(solution)/shard_map/while
  199.1 9.9 %copy-start.6 = (pred[90]{0:T(512)(128)(4,1)S(1)}, pred[90]{0:T(512)(128)(4,1)}, u32[]{:S(2)}) copy-start(pred[90]{0:T(512)(128)(4,1)} %get-tuple-element.962) | copy-start | bytes 274 | tf_op jit(solution)/shard_map/while
  613.4 20.4 %copy-start.30 = (s32[90,1]{0,1:T(1,128)S(1)}, s32[90,1]{0,1:T(1,128)}, u32[]{:S(2)}) copy-start(s32[90,1]{0,1:T(1,128)} %get-tuple-element.592) | copy-start | bytes 1084
  613.4 20.4 %copy-start.31 = (s32[90,1]{0,1:T(1,128)S(1)}, s32[90,1]{0,1:T(1,128)}, u32[]{:S(2)}) copy-start(s32[90,1]{0,1:T(1,128)} %get-tuple-element.593) | copy-start | bytes 1084
  613.4 20.4 %copy-start.26 = (s32[4,360]{1,0:T(4,128)S(1)}, s32[4,360]{1,0:T(4,128)}, u32[]{:S(2)}) copy-start(s32[4,360]{1,0:T(4,128)} %multiply_add_fusion) | copy-start | bytes 17284
  643.6 78.6 %all-to-all-start = ((f32[32,8,8,360]{3,2,1,0:T(8,128)}), f32[32,8,8,360]{3,2,1,0:T(8,128)}, u32[]{:S(2)}, u32[]{:S(2)}) async-start(f32[32,8,8,360]{3,2,1,0:T(8,128)} %bitcast.474), calls=%async_computation | async-start | bytes 6291456 | tf_op jit(solution)/shard_map/all_to_all | solution.py:142
  651.0 266.2 %all-reduce.7.cloned.1.call-start = ((), (), s32[]{:S(2)}) async-start(), calls=%async_computation.1 | async-start | bytes 2359296 | tf_op jit(solution)/shard_map/psum | solution.py:174
  655.8 71.7 %copy-start.32 = (f32[512]{0:T(512)S(1)}, f32[512]{0:T(512)}, u32[]{:S(2)}) copy-start(f32[512]{0:T(512)} %param.14) | copy-start | bytes 6148
  (518 other events, 4437.6 us)
Sparse Core Ops, SparseCore 0:
  785.5 131.6 all-reduce.6
where the time goes:
time: 938 us; the launch traced here: 930 us
  local copies, waits for them, and re-layouts  303 us (32%)
  other arithmetic  290 us (31%)
  waiting for transfers between devices  192 us (20%)
  matrix products  68.5 us (7%)
  blocking collectives  39.6 us (4%)
  loops' own time  14.8 us (2%)
  between operations  14.2 us (2%)
    while x713, other arithmetic  260 us
    psum x1, waiting for transfers between devices, local(): lax.psum((hidden_sum, bias_sum, out_sum), ('lat', 'lon'))  126 us
    all_to_all x1, waiting for transfers between devices, local(): lax.all_to_all(partial_grid, ('lat', 'lon'), split_axis=0, concat_axis=0,...  66.4 us
    broadcast_in_dim x46, local copies, waits for them, and re-layouts, advance_block(): jnp.where(restart_block[offset][:, None], seed_value, grow_block[offset][...  64.3 us
    mul x46, local copies, waits for them, and re-layouts, advance_block(): shrink_block[offset][:, None] * before_prev  61.7 us
    mul x46, local copies, waits for them, and re-layouts, advance_block(): grow_block[offset][:, None]  61 us
    psum x1, blocking collectives, local(): lax.psum((hidden_sum, bias_sum, out_sum), ('lat', 'lon'))  39.6 us
    dot_general x2, matrix products, spectral_coefficients(): jnp.einsum('fcpk,kpi->fcpi', spectra * selector, legendre, precision=lax....  38.5 us
  transfers between devices with their start and end apart: 2, of which 2 were waited for; matrix products, arithmetic and copies ran while one was open for 1% of the time, Pallas kernels for 0%

commit v1 on v0

v1 whole, which is shorter than its diff:
```python
import functools
import math

import jax
import jax.numpy as jnp
from jax import lax
from jax.experimental import pallas as pl
from jax.experimental.pallas import tpu as pltpu
from jax.sharding import PartitionSpec as P

NM = 720
NLON = 1440
F = 64
LANES = 128
SUBS = 8
STEPS = NM + 1
TABLE_ROWS = 728
VMEM_LIMIT = 56 * 1024 * 1024


def band_angles(row_ids, rows_all):
    return jnp.pi * (NM // 2 - rows_all // 2 + row_ids.astype(jnp.float32)) / NM


def pad_to(value, multiple):
    return (value + multiple - 1) // multiple * multiple


def coeff_kernel(
    first_ref, spectra_hbm, out_ref, spectra_ref, grow_ref, shrink_ref, table_ref, stage_ref,
    copy_sem, *, pair_count, rows_all, lat_rows, slot_count,
):
    per_block = LANES // rows_all
    vregs = pad_to(pair_count, SUBS * per_block) // (SUBS * per_block)
    step_tile = rows_all
    tile_total = pad_to(STEPS, step_tile) // step_tile
    pair_pad = pad_to(pair_count, SUBS)
    lat_count = rows_all // lat_rows
    first_pair = first_ref[0]

    fetch = pltpu.make_async_copy(spectra_hbm, spectra_ref, copy_sem)
    fetch.start()

    lane = lax.broadcasted_iota(jnp.int32, (SUBS, LANES), 1)
    sub = lax.broadcasted_iota(jnp.int32, (SUBS, LANES), 0)
    inner = lane & (rows_all - 1)
    which = lane // rows_all
    colatitude = band_angles(inner, rows_all)
    cosine = jnp.cos(colatitude)
    log_sine = jnp.log(jnp.sin(colatitude))

    def log_total(order_column):
        total = jnp.zeros((SUBS, LANES), jnp.float32)
        for tile in range(pad_to(NM, LANES) // LANES):
            term = (lane + tile * LANES).astype(jnp.float32)
            safe = jnp.maximum(term, 1.0)
            value = jnp.log((2.0 * safe + 1.0) / (2.0 * safe))
            total = total + jnp.where((term >= 1.0) & (term <= order_column), value, 0.0)
        return jnp.sum(total, axis=1, keepdims=True)

    def seed(order_of):
        total = jnp.zeros((SUBS, LANES), jnp.float32)
        for part in range(per_block):
            column = order_of(part).astype(jnp.float32)
            total = jnp.where(which == part, log_total(column), total)
        order = order_of(which).astype(jnp.float32)
        return jnp.exp(0.5 * total - 0.5 * math.log(4.0 * math.pi) + order * log_sine)

    firsts, seconds, switches = [], [], []
    for v in range(vregs):
        base = first_pair + (sub + v * SUBS) * per_block

        def order_first(part, base=base):
            return base + part

        def order_second(part, base=base):
            return NM - 1 - (base + part)

        firsts.append(seed(order_first))
        seconds.append(seed(order_second))
        pair = base + which
        switch = NM - pair
        switches.append(switch)
        for tile in range(tile_total):
            step = inner + tile * step_tile
            in_first = step < switch
            order = jnp.where(in_first, pair, NM - 1 - pair).astype(jnp.float32)
            degree = jnp.where(in_first, pair + step, step - 1).astype(jnp.float32)
            lower = degree - 1.0
            grow = jnp.sqrt(
                (4.0 * degree * degree - 1.0) / jnp.maximum(degree * degree - order * order, 1.0)
            )
            shrink = jnp.sqrt(
                jnp.maximum(lower * lower - order * order, 0.0)
                / jnp.maximum(4.0 * lower * lower - 1.0, 1.0)
            )
            start = step == 0
            grow_ref[tile, pl.ds(v * SUBS, SUBS), :] = jnp.where(start, 1.0, grow)
            shrink_ref[tile, pl.ds(v * SUBS, SUBS), :] = jnp.where(start, -1.0, shrink)

    def advance(tile, offset, state, grows, shrinks):
        previous, before = state
        index = which * rows_all + offset
        step = tile * step_tile + offset
        produced = []
        for v in range(vregs):
            grow = jnp.take_along_axis(grows[v], index, axis=1)
            shrink = jnp.take_along_axis(shrinks[v], index, axis=1)
            value = grow * (cosine * previous[v] - shrink * before[v])
            value = jnp.where(switches[v] == step, seconds[v], value)
            table_ref[pl.ds(v * SUBS * TABLE_ROWS + step, SUBS, stride=TABLE_ROWS), :] = value
            produced.append(value)
        return (tuple(produced), previous)

    def run_tile(tile, state, count, unroll):
        grows = [grow_ref[tile, pl.ds(v * SUBS, SUBS), :] for v in range(vregs)]
        shrinks = [shrink_ref[tile, pl.ds(v * SUBS, SUBS), :] for v in range(vregs)]

        def body(offset, carry):
            return advance(tile, offset, carry, grows, shrinks)

        return lax.fori_loop(0, count, body, state, unroll=unroll)

    zeros = tuple(jnp.zeros((SUBS, LANES), jnp.float32) for _ in range(vregs))
    state = (zeros, tuple(firsts))
    whole_tiles = STEPS // step_tile
    state = lax.fori_loop(
        0, whole_tiles, lambda tile, carry: run_tile(tile, carry, step_tile, 8), state
    )
    if STEPS % step_tile:
        run_tile(whole_tiles, state, STEPS % step_tile, STEPS % step_tile % 16)

    for row in range(slot_count):
        for part in range(4):
            stage_ref[row, pl.ds(part * pair_pad + pair_pad - SUBS, SUBS), :] = jnp.zeros(
                (SUBS, LANES), jnp.float32
            )
    fetch.wait()

    split = 256
    rows_half = 2 * slot_count * SUBS

    def split_parts(values):
        high = values.astype(jnp.bfloat16)
        low = (values - high.astype(jnp.float32)).astype(jnp.bfloat16)
        return high, low

    def product(left, right):
        left_high, left_low = left
        right_high, right_low = right
        dot = functools.partial(jnp.dot, preferred_element_type=jnp.float32)
        return (
            dot(left_high, right_high) + dot(left_low, right_high) + dot(left_high, right_low)
        )

    def group(start):
        values = spectra_ref[:, pl.ds(start, SUBS), :]
        step = lax.broadcasted_iota(jnp.int32, (1, SUBS, STEPS), 2)
        pair = first_pair + start + lax.broadcasted_iota(jnp.int32, (1, SUBS, STEPS), 1)
        in_first = step < NM - pair
        early = values[:, :, :split].reshape(rows_half, split)
        late = jnp.concatenate(
            [jnp.where(in_first, values, 0.0), jnp.where(in_first, 0.0, values)], axis=0
        )[:, :, split:].reshape(2 * rows_half, STEPS - split)
        early, late = split_parts(early), split_parts(late)
        total = jnp.zeros((2 * rows_half, LANES), jnp.float32)
        row_pair = lax.broadcasted_iota(jnp.int32, (2 * rows_half, LANES), 0) & (SUBS - 1)
        lane_part = lax.broadcasted_iota(jnp.int32, (2 * rows_half, LANES), 1) // rows_all
        first_block = start // per_block
        for block in range(0, SUBS // per_block, 2):
            tables = [
                table_ref[pl.ds((first_block + block + n) * TABLE_ROWS, STEPS), :]
                for n in range(2)
            ]
            table = jnp.concatenate(tables, axis=1)
            top = product(early, split_parts(table[:split]))
            bottom = product(late, split_parts(table[split:]))
            both = jnp.concatenate([bottom[:rows_half] + top, bottom[rows_half:]], axis=0)
            for n in range(2):
                keep = row_pair == (block + n) * per_block + lane_part
                total = total + jnp.where(keep, both[:, n * LANES : (n + 1) * LANES], 0.0)
        for part in range(1, per_block):
            total = total + pltpu.roll(total, LANES - part * rows_all, 1) if part == 1 else total
        total = total.astype(jnp.bfloat16).astype(jnp.float32)
        for half in range(2):
            for row in range(slot_count):
                for trig in range(2):
                    source = ((half * slot_count + row) * 2 + trig) * SUBS
                    target = (half * 2 + trig) * pair_pad + start
                    stage_ref[row, pl.ds(target, SUBS), :] = total[source : source + SUBS]

    def group_body(index, carry):
        group(pl.multiple_of(index * SUBS, SUBS))
        return carry

    lax.fori_loop(0, pair_count // SUBS, group_body, 0)
    if pair_count % SUBS:
        group(pair_count - SUBS)

    for row in range(slot_count):
        flipped = stage_ref[row].T
        out_ref[:, pl.ds(row * lat_rows, lat_rows), :] = flipped[:rows_all].reshape(
            lat_count, lat_rows, 4 * pair_pad
        )


def coefficients(spectra, first_pair, rows_all, lat_rows):
    slot_count, _, pair_count, steps = spectra.shape
    per_block = LANES // rows_all
    vregs = pad_to(pair_count, SUBS * per_block) // (SUBS * per_block)
    tile_total = pad_to(STEPS, rows_all) // rows_all
    pair_pad = pad_to(pair_count, SUBS)
    lat_count = rows_all // lat_rows
    kernel = functools.partial(
        coeff_kernel, pair_count=pair_count, rows_all=rows_all, lat_rows=lat_rows,
        slot_count=slot_count,
    )
    return pl.pallas_call(
        kernel,
        out_shape=jax.ShapeDtypeStruct(
            (lat_count, slot_count * lat_rows, 4 * pair_pad), jnp.float32
        ),
        in_specs=[
            pl.BlockSpec(memory_space=pltpu.SMEM),
            pl.BlockSpec(memory_space=pl.ANY),
        ],
        out_specs=pl.BlockSpec(memory_space=pltpu.VMEM),
        scratch_shapes=[
            pltpu.VMEM((2 * slot_count, pair_count, steps), jnp.float32),
            pltpu.VMEM((tile_total, vregs * SUBS, LANES), jnp.float32),
            pltpu.VMEM((tile_total, vregs * SUBS, LANES), jnp.float32),
            pltpu.VMEM((vregs * SUBS * TABLE_ROWS, LANES), jnp.float32),
            pltpu.VMEM((slot_count, 4 * pair_pad, LANES), jnp.float32),
            pltpu.SemaphoreType.DMA,
        ],
        compiler_params=pltpu.CompilerParams(vmem_limit_bytes=VMEM_LIMIT),
        name="coefficients",
    )(first_pair, spectra.reshape(2 * slot_count, pair_count, steps))


def grid_kernel(trig_ref, coeff_ref, out_ref, *, lon_count):
    rows = coeff_ref.shape[0] // lon_count * coeff_ref.shape[1]
    width = coeff_ref.shape[2]
    values = coeff_ref[...].reshape(rows // coeff_ref.shape[1], lon_count, coeff_ref.shape[1], width)
    total = None
    for block in range(lon_count):
        right = values[:, block].reshape(rows, width).astype(jnp.bfloat16)
        part = lax.dot_general(
            trig_ref[block], right, (((1,), (1,)), ((), ())), preferred_element_type=jnp.float32
        )
        total = part if total is None else total + part
    out_ref[...] = total


def grid_field(trig, coeffs, lon_count, lon_cols):
    lat_count = coeffs.shape[0] // lon_count
    rows = lat_count * coeffs.shape[1]
    width = trig.shape[3]
    return pl.pallas_call(
        functools.partial(grid_kernel, lon_count=lon_count),
        grid=(lon_count,),
        out_shape=jax.ShapeDtypeStruct((lon_count, lon_cols, rows), jnp.float32),
        in_specs=[
            pl.BlockSpec((None, lon_count, lon_cols, width), lambda j: (j, 0, 0, 0)),
            pl.BlockSpec(coeffs.shape, lambda j: (0, 0, 0)),
        ],
        out_specs=pl.BlockSpec((None, lon_cols, rows), lambda j: (j, 0, 0)),
        compiler_params=pltpu.CompilerParams(vmem_limit_bytes=VMEM_LIMIT),
        cost_estimate=pl.CostEstimate(
            flops=2 * NLON * lon_count * width * rows,
            bytes_accessed=trig.size * 2 + 2 * coeffs.size * 4,
            transcendentals=0,
        ),
        name="grid_field",
    )(trig, coeffs)


def trig_table(pair_count, lon_count, lon_cols):
    pair_pad = pad_to(pair_count, SUBS)
    block_ids = jnp.arange(lon_count, dtype=jnp.int32)[:, None, None, None]
    half_ids = jnp.arange(2, dtype=jnp.int32)[None, :, None, None]
    part_ids = jnp.arange(2, dtype=jnp.int32)[None, None, :, None]
    pair_ids = block_ids * pair_count + jnp.arange(pair_pad, dtype=jnp.int32)
    order = jnp.where(half_ids == 0, pair_ids, NM - 1 - pair_ids) + 0 * part_ids
    order = order.reshape(lon_count, 4 * pair_pad)
    is_sine = jnp.broadcast_to(part_ids, (lon_count, 2, 2, pair_pad)).reshape(lon_count, -1) == 1

    def angles(column_ids):
        phase_ids = order[:, None, :] * column_ids[None, :, None] % NLON
        phase = phase_ids.astype(jnp.float32) * (2.0 * jnp.pi / NLON)
        return jnp.cos(phase), jnp.sin(phase)

    fine_total = 20
    fine_cos, fine_sin = angles(jnp.arange(fine_total, dtype=jnp.int32))
    coarse_cos, coarse_sin = angles(jnp.arange(0, NLON, fine_total, dtype=jnp.int32))
    left = jnp.where(is_sine[:, None, :], coarse_sin, coarse_cos)
    right = jnp.where(is_sine[:, None, :], coarse_cos, -coarse_sin)
    table = left[:, :, None, :] * fine_cos[:, None] + right[:, :, None, :] * fine_sin[:, None]
    table = table.astype(jnp.bfloat16)
    table = table.reshape(lon_count, lon_count, lon_cols, 4 * pair_pad)
    return jnp.transpose(table, (1, 0, 2, 3))


def gelu_parts(preact):
    scale = math.sqrt(2.0 / math.pi)
    square = preact * preact
    bend = jnp.tanh(scale * (preact + 0.044715 * (square * preact)))
    half = 0.5 * (1.0 + bend)
    slope = half + (0.5 * preact) * (1.0 - bend * bend) * (
        scale * (1.0 + (3.0 * 0.044715) * square)
    )
    return preact * half, slope


def forward_kernel(latents_ref, w_ref, b_ref, slope_ref, hidden_t_ref, latents_t_ref):
    latents = latents_ref[...]
    preact = jnp.dot(latents, w_ref[...], preferred_element_type=jnp.float32) + b_ref[...]
    hidden, slope = gelu_parts(preact)
    slope_ref[...] = slope
    hidden_t_ref[...] = hidden.T.astype(jnp.bfloat16)
    latents_t_ref[...] = latents.T


def forward(latents, w_hidden, b_hidden):
    rows, cols, width = latents.shape
    cells = rows * cols
    return pl.pallas_call(
        forward_kernel,
        grid=(rows,),
        out_shape=(
            jax.ShapeDtypeStruct((rows, cols, width), jnp.float32),
            jax.ShapeDtypeStruct((rows, width, cols), jnp.bfloat16),
            jax.ShapeDtypeStruct((rows, width, cols), jnp.bfloat16),
        ),
        in_specs=[
            pl.BlockSpec((None, cols, width), lambda i: (i, 0, 0)),
            pl.BlockSpec((width, width), lambda i: (0, 0)),
            pl.BlockSpec((1, width), lambda i: (0, 0)),
        ],
        out_specs=(
            pl.BlockSpec((None, cols, width), lambda i: (i, 0, 0)),
            pl.BlockSpec((None, width, cols), lambda i: (i, 0, 0)),
            pl.BlockSpec((None, width, cols), lambda i: (i, 0, 0)),
        ),
        compiler_params=pltpu.CompilerParams(vmem_limit_bytes=VMEM_LIMIT),
        cost_estimate=pl.CostEstimate(
            flops=2 * cells * width * width,
            bytes_accessed=cells * width * 10,
            transcendentals=cells * width,
        ),
        name="forward",
    )(latents, w_hidden, b_hidden.reshape(1, width))


def backward_kernel(
    grid_ref, scale_ref, place_ref, w_out_ref, slope_ref, hidden_t_ref, latents_t_ref,
    preact_ref, sums_ref, field_ref, hidden_acc, out_acc, bias_acc, *, sum_rows,
):
    index = pl.program_id(0)
    total = pl.num_programs(0)
    blocks = grid_ref.shape[0]
    rows = field_ref.shape[0]
    width = hidden_acc.shape[0]

    @pl.when(index == 0)
    def _():
        field = None
        for block in range(blocks):
            scaled = (grid_ref[block] * scale_ref[block]).astype(jnp.bfloat16)
            part = jnp.dot(scaled, place_ref[block], preferred_element_type=jnp.float32)
            field = part if field is None else field + part
        field = field.astype(jnp.bfloat16)
        for row in range(rows):
            field_ref[row] = field[:, row * LANES : (row + 1) * LANES]
        hidden_acc[...] = jnp.zeros_like(hidden_acc)
        out_acc[...] = jnp.zeros_like(out_acc)
        bias_acc[...] = jnp.zeros_like(bias_acc)

    field = field_ref[index]
    back = jnp.dot(field, w_out_ref[...], preferred_element_type=jnp.float32)
    preact_back = (back * slope_ref[...]).astype(jnp.bfloat16)
    preact_ref[...] = preact_back
    hidden_acc[...] += jnp.dot(
        latents_t_ref[...], preact_back, preferred_element_type=jnp.float32
    )
    out_acc[...] += jnp.dot(hidden_t_ref[...], field, preferred_element_type=jnp.float32)
    bias_acc[...] += jnp.sum(preact_back.astype(jnp.float32), axis=0, keepdims=True)

    @pl.when(index == total - 1)
    def _():
        tiles = width // LANES
        for row_tile in range(width // SUBS):
            for tile in range(tiles):
                sums_ref[pl.ds((row_tile * tiles + tile) * SUBS, SUBS), :] = hidden_acc[
                    pl.ds(row_tile * SUBS, SUBS), pl.ds(tile * LANES, LANES)
                ]
        base = width * tiles
        flipped = out_acc[...].T
        for tile in range(tiles):
            sums_ref[pl.ds(base + tile * F, F), :] = flipped[:F, tile * LANES : (tile + 1) * LANES]
        base = base + tiles * F
        sums_ref[pl.ds(base, sum_rows - base), :] = jnp.zeros((sum_rows - base, LANES), jnp.float32)
        for tile in range(tiles):
            sums_ref[pl.ds(base + tile, 1), :] = bias_acc[:, tile * LANES : (tile + 1) * LANES]


def backward(grid, scale, place, w_out_t, slope, hidden_t, latents_t, sum_rows):
    rows, cols, width = slope.shape
    blocks, _, lanes = grid.shape
    cells = rows * cols
    return pl.pallas_call(
        functools.partial(backward_kernel, sum_rows=sum_rows),
        grid=(rows,),
        out_shape=(
            jax.ShapeDtypeStruct((rows, cols, width), jnp.bfloat16),
            jax.ShapeDtypeStruct((sum_rows, LANES), jnp.float32),
        ),
        in_specs=[
            pl.BlockSpec(grid.shape, lambda i: (0, 0, 0)),
            pl.BlockSpec(scale.shape, lambda i: (0, 0, 0)),
            pl.BlockSpec(place.shape, lambda i: (0, 0, 0)),
            pl.BlockSpec(w_out_t.shape, lambda i: (0, 0)),
            pl.BlockSpec((None, cols, width), lambda i: (i, 0, 0)),
            pl.BlockSpec((None, width, cols), lambda i: (i, 0, 0)),
            pl.BlockSpec((None, width, cols), lambda i: (i, 0, 0)),
        ],
        out_specs=(
            pl.BlockSpec((None, cols, width), lambda i: (i, 0, 0)),
            pl.BlockSpec((sum_rows, LANES), lambda i: (0, 0)),
        ),
        scratch_shapes=[
            pltpu.VMEM((rows, cols, LANES), jnp.bfloat16),
            pltpu.VMEM((width, width), jnp.float32),
            pltpu.VMEM((width, LANES), jnp.float32),
            pltpu.VMEM((1, width), jnp.float32),
        ],
        compiler_params=pltpu.CompilerParams(vmem_limit_bytes=VMEM_LIMIT),
        cost_estimate=pl.CostEstimate(
            flops=2 * cells * width * (width + 2 * LANES),
            bytes_accessed=cells * width * 10,
            transcendentals=0,
        ),
        name="backward",
    )(grid, scale, place, w_out_t, slope, hidden_t, latents_t)


def local(spectra, field_slot, field_weight, latents, w_hidden, b_hidden, w_out):
    slot_count, _, pair_count, _ = spectra.shape
    lat_rows, lon_cols, width = latents.shape
    lat_count = lax.axis_size("lat")
    lon_count = lax.axis_size("lon")
    rows_all = lat_rows * lat_count
    lat_index = lax.axis_index("lat")
    lon_index = lax.axis_index("lon")
    pair_pad = pad_to(pair_count, SUBS)

    first_pair = (lon_index * pair_count).astype(jnp.int32).reshape(1)
    coeffs = coefficients(spectra, first_pair, rows_all, lat_rows)
    share = slot_count * lat_rows // lon_count
    coeffs = coeffs.reshape(lat_count * lon_count, share, 4 * pair_pad)
    coeffs = lax.all_to_all(coeffs, ("lat", "lon"), split_axis=0, concat_axis=0, tiled=True)

    slope, hidden_t, latents_t = forward(latents, w_hidden, b_hidden)
    trig = trig_table(pair_count, lon_count, lon_cols)

    lanes = lat_count * share
    lane_ids = jnp.arange(lanes, dtype=jnp.int32)[None, :]
    block_ids = jnp.arange(lon_count, dtype=jnp.int32)[:, None]
    line = block_ids * share + lane_ids % share
    slot_ids = (lane_ids // share) * slot_count + line // lat_rows
    row_ids = line % lat_rows
    field_ids = field_slot[slot_ids]
    sine = jnp.sin(band_angles(lat_index * lat_rows + row_ids, rows_all))
    scale = (sine * field_weight[field_ids])[:, None, :]
    target = row_ids * LANES + field_ids
    place = (
        target[:, :, None] == jnp.arange(lat_rows * LANES, dtype=jnp.int32)[None, None, :]
    ).astype(jnp.bfloat16)
    w_out_t = jnp.concatenate([w_out.T, jnp.zeros((LANES - F, width), w_out.dtype)], axis=0)

    grid = grid_field(trig, coeffs, lon_count, lon_cols)
    grid = lax.all_to_all(grid, "lon", split_axis=0, concat_axis=0, tiled=True)

    device_count = lat_count * lon_count
    used_rows = width * width // LANES + F * width // LANES + width // LANES
    chunk = pad_to(pad_to(used_rows, device_count) // device_count, SUBS)
    sum_rows = chunk * device_count
    preact_back, sums = backward(
        grid, scale, place, w_out_t, slope, hidden_t, latents_t, sum_rows
    )
    latent_grad = lax.dot_general(
        preact_back, w_hidden, (((2,), (1,)), ((), ())), preferred_element_type=jnp.float32
    ).astype(jnp.bfloat16)

    sums = sums.reshape(lon_count, lat_count * chunk, LANES)
    sums = lax.all_to_all(sums, "lon", split_axis=0, concat_axis=0, tiled=True)
    sums = jnp.sum(sums, axis=0).reshape(lat_count, chunk, LANES)
    sums = lax.all_to_all(sums, "lat", split_axis=0, concat_axis=0, tiled=True)
    sums = jnp.sum(sums, axis=0) / math.sqrt(rows_all * NLON)
    sums = jnp.broadcast_to(sums[None], (lat_count, chunk, LANES))
    sums = lax.all_to_all(sums, "lat", split_axis=0, concat_axis=0, tiled=True)
    sums = jnp.broadcast_to(sums.reshape(1, lat_count * chunk, LANES), (lon_count, lat_count * chunk, LANES))
    sums = lax.all_to_all(sums, "lon", split_axis=0, concat_axis=0, tiled=True)
    sums = sums.reshape(sum_rows, LANES)

    tiles = width // LANES
    hidden_rows = width * tiles
    out_rows = F * tiles
    hidden_grad = (
        sums[:hidden_rows]
        .reshape(width // SUBS, tiles, SUBS, LANES)
        .transpose(0, 2, 1, 3)
        .reshape(width, width)
    )
    out_grad = (
        sums[hidden_rows : hidden_rows + out_rows]
        .reshape(tiles, F, LANES)
        .transpose(0, 2, 1)
        .reshape(width, F)
    )
    bias_grad = sums[hidden_rows + out_rows : hidden_rows + out_rows + tiles].reshape(width)
    return (latent_grad, hidden_grad, bias_grad, out_grad)


def solution(mesh):
    in_specs = (P("lat", None, "lon", None), P(), P(), P("lat", "lon", None), P(), P(), P())
    out_specs = (P("lat", "lon", None), P(), P(), P())
    return jax.shard_map(local, mesh=mesh, in_specs=in_specs, out_specs=out_specs, check_vma=False)
```

time: 938 us -> 177 us (0.19)
  local copies, waits for them, and re-layouts: 303 us -> 22.6 us
  other arithmetic: 290 us -> 12.3 us
  waiting for transfers between devices: 192 us -> 11.4 us
  matrix products: 68.5 us -> 5.19 us
  Pallas kernels: 0 us -> 59.1 us
  loops' own time: 14.8 us -> 0 us
  between operations: 14.2 us -> 0.83 us
  blocking collectives: 39.6 us -> 50.2 us
    while x713 -> x0, other arithmetic: 260 us -> none
    psum x1 -> x0, waiting for transfers between devices: 126 us -> none  [local(): lax.psum((hidden_sum, bias_sum, out_sum), ('lat', 'lon'))]
    mul x94 -> x1, local copies, waits for them, and re-layouts: 123 us -> 0.09 us  [angles(): phase_ids = order[:, None, :] * column_ids[None, :, None] % NLON]
    broadcast_in_dim x69 -> x2, local copies, waits for them, and re-layouts: 80.6 us -> 1.2 us  [the longest x1 1.18 us: local(): jnp.broadcast_to(sums.reshape(1, lat_count * chunk, LANES), (lon_count, l...]
    dot_general x10 -> x1, matrix products: 68.5 us -> 5.19 us  [local(): lax.dot_general(preact_back, w_hidden, (((2,), (1,)), ((), ())), preferre...]
    pallas_call x0 -> x4, Pallas kernels: none -> 59.1 us  [the longest x1 30.3 us: coefficients(): pl.pallas_call(kernel, out_shape=jax.ShapeDtypeStruct((lat_count, slot_co...]
    all_to_all x1 -> x3, waiting for transfers between devices: 66.4 us -> 11.4 us  [the longest x1 11.4 us: local(): sums = lax.all_to_all(sums, 'lon', split_axis=0, concat_axis=0, tiled=True)]
    all_to_all x0 -> x3, blocking collectives: none -> 50.2 us  [the longest x2 29.3 us: local(): sums = lax.all_to_all(sums, 'lat', split_axis=0, concat_axis=0, tiled=True)]
  transfers between devices with their start and end apart: 2 -> 3, of which waited for: 2 -> 1; matrix products, arithmetic and copies ran while one was open for 1% -> 17% of each run, Pallas kernels for 0% -> 6%
where the time goes in v1:
time: 177 us; the launch traced here: 176 us
  Pallas kernels  59.1 us (33%)
  blocking collectives  50.2 us (28%)
  local copies, waits for them, and re-layouts  22.6 us (13%)
  starting transfers between devices  14.8 us (8%)
  other arithmetic  12.3 us (7%)
  waiting for transfers between devices  11.4 us (6%)
  matrix products  5.19 us (3%)
    pallas_call x1, Pallas kernels, coefficients(): pl.pallas_call(kernel, out_shape=jax.ShapeDtypeStruct((lat_count, slot_co...  30.3 us
    all_to_all x2, blocking collectives, local(): sums = lax.all_to_all(sums, 'lat', split_axis=0, concat_axis=0, tiled=True)  29.3 us
    all_to_all x1, blocking collectives, local(): sums = lax.all_to_all(sums, 'lon', split_axis=0, concat_axis=0, tiled=True)  20.9 us
    pallas_call x1, Pallas kernels, backward(): pl.pallas_call(functools.partial(backward_kernel, sum_rows=sum_rows), gri...  12.9 us
    all_to_all x1, waiting for transfers between devices, local(): sums = lax.all_to_all(sums, 'lon', split_axis=0, concat_axis=0, tiled=True)  11.4 us
    pallas_call x1, Pallas kernels, forward(): pl.pallas_call(forward_kernel, grid=(rows,), out_shape=(jax.ShapeDtypeStr...  10.6 us
    all_to_all x1, starting transfers between devices, local(): lax.all_to_all(coeffs, ('lat', 'lon'), split_axis=0, concat_axis=0, tiled...  7.3 us
    unnamed x13, local copies, waits for them, and re-layouts  6.62 us
  transfers between devices with their start and end apart: 3, of which 1 were waited for; matrix products, arithmetic and copies ran while one was open for 17% of the time, Pallas kernels for 6%

profile of v1, /device:TPU:0, one launch (start us, length us, event | category | flops | bytes accessed | tf_op | source)
XLA Modules:
  0.0 176.4 jit_solution(9707372459558017382)
XLA Ops:
  0.6 4.8 %copy.18 = f32[8,2,90,721]{3,2,1,0:T(8,128)} copy(f32[8,2,90,721]{3,1,2,0:T(2,128)} %param.7) | data formatting | bytes 8305920 | tf_op args[0]
  5.5 30.3 %coefficients.1 = f32[8,64,384]{2,1,0:T(8,128)} custom-call(s32[1]{0:T(128)} %bitcast.2.first_ref, f32[16,90,721]{2,1,0:T(8,128)} %bitcast.40), custom_call_target="tpu_custom_call" | custom-call | tf_op jit(solution)/shard_map/coefficients/pallas_call | solution.py:218
  35.8 7.3 %all-to-all-start = ((f32[32,16,384]{2,1,0:T(8,128)}), f32[32,16,384]{2,1,0:T(8,128)S(1)}, u32[]{:S(2)}, u32[]{:S(2)}) async-start(f32[32,16,384]{2,1,0:T(8,128)} %bitcast.46), calls=%async_computation | async-start | bytes 1572864 | tf_op jit(solution)/shard_map/all_to_all | solution.py:461
  43.5 1.1 fusion.16
  44.6 4.1 %fusion.9 = (f32[4,72,384]{2,0,1:T(4,128)S(1)}, f32[4,72,384]{2,0,1:T(4,128)S(1)}) fusion(s32[72]{0:T(128)S(1)} %iota_multiply_fusion.1, s32[4,384]{1,0:T(4,128)S(1)} %mul.169, pred[384]{0:T(512)(128)(4,1)S(1)} %eq.42), kind=kLoop, calls=%fused_computation.18 | loop fusion | flops 1327104 | bytes 891552 | tf_op jit(solution)/shard_map/jit(_where)/select_n | solution.py:296
  48.7 4.7 %add_convert_fusion = bf16[4,72,20,384]{3,0,2,1:T(4,128)(2,1)} fusion(f32[4,20,384]{2,0,1:T(4,128)S(1)} %get-tuple-element.17, f32[4,72,384]{2,0,1:T(4,128)S(1)} %get-tuple-element.15, f32[4,20,384]{2,0,1:T(4,128)S(1)} %get-tuple-element.16, f32[4,72,384]{2,0,1:T(4,128)S(1)} %get-tuple-element.14), kind=kLoop, calls=%fused_computation.2 | loop fusion | flops 8847360 | bytes 5554176 | tf_op jit(solution)/shard_map/convert_element_type | solution.py:299
  53.4 4.9 %copy.23 = bf16[4,4,360,384]{3,2,0,1:T(8,128)(2,1)} copy(bf16[4,4,360,384]{3,0,2,1:T(4,128)(2,1)} %bitcast.42) | data formatting | bytes 8847360 | tf_op jit(solution)/shard_map/convert_element_type | solution.py:299
  58.5 3.3 %gather_fusion = s32[512]{0:T(512)S(1)} fusion(s32[64]{0:T(128)S(1)} %copy-done, s32[1024]{0:T(1024)S(1)} %pad_clamp_fusion.1), kind=kCustom, calls=%fused_computation | custom fusion | bytes 6144 | tf_op jit(solution)/shard_map/gather | solution.py:472
  61.9 3.3 %gather_fusion.1 = f32[512]{0:T(512)S(1)} fusion(f32[64]{0:T(128)S(1)} %copy-done.1, s32[1024]{0:T(1024)S(1)} %pad_clamp_fusion), kind=kCustom, calls=%fused_computation.1 | custom fusion | bytes 6144 | tf_op jit(solution)/shard_map/gather | solution.py:474
  66.0 0.9 copy-done.2
  66.9 5.2 %grid_field.1 = f32[4,360,128]{2,1,0:T(8,128)} custom-call(bf16[4,4,360,384]{3,2,1,0:T(8,128)(2,1)} %bitcast.41, f32[32,16,384]{2,1,0:T(8,128)} %copy-done.2), custom_call_target="tpu_custom_call" | custom-call | flops 566231040 | bytes 5996544 | tf_op jit(solution)/shard_map/grid_field/pallas_call | solution.py:259
  72.1 3.9 %all-to-all-start.1 = ((f32[4,360,128]{2,1,0:T(8,128)}), f32[4,360,128]{2,1,0:T(8,128)S(1)}, u32[]{:S(2)}, u32[]{:S(2)}) async-start(f32[4,360,128]{2,1,0:T(8,128)} %grid_field.1), calls=%async_computation.1 | async-start | bytes 1474560 | tf_op jit(solution)/shard_map/all_to_all | solution.py:482
  76.1 10.6 %forward.1 = (f32[8,360,512]{2,1,0:T(8,128)}, bf16[8,512,360]{2,1,0:T(8,128)(2,1)}, bf16[8,512,360]{2,1,0:T(8,128)(2,1)}) custom-call(bf16[8,360,512]{2,1,0:T(8,128)(2,1)} %latents_ref.1, bf16[512,512]{1,0:T(8,128)(2,1)} %w_ref.1, f32[1,512]{1,0:T(1,128)} %bitcast.55), custom_call_target="tpu_custom_call" | custom-call | flops 1509949440 | bytes 14745600 | tf_op jit(solution)/shard_map/forward/pallas_call | solution.py:327
  87.3 1.2 fusion.place_ref
  88.6 0.9 copy-done.3
  89.4 12.9 %backward.1 = (bf16[8,360,512]{2,1,0:T(8,128)(2,1)}, f32[2560,128]{1,0:T(8,128)}) custom-call(f32[4,360,128]{2,1,0:T(8,128)} %copy-done.3, f32[4,1,128]{2,1,0:T(1,128)} %fusion.23.scale_ref, bf16[4,128,1024]{2,1,0:T(8,128)(2,1)} %fusion.place_ref, bf16[128,512]{1,0:T(8,128)(2,1)} %concatenate.3.w_out_ref, f32[8,360,512]{2,1,0:T(8,128)} %get-tuple-element.9.slope_ref, ...), custom_call_target="tpu_custom_call" | custom-call | flops 2264924160 | bytes 14745600 | tf_op jit(solution)/shard_map/backward/pallas_call | solution.py:411
  102.4 20.9 %all_to_all.30 = f32[4,640,128]{2,1,0:T(8,128)S(1)} all-to-all(f32[4,640,128]{2,1,0:T(8,128)} %bitcast.47), channel_id=1, replica_groups=mesh['lat'=8,'lon'=4] {'lon'}, dimensions={0} | all-to-all | bytes 2621440 | tf_op jit(solution)/shard_map/all_to_all | solution.py:496
  123.4 15.8 %all_to_all.31 = f32[8,80,128]{2,1,0:T(8,128)S(1)} all-to-all(f32[8,80,128]{2,1,0:T(8,128)S(1)} %bitcast.48), channel_id=1, replica_groups=mesh['lat'=8,'lon'=4] {'lat'}, dimensions={0} | all-to-all | bytes 655360 | tf_op jit(solution)/shard_map/all_to_all | solution.py:498
  139.2 13.5 %all_to_all.32 = f32[8,80,128]{2,1,0:T(8,128)S(1)} all-to-all(f32[8,80,128]{2,1,0:T(8,128)S(1)} %broadcast_in_dim.48), channel_id=1, replica_groups=mesh['lat'=8,'lon'=4] {'lat'}, dimensions={0} | all-to-all | bytes 655360 | tf_op jit(solution)/shard_map/all_to_all | solution.py:501
  152.7 1.2 broadcast_in_dim.50
  153.9 3.5 %all-to-all-start.5 = ((f32[4,640,128]{2,1,0:T(8,128)}), f32[4,640,128]{2,1,0:T(8,128)S(1)}, u32[]{:S(2)}, u32[]{:S(2)}) async-start(f32[4,640,128]{2,1,0:T(8,128)} %broadcast_in_dim.50), calls=%async_computation.5 | async-start | bytes 2621440 | tf_op jit(solution)/shard_map/all_to_all | solution.py:503
  157.5 5.2 %convolution_convert_fusion = bf16[8,360,512]{2,1,0:T(8,128)(2,1)} fusion(bf16[8,360,512]{2,1,0:T(8,128)(2,1)} %get-tuple-element.12, bf16[512,512]{1,0:T(8,128)(2,1)S(1)} %copy-done.5), kind=kOutput, calls=%fused_computation.4 | convolution fusion | flops 1511424000 | bytes 6422528 | tf_op jit(solution)/shard_map/dot_general | solution.py:491
  162.6 11.4 %all-to-all-done.5 = f32[4,640,128]{2,1,0:T(8,128)S(1)} async-done(((f32[4,640,128]{2,1,0:T(8,128)}), f32[4,640,128]{2,1,0:T(8,128)S(1)}, u32[]{:S(2)}, u32[]{:S(2)}) %all-to-all-start.5) | async-done | bytes 1310752 | tf_op jit(solution)/shard_map/all_to_all | solution.py:503
  174.7 1.0 slice.16
  (38 shorter events, 3.4 us)
Async XLA Ops:
  0.6 57.8 %copy-start = (s32[64]{0:T(128)S(1)}, s32[64]{0:T(128)}, u32[]{:S(2)}) copy-start(s32[64]{0:T(128)} %param.8) | copy-start | bytes 772
  35.8 30.1 %all-to-all-start = ((f32[32,16,384]{2,1,0:T(8,128)}), f32[32,16,384]{2,1,0:T(8,128)S(1)}, u32[]{:S(2)}, u32[]{:S(2)}) async-start(f32[32,16,384]{2,1,0:T(8,128)} %bitcast.46), calls=%async_computation | async-start | bytes 1572864 | tf_op jit(solution)/shard_map/all_to_all | solution.py:461
  58.4 3.5 %copy-start.1 = (f32[64]{0:T(128)S(1)}, f32[64]{0:T(128)}, u32[]{:S(2)}) copy-start(f32[64]{0:T(128)} %param.9) | copy-start | bytes 772
  58.4 6.9 %copy-start.4 = (bf16[512,64]{0,1:T(8,128)(2,1)S(1)}, bf16[512,64]{0,1:T(8,128)(2,1)}, u32[]{:S(2)}) copy-start(bf16[512,64]{0,1:T(8,128)(2,1)} %param.13) | copy-start | bytes 196612
  66.0 0.9 copy-start.2
  72.1 16.4 %all-to-all-start.1 = ((f32[4,360,128]{2,1,0:T(8,128)}), f32[4,360,128]{2,1,0:T(8,128)S(1)}, u32[]{:S(2)}, u32[]{:S(2)}) async-start(f32[4,360,128]{2,1,0:T(8,128)} %grid_field.1), calls=%async_computation.1 | async-start | bytes 1474560 | tf_op jit(solution)/shard_map/all_to_all | solution.py:482
  88.5 0.9 copy-start.3
  123.3 34.1 %copy-start.5 = (bf16[512,512]{1,0:T(8,128)(2,1)S(1)}, bf16[512,512]{1,0:T(8,128)(2,1)}, u32[]{:S(2)}) copy-start(bf16[512,512]{1,0:T(8,128)(2,1)} %w_ref.1) | copy-start | bytes 1572868
  153.9 20.2 %all-to-all-start.5 = ((f32[4,640,128]{2,1,0:T(8,128)}), f32[4,640,128]{2,1,0:T(8,128)S(1)}, u32[]{:S(2)}, u32[]{:S(2)}) async-start(f32[4,640,128]{2,1,0:T(8,128)} %broadcast_in_dim.50), calls=%async_computation.5 | async-start | bytes 2621440 | tf_op jit(solution)/shard_map/all_to_all | solution.py:503

commit v2 on v1

v2 whole, which is shorter than its diff:
```python
import functools
import math

import jax
import jax.numpy as jnp
from jax import lax
from jax.experimental import pallas as pl
from jax.experimental.pallas import tpu as pltpu
from jax.sharding import PartitionSpec as P

NM = 720
NLON = 1440
F = 64
LANES = 128
SUBS = 8
STEPS = NM + 1
PAIRS = 4
TABLE_ROWS = 728
VMEM_LIMIT = 56 * 1024 * 1024


def band_angles(row_ids, rows_all):
    return jnp.pi * (NM // 2 - rows_all // 2 + row_ids.astype(jnp.float32)) / NM


def pad_to(value, multiple):
    return (value + multiple - 1) // multiple * multiple


def coeff_kernel(
    first_ref, spectra_hbm, out_ref, spectra_ref, grow_ref, shrink_ref, table_ref, stage_ref,
    copy_sem, *, pair_count, rows_all, lat_rows, slot_count,
):
    per_block = LANES // rows_all
    vregs = pad_to(pair_count, SUBS * per_block) // (SUBS * per_block)
    step_tile = rows_all
    tile_total = pad_to(STEPS, step_tile) // step_tile
    pair_pad = pad_to(pair_count, SUBS)
    lat_count = rows_all // lat_rows
    first_pair = first_ref[0]

    fetch = pltpu.make_async_copy(spectra_hbm, spectra_ref, copy_sem)
    fetch.start()

    lane = lax.broadcasted_iota(jnp.int32, (SUBS, LANES), 1)
    sub = lax.broadcasted_iota(jnp.int32, (SUBS, LANES), 0)
    inner = lane & (rows_all - 1)
    which = lane // rows_all
    colatitude = band_angles(inner, rows_all)
    cosine = jnp.cos(colatitude)
    log_sine = jnp.log(jnp.sin(colatitude))

    def log_total(order_column):
        total = jnp.zeros((SUBS, LANES), jnp.float32)
        for tile in range(pad_to(NM, LANES) // LANES):
            term = (lane + tile * LANES).astype(jnp.float32)
            safe = jnp.maximum(term, 1.0)
            value = jnp.log((2.0 * safe + 1.0) / (2.0 * safe))
            total = total + jnp.where((term >= 1.0) & (term <= order_column), value, 0.0)
        return jnp.sum(total, axis=1, keepdims=True)

    def seed(order_of):
        total = jnp.zeros((SUBS, LANES), jnp.float32)
        for part in range(per_block):
            column = order_of(part).astype(jnp.float32)
            total = jnp.where(which == part, log_total(column), total)
        order = order_of(which).astype(jnp.float32)
        return jnp.exp(0.5 * total - 0.5 * math.log(4.0 * math.pi) + order * log_sine)

    firsts, seconds, switches = [], [], []
    for v in range(vregs):
        base = first_pair + (sub + v * SUBS) * per_block

        def order_first(part, base=base):
            return base + part

        def order_second(part, base=base):
            return NM - 1 - (base + part)

        firsts.append(seed(order_first))
        seconds.append(seed(order_second))
        pair = base + which
        switch = NM - pair
        switches.append(switch)
        for tile in range(tile_total):
            step = inner + tile * step_tile
            in_first = step < switch
            order = jnp.where(in_first, pair, NM - 1 - pair).astype(jnp.float32)
            degree = jnp.where(in_first, pair + step, step - 1).astype(jnp.float32)
            lower = degree - 1.0
            grow = jnp.sqrt(
                (4.0 * degree * degree - 1.0) / jnp.maximum(degree * degree - order * order, 1.0)
            )
            shrink = jnp.sqrt(
                jnp.maximum(lower * lower - order * order, 0.0)
                / jnp.maximum(4.0 * lower * lower - 1.0, 1.0)
            )
            start = step == 0
            grow_ref[tile, pl.ds(v * SUBS, SUBS), :] = jnp.where(start, 1.0, grow)
            shrink_ref[tile, pl.ds(v * SUBS, SUBS), :] = jnp.where(start, -1.0, shrink)

    def advance(tile, offset, state, grows, shrinks):
        previous, before = state
        index = which * rows_all + offset
        step = tile * step_tile + offset
        produced = []
        for v in range(vregs):
            grow = jnp.take_along_axis(grows[v], index, axis=1)
            shrink = jnp.take_along_axis(shrinks[v], index, axis=1)
            value = grow * (cosine * previous[v] - shrink * before[v])
            value = jnp.where(switches[v] == step, seconds[v], value)
            table_ref[pl.ds(v * SUBS * TABLE_ROWS + step, SUBS, stride=TABLE_ROWS), :] = value
            produced.append(value)
        return (tuple(produced), previous)

    def run_tile(tile, state, count, unroll):
        grows = [grow_ref[tile, pl.ds(v * SUBS, SUBS), :] for v in range(vregs)]
        shrinks = [shrink_ref[tile, pl.ds(v * SUBS, SUBS), :] for v in range(vregs)]

        def body(offset, carry):
            return advance(tile, offset, carry, grows, shrinks)

        return lax.fori_loop(0, count, body, state, unroll=unroll)

    zeros = tuple(jnp.zeros((SUBS, LANES), jnp.float32) for _ in range(vregs))
    state = (zeros, tuple(firsts))
    whole_tiles = STEPS // step_tile
    state = lax.fori_loop(
        0, whole_tiles, lambda tile, carry: run_tile(tile, carry, step_tile, 8), state
    )
    if STEPS % step_tile:
        run_tile(whole_tiles, state, STEPS % step_tile, STEPS % step_tile % 16)

    for row in range(slot_count):
        for half in range(2):
            stage_ref[row, pl.ds((half + 1) * 2 * pair_pad - 2 * SUBS, 2 * SUBS), :] = jnp.zeros(
                (2 * SUBS, LANES), jnp.float32
            )
    fetch.wait()

    rows_half = slot_count * SUBS
    edges = (0, 256, 512, STEPS)
    dot = functools.partial(jnp.dot, preferred_element_type=jnp.float32)

    def split_parts(values):
        high = values.astype(jnp.bfloat16)
        low = (values - high.astype(jnp.float32)).astype(jnp.bfloat16)
        return high, low

    def product(left, right):
        left_high, left_low = split_parts(left)
        right_high, right_low = split_parts(right)
        if left.shape[1] % LANES:
            return (
                dot(left_high, right_high) + dot(left_low, right_high) + dot(left_high, right_low)
            )
        return dot(
            jnp.concatenate([left_high, left_low, left_high], axis=1),
            jnp.concatenate([right_high, right_high, right_low], axis=0),
        )

    def group(start):
        values = spectra_ref[:, pl.ds(start, PAIRS), :, :].reshape(slot_count, SUBS, STEPS)
        step = lax.broadcasted_iota(jnp.int32, (1, SUBS, STEPS), 2)
        row_pair = lax.broadcasted_iota(jnp.int32, (1, SUBS, STEPS), 1) // 2
        in_first = step < NM - (first_pair + start + row_pair)
        lower = jnp.where(in_first, values, 0.0)
        upper = jnp.where(in_first, 0.0, values)
        first_block = start // per_block
        blocks = PAIRS // per_block
        table = jnp.concatenate(
            [table_ref[pl.ds((first_block + n) * TABLE_ROWS, STEPS), :] for n in range(blocks)],
            axis=1,
        )
        begin, end = edges[0], edges[1]
        base = product(
            values[:, :, begin:end].reshape(rows_half, end - begin), table[begin:end]
        )
        rest = None
        for begin, end in zip(edges[1:-1], edges[2:]):
            left = jnp.concatenate([lower[:, :, begin:end], upper[:, :, begin:end]], axis=0)
            part = product(left.reshape(2 * rows_half, end - begin), table[begin:end])
            rest = part if rest is None else rest + part
        both = jnp.concatenate([rest[:rows_half] + base, rest[rows_half:]], axis=0)
        row_id = lax.broadcasted_iota(jnp.int32, (2 * rows_half, LANES), 0) % SUBS // 2
        lane_part = lax.broadcasted_iota(jnp.int32, (2 * rows_half, LANES), 1) // rows_all
        total = jnp.zeros((2 * rows_half, LANES), jnp.float32)
        for block in range(blocks):
            keep = row_id == block * per_block + lane_part
            total = total + jnp.where(keep, both[:, block * LANES : (block + 1) * LANES], 0.0)
        if per_block == 2:
            total = total + pltpu.roll(total, rows_all, 1)
        total = total.astype(jnp.bfloat16).astype(jnp.float32)
        for half in range(2):
            for row in range(slot_count):
                source = (half * slot_count + row) * SUBS
                stage_ref[row, pl.ds(half * 2 * pair_pad + 2 * start, SUBS), :] = total[
                    source : source + SUBS
                ]

    def group_body(index, carry):
        group(index * PAIRS)
        return carry

    lax.fori_loop(0, pair_count // PAIRS, group_body, 0)
    if pair_count % PAIRS:
        group(pair_count - PAIRS)

    for row in range(slot_count):
        flipped = stage_ref[row].T
        out_ref[:, pl.ds(row * lat_rows, lat_rows), :] = flipped[:rows_all].reshape(
            lat_count, lat_rows, 4 * pair_pad
        )


def coefficients(spectra, first_pair, rows_all, lat_rows):
    slot_count, _, pair_count, steps = spectra.shape
    per_block = LANES // rows_all
    vregs = pad_to(pair_count, SUBS * per_block) // (SUBS * per_block)
    tile_total = pad_to(STEPS, rows_all) // rows_all
    pair_pad = pad_to(pair_count, SUBS)
    lat_count = rows_all // lat_rows
    kernel = functools.partial(
        coeff_kernel, pair_count=pair_count, rows_all=rows_all, lat_rows=lat_rows,
        slot_count=slot_count,
    )
    return pl.pallas_call(
        kernel,
        out_shape=jax.ShapeDtypeStruct(
            (lat_count, slot_count * lat_rows, 4 * pair_pad), jnp.float32
        ),
        in_specs=[
            pl.BlockSpec(memory_space=pltpu.SMEM),
            pl.BlockSpec(memory_space=pl.ANY),
        ],
        out_specs=pl.BlockSpec(memory_space=pltpu.VMEM),
        scratch_shapes=[
            pltpu.VMEM((slot_count, pair_count, 2, steps), jnp.float32),
            pltpu.VMEM((tile_total, vregs * SUBS, LANES), jnp.float32),
            pltpu.VMEM((tile_total, vregs * SUBS, LANES), jnp.float32),
            pltpu.VMEM((vregs * SUBS * TABLE_ROWS, LANES), jnp.float32),
            pltpu.VMEM((slot_count, 4 * pair_pad, LANES), jnp.float32),
            pltpu.SemaphoreType.DMA,
        ],
        compiler_params=pltpu.CompilerParams(vmem_limit_bytes=VMEM_LIMIT),
        name="coefficients",
    )(first_pair, jnp.transpose(spectra, (0, 2, 1, 3)))


def trig_kernel(out_ref, *, pair_count, pair_pad, quarter, fine_total):
    block = pl.program_id(0)
    width = 4 * pair_pad
    coarse_total = pad_to(quarter // fine_total, SUBS)

    def orders(rows):
        lane = lax.broadcasted_iota(jnp.int32, (rows, width), 1)
        upper = lane >= 2 * pair_pad
        pair = jnp.where(upper, lane - 2 * pair_pad, lane)
        is_sine = (pair & 1) == 1
        pair = block * pair_count + (pair >> 1)
        return jnp.where(upper, NM - 1 - pair, pair), is_sine

    def angles(rows, spacing):
        order, _ = orders(rows)
        column = lax.broadcasted_iota(jnp.int32, (rows, width), 0) * spacing
        phase = (order * column % NLON).astype(jnp.float32) * (2.0 * math.pi / NLON)
        return jnp.cos(phase), jnp.sin(phase)

    fine_cos, fine_sin = angles(fine_total, 1)
    coarse_cos, coarse_sin = angles(coarse_total, fine_total)
    order, is_sine = orders(1)
    weights = []
    for turn in range(4):
        side = (order * turn) & 3
        even = jnp.where(side == 0, 1.0, jnp.where(side == 2, -1.0, 0.0))
        odd = jnp.where(side == 1, 1.0, jnp.where(side == 3, -1.0, 0.0))
        weights.append((jnp.where(is_sine, odd, even), jnp.where(is_sine, even, -odd)))
    for tile in range(quarter // fine_total):
        left, right = coarse_cos[tile : tile + 1], coarse_sin[tile : tile + 1]
        cosine = left * fine_cos - right * fine_sin
        sine = right * fine_cos + left * fine_sin
        for turn in range(4):
            on_cos, on_sin = weights[turn]
            out_ref[pl.ds(turn * quarter + tile * fine_total, fine_total), :] = (
                on_cos * cosine + on_sin * sine
            ).astype(jnp.bfloat16)


def trig_table(pair_count, lon_count):
    pair_pad = pad_to(pair_count, SUBS)
    quarter = NLON // 4
    fine_total = 40
    return pl.pallas_call(
        functools.partial(
            trig_kernel, pair_count=pair_count, pair_pad=pair_pad, quarter=quarter,
            fine_total=fine_total,
        ),
        grid=(lon_count,),
        out_shape=jax.ShapeDtypeStruct((lon_count, NLON, 4 * pair_pad), jnp.bfloat16),
        out_specs=pl.BlockSpec((None, NLON, 4 * pair_pad), lambda b: (b, 0, 0)),
        compiler_params=pltpu.CompilerParams(vmem_limit_bytes=VMEM_LIMIT),
        cost_estimate=pl.CostEstimate(
            flops=20 * lon_count * NLON * pair_pad,
            bytes_accessed=lon_count * NLON * 8 * pair_pad,
            transcendentals=0,
        ),
        name="trig_table",
    )()


def grid_kernel(trig_ref, coeff_ref, out_ref, right_ref, *, lon_count):
    share = coeff_ref.shape[1]
    width = coeff_ref.shape[2]
    rows = coeff_ref.shape[0] // lon_count * share

    @pl.when(pl.program_id(0) == 0)
    def _():
        values = coeff_ref[...].reshape(rows // share, lon_count, share, width)
        for block in range(lon_count):
            right_ref[block] = values[:, block].reshape(rows, width).T.astype(jnp.bfloat16)

    total = None
    for block in range(lon_count):
        part = jnp.dot(trig_ref[block], right_ref[block], preferred_element_type=jnp.float32)
        total = part if total is None else total + part
    out_ref[...] = total


def grid_field(trig, coeffs, lon_count):
    share = coeffs.shape[1]
    rows = coeffs.shape[0] // lon_count * share
    width = trig.shape[2]
    pieces = 4
    cols = NLON // pieces
    return pl.pallas_call(
        functools.partial(grid_kernel, lon_count=lon_count),
        grid=(pieces,),
        out_shape=jax.ShapeDtypeStruct((NLON, rows), jnp.float32),
        in_specs=[
            pl.BlockSpec((lon_count, cols, width), lambda j: (0, j, 0)),
            pl.BlockSpec(coeffs.shape, lambda j: (0, 0, 0)),
        ],
        out_specs=pl.BlockSpec((cols, rows), lambda j: (j, 0)),
        scratch_shapes=[pltpu.VMEM((lon_count, width, rows), jnp.bfloat16)],
        compiler_params=pltpu.CompilerParams(vmem_limit_bytes=VMEM_LIMIT),
        cost_estimate=pl.CostEstimate(
            flops=2 * NLON * lon_count * width * rows,
            bytes_accessed=trig.size * 2 + 2 * coeffs.size * 4,
            transcendentals=0,
        ),
        name="grid_field",
    )(trig, coeffs)


def gelu_parts(preact):
    scale = math.sqrt(2.0 / math.pi)
    square = preact * preact
    bend = jnp.tanh(scale * (preact + 0.044715 * (square * preact)))
    half = 0.5 * (1.0 + bend)
    slope = half + (0.5 * preact) * (1.0 - bend * bend) * (
        scale * (1.0 + (3.0 * 0.044715) * square)
    )
    return preact * half, slope


def forward_kernel(latents_ref, w_ref, b_ref, slope_ref, hidden_t_ref, latents_t_ref):
    latents = latents_ref[...]
    preact = jnp.dot(latents, w_ref[...], preferred_element_type=jnp.float32) + b_ref[...]
    hidden, slope = gelu_parts(preact)
    slope_ref[...] = slope
    hidden_t_ref[...] = hidden.T.astype(jnp.bfloat16)
    latents_t_ref[...] = latents.T


def forward(latents, w_hidden, b_hidden, parts):
    cells, width = latents.shape
    cols = cells // parts
    return pl.pallas_call(
        forward_kernel,
        grid=(parts,),
        out_shape=(
            jax.ShapeDtypeStruct((cells, width), jnp.float32),
            jax.ShapeDtypeStruct((parts, width, cols), jnp.bfloat16),
            jax.ShapeDtypeStruct((parts, width, cols), jnp.bfloat16),
        ),
        in_specs=[
            pl.BlockSpec((cols, width), lambda i: (i, 0)),
            pl.BlockSpec((width, width), lambda i: (0, 0)),
            pl.BlockSpec((1, width), lambda i: (0, 0)),
        ],
        out_specs=(
            pl.BlockSpec((cols, width), lambda i: (i, 0)),
            pl.BlockSpec((None, width, cols), lambda i: (i, 0, 0)),
            pl.BlockSpec((None, width, cols), lambda i: (i, 0, 0)),
        ),
        compiler_params=pltpu.CompilerParams(vmem_limit_bytes=VMEM_LIMIT),
        cost_estimate=pl.CostEstimate(
            flops=2 * cells * width * width,
            bytes_accessed=cells * width * 10,
            transcendentals=cells * width,
        ),
        name="forward",
    )(latents, w_hidden, b_hidden.reshape(1, width))


def backward_kernel(
    core_ref, grid_ref, scale_ref, place_ref, w_out_ref, slope_ref, hidden_t_ref, latents_t_ref,
    preact_ref, keep_ref, send_ref, field_ref, hidden_acc, out_acc, bias_acc, sums_ref,
):
    index = pl.program_id(0)
    total = pl.num_programs(0)
    blocks = grid_ref.shape[0]
    lon_cols = grid_ref.shape[1]
    width = hidden_acc.shape[0]
    cols = slope_ref.shape[0]
    sum_rows = sums_ref.shape[0]

    @pl.when(index == 0)
    def _():
        field = None
        for block in range(blocks):
            scaled = (grid_ref[block] * scale_ref[block]).astype(jnp.bfloat16)
            part = jnp.dot(scaled, place_ref[block], preferred_element_type=jnp.float32)
            field = part if field is None else field + part
        for row in range(field.shape[1] // LANES):
            field_ref[pl.ds(row * lon_cols, lon_cols), :] = field[
                :, row * LANES : (row + 1) * LANES
            ]
        hidden_acc[...] = jnp.zeros_like(hidden_acc)
        out_acc[...] = jnp.zeros_like(out_acc)
        bias_acc[...] = jnp.zeros_like(bias_acc)

    field = field_ref[pl.ds(pl.multiple_of(index * cols, SUBS), cols), :].astype(jnp.bfloat16)
    back = jnp.dot(field, w_out_ref[...], preferred_element_type=jnp.float32)
    preact_back = (back * slope_ref[...]).astype(jnp.bfloat16)
    preact_ref[...] = preact_back
    hidden_acc[...] += jnp.dot(
        latents_t_ref[...], preact_back, preferred_element_type=jnp.float32
    )
    out_acc[...] += jnp.dot(hidden_t_ref[...], field, preferred_element_type=jnp.float32)
    bias_acc[...] += jnp.sum(preact_back.astype(jnp.float32), axis=0, keepdims=True)

    @pl.when(index == total - 1)
    def _():
        tiles = width // LANES
        for row_tile in range(width // SUBS):
            for tile in range(tiles):
                sums_ref[pl.ds((row_tile * tiles + tile) * SUBS, SUBS), :] = hidden_acc[
                    pl.ds(row_tile * SUBS, SUBS), pl.ds(tile * LANES, LANES)
                ]
        base = width * tiles
        flipped = out_acc[...].T
        for tile in range(tiles):
            sums_ref[pl.ds(base + tile * F, F), :] = flipped[:F, tile * LANES : (tile + 1) * LANES]
        base = base + tiles * F
        sums_ref[pl.ds(base, sum_rows - base), :] = jnp.zeros((sum_rows - base, LANES), jnp.float32)
        for tile in range(tiles):
            sums_ref[pl.ds(base + tile, 1), :] = bias_acc[:, tile * LANES : (tile + 1) * LANES]
        half = sum_rows // 2
        mine = core_ref[0]
        keep_ref[...] = sums_ref[pl.ds(pl.multiple_of(mine * half, SUBS), half), :]
        send_ref[...] = sums_ref[pl.ds(pl.multiple_of((1 - mine) * half, SUBS), half), :]


def backward(core, grid, scale, place, w_out_t, slope, hidden_t, latents_t, sum_rows):
    cells, width = slope.shape
    parts, _, cols = hidden_t.shape
    half = (sum_rows // 2, LANES)
    whole3 = lambda i: (0, 0, 0)
    whole2 = lambda i: (0, 0)
    return pl.pallas_call(
        backward_kernel,
        grid=(parts,),
        out_shape=(
            jax.ShapeDtypeStruct((cells, width), jnp.bfloat16),
            jax.ShapeDtypeStruct(half, jnp.float32),
            jax.ShapeDtypeStruct(half, jnp.float32),
        ),
        in_specs=[
            pl.BlockSpec(memory_space=pltpu.SMEM),
            pl.BlockSpec(grid.shape, whole3),
            pl.BlockSpec(scale.shape, whole3),
            pl.BlockSpec(place.shape, whole3),
            pl.BlockSpec(w_out_t.shape, whole2),
            pl.BlockSpec((cols, width), lambda i: (i, 0)),
            pl.BlockSpec((None, width, cols), lambda i: (i, 0, 0)),
            pl.BlockSpec((None, width, cols), lambda i: (i, 0, 0)),
        ],
        out_specs=(
            pl.BlockSpec((cols, width), lambda i: (i, 0)),
            pl.BlockSpec(half, whole2),
            pl.BlockSpec(half, whole2),
        ),
        scratch_shapes=[
            pltpu.VMEM((cells, LANES), jnp.float32),
            pltpu.VMEM((width, width), jnp.float32),
            pltpu.VMEM((width, LANES), jnp.float32),
            pltpu.VMEM((1, width), jnp.float32),
            pltpu.VMEM((sum_rows, LANES), jnp.float32),
        ],
        compiler_params=pltpu.CompilerParams(vmem_limit_bytes=VMEM_LIMIT),
        cost_estimate=pl.CostEstimate(
            flops=2 * cells * width * (width + 2 * LANES),
            bytes_accessed=cells * width * 10,
            transcendentals=0,
        ),
        name="backward",
    )(core, grid, scale, place, w_out_t, slope, hidden_t, latents_t)


def add_kernel(index_ref, *refs, inputs, outputs, factor):
    size = refs[0].shape[0] // outputs
    for part in range(outputs):
        start = 0 if outputs == 1 else pl.multiple_of((index_ref[0] ^ part) * size, SUBS)
        total = refs[0][pl.ds(start, size), :]
        for piece in refs[1:inputs]:
            total = total + piece[pl.ds(start, size), :]
        if factor is not None:
            total = total * factor
        refs[inputs + part][...] = total


def add_pieces(index, pieces, outputs, factor=None):
    rows = pieces[0].shape[0]
    size = rows // outputs
    return pl.pallas_call(
        functools.partial(add_kernel, inputs=len(pieces), outputs=outputs, factor=factor),
        out_shape=[jax.ShapeDtypeStruct((size, LANES), jnp.float32)] * outputs,
        in_specs=[pl.BlockSpec(memory_space=pltpu.SMEM)]
        + [pl.BlockSpec(memory_space=pltpu.VMEM)] * len(pieces),
        out_specs=[pl.BlockSpec(memory_space=pltpu.VMEM)] * outputs,
        cost_estimate=pl.CostEstimate(
            flops=len(pieces) * rows * LANES,
            bytes_accessed=4 * (len(pieces) + 1) * rows * LANES,
            transcendentals=0,
        ),
        name="add_pieces",
    )(index, *pieces)


def finish_kernel(
    place_ref, own_ref, other_ref, hidden_ref, bias_ref, out_ref, flat_ref, *, lon_count, depth
):
    core, lon, deep = place_ref[0], place_ref[1], place_ref[2]
    size = own_ref.shape[0] // (lon_count * depth)
    for half, source in enumerate((own_ref, other_ref)):
        for part in range(lon_count):
            for piece in range(depth):
                start = (((core ^ half) * lon_count + (lon ^ part)) * depth + (deep ^ piece)) * size
                flat_ref[pl.ds(pl.multiple_of(start, SUBS), size), :] = source[
                    pl.ds((part * depth + piece) * size, size), :
                ]
    width = hidden_ref.shape[0]
    tiles = width // LANES
    for row_tile in range(width // SUBS):
        for tile in range(tiles):
            hidden_ref[pl.ds(row_tile * SUBS, SUBS), pl.ds(tile * LANES, LANES)] = flat_ref[
                pl.ds((row_tile * tiles + tile) * SUBS, SUBS), :
            ]
    base = width * tiles
    for tile in range(tiles):
        out_ref[:, pl.ds(tile * LANES, LANES)] = flat_ref[pl.ds(base + tile * F, F), :]
        bias_ref[:, pl.ds(tile * LANES, LANES)] = flat_ref[pl.ds(base + tiles * F + tile, 1), :]


def finish(place, own, other, width, lon_count, depth):
    return pl.pallas_call(
        functools.partial(finish_kernel, lon_count=lon_count, depth=depth),
        out_shape=(
            jax.ShapeDtypeStruct((width, width), jnp.float32),
            jax.ShapeDtypeStruct((1, width), jnp.float32),
            jax.ShapeDtypeStruct((F, width), jnp.float32),
        ),
        in_specs=[pl.BlockSpec(memory_space=pltpu.SMEM)]
        + [pl.BlockSpec(memory_space=pltpu.VMEM)] * 2,
        out_specs=(pl.BlockSpec(memory_space=pltpu.VMEM),) * 3,
        scratch_shapes=[pltpu.VMEM((2 * own.shape[0], LANES), jnp.float32)],
        name="finish",
    )(place, own, other)


def swap(value, axis, bits):
    count = lax.axis_size(axis)
    return lax.ppermute(value, axis, [(i, i ^ bits) for i in range(count)])


def local(spectra, field_slot, field_weight, latents, w_hidden, b_hidden, w_out):
    slot_count, _, pair_count, _ = spectra.shape
    lat_rows, lon_cols, width = latents.shape
    lat_count = lax.axis_size("lat")
    lon_count = lax.axis_size("lon")
    rows_all = lat_rows * lat_count
    lat_index = lax.axis_index("lat").astype(jnp.int32)
    lon_index = lax.axis_index("lon").astype(jnp.int32)
    pair_pad = pad_to(pair_count, SUBS)
    cells = lat_rows * lon_cols
    parts = 4

    coeffs = coefficients(spectra, (lon_index * pair_count).reshape(1), rows_all, lat_rows)
    share = slot_count * lat_rows // lon_count
    coeffs = coeffs.reshape(lat_count * lon_count, share, 4 * pair_pad)
    coeffs = lax.all_to_all(coeffs, ("lat", "lon"), split_axis=0, concat_axis=0, tiled=True)

    slope, hidden_t, latents_t = forward(
        latents.reshape(cells, width), w_hidden, b_hidden, parts
    )
    trig = trig_table(pair_count, lon_count)

    lanes = lat_count * share

    def spread(values):
        values = jnp.broadcast_to(values, (lat_count, slot_count, lat_rows))
        values = values.reshape(lat_count, lon_count, share)
        return jnp.transpose(values, (1, 0, 2)).reshape(lon_count, lanes)

    field_ids = spread(field_slot.reshape(lat_count, slot_count, 1))
    row_ids = spread(jnp.arange(lat_rows, dtype=jnp.int32).reshape(1, 1, lat_rows))
    chosen = field_ids[:, :, None] == jnp.arange(F, dtype=jnp.int32)
    weight = jnp.sum(jnp.where(chosen, field_weight, 0.0), axis=2)
    sine = jnp.sin(band_angles(lat_index * lat_rows + row_ids, rows_all))
    scale = (sine * weight)[:, None, :]
    target = row_ids * LANES + field_ids
    place = (
        target[:, :, None] == jnp.arange(lat_rows * LANES, dtype=jnp.int32)[None, None, :]
    ).astype(jnp.bfloat16)
    w_out_t = jnp.concatenate([w_out.T, jnp.zeros((LANES - F, width), w_out.dtype)], axis=0)

    coeffs, slope, hidden_t, latents_t, trig, scale, place, w_out_t = lax.optimization_barrier(
        (coeffs, slope, hidden_t, latents_t, trig, scale, place, w_out_t)
    )
    grid = grid_field(trig, coeffs, lon_count).reshape(lon_count, lon_cols, lanes)
    grid = lax.all_to_all(grid, "lon", split_axis=0, concat_axis=0, tiled=True)

    device_count = lat_count * lon_count
    used_rows = (width + F + 1) * width // LANES
    chunk = pad_to(pad_to(used_rows, device_count) // device_count, SUBS)
    core_index, deep_index = lat_index & 1, lat_index >> 1
    depth = lat_count // 2
    preact_back, keep, send = backward(
        core_index.reshape(1), grid, scale, place, w_out_t, slope, hidden_t, latents_t,
        chunk * device_count,
    )
    latent_grad = lax.dot_general(
        preact_back, w_hidden, (((1,), (1,)), ((), ())), preferred_element_type=jnp.float32
    ).astype(jnp.bfloat16)

    pieces = add_pieces(
        lon_index.reshape(1), [keep, swap(send, "lat", 1)], lon_count
    )
    arrived = [swap(pieces[part], "lon", part) for part in range(1, lon_count)]
    pieces = add_pieces(deep_index.reshape(1), [pieces[0]] + arrived, depth)
    arrived = [swap(pieces[part], "lat", 2 * part) for part in range(1, depth)]
    norm = 1.0 / math.sqrt(rows_all * NLON)
    total = add_pieces(deep_index.reshape(1), [pieces[0]] + arrived, 1, norm)[0]
    total = jnp.concatenate([total] + [swap(total, "lat", 2 * part) for part in range(1, depth)])
    total = jnp.concatenate([total] + [swap(total, "lon", part) for part in range(1, lon_count)])
    other = swap(total, "lat", 1)
    hidden_grad, bias_grad, out_grad = finish(
        jnp.stack([core_index, lon_index, deep_index]), total, other, width, lon_count, depth
    )
    return (
        latent_grad.reshape(lat_rows, lon_cols, width),
        hidden_grad,
        bias_grad.reshape(width),
        out_grad.T,
    )


def solution(mesh):
    in_specs = (P("lat", None, "lon", None), P(), P(), P("lat", "lon", None), P(), P(), P())
    out_specs = (P("lat", "lon", None), P(), P(), P())
    return jax.shard_map(local, mesh=mesh, in_specs=in_specs, out_specs=out_specs, check_vma=False)
```

time: 177 us -> 149 us (0.84)
  blocking collectives: 50.2 us -> 0 us
  waiting for transfers between devices: 11.4 us -> 37.1 us
  local copies, waits for them, and re-layouts: 22.6 us -> 6.96 us
  starting transfers between devices: 14.8 us -> 26.7 us
  other arithmetic: 12.3 us -> 3.44 us
  Pallas kernels: 59.1 us -> 67.5 us
    all_to_all x3 -> x0, blocking collectives: 50.2 us -> none  [the longest x2 29.3 us: local(): sums = lax.all_to_all(sums, 'lat', split_axis=0, concat_axis=0, tiled=True)]
    ppermute x0 -> x14, waiting for transfers between devices: none -> 22 us  [swap(): return lax.ppermute(value, axis, [(i, i ^ bits) for i in range(count)])]
    ppermute x0 -> x14, starting transfers between devices: none -> 16 us  [swap(): return lax.ppermute(value, axis, [(i, i ^ bits) for i in range(count)])]
    all_to_all x1 -> x0, waiting for transfers between devices: 11.4 us -> none  [local(): sums = lax.all_to_all(sums, 'lon', split_axis=0, concat_axis=0, tiled=True)]
    all_to_all x1, waiting for transfers between devices: 0.01 us -> 10.4 us  [local(): grid = lax.all_to_all(grid, 'lon', split_axis=0, concat_axis=0, tiled=True)]
    pallas_call x2 -> x7, Pallas kernels: 23.5 us -> 31.9 us  [the longest x1 10.6 us: backward(): pl.pallas_call(backward_kernel, grid=(parts,), out_shape=(jax.ShapeDtypeS...]
    gather x2 -> x0, local copies, waits for them, and re-layouts: 6.7 us -> none  [the longest x1 3.35 us: local(): field_ids = field_slot[slot_ids]]
    convert_element_type x1 -> x0, local copies, waits for them, and re-layouts: 4.92 us -> none  [trig_table(): table = table.astype(jnp.bfloat16)]
  transfers between devices with their start and end apart: 3 -> 16, of which waited for: 1 -> 12; matrix products, arithmetic and copies ran while one was open for 17% -> 7% of each run, Pallas kernels for 6% -> 9%
where the time goes in v2:
time: 149 us; the launch traced here: 148 us
  Pallas kernels  67.5 us (45%)
  waiting for transfers between devices  37.1 us (25%)
  starting transfers between devices  26.7 us (18%)
  local copies, waits for them, and re-layouts  6.96 us (5%)
  matrix products  5.16 us (3%)
  other arithmetic  3.44 us (2%)
    pallas_call x1, Pallas kernels, coefficients(): pl.pallas_call(kernel, out_shape=jax.ShapeDtypeStruct((lat_count, slot_co...  30.2 us
    ppermute x14, waiting for transfers between devices, swap(): return lax.ppermute(value, axis, [(i, i ^ bits) for i in range(count)])  22 us
    ppermute x14, starting transfers between devices, swap(): return lax.ppermute(value, axis, [(i, i ^ bits) for i in range(count)])  16 us
    pallas_call x1, Pallas kernels, backward(): pl.pallas_call(backward_kernel, grid=(parts,), out_shape=(jax.ShapeDtypeS...  10.6 us
    all_to_all x1, waiting for transfers between devices, local(): grid = lax.all_to_all(grid, 'lon', split_axis=0, concat_axis=0, tiled=True)  10.4 us
    pallas_call x1, Pallas kernels, forward(): pl.pallas_call(forward_kernel, grid=(parts,), out_shape=(jax.ShapeDtypeSt...  8.98 us
    all_to_all x1, starting transfers between devices, local(): lax.all_to_all(coeffs, ('lat', 'lon'), split_axis=0, concat_axis=0, tiled...  7.3 us
    unnamed x36, local copies, waits for them, and re-layouts  5.64 us
  transfers between devices with their start and end apart: 16, of which 12 were waited for; matrix products, arithmetic and copies ran while one was open for 7% of the time, Pallas kernels for 9%

profile of v2, /device:TPU:0, one launch (start us, length us, event | category | flops | bytes accessed | tf_op | source)
XLA Modules:
  0.0 147.8 jit_solution(13431974613775828671)
XLA Ops:
  0.7 30.2 %coefficients.1 = f32[8,64,384]{2,1,0:T(8,128)} custom-call(s32[1]{0:T(128)} %bitcast.1.first_ref, f32[8,90,2,721]{3,2,1,0:T(2,128)} %bitcast.17), custom_call_target="tpu_custom_call" | custom-call | tf_op jit(solution)/shard_map/coefficients/pallas_call | solution.py:227
  30.9 7.3 %all-to-all-start = ((f32[32,16,384]{2,1,0:T(8,128)}), f32[32,16,384]{2,1,0:T(8,128)S(1)}, u32[]{:S(2)}, u32[]{:S(2)}) async-start(f32[32,16,384]{2,1,0:T(8,128)} %bitcast.18), calls=%async_computation | async-start | bytes 1572864 | tf_op jit(solution)/shard_map/all_to_all | solution.py:602
  40.3 4.4 %trig_table.1.trig_ref = bf16[4,1440,384]{2,1,0:T(8,128)(2,1)} custom-call(), custom_call_target="tpu_custom_call" | custom-call | flops 11059200 | bytes 4423680 | tf_op jit(solution)/shard_map/trig_table/pallas_call | solution.py:293
  44.7 9.0 %forward.1 = (f32[2880,512]{1,0:T(8,128)}, bf16[4,512,720]{2,1,0:T(8,128)(2,1)}, bf16[4,512,720]{2,1,0:T(8,128)(2,1)}) custom-call(bf16[2880,512]{1,0:T(8,128)(2,1)} %bitcast.23, bf16[512,512]{1,0:T(8,128)(2,1)} %w_ref.1, f32[1,512]{1,0:T(1,128)} %bitcast.25), custom_call_target="tpu_custom_call" | custom-call | flops 1509949440 | bytes 14745600 | tf_op jit(solution)/shard_map/forward/pallas_call | solution.py:378
  54.9 4.7 %all-to-all-done.coeff_ref = f32[32,16,384]{2,1,0:T(8,128)S(1)} async-done(((f32[32,16,384]{2,1,0:T(8,128)}), f32[32,16,384]{2,1,0:T(8,128)S(1)}, u32[]{:S(2)}, u32[]{:S(2)}) %all-to-all-start) | async-done | bytes 786464 | tf_op jit(solution)/shard_map/all_to_all | solution.py:602
  60.5 5.4 %grid_field.1 = f32[1440,128]{1,0:T(8,128)} custom-call(bf16[4,1440,384]{2,1,0:T(8,128)(2,1)} %trig_table.1.trig_ref, f32[32,16,384]{2,1,0:T(8,128)} %copy-done), custom_call_target="tpu_custom_call" | custom-call | flops 566231040 | bytes 5996544 | tf_op jit(solution)/shard_map/grid_field/pallas_call | solution.py:335
  65.8 3.5 %all-to-all-start.1 = ((f32[4,360,128]{2,1,0:T(8,128)}), f32[4,360,128]{2,1,0:T(8,128)S(1)}, u32[]{:S(2)}, u32[]{:S(2)}) async-start(f32[4,360,128]{2,1,0:T(8,128)} %bitcast.19), calls=%async_computation.1 | async-start | bytes 1474560 | tf_op jit(solution)/shard_map/all_to_all | solution.py:632
  69.3 10.4 %all-to-all-done.1.grid_ref = f32[4,360,128]{2,1,0:T(8,128)S(1)} async-done(((f32[4,360,128]{2,1,0:T(8,128)}), f32[4,360,128]{2,1,0:T(8,128)S(1)}, u32[]{:S(2)}, u32[]{:S(2)}) %all-to-all-start.1) | async-done | bytes 737312 | tf_op jit(solution)/shard_map/all_to_all | solution.py:632
  80.6 10.6 %backward.1 = (bf16[2880,512]{1,0:T(8,128)(2,1)}, f32[1280,128]{1,0:T(8,128)}, f32[1280,128]{1,0:T(8,128)}) custom-call(s32[1]{0:T(128)} %bitcast.core_ref, f32[4,360,128]{2,1,0:T(8,128)} %copy-done.1, f32[4,1,128]{2,1,0:T(1,128)} %mul.38.scale_ref, bf16[4,128,1024]{2,1,0:T(8,128)(2,1)} %fusion.place_ref, bf16[128,512]{1,0:T(8,128)(2,1)} %concatenate.10.w_out_ref, ...), custom_call_target="tpu_custom_call" | custom-call | flops 2264924160 | bytes 14745600 | tf_op jit(solution)/shard_map/backward/pallas_call | solution.py:471
  91.3 2.3 %collective-permute-done.refs_1_ = f32[1280,128]{1,0:T(8,128)S(1)} collective-permute-done((f32[1280,128]{1,0:T(8,128)}, f32[1280,128]{1,0:T(8,128)S(1)}, u32[]{:S(2)}, u32[]{:S(2)}) %collective-permute-start) | collective-permute-done | bytes 655392 | tf_op jit(solution)/shard_map/ppermute | solution.py:584
  94.4 2.2 %add_pieces.3 = (f32[320,128]{1,0:T(8,128)}, f32[320,128]{1,0:T(8,128)}, f32[320,128]{1,0:T(8,128)}, f32[320,128]{1,0:T(8,128)}) custom-call(s32[1]{0:T(128)} %bitcast.11.index_ref, f32[1280,128]{1,0:T(8,128)} %get-tuple-element.41.refs_0_, f32[1280,128]{1,0:T(8,128)} %copy-done.4), custom_call_target="tpu_custom_call" | custom-call | flops 327680 | bytes 1966080 | tf_op jit(solution)/shard_map/add_pieces/pallas_call | solution.py:526
  98.6 1.5 %collective-permute-start.3 = (f32[320,128]{1,0:T(8,128)}, f32[320,128]{1,0:T(8,128)S(1)}, u32[]{:S(2)}, u32[]{:S(2)}) collective-permute-start(f32[320,128]{1,0:T(8,128)} %get-tuple-element.46), channel_id=1, source_target_pairs={{0,3},{1,2},{2,1},{3,0},{4,7},{5,6},{6,5},{7,4},{8,11},{9,10},{10,... | collective-permute-start | bytes 491528 | tf_op jit(solution)/shard_map/ppermute | solution.py:584
  100.1 3.8 %collective-permute-done.1.refs_1_ = f32[320,128]{1,0:T(8,128)S(1)} collective-permute-done((f32[320,128]{1,0:T(8,128)}, f32[320,128]{1,0:T(8,128)S(1)}, u32[]{:S(2)}, u32[]{:S(2)}) %collective-permute-start.1) | collective-permute-done | bytes 163872 | tf_op jit(solution)/shard_map/ppermute | solution.py:584
  103.9 3.9 %collective-permute-done.2.refs_2_ = f32[320,128]{1,0:T(8,128)S(1)} collective-permute-done((f32[320,128]{1,0:T(8,128)}, f32[320,128]{1,0:T(8,128)S(1)}, u32[]{:S(2)}, u32[]{:S(2)}) %collective-permute-start.2) | collective-permute-done | bytes 163872 | tf_op jit(solution)/shard_map/ppermute | solution.py:584
  108.5 1.8 %add_pieces.4 = (f32[80,128]{1,0:T(8,128)}, f32[80,128]{1,0:T(8,128)}, f32[80,128]{1,0:T(8,128)}, f32[80,128]{1,0:T(8,128)}) custom-call(s32[1]{0:T(128)} %bitcast.12.index_ref, f32[320,128]{1,0:T(8,128)} %get-tuple-element.43.refs_0_, f32[320,128]{1,0:T(8,128)} %copy-done.5, f32[320,128]{1,0:T(8,128)} %copy-done.6, f32[320,128]{1,0:T(8,128)} %copy-done.7), custom_call_target="tpu_custom_call" | custom-call | flops 163840 | bytes 819200 | tf_op jit(solution)/shard_map/add_pieces/pallas_call | solution.py:526
  111.8 2.8 %collective-permute-start.6 = (f32[80,128]{1,0:T(8,128)}, f32[80,128]{1,0:T(8,128)S(1)}, u32[]{:S(2)}, u32[]{:S(2)}) collective-permute-start(f32[80,128]{1,0:T(8,128)} %get-tuple-element.50), channel_id=1, source_target_pairs={{0,24},{4,28},{8,16},{12,20},{16,8},{20,12},{24,0},{28,4},{1,25},{... | collective-permute-start | bytes 122888 | tf_op jit(solution)/shard_map/ppermute | solution.py:584
  114.7 1.5 %collective-permute-done.5.refs_2_ = f32[80,128]{1,0:T(8,128)S(1)} collective-permute-done((f32[80,128]{1,0:T(8,128)}, f32[80,128]{1,0:T(8,128)S(1)}, u32[]{:S(2)}, u32[]{:S(2)}) %collective-permute-start.5) | collective-permute-done | bytes 40992 | tf_op jit(solution)/shard_map/ppermute | solution.py:584
  116.2 1.7 %collective-permute-done.6.refs_3_ = f32[80,128]{1,0:T(8,128)S(1)} collective-permute-done((f32[80,128]{1,0:T(8,128)}, f32[80,128]{1,0:T(8,128)S(1)}, u32[]{:S(2)}, u32[]{:S(2)}) %collective-permute-start.6) | collective-permute-done | bytes 40992 | tf_op jit(solution)/shard_map/ppermute | solution.py:584
  119.9 3.4 %collective-permute-start.8 = (f32[80,128]{1,0:T(8,128)}, f32[80,128]{1,0:T(8,128)S(1)}, u32[]{:S(2)}, u32[]{:S(2)}) collective-permute-start(f32[80,128]{1,0:T(8,128)} %add_pieces.5), channel_id=1, source_target_pairs={{0,16},{4,20},{8,24},{12,28},{16,0},{20,4},{24,8},{28,12},{1,17},{... | collective-permute-start | bytes 122888 | tf_op jit(solution)/shard_map/ppermute | solution.py:584
  125.8 3.5 %collective-permute-done.9 = f32[80,128]{1,0:T(8,128)S(1)} collective-permute-done((f32[80,128]{1,0:T(8,128)}, f32[80,128]{1,0:T(8,128)S(1)}, u32[]{:S(2)}, u32[]{:S(2)}) %collective-permute-start.9) | collective-permute-done | bytes 40992 | tf_op jit(solution)/shard_map/ppermute | solution.py:584
  133.7 1.8 %collective-permute-done.10 = f32[320,128]{1,0:T(8,128)S(1)} collective-permute-done((f32[320,128]{1,0:T(8,128)S(1)}, f32[320,128]{1,0:T(8,128)S(1)}, u32[]{:S(2)}, u32[]{:S(2)}) %collective-permute-start.10) | collective-permute-done | bytes 163872 | tf_op jit(solution)/shard_map/ppermute | solution.py:584
  136.9 1.6 %collective-permute-done.12 = f32[320,128]{1,0:T(8,128)S(1)} collective-permute-done((f32[320,128]{1,0:T(8,128)S(1)}, f32[320,128]{1,0:T(8,128)S(1)}, u32[]{:S(2)}, u32[]{:S(2)}) %collective-permute-start.12) | collective-permute-done | bytes 163872 | tf_op jit(solution)/shard_map/ppermute | solution.py:584
  139.3 5.2 %convolution_convert_fusion = bf16[2880,512]{1,0:T(8,128)(2,1)} fusion(bf16[2880,512]{1,0:T(8,128)(2,1)} %get-tuple-element.40, bf16[512,512]{1,0:T(8,128)(2,1)S(1)} %copy-done.14), kind=kOutput, calls=%fused_computation | convolution fusion | flops 1511424000 | bytes 6422528 | tf_op jit(solution)/shard_map/dot_general | solution.py:643
  145.3 2.5 %finish.1 = (f32[512,512]{1,0:T(8,128)}, f32[1,512]{1,0:T(1,128)}, f32[64,512]{1,0:T(8,128)}) custom-call(s32[3]{0:T(128)} %pad_add_fusion.place_ref, f32[1280,128]{1,0:T(8,128)} %copy-done.2, f32[1280,128]{1,0:T(8,128)} %copy-done.3), custom_call_target="tpu_custom_call" | custom-call | tf_op jit(solution)/shard_map/finish/pallas_call | solution.py:567
  (75 shorter events, 22.1 us)
Async XLA Ops:
  0.6 37.8 %copy-start.12 = (s32[64]{0:T(128)S(1)}, s32[64]{0:T(128)}, u32[]{:S(2)}) copy-start(s32[64]{0:T(128)} %param.8) | copy-start | bytes 772
  0.6 38.3 %copy-start.13 = (f32[64]{0:T(128)S(1)}, f32[64]{0:T(128)}, u32[]{:S(2)}) copy-start(f32[64]{0:T(128)} %param.9) | copy-start | bytes 772
  0.7 39.0 %copy-start.8 = (bf16[512,64]{0,1:T(8,128)(2,1)S(1)}, bf16[512,64]{0,1:T(8,128)(2,1)}, u32[]{:S(2)}) copy-start(bf16[512,64]{0,1:T(8,128)(2,1)} %param.13) | copy-start | bytes 196612
  30.9 28.7 %all-to-all-start = ((f32[32,16,384]{2,1,0:T(8,128)}), f32[32,16,384]{2,1,0:T(8,128)S(1)}, u32[]{:S(2)}, u32[]{:S(2)}) async-start(f32[32,16,384]{2,1,0:T(8,128)} %bitcast.18), calls=%async_computation | async-start | bytes 1572864 | tf_op jit(solution)/shard_map/all_to_all | solution.py:602
  65.8 13.9 %all-to-all-start.1 = ((f32[4,360,128]{2,1,0:T(8,128)}), f32[4,360,128]{2,1,0:T(8,128)S(1)}, u32[]{:S(2)}, u32[]{:S(2)}) async-start(f32[4,360,128]{2,1,0:T(8,128)} %bitcast.19), calls=%async_computation.1 | async-start | bytes 1474560 | tf_op jit(solution)/shard_map/all_to_all | solution.py:632
  91.2 48.1 %copy-start.14 = (bf16[512,512]{1,0:T(8,128)(2,1)S(1)}, bf16[512,512]{1,0:T(8,128)(2,1)}, u32[]{:S(2)}) copy-start(bf16[512,512]{1,0:T(8,128)(2,1)} %w_ref.1) | copy-start | bytes 1572868
  91.2 2.4 %collective-permute-start = (f32[1280,128]{1,0:T(8,128)}, f32[1280,128]{1,0:T(8,128)S(1)}, u32[]{:S(2)}, u32[]{:S(2)}) collective-permute-start(f32[1280,128]{1,0:T(8,128)} %get-tuple-element.42), channel_id=1, source_target_pairs={{0,4},{4,0},{8,12},{12,8},{16,20},{20,16},{24,28},{28,24},{1,5},{5... | collective-permute-start | bytes 1966088 | tf_op jit(solution)/shard_map/ppermute | solution.py:584
  96.6 7.3 %collective-permute-start.1 = (f32[320,128]{1,0:T(8,128)}, f32[320,128]{1,0:T(8,128)S(1)}, u32[]{:S(2)}, u32[]{:S(2)}) collective-permute-start(f32[320,128]{1,0:T(8,128)} %get-tuple-element.44), channel_id=1, source_target_pairs={{0,1},{1,0},{2,3},{3,2},{4,5},{5,4},{6,7},{7,6},{8,9},{9,8},{10,11... | collective-permute-start | bytes 491528 | tf_op jit(solution)/shard_map/ppermute | solution.py:584
  98.0 9.7 %collective-permute-start.2 = (f32[320,128]{1,0:T(8,128)}, f32[320,128]{1,0:T(8,128)S(1)}, u32[]{:S(2)}, u32[]{:S(2)}) collective-permute-start(f32[320,128]{1,0:T(8,128)} %get-tuple-element.45), channel_id=1, source_target_pairs={{0,2},{1,3},{2,0},{3,1},{4,6},{5,7},{6,4},{7,5},{8,10},{9,11},{10,... | collective-permute-start | bytes 491528 | tf_op jit(solution)/shard_map/ppermute | solution.py:584
  98.6 9.1 %collective-permute-start.3 = (f32[320,128]{1,0:T(8,128)}, f32[320,128]{1,0:T(8,128)S(1)}, u32[]{:S(2)}, u32[]{:S(2)}) collective-permute-start(f32[320,128]{1,0:T(8,128)} %get-tuple-element.46), channel_id=1, source_target_pairs={{0,3},{1,2},{2,1},{3,0},{4,7},{5,6},{6,5},{7,4},{8,11},{9,10},{10,... | collective-permute-start | bytes 491528 | tf_op jit(solution)/shard_map/ppermute | solution.py:584
  103.9 3.9 %copy-start.5 = (f32[320,128]{1,0:T(8,128)}, f32[320,128]{1,0:T(8,128)S(1)}, u32[]{:S(2)}) copy-start(f32[320,128]{1,0:T(8,128)S(1)} %collective-permute-done.1.refs_1_) | copy-start | bytes 491524
  110.3 4.4 %collective-permute-start.4 = (f32[80,128]{1,0:T(8,128)}, f32[80,128]{1,0:T(8,128)S(1)}, u32[]{:S(2)}, u32[]{:S(2)}) collective-permute-start(f32[80,128]{1,0:T(8,128)} %get-tuple-element.48), channel_id=1, source_target_pairs={{0,8},{4,12},{8,0},{12,4},{16,24},{20,28},{24,16},{28,20},{1,9},{5... | collective-permute-start | bytes 122888 | tf_op jit(solution)/shard_map/ppermute | solution.py:584
  111.1 5.1 %collective-permute-start.5 = (f32[80,128]{1,0:T(8,128)}, f32[80,128]{1,0:T(8,128)S(1)}, u32[]{:S(2)}, u32[]{:S(2)}) collective-permute-start(f32[80,128]{1,0:T(8,128)} %get-tuple-element.49), channel_id=1, source_target_pairs={{0,16},{4,20},{8,24},{12,28},{16,0},{20,4},{24,8},{28,12},{1,17},{... | collective-permute-start | bytes 122888 | tf_op jit(solution)/shard_map/ppermute | solution.py:584
  111.8 6.0 %collective-permute-start.6 = (f32[80,128]{1,0:T(8,128)}, f32[80,128]{1,0:T(8,128)S(1)}, u32[]{:S(2)}, u32[]{:S(2)}) collective-permute-start(f32[80,128]{1,0:T(8,128)} %get-tuple-element.50), channel_id=1, source_target_pairs={{0,24},{4,28},{8,16},{12,20},{16,8},{20,12},{24,0},{28,4},{1,25},{... | collective-permute-start | bytes 122888 | tf_op jit(solution)/shard_map/ppermute | solution.py:584
  114.7 3.2 %copy-start.9 = (f32[80,128]{1,0:T(8,128)}, f32[80,128]{1,0:T(8,128)S(1)}, u32[]{:S(2)}) copy-start(f32[80,128]{1,0:T(8,128)S(1)} %collective-permute-done.4.refs_1_) | copy-start | bytes 122884
  116.2 1.7 %copy-start.10 = (f32[80,128]{1,0:T(8,128)}, f32[80,128]{1,0:T(8,128)S(1)}, u32[]{:S(2)}) copy-start(f32[80,128]{1,0:T(8,128)S(1)} %collective-permute-done.5.refs_2_) | copy-start | bytes 122884
  119.9 5.2 %collective-permute-start.7 = (f32[80,128]{1,0:T(8,128)}, f32[80,128]{1,0:T(8,128)S(1)}, u32[]{:S(2)}, u32[]{:S(2)}) collective-permute-start(f32[80,128]{1,0:T(8,128)} %add_pieces.5), channel_id=1, source_target_pairs={{0,8},{4,12},{8,0},{12,4},{16,24},{20,28},{24,16},{28,20},{1,9},{5... | collective-permute-start | bytes 122888 | tf_op jit(solution)/shard_map/ppermute | solution.py:584
  119.9 5.9 %collective-permute-start.8 = (f32[80,128]{1,0:T(8,128)}, f32[80,128]{1,0:T(8,128)S(1)}, u32[]{:S(2)}, u32[]{:S(2)}) collective-permute-start(f32[80,128]{1,0:T(8,128)} %add_pieces.5), channel_id=1, source_target_pairs={{0,16},{4,20},{8,24},{12,28},{16,0},{20,4},{24,8},{28,12},{1,17},{... | collective-permute-start | bytes 122888 | tf_op jit(solution)/shard_map/ppermute | solution.py:584
  123.3 6.0 %collective-permute-start.9 = (f32[80,128]{1,0:T(8,128)}, f32[80,128]{1,0:T(8,128)S(1)}, u32[]{:S(2)}, u32[]{:S(2)}) collective-permute-start(f32[80,128]{1,0:T(8,128)} %add_pieces.5), channel_id=1, source_target_pairs={{0,24},{4,28},{8,16},{12,20},{16,8},{20,12},{24,0},{28,4},{1,25},{... | collective-permute-start | bytes 122888 | tf_op jit(solution)/shard_map/ppermute | solution.py:584
  130.1 5.4 %collective-permute-start.10 = (f32[320,128]{1,0:T(8,128)S(1)}, f32[320,128]{1,0:T(8,128)S(1)}, u32[]{:S(2)}, u32[]{:S(2)}) collective-permute-start(f32[320,128]{1,0:T(8,128)S(1)} %pad_maximum_fusion), channel_id=1, source_target_pairs={{0,1},{1,0},{2,3},{3,2},{4,5},{5,4},{6,7},{7,6},{8,9},{9,8},{10,11... | collective-permute-start | bytes 491528 | tf_op jit(solution)/shard_map/ppermute | solution.py:584
  130.8 6.1 %collective-permute-start.11 = (f32[320,128]{1,0:T(8,128)S(1)}, f32[320,128]{1,0:T(8,128)S(1)}, u32[]{:S(2)}, u32[]{:S(2)}) collective-permute-start(f32[320,128]{1,0:T(8,128)S(1)} %pad_maximum_fusion), channel_id=1, source_target_pairs={{0,2},{1,3},{2,0},{3,1},{4,6},{5,7},{6,4},{7,5},{8,10},{9,11},{10,... | collective-permute-start | bytes 491528 | tf_op jit(solution)/shard_map/ppermute | solution.py:584
  132.2 6.2 %collective-permute-start.12 = (f32[320,128]{1,0:T(8,128)S(1)}, f32[320,128]{1,0:T(8,128)S(1)}, u32[]{:S(2)}, u32[]{:S(2)}) collective-permute-start(f32[320,128]{1,0:T(8,128)S(1)} %pad_maximum_fusion), channel_id=1, source_target_pairs={{0,3},{1,2},{2,1},{3,0},{4,7},{5,6},{6,5},{7,4},{8,11},{9,10},{10,... | collective-permute-start | bytes 491528 | tf_op jit(solution)/shard_map/ppermute | solution.py:584
  138.5 6.0 %copy-start.2 = (f32[1280,128]{1,0:T(8,128)}, f32[1280,128]{1,0:T(8,128)S(1)}, u32[]{:S(2)}) copy-start(f32[1280,128]{1,0:T(8,128)S(1)} %constant_dynamic-update-slice_fusion.own_ref) | copy-start | bytes 1966084
  138.5 6.0 %collective-permute-start.13 = (f32[1280,128]{1,0:T(8,128)S(1)}, f32[1280,128]{1,0:T(8,128)S(1)}, u32[]{:S(2)}, u32[]{:S(2)}) collective-permute-start(f32[1280,128]{1,0:T(8,128)S(1)} %constant_dynamic-update-slice_fusion.own_ref), channel_id=1, source_target_pairs={{0,4},{4,0},{8,12},{12,8},{16,20},{20,16},{24,28},{28,24},{1,5},{5... | collective-permute-start | bytes 1966088 | tf_op jit(solution)/shard_map/ppermute | solution.py:584
  (7 other events, 5.4 us)

commit v3 on v2

--- a/solution.py
+++ b/solution.py
@@ -15,7 +15,7 @@
 SUBS = 8
 STEPS = NM + 1
 PAIRS = 4
-TABLE_ROWS = 728
+TABLE_ROWS = 729
 VMEM_LIMIT = 56 * 1024 * 1024
 
 
@@ -268,22 +268,14 @@
 
     fine_cos, fine_sin = angles(fine_total, 1)
     coarse_cos, coarse_sin = angles(coarse_total, fine_total)
-    order, is_sine = orders(1)
-    weights = []
-    for turn in range(4):
-        side = (order * turn) & 3
-        even = jnp.where(side == 0, 1.0, jnp.where(side == 2, -1.0, 0.0))
-        odd = jnp.where(side == 1, 1.0, jnp.where(side == 3, -1.0, 0.0))
-        weights.append((jnp.where(is_sine, odd, even), jnp.where(is_sine, even, -odd)))
+    _, is_sine = orders(fine_total)
     for tile in range(quarter // fine_total):
         left, right = coarse_cos[tile : tile + 1], coarse_sin[tile : tile + 1]
         cosine = left * fine_cos - right * fine_sin
         sine = right * fine_cos + left * fine_sin
-        for turn in range(4):
-            on_cos, on_sin = weights[turn]
-            out_ref[pl.ds(turn * quarter + tile * fine_total, fine_total), :] = (
-                on_cos * cosine + on_sin * sine
-            ).astype(jnp.bfloat16)
+        out_ref[pl.ds(tile * fine_total, fine_total), :] = jnp.where(
+            is_sine, sine, cosine
+        ).astype(jnp.bfloat16)
 
 
 def trig_table(pair_count, lon_count):
@@ -296,52 +288,60 @@
             fine_total=fine_total,
         ),
         grid=(lon_count,),
-        out_shape=jax.ShapeDtypeStruct((lon_count, NLON, 4 * pair_pad), jnp.bfloat16),
-        out_specs=pl.BlockSpec((None, NLON, 4 * pair_pad), lambda b: (b, 0, 0)),
+        out_shape=jax.ShapeDtypeStruct((lon_count, quarter, 4 * pair_pad), jnp.bfloat16),
+        out_specs=pl.BlockSpec((None, quarter, 4 * pair_pad), lambda b: (b, 0, 0)),
         compiler_params=pltpu.CompilerParams(vmem_limit_bytes=VMEM_LIMIT),
         cost_estimate=pl.CostEstimate(
-            flops=20 * lon_count * NLON * pair_pad,
-            bytes_accessed=lon_count * NLON * 8 * pair_pad,
+            flops=24 * lon_count * quarter * pair_pad,
+            bytes_accessed=lon_count * quarter * 8 * pair_pad,
             transcendentals=0,
         ),
         name="trig_table",
     )()
 
 
-def grid_kernel(trig_ref, coeff_ref, out_ref, right_ref, *, lon_count):
+def grid_kernel(trig_ref, coeff_ref, out_ref, right_ref, *, lon_count, pair_count):
     share = coeff_ref.shape[1]
     width = coeff_ref.shape[2]
     rows = coeff_ref.shape[0] // lon_count * share
-
-    @pl.when(pl.program_id(0) == 0)
-    def _():
-        values = coeff_ref[...].reshape(rows // share, lon_count, share, width)
-        for block in range(lon_count):
-            right_ref[block] = values[:, block].reshape(rows, width).T.astype(jnp.bfloat16)
-
+    values = coeff_ref[...].reshape(rows // share, lon_count, share, width)
+    line = lax.broadcasted_iota(jnp.int32, (width, rows), 0)
+    upper = line >= width // 2
+    pair = jnp.where(upper, line - width // 2, line)
+    is_sine = (pair & 1) == 1
+    for block in range(lon_count):
+        flat = values[:, block].reshape(rows, width).T
+        swapped = jnp.where(is_sine, -pltpu.roll(flat, 1, 0), pltpu.roll(flat, width - 1, 0))
+        order = block * pair_count + (pair >> 1)
+        order = jnp.where(upper, NM - 1 - order, order) & 3
+        odd = (order & 1) == 1
+        flip = jnp.where(odd, -flat, flat)
+        turned = jnp.where(order == 1, swapped, jnp.where(order == 3, -swapped, flat))
+        turned = jnp.where(order == 2, -flat, turned)
+        back = jnp.where(odd, -turned, turned)
+        for turn, part in enumerate((flat, turned, flip, back)):
+            right_ref[pl.ds(block * width, width), pl.ds(turn * rows, rows)] = part.astype(
+                jnp.bfloat16
+            )
     total = None
     for block in range(lon_count):
-        part = jnp.dot(trig_ref[block], right_ref[block], preferred_element_type=jnp.float32)
+        part = jnp.dot(
+            trig_ref[block],
+            right_ref[pl.ds(block * width, width), :],
+            preferred_element_type=jnp.float32,
+        )
         total = part if total is None else total + part
-    out_ref[...] = total
-
-
-def grid_field(trig, coeffs, lon_count):
-    share = coeffs.shape[1]
-    rows = coeffs.shape[0] // lon_count * share
-    width = trig.shape[2]
-    pieces = 4
-    cols = NLON // pieces
+    for turn in range(4):
+        out_ref[turn] = total[:, turn * rows : (turn + 1) * rows]
+
+
+def grid_field(trig, coeffs, pair_count):
+    lon_count, quarter, width = trig.shape
+    rows = coeffs.shape[0] // lon_count * coeffs.shape[1]
     return pl.pallas_call(
-        functools.partial(grid_kernel, lon_count=lon_count),
-        grid=(pieces,),
-        out_shape=jax.ShapeDtypeStruct((NLON, rows), jnp.float32),
-        in_specs=[
-            pl.BlockSpec((lon_count, cols, width), lambda j: (0, j, 0)),
-            pl.BlockSpec(coeffs.shape, lambda j: (0, 0, 0)),
-        ],
-        out_specs=pl.BlockSpec((cols, rows), lambda j: (j, 0)),
-        scratch_shapes=[pltpu.VMEM((lon_count, width, rows), jnp.bfloat16)],
+        functools.partial(grid_kernel, lon_count=lon_count, pair_count=pair_count),
+        out_shape=jax.ShapeDtypeStruct((4, quarter, rows), jnp.float32),
+        scratch_shapes=[pltpu.VMEM((lon_count * width, 4 * rows), jnp.bfloat16)],
         compiler_params=pltpu.CompilerParams(vmem_limit_bytes=VMEM_LIMIT),
         cost_estimate=pl.CostEstimate(
             flops=2 * NLON * lon_count * width * rows,
@@ -538,18 +538,17 @@
     )(index, *pieces)
 
 
-def finish_kernel(
-    place_ref, own_ref, other_ref, hidden_ref, bias_ref, out_ref, flat_ref, *, lon_count, depth
-):
+def finish_kernel(place_ref, *refs, lon_count, depth):
+    hidden_ref, bias_ref, out_ref, flat_ref = refs[2 * lon_count :]
     core, lon, deep = place_ref[0], place_ref[1], place_ref[2]
-    size = own_ref.shape[0] // (lon_count * depth)
-    for half, source in enumerate((own_ref, other_ref)):
+    size = refs[0].shape[0] // depth
+    for half in range(2):
         for part in range(lon_count):
             for piece in range(depth):
                 start = (((core ^ half) * lon_count + (lon ^ part)) * depth + (deep ^ piece)) * size
-                flat_ref[pl.ds(pl.multiple_of(start, SUBS), size), :] = source[
-                    pl.ds((part * depth + piece) * size, size), :
-                ]
+                flat_ref[pl.ds(pl.multiple_of(start, SUBS), size), :] = refs[
+                    half * lon_count + part
+                ][pl.ds(piece * size, size), :]
     width = hidden_ref.shape[0]
     tiles = width // LANES
     for row_tile in range(width // SUBS):
@@ -563,7 +562,8 @@
         bias_ref[:, pl.ds(tile * LANES, LANES)] = flat_ref[pl.ds(base + tiles * F + tile, 1), :]
 
 
-def finish(place, own, other, width, lon_count, depth):
+def finish(place, pieces, width, depth):
+    lon_count = len(pieces) // 2
     return pl.pallas_call(
         functools.partial(finish_kernel, lon_count=lon_count, depth=depth),
         out_shape=(
@@ -572,11 +572,11 @@
             jax.ShapeDtypeStruct((F, width), jnp.float32),
         ),
         in_specs=[pl.BlockSpec(memory_space=pltpu.SMEM)]
-        + [pl.BlockSpec(memory_space=pltpu.VMEM)] * 2,
+        + [pl.BlockSpec(memory_space=pltpu.VMEM)] * len(pieces),
         out_specs=(pl.BlockSpec(memory_space=pltpu.VMEM),) * 3,
-        scratch_shapes=[pltpu.VMEM((2 * own.shape[0], LANES), jnp.float32)],
+        scratch_shapes=[pltpu.VMEM((len(pieces) * pieces[0].shape[0], LANES), jnp.float32)],
         name="finish",
-    )(place, own, other)
+    )(place, *pieces)
 
 
 def swap(value, axis, bits):
@@ -625,16 +625,19 @@
     ).astype(jnp.bfloat16)
     w_out_t = jnp.concatenate([w_out.T, jnp.zeros((LANES - F, width), w_out.dtype)], axis=0)
 
-    coeffs, slope, hidden_t, latents_t, trig, scale, place, w_out_t = lax.optimization_barrier(
-        (coeffs, slope, hidden_t, latents_t, trig, scale, place, w_out_t)
-    )
-    grid = grid_field(trig, coeffs, lon_count).reshape(lon_count, lon_cols, lanes)
+    core_index, deep_index = lat_index & 1, lat_index >> 1
+    spots = jnp.stack([core_index, lon_index, deep_index])
+    coeffs, slope, hidden_t, latents_t, trig, scale, place, w_out_t, spots = (
+        lax.optimization_barrier(
+            (coeffs, slope, hidden_t, latents_t, trig, scale, place, w_out_t, spots)
+        )
+    )
+    grid = grid_field(trig, coeffs, pair_count).reshape(lon_count, lon_cols, lanes)
     grid = lax.all_to_all(grid, "lon", split_axis=0, concat_axis=0, tiled=True)
 
     device_count = lat_count * lon_count
     used_rows = (width + F + 1) * width // LANES
     chunk = pad_to(pad_to(used_rows, device_count) // device_count, SUBS)
-    core_index, deep_index = lat_index & 1, lat_index >> 1
     depth = lat_count // 2
     preact_back, keep, send = backward(
         core_index.reshape(1), grid, scale, place, w_out_t, slope, hidden_t, latents_t,
@@ -648,16 +651,15 @@
         lon_index.reshape(1), [keep, swap(send, "lat", 1)], lon_count
     )
     arrived = [swap(pieces[part], "lon", part) for part in range(1, lon_count)]
+    arrived, latent_grad = lax.optimization_barrier((arrived, latent_grad))
     pieces = add_pieces(deep_index.reshape(1), [pieces[0]] + arrived, depth)
     arrived = [swap(pieces[part], "lat", 2 * part) for part in range(1, depth)]
     norm = 1.0 / math.sqrt(rows_all * NLON)
     total = add_pieces(deep_index.reshape(1), [pieces[0]] + arrived, 1, norm)[0]
     total = jnp.concatenate([total] + [swap(total, "lat", 2 * part) for part in range(1, depth)])
-    total = jnp.concatenate([total] + [swap(total, "lon", part) for part in range(1, lon_count)])
-    other = swap(total, "lat", 1)
-    hidden_grad, bias_grad, out_grad = finish(
-        jnp.stack([core_index, lon_index, deep_index]), total, other, width, lon_count, depth
-    )
+    totals = [total] + [swap(total, "lon", part) for part in range(1, lon_count)]
+    totals = totals + [swap(piece, "lat", 1) for piece in totals]
+    hidden_grad, bias_grad, out_grad = finish(spots, totals, width, depth)
     return (
         latent_grad.reshape(lat_rows, lon_cols, width),
         hidden_grad,

time: 149 us -> 142 us (0.953)
  blocking collectives: 0 us -> 15.3 us
  waiting for transfers between devices: 37.1 us -> 21.8 us
  starting transfers between devices: 26.7 us -> 23.6 us
  Pallas kernels: 67.5 us -> 65.2 us
    all_to_all x0 -> x1, blocking collectives: none -> 15.3 us  [local(): grid = lax.all_to_all(grid, 'lon', split_axis=0, concat_axis=0, tiled=True)]
    all_to_all x1 -> x0, waiting for transfers between devices: 10.4 us -> none  [local(): grid = lax.all_to_all(grid, 'lon', split_axis=0, concat_axis=0, tiled=True)]
    ppermute x14 -> x17, waiting for transfers between devices: 22 us -> 16.5 us  [swap(): return lax.ppermute(value, axis, [(i, i ^ bits) for i in range(count)])]
    all_to_all x1 -> x0, starting transfers between devices: 3.49 us -> none  [local(): grid = lax.all_to_all(grid, 'lon', split_axis=0, concat_axis=0, tiled=True)]
    pallas_call x1, Pallas kernels: 5.38 us -> 3.67 us  [grid_field(): pl.pallas_call(functools.partial(grid_kernel, lon_count=lon_count, pair_c...]
    unnamed x36 -> x40, local copies, waits for them, and re-layouts: 5.64 us -> 4.19 us
    ppermute x14 -> x17, starting transfers between devices: 16 us -> 16.3 us  [swap(): return lax.ppermute(value, axis, [(i, i ^ bits) for i in range(count)])]
  transfers between devices with their start and end apart: 16 -> 18, of which waited for: 12 -> 12; matrix products, arithmetic and copies ran while one was open for 7% -> 6% of each run, Pallas kernels for 9% -> 9%
where the time goes in v3:
time: 142 us; the launch traced here: 141 us
  Pallas kernels  65.2 us (46%)
  starting transfers between devices  23.6 us (17%)
  waiting for transfers between devices  21.8 us (15%)
  blocking collectives  15.3 us (11%)
  local copies, waits for them, and re-layouts  5.5 us (4%)
  matrix products  5.16 us (4%)
  other arithmetic  3.4 us (2%)
    pallas_call x1, Pallas kernels, coefficients(): pl.pallas_call(kernel, out_shape=jax.ShapeDtypeStruct((lat_count, slot_co...  30.8 us
    ppermute x17, waiting for transfers between devices, swap(): return lax.ppermute(value, axis, [(i, i ^ bits) for i in range(count)])  16.5 us
    ppermute x17, starting transfers between devices, swap(): return lax.ppermute(value, axis, [(i, i ^ bits) for i in range(count)])  16.3 us
    all_to_all x1, blocking collectives, local(): grid = lax.all_to_all(grid, 'lon', split_axis=0, concat_axis=0, tiled=True)  15.3 us
    pallas_call x1, Pallas kernels, backward(): pl.pallas_call(backward_kernel, grid=(parts,), out_shape=(jax.ShapeDtypeS...  10.6 us
    pallas_call x1, Pallas kernels, forward(): pl.pallas_call(forward_kernel, grid=(parts,), out_shape=(jax.ShapeDtypeSt...  9.04 us
    all_to_all x1, starting transfers between devices, local(): lax.all_to_all(coeffs, ('lat', 'lon'), split_axis=0, concat_axis=0, tiled...  7.3 us
    pallas_call x3, Pallas kernels, add_pieces(): pl.pallas_call(functools.partial(add_kernel, inputs=len(pieces), outputs=...  5.52 us
  transfers between devices with their start and end apart: 18, of which 12 were waited for; matrix products, arithmetic and copies ran while one was open for 6% of the time, Pallas kernels for 9%

profile of v3, /device:TPU:0, one launch (start us, length us, event | category | flops | bytes accessed | tf_op | source)
XLA Modules:
  0.0 140.9 jit_solution(15364230058904968151)
XLA Ops:
  0.7 30.8 %coefficients.1 = f32[8,64,384]{2,1,0:T(8,128)} custom-call(s32[1]{0:T(128)} %bitcast.2.first_ref, f32[8,90,2,721]{3,2,1,0:T(2,128)} %bitcast.16), custom_call_target="tpu_custom_call" | custom-call | tf_op jit(solution)/shard_map/coefficients/pallas_call | solution.py:227
  31.5 7.3 %all-to-all-start = ((f32[32,16,384]{2,1,0:T(8,128)}), f32[32,16,384]{2,1,0:T(8,128)S(1)}, u32[]{:S(2)}, u32[]{:S(2)}) async-start(f32[32,16,384]{2,1,0:T(8,128)} %bitcast.17), calls=%async_computation | async-start | bytes 1572864 | tf_op jit(solution)/shard_map/all_to_all | solution.py:602
  40.9 3.0 %trig_table.1.trig_ref = bf16[4,360,384]{2,1,0:T(8,128)(2,1)} custom-call(), custom_call_target="tpu_custom_call" | custom-call | flops 3317760 | bytes 1105920 | tf_op jit(solution)/shard_map/trig_table/pallas_call | solution.py:285
  44.6 9.0 %forward.1 = (f32[2880,512]{1,0:T(8,128)}, bf16[4,512,720]{2,1,0:T(8,128)(2,1)}, bf16[4,512,720]{2,1,0:T(8,128)(2,1)}) custom-call(bf16[2880,512]{1,0:T(8,128)(2,1)} %bitcast.21, bf16[512,512]{1,0:T(8,128)(2,1)} %w_ref.1, f32[1,512]{1,0:T(1,128)} %bitcast.23), custom_call_target="tpu_custom_call" | custom-call | flops 1509949440 | bytes 14745600 | tf_op jit(solution)/shard_map/forward/pallas_call | solution.py:378
  54.8 5.4 %all-to-all-done.coeff_ref = f32[32,16,384]{2,1,0:T(8,128)S(1)} async-done(((f32[32,16,384]{2,1,0:T(8,128)}), f32[32,16,384]{2,1,0:T(8,128)S(1)}, u32[]{:S(2)}, u32[]{:S(2)}) %all-to-all-start) | async-done | bytes 786464 | tf_op jit(solution)/shard_map/all_to_all | solution.py:602
  61.1 3.7 %grid_field.1 = f32[4,360,128]{2,1,0:T(8,128)} custom-call(bf16[4,360,384]{2,1,0:T(8,128)(2,1)} %trig_table.1.trig_ref, f32[32,16,384]{2,1,0:T(8,128)} %copy-done), custom_call_target="tpu_custom_call" | custom-call | flops 566231040 | bytes 2678784 | tf_op jit(solution)/shard_map/grid_field/pallas_call | solution.py:341
  64.8 15.3 %all_to_all.10.grid_ref = f32[4,360,128]{2,1,0:T(8,128)} all-to-all(f32[4,360,128]{2,1,0:T(8,128)} %grid_field.1), channel_id=1, replica_groups=mesh['lat'=8,'lon'=4] {'lon'}, dimensions={0} | all-to-all | bytes 1474560 | tf_op jit(solution)/shard_map/all_to_all | solution.py:636
  80.1 10.6 %backward.1 = (bf16[2880,512]{1,0:T(8,128)(2,1)}, f32[1280,128]{1,0:T(8,128)}, f32[1280,128]{1,0:T(8,128)}) custom-call(s32[1]{0:T(128)} %bitcast.1.core_ref, f32[4,360,128]{2,1,0:T(8,128)} %all_to_all.10.grid_ref, f32[4,1,128]{2,1,0:T(1,128)} %mul.38.scale_ref, bf16[4,128,1024]{2,1,0:T(8,128)(2,1)} %fusion.place_ref, ...), custom_call_target="tpu_custom_call" | custom-call | flops 2264924160 | bytes 14745600 | tf_op jit(solution)/shard_map/backward/pallas_call | solution.py:471
  90.8 2.3 %collective-permute-done.refs_1_ = f32[1280,128]{1,0:T(8,128)S(1)} collective-permute-done((f32[1280,128]{1,0:T(8,128)}, f32[1280,128]{1,0:T(8,128)S(1)}, u32[]{:S(2)}, u32[]{:S(2)}) %collective-permute-start) | collective-permute-done | bytes 655392 | tf_op jit(solution)/shard_map/ppermute | solution.py:584
  93.9 2.2 %add_pieces.3 = (f32[320,128]{1,0:T(8,128)}, f32[320,128]{1,0:T(8,128)}, f32[320,128]{1,0:T(8,128)}, f32[320,128]{1,0:T(8,128)}) custom-call(s32[1]{0:T(128)} %bitcast.index_ref, f32[1280,128]{1,0:T(8,128)} %get-tuple-element.45.refs_0_, f32[1280,128]{1,0:T(8,128)} %copy-done.2), custom_call_target="tpu_custom_call" | custom-call | flops 327680 | bytes 1966080 | tf_op jit(solution)/shard_map/add_pieces/pallas_call | solution.py:526
  97.5 2.1 %collective-permute-start.3 = (f32[320,128]{1,0:T(8,128)}, f32[320,128]{1,0:T(8,128)S(1)}, u32[]{:S(2)}, u32[]{:S(2)}) collective-permute-start(f32[320,128]{1,0:T(8,128)} %get-tuple-element.49), channel_id=1, source_target_pairs={{0,3},{1,2},{2,1},{3,0},{4,7},{5,6},{6,5},{7,4},{8,11},{9,10},{10,... | collective-permute-start | bytes 491528 | tf_op jit(solution)/shard_map/ppermute | solution.py:584
  99.6 5.2 %convolution_convert_fusion = bf16[2880,512]{1,0:T(8,128)(2,1)} fusion(bf16[2880,512]{1,0:T(8,128)(2,1)} %get-tuple-element.50, bf16[512,512]{1,0:T(8,128)(2,1)S(1)} %copy-done.19), kind=kOutput, calls=%fused_computation | convolution fusion | flops 1511424000 | bytes 6422528 | tf_op jit(solution)/shard_map/dot_general | solution.py:646
  104.8 1.8 %collective-permute-done.2.refs_2_ = f32[320,128]{1,0:T(8,128)S(1)} collective-permute-done((f32[320,128]{1,0:T(8,128)}, f32[320,128]{1,0:T(8,128)S(1)}, u32[]{:S(2)}, u32[]{:S(2)}) %collective-permute-start.2) | collective-permute-done | bytes 163872 | tf_op jit(solution)/shard_map/ppermute | solution.py:584
  107.3 1.8 %add_pieces.4 = (f32[80,128]{1,0:T(8,128)}, f32[80,128]{1,0:T(8,128)}, f32[80,128]{1,0:T(8,128)}, f32[80,128]{1,0:T(8,128)}) custom-call(s32[1]{0:T(128)} %bitcast.10.index_ref, f32[320,128]{1,0:T(8,128)} %get-tuple-element.53.refs_0_, f32[320,128]{1,0:T(8,128)} %copy-done.10, f32[320,128]{1,0:T(8,128)} %copy-done.11, f32[320,128]{1,0:T(8,128)} %copy-done.12), custom_call_target="tpu_custom_call" | custom-call | flops 163840 | bytes 819200 | tf_op jit(solution)/shard_map/add_pieces/pallas_call | solution.py:526
  110.7 2.8 %collective-permute-start.6 = (f32[80,128]{1,0:T(8,128)}, f32[80,128]{1,0:T(8,128)S(1)}, u32[]{:S(2)}, u32[]{:S(2)}) collective-permute-start(f32[80,128]{1,0:T(8,128)} %get-tuple-element.60), channel_id=1, source_target_pairs={{0,24},{4,28},{8,16},{12,20},{16,8},{20,12},{24,0},{28,4},{1,25},{... | collective-permute-start | bytes 122888 | tf_op jit(solution)/shard_map/ppermute | solution.py:584
  115.1 1.7 %collective-permute-done.6.refs_3_ = f32[80,128]{1,0:T(8,128)S(1)} collective-permute-done((f32[80,128]{1,0:T(8,128)}, f32[80,128]{1,0:T(8,128)S(1)}, u32[]{:S(2)}, u32[]{:S(2)}) %collective-permute-start.6) | collective-permute-done | bytes 40992 | tf_op jit(solution)/shard_map/ppermute | solution.py:584
  118.8 2.8 %collective-permute-start.9 = (f32[80,128]{1,0:T(8,128)}, f32[80,128]{1,0:T(8,128)S(1)}, u32[]{:S(2)}, u32[]{:S(2)}) collective-permute-start(f32[80,128]{1,0:T(8,128)} %add_pieces.5), channel_id=1, source_target_pairs={{0,24},{4,28},{8,16},{12,20},{16,8},{20,12},{24,0},{28,4},{1,25},{... | collective-permute-start | bytes 122888 | tf_op jit(solution)/shard_map/ppermute | solution.py:584
  121.6 1.6 %collective-permute-start.7 = (f32[80,128]{1,0:T(8,128)}, f32[80,128]{1,0:T(8,128)S(1)}, u32[]{:S(2)}, u32[]{:S(2)}) collective-permute-start(f32[80,128]{1,0:T(8,128)} %add_pieces.5), channel_id=1, source_target_pairs={{0,8},{4,12},{8,0},{12,4},{16,24},{20,28},{24,16},{28,20},{1,9},{5... | collective-permute-start | bytes 122888 | tf_op jit(solution)/shard_map/ppermute | solution.py:584
  123.2 1.6 %collective-permute-done.9 = f32[80,128]{1,0:T(8,128)S(1)} collective-permute-done((f32[80,128]{1,0:T(8,128)}, f32[80,128]{1,0:T(8,128)S(1)}, u32[]{:S(2)}, u32[]{:S(2)}) %collective-permute-start.9) | collective-permute-done | bytes 40992 | tf_op jit(solution)/shard_map/ppermute | solution.py:584
  124.8 1.9 %collective-permute-done.8 = f32[80,128]{1,0:T(8,128)S(1)} collective-permute-done((f32[80,128]{1,0:T(8,128)}, f32[80,128]{1,0:T(8,128)S(1)}, u32[]{:S(2)}, u32[]{:S(2)}) %collective-permute-start.8) | collective-permute-done | bytes 40992 | tf_op jit(solution)/shard_map/ppermute | solution.py:584
  127.6 1.5 %collective-permute-start.12 = (f32[320,128]{1,0:T(8,128)S(1)}, f32[320,128]{1,0:T(8,128)S(1)}, u32[]{:S(2)}, u32[]{:S(2)}) collective-permute-start(f32[320,128]{1,0:T(8,128)S(1)} %pad_maximum_fusion.refs_0_), channel_id=1, source_target_pairs={{0,3},{1,2},{2,1},{3,0},{4,7},{5,6},{6,5},{7,4},{8,11},{9,10},{10,... | collective-permute-start | bytes 491528 | tf_op jit(solution)/shard_map/ppermute | solution.py:584
  131.1 2.8 %collective-permute-done.12.refs_3_ = f32[320,128]{1,0:T(8,128)S(1)} collective-permute-done((f32[320,128]{1,0:T(8,128)S(1)}, f32[320,128]{1,0:T(8,128)S(1)}, u32[]{:S(2)}, u32[]{:S(2)}) %collective-permute-start.12) | collective-permute-done | bytes 163872 | tf_op jit(solution)/shard_map/ppermute | solution.py:584
  133.9 1.6 %collective-permute-done.11.refs_2_ = f32[320,128]{1,0:T(8,128)S(1)} collective-permute-done((f32[320,128]{1,0:T(8,128)S(1)}, f32[320,128]{1,0:T(8,128)S(1)}, u32[]{:S(2)}, u32[]{:S(2)}) %collective-permute-start.11) | collective-permute-done | bytes 163872 | tf_op jit(solution)/shard_map/ppermute | solution.py:584
  138.3 2.6 %finish.1 = (f32[512,512]{1,0:T(8,128)}, f32[1,512]{1,0:T(1,128)}, f32[64,512]{1,0:T(8,128)}) custom-call(s32[3]{0:T(128)} %pad_add_fusion.place_ref, f32[320,128]{1,0:T(8,128)} %copy-done.1, f32[320,128]{1,0:T(8,128)} %copy-done.5, f32[320,128]{1,0:T(8,128)} %copy-done.4, f32[320,128]{1,0:T(8,128)} %copy-done.3, f32[320,128]{1,0:T(8,128)} %copy-done.6, ...), custom_call_target="tpu_custom_call" | custom-call | tf_op jit(solution)/shard_map/finish/pallas_call | solution.py:567
  (83 shorter events, 18.4 us)
Async XLA Ops:
  0.6 38.3 %copy-start.17 = (s32[64]{0:T(128)S(1)}, s32[64]{0:T(128)}, u32[]{:S(2)}) copy-start(s32[64]{0:T(128)} %param.8) | copy-start | bytes 772
  0.6 38.9 %copy-start.18 = (f32[64]{0:T(128)S(1)}, f32[64]{0:T(128)}, u32[]{:S(2)}) copy-start(f32[64]{0:T(128)} %param.9) | copy-start | bytes 772
  0.7 39.6 %copy-start.13 = (bf16[512,64]{0,1:T(8,128)(2,1)S(1)}, bf16[512,64]{0,1:T(8,128)(2,1)}, u32[]{:S(2)}) copy-start(bf16[512,64]{0,1:T(8,128)(2,1)} %param.13) | copy-start | bytes 196612
  31.5 28.7 %all-to-all-start = ((f32[32,16,384]{2,1,0:T(8,128)}), f32[32,16,384]{2,1,0:T(8,128)S(1)}, u32[]{:S(2)}, u32[]{:S(2)}) async-start(f32[32,16,384]{2,1,0:T(8,128)} %bitcast.17), calls=%async_computation | async-start | bytes 1572864 | tf_op jit(solution)/shard_map/all_to_all | solution.py:602
  80.1 19.5 %copy-start.19 = (bf16[512,512]{1,0:T(8,128)(2,1)S(1)}, bf16[512,512]{1,0:T(8,128)(2,1)}, u32[]{:S(2)}) copy-start(bf16[512,512]{1,0:T(8,128)(2,1)} %w_ref.1) | copy-start | bytes 1572868
  90.8 2.3 %collective-permute-start = (f32[1280,128]{1,0:T(8,128)}, f32[1280,128]{1,0:T(8,128)S(1)}, u32[]{:S(2)}, u32[]{:S(2)}) collective-permute-start(f32[1280,128]{1,0:T(8,128)} %get-tuple-element.46), channel_id=1, source_target_pairs={{0,4},{4,0},{8,12},{12,8},{16,20},{20,16},{24,28},{28,24},{1,5},{5... | collective-permute-start | bytes 1966088 | tf_op jit(solution)/shard_map/ppermute | solution.py:584
  96.1 8.7 %collective-permute-start.1 = (f32[320,128]{1,0:T(8,128)}, f32[320,128]{1,0:T(8,128)S(1)}, u32[]{:S(2)}, u32[]{:S(2)}) collective-permute-start(f32[320,128]{1,0:T(8,128)} %get-tuple-element.47), channel_id=1, source_target_pairs={{0,1},{1,0},{2,3},{3,2},{4,5},{5,4},{6,7},{7,6},{8,9},{9,8},{10,11... | collective-permute-start | bytes 491528 | tf_op jit(solution)/shard_map/ppermute | solution.py:584
  96.9 9.7 %collective-permute-start.2 = (f32[320,128]{1,0:T(8,128)}, f32[320,128]{1,0:T(8,128)S(1)}, u32[]{:S(2)}, u32[]{:S(2)}) collective-permute-start(f32[320,128]{1,0:T(8,128)} %get-tuple-element.48), channel_id=1, source_target_pairs={{0,2},{1,3},{2,0},{3,1},{4,6},{5,7},{6,4},{7,5},{8,10},{9,11},{10,... | collective-permute-start | bytes 491528 | tf_op jit(solution)/shard_map/ppermute | solution.py:584
  97.5 9.1 %collective-permute-start.3 = (f32[320,128]{1,0:T(8,128)}, f32[320,128]{1,0:T(8,128)S(1)}, u32[]{:S(2)}, u32[]{:S(2)}) collective-permute-start(f32[320,128]{1,0:T(8,128)} %get-tuple-element.49), channel_id=1, source_target_pairs={{0,3},{1,2},{2,1},{3,0},{4,7},{5,6},{6,5},{7,4},{8,11},{9,10},{10,... | collective-permute-start | bytes 491528 | tf_op jit(solution)/shard_map/ppermute | solution.py:584
  109.2 4.4 %collective-permute-start.4 = (f32[80,128]{1,0:T(8,128)}, f32[80,128]{1,0:T(8,128)S(1)}, u32[]{:S(2)}, u32[]{:S(2)}) collective-permute-start(f32[80,128]{1,0:T(8,128)} %get-tuple-element.58), channel_id=1, source_target_pairs={{0,8},{4,12},{8,0},{12,4},{16,24},{20,28},{24,16},{28,20},{1,9},{5... | collective-permute-start | bytes 122888 | tf_op jit(solution)/shard_map/ppermute | solution.py:584
  110.0 5.1 %collective-permute-start.5 = (f32[80,128]{1,0:T(8,128)}, f32[80,128]{1,0:T(8,128)S(1)}, u32[]{:S(2)}, u32[]{:S(2)}) collective-permute-start(f32[80,128]{1,0:T(8,128)} %get-tuple-element.59), channel_id=1, source_target_pairs={{0,16},{4,20},{8,24},{12,28},{16,0},{20,4},{24,8},{28,12},{1,17},{... | collective-permute-start | bytes 122888 | tf_op jit(solution)/shard_map/ppermute | solution.py:584
  110.7 6.0 %collective-permute-start.6 = (f32[80,128]{1,0:T(8,128)}, f32[80,128]{1,0:T(8,128)S(1)}, u32[]{:S(2)}, u32[]{:S(2)}) collective-permute-start(f32[80,128]{1,0:T(8,128)} %get-tuple-element.60), channel_id=1, source_target_pairs={{0,24},{4,28},{8,16},{12,20},{16,8},{20,12},{24,0},{28,4},{1,25},{... | collective-permute-start | bytes 122888 | tf_op jit(solution)/shard_map/ppermute | solution.py:584
  118.8 6.0 %collective-permute-start.9 = (f32[80,128]{1,0:T(8,128)}, f32[80,128]{1,0:T(8,128)S(1)}, u32[]{:S(2)}, u32[]{:S(2)}) collective-permute-start(f32[80,128]{1,0:T(8,128)} %add_pieces.5), channel_id=1, source_target_pairs={{0,24},{4,28},{8,16},{12,20},{16,8},{20,12},{24,0},{28,4},{1,25},{... | collective-permute-start | bytes 122888 | tf_op jit(solution)/shard_map/ppermute | solution.py:584
  121.6 5.1 %collective-permute-start.8 = (f32[80,128]{1,0:T(8,128)}, f32[80,128]{1,0:T(8,128)S(1)}, u32[]{:S(2)}, u32[]{:S(2)}) collective-permute-start(f32[80,128]{1,0:T(8,128)} %add_pieces.5), channel_id=1, source_target_pairs={{0,16},{4,20},{8,24},{12,28},{16,0},{20,4},{24,8},{28,12},{1,17},{... | collective-permute-start | bytes 122888 | tf_op jit(solution)/shard_map/ppermute | solution.py:584
  121.6 5.1 %collective-permute-start.7 = (f32[80,128]{1,0:T(8,128)}, f32[80,128]{1,0:T(8,128)S(1)}, u32[]{:S(2)}, u32[]{:S(2)}) collective-permute-start(f32[80,128]{1,0:T(8,128)} %add_pieces.5), channel_id=1, source_target_pairs={{0,8},{4,12},{8,0},{12,4},{16,24},{20,28},{24,16},{28,20},{1,9},{5... | collective-permute-start | bytes 122888 | tf_op jit(solution)/shard_map/ppermute | solution.py:584
  127.5 9.7 %copy-start.1 = (f32[320,128]{1,0:T(8,128)}, f32[320,128]{1,0:T(8,128)S(1)}, u32[]{:S(2)}) copy-start(f32[320,128]{1,0:T(8,128)S(1)} %pad_maximum_fusion.refs_0_) | copy-start | bytes 491524
  127.6 6.4 %collective-permute-start.12 = (f32[320,128]{1,0:T(8,128)S(1)}, f32[320,128]{1,0:T(8,128)S(1)}, u32[]{:S(2)}, u32[]{:S(2)}) collective-permute-start(f32[320,128]{1,0:T(8,128)S(1)} %pad_maximum_fusion.refs_0_), channel_id=1, source_target_pairs={{0,3},{1,2},{2,1},{3,0},{4,7},{5,6},{6,5},{7,4},{8,11},{9,10},{10,... | collective-permute-start | bytes 491528 | tf_op jit(solution)/shard_map/ppermute | solution.py:584
  129.1 6.5 %collective-permute-start.11 = (f32[320,128]{1,0:T(8,128)S(1)}, f32[320,128]{1,0:T(8,128)S(1)}, u32[]{:S(2)}, u32[]{:S(2)}) collective-permute-start(f32[320,128]{1,0:T(8,128)S(1)} %pad_maximum_fusion.refs_0_), channel_id=1, source_target_pairs={{0,2},{1,3},{2,0},{3,1},{4,6},{5,7},{6,4},{7,5},{8,10},{9,11},{10,... | collective-permute-start | bytes 491528 | tf_op jit(solution)/shard_map/ppermute | solution.py:584
  130.3 5.3 %collective-permute-start.10 = (f32[320,128]{1,0:T(8,128)S(1)}, f32[320,128]{1,0:T(8,128)S(1)}, u32[]{:S(2)}, u32[]{:S(2)}) collective-permute-start(f32[320,128]{1,0:T(8,128)S(1)} %pad_maximum_fusion.refs_0_), channel_id=1, source_target_pairs={{0,1},{1,0},{2,3},{3,2},{4,5},{5,4},{6,7},{7,6},{8,9},{9,8},{10,11... | collective-permute-start | bytes 491528 | tf_op jit(solution)/shard_map/ppermute | solution.py:584
  131.1 5.0 %collective-permute-start.13 = (f32[320,128]{1,0:T(8,128)S(1)}, f32[320,128]{1,0:T(8,128)S(1)}, u32[]{:S(2)}, u32[]{:S(2)}) collective-permute-start(f32[320,128]{1,0:T(8,128)S(1)} %pad_maximum_fusion.refs_0_), channel_id=1, source_target_pairs={{0,4},{4,0},{8,12},{12,8},{16,20},{20,16},{24,28},{28,24},{1,5},{5... | collective-permute-start | bytes 491528 | tf_op jit(solution)/shard_map/ppermute | solution.py:584
  133.9 3.3 %copy-start.3 = (f32[320,128]{1,0:T(8,128)}, f32[320,128]{1,0:T(8,128)S(1)}, u32[]{:S(2)}) copy-start(f32[320,128]{1,0:T(8,128)S(1)} %collective-permute-done.12.refs_3_) | copy-start | bytes 491524
  133.9 2.2 %collective-permute-start.16 = (f32[320,128]{1,0:T(8,128)S(1)}, f32[320,128]{1,0:T(8,128)S(1)}, u32[]{:S(2)}, u32[]{:S(2)}) collective-permute-start(f32[320,128]{1,0:T(8,128)S(1)} %collective-permute-done.12.refs_3_), channel_id=1, source_target_pairs={{0,4},{4,0},{8,12},{12,8},{16,20},{20,16},{24,28},{28,24},{1,5},{5... | collective-permute-start | bytes 491528 | tf_op jit(solution)/shard_map/ppermute | solution.py:584
  135.6 1.4 collective-permute-start.15
  135.7 1.6 %collective-permute-start.14 = (f32[320,128]{1,0:T(8,128)S(1)}, f32[320,128]{1,0:T(8,128)S(1)}, u32[]{:S(2)}, u32[]{:S(2)}) collective-permute-start(f32[320,128]{1,0:T(8,128)S(1)} %collective-permute-done.10.refs_1_), channel_id=1, source_target_pairs={{0,4},{4,0},{8,12},{12,8},{16,20},{20,16},{24,28},{28,24},{1,5},{5... | collective-permute-start | bytes 491528 | tf_op jit(solution)/shard_map/ppermute | solution.py:584
  (14 other events, 17.2 us)

commit v4 on v3

--- a/solution.py
+++ b/solution.py
@@ -15,8 +15,9 @@
 SUBS = 8
 STEPS = NM + 1
 PAIRS = 4
-TABLE_ROWS = 729
-VMEM_LIMIT = 56 * 1024 * 1024
+TABLE_ROWS = 728
+MIB = 1024 * 1024
+VMEM_LIMIT = 56 * MIB
 
 
 def band_angles(row_ids, rows_all):
@@ -28,13 +29,12 @@
 
 
 def coeff_kernel(
-    first_ref, spectra_hbm, out_ref, spectra_ref, grow_ref, shrink_ref, table_ref, stage_ref,
-    copy_sem, *, pair_count, rows_all, lat_rows, slot_count,
+    first_ref, spectra_hbm, out_ref, spectra_ref, grow_ref, factor_ref, scale_ref, table_ref,
+    stage_ref, copy_sem, *, pair_count, rows_all, lat_rows, slot_count,
 ):
     per_block = LANES // rows_all
     vregs = pad_to(pair_count, SUBS * per_block) // (SUBS * per_block)
     step_tile = rows_all
-    tile_total = pad_to(STEPS, step_tile) // step_tile
     pair_pad = pad_to(pair_count, SUBS)
     lat_count = rows_all // lat_rows
     first_pair = first_ref[0]
@@ -67,6 +67,32 @@
         order = order_of(which).astype(jnp.float32)
         return jnp.exp(0.5 * total - 0.5 * math.log(4.0 * math.pi) + order * log_sine)
 
+    pairs = vregs * SUBS * per_block
+    steps_pad = pad_to(STEPS, LANES)
+    step = lax.broadcasted_iota(jnp.int32, (pairs, steps_pad), 1)
+    pair = first_pair + lax.broadcasted_iota(jnp.int32, (pairs, steps_pad), 0)
+    switch = NM - pair
+    in_first = step < switch
+    order = jnp.where(in_first, pair, NM - 1 - pair).astype(jnp.float32)
+    degree = jnp.where(in_first, pair + step, step - 1).astype(jnp.float32)
+    grow = jnp.sqrt(
+        jnp.maximum(4.0 * degree * degree - 1.0, 1.0)
+        / jnp.maximum(degree * degree - order * order, 1.0)
+    )
+    since = jnp.where(in_first, step, step - switch)
+    scale = jnp.where(since >= 2, grow / pltpu.roll(grow, 1, 1), 1.0)
+    shift = 2
+    while shift < STEPS:
+        scale = jnp.where(since >= shift, scale * pltpu.roll(scale, shift, 1), scale)
+        shift = 2 * shift
+    factor = grow * pltpu.roll(scale, 1, 1) / scale
+    for tile in range(steps_pad // LANES):
+        factor_ref[tile] = factor[:, tile * LANES : (tile + 1) * LANES]
+        for row in range(0, pairs, SUBS):
+            piece = scale[row : row + SUBS, tile * LANES : (tile + 1) * LANES]
+            for part in range(2):
+                scale_ref[tile, pl.ds(2 * row + part, SUBS, stride=2), :] = piece
+
     firsts, seconds, switches = [], [], []
     for v in range(vregs):
         base = first_pair + (sub + v * SUBS) * per_block
@@ -79,51 +105,45 @@
 
         firsts.append(seed(order_first))
         seconds.append(seed(order_second))
-        pair = base + which
-        switch = NM - pair
-        switches.append(switch)
-        for tile in range(tile_total):
-            step = inner + tile * step_tile
-            in_first = step < switch
-            order = jnp.where(in_first, pair, NM - 1 - pair).astype(jnp.float32)
-            degree = jnp.where(in_first, pair + step, step - 1).astype(jnp.float32)
-            lower = degree - 1.0
-            grow = jnp.sqrt(
-                (4.0 * degree * degree - 1.0) / jnp.maximum(degree * degree - order * order, 1.0)
-            )
-            shrink = jnp.sqrt(
-                jnp.maximum(lower * lower - order * order, 0.0)
-                / jnp.maximum(4.0 * lower * lower - 1.0, 1.0)
-            )
-            start = step == 0
-            grow_ref[tile, pl.ds(v * SUBS, SUBS), :] = jnp.where(start, 1.0, grow)
-            shrink_ref[tile, pl.ds(v * SUBS, SUBS), :] = jnp.where(start, -1.0, shrink)
-
-    def advance(tile, offset, state, grows, shrinks):
+        switches.append(NM - (base + which))
+        rows = pl.ds(v * SUBS, SUBS)
+        for tile in range(steps_pad // LANES):
+            if per_block == 1:
+                grow_ref[tile, rows, :] = factor_ref[tile, rows, :]
+            else:
+                even = factor_ref[tile, pl.ds(2 * v * SUBS, SUBS, stride=2), :]
+                odd = factor_ref[tile, pl.ds(2 * v * SUBS + 1, SUBS, stride=2), :]
+                low = lane < rows_all
+                grow_ref[2 * tile, rows, :] = jnp.where(low, even, pltpu.roll(odd, rows_all, 1))
+                grow_ref[2 * tile + 1, rows, :] = jnp.where(
+                    low, pltpu.roll(even, rows_all, 1), odd
+                )
+
+    def advance(tile, offset, state, grows):
         previous, before = state
         index = which * rows_all + offset
         step = tile * step_tile + offset
-        produced = []
+        produced, kept = [], []
         for v in range(vregs):
             grow = jnp.take_along_axis(grows[v], index, axis=1)
-            shrink = jnp.take_along_axis(shrinks[v], index, axis=1)
-            value = grow * (cosine * previous[v] - shrink * before[v])
-            value = jnp.where(switches[v] == step, seconds[v], value)
+            value = (grow * cosine) * previous[v] - before[v]
+            restart = switches[v] == step
+            value = jnp.where(restart, seconds[v], value)
             table_ref[pl.ds(v * SUBS * TABLE_ROWS + step, SUBS, stride=TABLE_ROWS), :] = value
             produced.append(value)
-        return (tuple(produced), previous)
+            kept.append(jnp.where(restart, 0.0, previous[v]))
+        return (tuple(produced), tuple(kept))
 
     def run_tile(tile, state, count, unroll):
         grows = [grow_ref[tile, pl.ds(v * SUBS, SUBS), :] for v in range(vregs)]
-        shrinks = [shrink_ref[tile, pl.ds(v * SUBS, SUBS), :] for v in range(vregs)]
 
         def body(offset, carry):
-            return advance(tile, offset, carry, grows, shrinks)
+            return advance(tile, offset, carry, grows)
 
         return lax.fori_loop(0, count, body, state, unroll=unroll)
 
     zeros = tuple(jnp.zeros((SUBS, LANES), jnp.float32) for _ in range(vregs))
-    state = (zeros, tuple(firsts))
+    state = (zeros, tuple(-value for value in firsts))
     whole_tiles = STEPS // step_tile
     state = lax.fori_loop(
         0, whole_tiles, lambda tile, carry: run_tile(tile, carry, step_tile, 8), state
@@ -150,17 +170,17 @@
     def product(left, right):
         left_high, left_low = split_parts(left)
         right_high, right_low = split_parts(right)
-        if left.shape[1] % LANES:
-            return (
-                dot(left_high, right_high) + dot(left_low, right_high) + dot(left_high, right_low)
-            )
-        return dot(
-            jnp.concatenate([left_high, left_low, left_high], axis=1),
-            jnp.concatenate([right_high, right_high, right_low], axis=0),
-        )
+        rows = left.shape[0]
+        both = dot(jnp.concatenate([left_high, left_low], axis=0), right_high)
+        return both[:rows] + both[rows:] + dot(left_high, right_low)
 
     def group(start):
         values = spectra_ref[:, pl.ds(start, PAIRS), :, :].reshape(slot_count, SUBS, STEPS)
+        scale = jnp.concatenate(
+            [scale_ref[tile, pl.ds(2 * start, SUBS), :] for tile in range(scale_ref.shape[0])],
+            axis=1,
+        )
+        values = values * scale[:, :STEPS]
         step = lax.broadcasted_iota(jnp.int32, (1, SUBS, STEPS), 2)
         row_pair = lax.broadcasted_iota(jnp.int32, (1, SUBS, STEPS), 1) // 2
         in_first = step < NM - (first_pair + start + row_pair)
@@ -217,7 +237,8 @@
     slot_count, _, pair_count, steps = spectra.shape
     per_block = LANES // rows_all
     vregs = pad_to(pair_count, SUBS * per_block) // (SUBS * per_block)
-    tile_total = pad_to(STEPS, rows_all) // rows_all
+    pairs = vregs * SUBS * per_block
+    tile_total = pad_to(STEPS, LANES) // rows_all
     pair_pad = pad_to(pair_count, SUBS)
     lat_count = rows_all // lat_rows
     kernel = functools.partial(
@@ -237,7 +258,8 @@
         scratch_shapes=[
             pltpu.VMEM((slot_count, pair_count, 2, steps), jnp.float32),
             pltpu.VMEM((tile_total, vregs * SUBS, LANES), jnp.float32),
-            pltpu.VMEM((tile_total, vregs * SUBS, LANES), jnp.float32),
+            pltpu.VMEM((pad_to(STEPS, LANES) // LANES, pairs, LANES), jnp.float32),
+            pltpu.VMEM((pad_to(STEPS, LANES) // LANES, 2 * pairs, LANES), jnp.float32),
             pltpu.VMEM((vregs * SUBS * TABLE_ROWS, LANES), jnp.float32),
             pltpu.VMEM((slot_count, 4 * pair_pad, LANES), jnp.float32),
             pltpu.SemaphoreType.DMA,
@@ -342,7 +364,7 @@
         functools.partial(grid_kernel, lon_count=lon_count, pair_count=pair_count),
         out_shape=jax.ShapeDtypeStruct((4, quarter, rows), jnp.float32),
         scratch_shapes=[pltpu.VMEM((lon_count * width, 4 * rows), jnp.bfloat16)],
-        compiler_params=pltpu.CompilerParams(vmem_limit_bytes=VMEM_LIMIT),
+        compiler_params=pltpu.CompilerParams(vmem_limit_bytes=16 * MIB),
         cost_estimate=pl.CostEstimate(
             flops=2 * NLON * lon_count * width * rows,
             bytes_accessed=trig.size * 2 + 2 * coeffs.size * 4,
@@ -393,7 +415,7 @@
             pl.BlockSpec((None, width, cols), lambda i: (i, 0, 0)),
             pl.BlockSpec((None, width, cols), lambda i: (i, 0, 0)),
         ),
-        compiler_params=pltpu.CompilerParams(vmem_limit_bytes=VMEM_LIMIT),
+        compiler_params=pltpu.CompilerParams(vmem_limit_bytes=32 * MIB),
         cost_estimate=pl.CostEstimate(
             flops=2 * cells * width * width,
             bytes_accessed=cells * width * 10,
@@ -498,7 +520,7 @@
             pltpu.VMEM((1, width), jnp.float32),
             pltpu.VMEM((sum_rows, LANES), jnp.float32),
         ],
-        compiler_params=pltpu.CompilerParams(vmem_limit_bytes=VMEM_LIMIT),
+        compiler_params=pltpu.CompilerParams(vmem_limit_bytes=32 * MIB),
         cost_estimate=pl.CostEstimate(
             flops=2 * cells * width * (width + 2 * LANES),
             bytes_accessed=cells * width * 10,
@@ -534,6 +556,7 @@
             bytes_accessed=4 * (len(pieces) + 1) * rows * LANES,
             transcendentals=0,
         ),
+        compiler_params=pltpu.CompilerParams(vmem_limit_bytes=6 * MIB),
         name="add_pieces",
     )(index, *pieces)
 
@@ -575,6 +598,7 @@
         + [pl.BlockSpec(memory_space=pltpu.VMEM)] * len(pieces),
         out_specs=(pl.BlockSpec(memory_space=pltpu.VMEM),) * 3,
         scratch_shapes=[pltpu.VMEM((len(pieces) * pieces[0].shape[0], LANES), jnp.float32)],
+        compiler_params=pltpu.CompilerParams(vmem_limit_bytes=8 * MIB),
         name="finish",
     )(place, *pieces)
 

time: 142 us -> 121 us (0.85)
  Pallas kernels: 65.2 us -> 44.4 us
  local copies, waits for them, and re-layouts: 5.5 us -> 13 us
  other arithmetic: 3.4 us -> 0.48 us
  blocking collectives: 15.3 us -> 13.5 us
  matrix products: 5.16 us -> 3.43 us
    unnamed x40 -> x28, local copies, waits for them, and re-layouts: 4.19 us -> 12.3 us
    pallas_call x3, Pallas kernels: 5.52 us -> 0.13 us  [add_pieces(): pl.pallas_call(functools.partial(add_kernel, inputs=len(pieces), outputs=...]
    pallas_call x1, Pallas kernels: 10.6 us -> 5.26 us  [backward(): pl.pallas_call(backward_kernel, grid=(parts,), out_shape=(jax.ShapeDtypeS...]
    pallas_call x1, Pallas kernels: 30.8 us -> 27.1 us  [coefficients(): pl.pallas_call(kernel, out_shape=jax.ShapeDtypeStruct((lat_count, slot_co...]
    pallas_call x1, Pallas kernels: 9.04 us -> 5.87 us  [forward(): pl.pallas_call(forward_kernel, grid=(parts,), out_shape=(jax.ShapeDtypeSt...]
    pallas_call x1, Pallas kernels: 3.67 us -> 1.3 us  [grid_field(): pl.pallas_call(functools.partial(grid_kernel, lon_count=lon_count, pair_c...]
    all_to_all x1, blocking collectives: 15.3 us -> 13.5 us  [local(): grid = lax.all_to_all(grid, 'lon', split_axis=0, concat_axis=0, tiled=True)]
    all_to_all x1, waiting for transfers between devices: 5.36 us -> 3.53 us  [local(): lax.all_to_all(coeffs, ('lat', 'lon'), split_axis=0, concat_axis=0, tiled...]
  transfers between devices with their start and end apart: 18 -> 18, of which waited for: 12 -> 12; matrix products, arithmetic and copies ran while one was open for 6% -> 4% of each run, Pallas kernels for 9% -> 7%
where the time goes in v4:
time: 121 us; the launch traced here: 120 us
  Pallas kernels  44.4 us (37%)
  starting transfers between devices  23.9 us (20%)
  waiting for transfers between devices  20.9 us (17%)
  blocking collectives  13.5 us (11%)
  local copies, waits for them, and re-layouts  13 us (11%)
  matrix products  3.43 us (3%)
    pallas_call x1, Pallas kernels, coefficients(): pl.pallas_call(kernel, out_shape=jax.ShapeDtypeStruct((lat_count, slot_co...  27.1 us
    ppermute x17, waiting for transfers between devices, swap(): return lax.ppermute(value, axis, [(i, i ^ bits) for i in range(count)])  17.4 us
    ppermute x17, starting transfers between devices, swap(): return lax.ppermute(value, axis, [(i, i ^ bits) for i in range(count)])  16.6 us
    all_to_all x1, blocking collectives, local(): grid = lax.all_to_all(grid, 'lon', split_axis=0, concat_axis=0, tiled=True)  13.5 us
    unnamed x28, local copies, waits for them, and re-layouts  12.3 us
    all_to_all x1, starting transfers between devices, local(): lax.all_to_all(coeffs, ('lat', 'lon'), split_axis=0, concat_axis=0, tiled...  7.3 us
    pallas_call x1, Pallas kernels, forward(): pl.pallas_call(forward_kernel, grid=(parts,), out_shape=(jax.ShapeDtypeSt...  5.87 us
    pallas_call x1, Pallas kernels, backward(): pl.pallas_call(backward_kernel, grid=(parts,), out_shape=(jax.ShapeDtypeS...  5.26 us
  transfers between devices with their start and end apart: 18, of which 12 were waited for; matrix products, arithmetic and copies ran while one was open for 4% of the time, Pallas kernels for 7%

profile of v4, /device:TPU:0, one launch (start us, length us, event | category | flops | bytes accessed | tf_op | source)
XLA Modules:
  0.0 120.3 jit_solution(16009088917653267308)
XLA Ops:
  0.7 27.1 %coefficients.1 = f32[8,64,384]{2,1,0:T(8,128)} custom-call(s32[1]{0:T(128)} %bitcast.2.first_ref, f32[8,90,2,721]{3,2,1,0:T(2,128)} %bitcast.18), custom_call_target="tpu_custom_call" | custom-call | tf_op jit(solution)/shard_map/coefficients/pallas_call | solution.py:248
  27.8 7.3 %all-to-all-start = ((f32[32,16,384]{2,1,0:T(8,128)}), f32[32,16,384]{2,1,0:T(8,128)S(1)}, u32[]{:S(2)}, u32[]{:S(2)}) async-start(f32[32,16,384]{2,1,0:T(8,128)} %bitcast.19), calls=%async_computation | async-start | bytes 1572864 | tf_op jit(solution)/shard_map/all_to_all | solution.py:626
  36.0 3.0 %trig_table.1.trig_ref = bf16[4,360,384]{2,1,0:T(8,128)(2,1)} custom-call(), custom_call_target="tpu_custom_call" | custom-call | flops 3317760 | bytes 1105920 | tf_op jit(solution)/shard_map/trig_table/pallas_call | solution.py:307
  39.1 1.8 %copy-done.7 = bf16[8,360,512]{2,1,0:T(8,128)(2,1)S(1)} copy-done((bf16[8,360,512]{2,1,0:T(8,128)(2,1)S(1)}, bf16[8,360,512]{2,1,0:T(8,128)(2,1)}, u32[]{:S(2)}) %copy-start.7) | copy-done | bytes 2949144
  40.9 5.9 %forward.1 = (f32[2880,512]{1,0:T(8,128)S(1)}, bf16[4,512,720]{2,1,0:T(8,128)(2,1)S(1)}, bf16[4,512,720]{2,1,0:T(8,128)(2,1)S(1)}) custom-call(bf16[2880,512]{1,0:T(8,128)(2,1)S(1)} %bitcast.16, bf16[512,512]{1,0:T(8,128)(2,1)S(1)} %copy-done.8, f32[1,512]{1,0:T(1,128)S(1)} %bitcast.17), custom_call_target="tpu_custom_call" | custom-call | flops 1509949440 | bytes 14745600 | tf_op jit(solution)/shard_map/forward/pallas_call | solution.py:400
  46.8 2.5 %copy-done = f32[2880,512]{1,0:T(8,128)} copy-done((f32[2880,512]{1,0:T(8,128)}, f32[2880,512]{1,0:T(8,128)S(1)}, u32[]{:S(2)}) %copy-start) | copy-done | bytes 5898264
  49.4 1.6 %copy-done.3 = bf16[4,512,720]{2,1,0:T(8,128)(2,1)} copy-done((bf16[4,512,720]{2,1,0:T(8,128)(2,1)}, bf16[4,512,720]{2,1,0:T(8,128)(2,1)S(1)}, u32[]{:S(2)}) %copy-start.3) | copy-done | bytes 2949144
  51.0 1.7 %copy-done.5 = bf16[4,512,720]{2,1,0:T(8,128)(2,1)} copy-done((bf16[4,512,720]{2,1,0:T(8,128)(2,1)}, bf16[4,512,720]{2,1,0:T(8,128)(2,1)S(1)}, u32[]{:S(2)}) %copy-start.5) | copy-done | bytes 2949144
  53.0 3.5 %all-to-all-done.coeff_ref = f32[32,16,384]{2,1,0:T(8,128)S(1)} async-done(((f32[32,16,384]{2,1,0:T(8,128)}), f32[32,16,384]{2,1,0:T(8,128)S(1)}, u32[]{:S(2)}, u32[]{:S(2)}) %all-to-all-start) | async-done | bytes 786464 | tf_op jit(solution)/shard_map/all_to_all | solution.py:626
  57.8 13.5 %all_to_all.10.grid_ref = f32[4,360,128]{2,1,0:T(8,128)S(1)} all-to-all(f32[4,360,128]{2,1,0:T(8,128)S(1)} %grid_field.1), channel_id=1, replica_groups=mesh['lat'=8,'lon'=4] {'lon'}, dimensions={0} | all-to-all | bytes 1474560 | tf_op jit(solution)/shard_map/all_to_all | solution.py:660
  71.3 2.7 %copy-done.1 = f32[2880,512]{1,0:T(8,128)S(1)} copy-done((f32[2880,512]{1,0:T(8,128)S(1)}, f32[2880,512]{1,0:T(8,128)}, u32[]{:S(2)}) %copy-start.1) | copy-done | bytes 5898264
  73.9 1.9 %copy-done.6 = bf16[4,512,720]{2,1,0:T(8,128)(2,1)S(1)} copy-done((bf16[4,512,720]{2,1,0:T(8,128)(2,1)S(1)}, bf16[4,512,720]{2,1,0:T(8,128)(2,1)}, u32[]{:S(2)}) %copy-start.6) | copy-done | bytes 2949144
  75.8 5.3 %backward.1 = (bf16[2880,512]{1,0:T(8,128)(2,1)S(1)}, f32[1280,128]{1,0:T(8,128)S(1)}, f32[1280,128]{1,0:T(8,128)S(1)}) custom-call(s32[1]{0:T(128)} %bitcast.1.core_ref, f32[4,360,128]{2,1,0:T(8,128)S(1)} %all_to_all.10.grid_ref, f32[4,1,128]{2,1,0:T(1,128)S(1)} %mul.38.scale_ref, bf16[4,128,1024]{2,1,0:T(8,128)(2,1)S(1)} %fusion.place_ref, ...), custom_call_target="tpu_custom_call" | custom-call | flops 2264924160 | bytes 14745600 | tf_op jit(solution)/shard_map/backward/pallas_call | solution.py:493
  81.2 2.1 %collective-permute-done.refs_1_ = f32[1280,128]{1,0:T(8,128)S(1)} collective-permute-done((f32[1280,128]{1,0:T(8,128)S(1)}, f32[1280,128]{1,0:T(8,128)S(1)}, u32[]{:S(2)}, u32[]{:S(2)}) %collective-permute-start) | collective-permute-done | bytes 655392 | tf_op jit(solution)/shard_map/ppermute | solution.py:608
  84.8 2.2 %collective-permute-start.3 = (f32[320,128]{1,0:T(8,128)S(1)}, f32[320,128]{1,0:T(8,128)S(1)}, u32[]{:S(2)}, u32[]{:S(2)}) collective-permute-start(f32[320,128]{1,0:T(8,128)S(1)} %get-tuple-element.49), channel_id=1, source_target_pairs={{0,3},{1,2},{2,1},{3,0},{4,7},{5,6},{6,5},{7,4},{8,11},{9,10},{10,... | collective-permute-start | bytes 491528 | tf_op jit(solution)/shard_map/ppermute | solution.py:608
  86.9 3.4 %convolution_convert_fusion = bf16[2880,512]{1,0:T(8,128)(2,1)} fusion(bf16[2880,512]{1,0:T(8,128)(2,1)S(1)} %get-tuple-element.50, bf16[512,512]{1,0:T(8,128)(2,1)S(1)} %copy-done.9), kind=kOutput, calls=%fused_computation | convolution fusion | flops 1511424000 | bytes 6422528 | tf_op jit(solution)/shard_map/dot_general | solution.py:670
  90.5 3.2 %collective-permute-done.2.refs_2_ = f32[320,128]{1,0:T(8,128)S(1)} collective-permute-done((f32[320,128]{1,0:T(8,128)S(1)}, f32[320,128]{1,0:T(8,128)S(1)}, u32[]{:S(2)}, u32[]{:S(2)}) %collective-permute-start.2) | collective-permute-done | bytes 163872 | tf_op jit(solution)/shard_map/ppermute | solution.py:608
  96.2 2.0 %collective-permute-start.6 = (f32[80,128]{1,0:T(8,128)S(1)}, f32[80,128]{1,0:T(8,128)S(1)}, u32[]{:S(2)}, u32[]{:S(2)}) collective-permute-start(f32[80,128]{1,0:T(8,128)S(1)} %get-tuple-element.60), channel_id=1, source_target_pairs={{0,24},{4,28},{8,16},{12,20},{16,8},{20,12},{24,0},{28,4},{1,25},{... | collective-permute-start | bytes 122888 | tf_op jit(solution)/shard_map/ppermute | solution.py:608
  98.2 2.2 %collective-permute-done.5.refs_2_ = f32[80,128]{1,0:T(8,128)S(1)} collective-permute-done((f32[80,128]{1,0:T(8,128)S(1)}, f32[80,128]{1,0:T(8,128)S(1)}, u32[]{:S(2)}, u32[]{:S(2)}) %collective-permute-start.5) | collective-permute-done | bytes 40992 | tf_op jit(solution)/shard_map/ppermute | solution.py:608
  102.0 2.1 %collective-permute-start.9 = (f32[80,128]{1,0:T(8,128)S(1)}, f32[80,128]{1,0:T(8,128)S(1)}, u32[]{:S(2)}, u32[]{:S(2)}) collective-permute-start(f32[80,128]{1,0:T(8,128)S(1)} %add_pieces.5), channel_id=1, source_target_pairs={{0,24},{4,28},{8,16},{12,20},{16,8},{20,12},{24,0},{28,4},{1,25},{... | collective-permute-start | bytes 122888 | tf_op jit(solution)/shard_map/ppermute | solution.py:608
  104.1 2.4 %collective-permute-start.7 = (f32[80,128]{1,0:T(8,128)S(1)}, f32[80,128]{1,0:T(8,128)S(1)}, u32[]{:S(2)}, u32[]{:S(2)}) collective-permute-start(f32[80,128]{1,0:T(8,128)S(1)} %add_pieces.5), channel_id=1, source_target_pairs={{0,8},{4,12},{8,0},{12,4},{16,24},{20,28},{24,16},{28,20},{1,9},{5... | collective-permute-start | bytes 122888 | tf_op jit(solution)/shard_map/ppermute | solution.py:608
  112.5 2.8 %collective-permute-done.12.refs_3_ = f32[320,128]{1,0:T(8,128)S(1)} collective-permute-done((f32[320,128]{1,0:T(8,128)S(1)}, f32[320,128]{1,0:T(8,128)S(1)}, u32[]{:S(2)}, u32[]{:S(2)}) %collective-permute-start.12) | collective-permute-done | bytes 163872 | tf_op jit(solution)/shard_map/ppermute | solution.py:608
  115.4 1.6 %collective-permute-done.11.refs_2_ = f32[320,128]{1,0:T(8,128)S(1)} collective-permute-done((f32[320,128]{1,0:T(8,128)S(1)}, f32[320,128]{1,0:T(8,128)S(1)}, u32[]{:S(2)}, u32[]{:S(2)}) %collective-permute-start.11) | collective-permute-done | bytes 163872 | tf_op jit(solution)/shard_map/ppermute | solution.py:608
  118.6 1.7 %finish.1 = (f32[512,512]{1,0:T(8,128)}, f32[1,512]{1,0:T(1,128)}, f32[64,512]{1,0:T(8,128)}) custom-call(s32[3]{0:T(128)S(1)} %pad_add_fusion.place_ref, f32[320,128]{1,0:T(8,128)S(1)} %pad_maximum_fusion.refs_0_, f32[320,128]{1,0:T(8,128)S(1)} %collective-permute-done.10.refs_1_, f32[320,128]{1,0:T(8,128)S(1)} %collective-permute-done.11.refs_2_, ...), custom_call_target="tpu_custom_call" | custom-call | tf_op jit(solution)/shard_map/finish/pallas_call | solution.py:590
  (71 shorter events, 16.0 us)
Async XLA Ops:
  0.6 34.6 %copy-start.12 = (s32[64]{0:T(128)S(1)}, s32[64]{0:T(128)}, u32[]{:S(2)}) copy-start(s32[64]{0:T(128)} %param.8) | copy-start | bytes 772
  0.6 35.2 %copy-start.13 = (f32[64]{0:T(128)S(1)}, f32[64]{0:T(128)}, u32[]{:S(2)}) copy-start(f32[64]{0:T(128)} %param.9) | copy-start | bytes 772
  0.7 35.3 %copy-start.11 = (bf16[512,64]{0,1:T(8,128)(2,1)S(1)}, bf16[512,64]{0,1:T(8,128)(2,1)}, u32[]{:S(2)}) copy-start(bf16[512,64]{0,1:T(8,128)(2,1)} %param.13) | copy-start | bytes 196612
  0.7 38.4 %copy-start.8 = (bf16[512,512]{1,0:T(8,128)(2,1)S(1)}, bf16[512,512]{1,0:T(8,128)(2,1)}, u32[]{:S(2)}) copy-start(bf16[512,512]{1,0:T(8,128)(2,1)} %w_ref.1) | copy-start | bytes 1572868
  0.7 38.4 %copy-start.10 = (f32[512]{0:T(512)S(1)}, f32[512]{0:T(512)}, u32[]{:S(2)}) copy-start(f32[512]{0:T(512)} %param.12) | copy-start | bytes 6148
  27.8 28.7 %all-to-all-start = ((f32[32,16,384]{2,1,0:T(8,128)}), f32[32,16,384]{2,1,0:T(8,128)S(1)}, u32[]{:S(2)}, u32[]{:S(2)}) async-start(f32[32,16,384]{2,1,0:T(8,128)} %bitcast.19), calls=%async_computation | async-start | bytes 1572864 | tf_op jit(solution)/shard_map/all_to_all | solution.py:626
  40.9 15.6 %copy-start.2 = (bf16[4,360,384]{2,1,0:T(8,128)(2,1)S(1)}, bf16[4,360,384]{2,1,0:T(8,128)(2,1)}, u32[]{:S(2)}) copy-start(bf16[4,360,384]{2,1,0:T(8,128)(2,1)} %trig_table.1.trig_ref) | copy-start | bytes 3317764
  81.1 2.2 %collective-permute-start = (f32[1280,128]{1,0:T(8,128)S(1)}, f32[1280,128]{1,0:T(8,128)S(1)}, u32[]{:S(2)}, u32[]{:S(2)}) collective-permute-start(f32[1280,128]{1,0:T(8,128)S(1)} %get-tuple-element.46), channel_id=1, source_target_pairs={{0,4},{4,0},{8,12},{12,8},{16,20},{20,16},{24,28},{28,24},{1,5},{5... | collective-permute-start | bytes 1966088 | tf_op jit(solution)/shard_map/ppermute | solution.py:608
  83.4 7.1 %collective-permute-start.1 = (f32[320,128]{1,0:T(8,128)S(1)}, f32[320,128]{1,0:T(8,128)S(1)}, u32[]{:S(2)}, u32[]{:S(2)}) collective-permute-start(f32[320,128]{1,0:T(8,128)S(1)} %get-tuple-element.47), channel_id=1, source_target_pairs={{0,1},{1,0},{2,3},{3,2},{4,5},{5,4},{6,7},{7,6},{8,9},{9,8},{10,11... | collective-permute-start | bytes 491528 | tf_op jit(solution)/shard_map/ppermute | solution.py:608
  84.2 9.5 %collective-permute-start.2 = (f32[320,128]{1,0:T(8,128)S(1)}, f32[320,128]{1,0:T(8,128)S(1)}, u32[]{:S(2)}, u32[]{:S(2)}) collective-permute-start(f32[320,128]{1,0:T(8,128)S(1)} %get-tuple-element.48), channel_id=1, source_target_pairs={{0,2},{1,3},{2,0},{3,1},{4,6},{5,7},{6,4},{7,5},{8,10},{9,11},{10,... | collective-permute-start | bytes 491528 | tf_op jit(solution)/shard_map/ppermute | solution.py:608
  84.8 8.9 %collective-permute-start.3 = (f32[320,128]{1,0:T(8,128)S(1)}, f32[320,128]{1,0:T(8,128)S(1)}, u32[]{:S(2)}, u32[]{:S(2)}) collective-permute-start(f32[320,128]{1,0:T(8,128)S(1)} %get-tuple-element.49), channel_id=1, source_target_pairs={{0,3},{1,2},{2,1},{3,0},{4,7},{5,6},{6,5},{7,4},{8,11},{9,10},{10,... | collective-permute-start | bytes 491528 | tf_op jit(solution)/shard_map/ppermute | solution.py:608
  93.7 4.5 %collective-permute-start.4 = (f32[80,128]{1,0:T(8,128)S(1)}, f32[80,128]{1,0:T(8,128)S(1)}, u32[]{:S(2)}, u32[]{:S(2)}) collective-permute-start(f32[80,128]{1,0:T(8,128)S(1)} %get-tuple-element.58), channel_id=1, source_target_pairs={{0,8},{4,12},{8,0},{12,4},{16,24},{20,28},{24,16},{28,20},{1,9},{5... | collective-permute-start | bytes 122888 | tf_op jit(solution)/shard_map/ppermute | solution.py:608
  94.6 5.8 %collective-permute-start.5 = (f32[80,128]{1,0:T(8,128)S(1)}, f32[80,128]{1,0:T(8,128)S(1)}, u32[]{:S(2)}, u32[]{:S(2)}) collective-permute-start(f32[80,128]{1,0:T(8,128)S(1)} %get-tuple-element.59), channel_id=1, source_target_pairs={{0,16},{4,20},{8,24},{12,28},{16,0},{20,4},{24,8},{28,12},{1,17},{... | collective-permute-start | bytes 122888 | tf_op jit(solution)/shard_map/ppermute | solution.py:608
  96.2 5.8 %collective-permute-start.6 = (f32[80,128]{1,0:T(8,128)S(1)}, f32[80,128]{1,0:T(8,128)S(1)}, u32[]{:S(2)}, u32[]{:S(2)}) collective-permute-start(f32[80,128]{1,0:T(8,128)S(1)} %get-tuple-element.60), channel_id=1, source_target_pairs={{0,24},{4,28},{8,16},{12,20},{16,8},{20,12},{24,0},{28,4},{1,25},{... | collective-permute-start | bytes 122888 | tf_op jit(solution)/shard_map/ppermute | solution.py:608
  102.0 5.9 %collective-permute-start.9 = (f32[80,128]{1,0:T(8,128)S(1)}, f32[80,128]{1,0:T(8,128)S(1)}, u32[]{:S(2)}, u32[]{:S(2)}) collective-permute-start(f32[80,128]{1,0:T(8,128)S(1)} %add_pieces.5), channel_id=1, source_target_pairs={{0,24},{4,28},{8,16},{12,20},{16,8},{20,12},{24,0},{28,4},{1,25},{... | collective-permute-start | bytes 122888 | tf_op jit(solution)/shard_map/ppermute | solution.py:608
  104.1 4.9 %collective-permute-start.8 = (f32[80,128]{1,0:T(8,128)S(1)}, f32[80,128]{1,0:T(8,128)S(1)}, u32[]{:S(2)}, u32[]{:S(2)}) collective-permute-start(f32[80,128]{1,0:T(8,128)S(1)} %add_pieces.5), channel_id=1, source_target_pairs={{0,16},{4,20},{8,24},{12,28},{16,0},{20,4},{24,8},{28,12},{1,17},{... | collective-permute-start | bytes 122888 | tf_op jit(solution)/shard_map/ppermute | solution.py:608
  104.1 4.9 %collective-permute-start.7 = (f32[80,128]{1,0:T(8,128)S(1)}, f32[80,128]{1,0:T(8,128)S(1)}, u32[]{:S(2)}, u32[]{:S(2)}) collective-permute-start(f32[80,128]{1,0:T(8,128)S(1)} %add_pieces.5), channel_id=1, source_target_pairs={{0,8},{4,12},{8,0},{12,4},{16,24},{20,28},{24,16},{28,20},{1,9},{5... | collective-permute-start | bytes 122888 | tf_op jit(solution)/shard_map/ppermute | solution.py:608
  109.0 6.4 %collective-permute-start.12 = (f32[320,128]{1,0:T(8,128)S(1)}, f32[320,128]{1,0:T(8,128)S(1)}, u32[]{:S(2)}, u32[]{:S(2)}) collective-permute-start(f32[320,128]{1,0:T(8,128)S(1)} %pad_maximum_fusion.refs_0_), channel_id=1, source_target_pairs={{0,3},{1,2},{2,1},{3,0},{4,7},{5,6},{6,5},{7,4},{8,11},{9,10},{10,... | collective-permute-start | bytes 491528 | tf_op jit(solution)/shard_map/ppermute | solution.py:608
  110.5 6.5 %collective-permute-start.11 = (f32[320,128]{1,0:T(8,128)S(1)}, f32[320,128]{1,0:T(8,128)S(1)}, u32[]{:S(2)}, u32[]{:S(2)}) collective-permute-start(f32[320,128]{1,0:T(8,128)S(1)} %pad_maximum_fusion.refs_0_), channel_id=1, source_target_pairs={{0,2},{1,3},{2,0},{3,1},{4,6},{5,7},{6,4},{7,5},{8,10},{9,11},{10,... | collective-permute-start | bytes 491528 | tf_op jit(solution)/shard_map/ppermute | solution.py:608
  111.7 5.3 %collective-permute-start.10 = (f32[320,128]{1,0:T(8,128)S(1)}, f32[320,128]{1,0:T(8,128)S(1)}, u32[]{:S(2)}, u32[]{:S(2)}) collective-permute-start(f32[320,128]{1,0:T(8,128)S(1)} %pad_maximum_fusion.refs_0_), channel_id=1, source_target_pairs={{0,1},{1,0},{2,3},{3,2},{4,5},{5,4},{6,7},{7,6},{8,9},{9,8},{10,11... | collective-permute-start | bytes 491528 | tf_op jit(solution)/shard_map/ppermute | solution.py:608
  112.5 5.0 %collective-permute-start.13 = (f32[320,128]{1,0:T(8,128)S(1)}, f32[320,128]{1,0:T(8,128)S(1)}, u32[]{:S(2)}, u32[]{:S(2)}) collective-permute-start(f32[320,128]{1,0:T(8,128)S(1)} %pad_maximum_fusion.refs_0_), channel_id=1, source_target_pairs={{0,4},{4,0},{8,12},{12,8},{16,20},{20,16},{24,28},{28,24},{1,5},{5... | collective-permute-start | bytes 491528 | tf_op jit(solution)/shard_map/ppermute | solution.py:608
  115.4 2.2 %collective-permute-start.16 = (f32[320,128]{1,0:T(8,128)S(1)}, f32[320,128]{1,0:T(8,128)S(1)}, u32[]{:S(2)}, u32[]{:S(2)}) collective-permute-start(f32[320,128]{1,0:T(8,128)S(1)} %collective-permute-done.12.refs_3_), channel_id=1, source_target_pairs={{0,4},{4,0},{8,12},{12,8},{16,20},{20,16},{24,28},{28,24},{1,5},{5... | collective-permute-start | bytes 491528 | tf_op jit(solution)/shard_map/ppermute | solution.py:608
  117.0 1.4 %collective-permute-start.15 = (f32[320,128]{1,0:T(8,128)S(1)}, f32[320,128]{1,0:T(8,128)S(1)}, u32[]{:S(2)}, u32[]{:S(2)}) collective-permute-start(f32[320,128]{1,0:T(8,128)S(1)} %collective-permute-done.11.refs_2_), channel_id=1, source_target_pairs={{0,4},{4,0},{8,12},{12,8},{16,20},{20,16},{24,28},{28,24},{1,5},{5... | collective-permute-start | bytes 491528 | tf_op jit(solution)/shard_map/ppermute | solution.py:608
  117.1 1.6 %collective-permute-start.14 = (f32[320,128]{1,0:T(8,128)S(1)}, f32[320,128]{1,0:T(8,128)S(1)}, u32[]{:S(2)}, u32[]{:S(2)}) collective-permute-start(f32[320,128]{1,0:T(8,128)S(1)} %collective-permute-done.10.refs_1_), channel_id=1, source_target_pairs={{0,4},{4,0},{8,12},{12,8},{16,20},{20,16},{24,28},{28,24},{1,5},{5... | collective-permute-start | bytes 491528 | tf_op jit(solution)/shard_map/ppermute | solution.py:608
  (8 other events, 38.2 us)

commit v5 on v4

--- a/solution.py
+++ b/solution.py
@@ -15,7 +15,6 @@
 SUBS = 8
 STEPS = NM + 1
 PAIRS = 4
-TABLE_ROWS = 728
 MIB = 1024 * 1024
 VMEM_LIMIT = 56 * MIB
 
@@ -35,6 +34,7 @@
     per_block = LANES // rows_all
     vregs = pad_to(pair_count, SUBS * per_block) // (SUBS * per_block)
     step_tile = rows_all
+    stride = vregs * SUBS + 1
     pair_pad = pad_to(pair_count, SUBS)
     lat_count = rows_all // lat_rows
     first_pair = first_ref[0]
@@ -129,7 +129,7 @@
             value = (grow * cosine) * previous[v] - before[v]
             restart = switches[v] == step
             value = jnp.where(restart, seconds[v], value)
-            table_ref[pl.ds(v * SUBS * TABLE_ROWS + step, SUBS, stride=TABLE_ROWS), :] = value
+            table_ref[pl.ds(step * stride + v * SUBS, SUBS), :] = value
             produced.append(value)
             kept.append(jnp.where(restart, 0.0, previous[v]))
         return (tuple(produced), tuple(kept))
@@ -189,7 +189,7 @@
         first_block = start // per_block
         blocks = PAIRS // per_block
         table = jnp.concatenate(
-            [table_ref[pl.ds((first_block + n) * TABLE_ROWS, STEPS), :] for n in range(blocks)],
+            [table_ref[pl.ds(first_block + n, STEPS, stride=stride), :] for n in range(blocks)],
             axis=1,
         )
         begin, end = edges[0], edges[1]
@@ -260,11 +260,11 @@
             pltpu.VMEM((tile_total, vregs * SUBS, LANES), jnp.float32),
             pltpu.VMEM((pad_to(STEPS, LANES) // LANES, pairs, LANES), jnp.float32),
             pltpu.VMEM((pad_to(STEPS, LANES) // LANES, 2 * pairs, LANES), jnp.float32),
-            pltpu.VMEM((vregs * SUBS * TABLE_ROWS, LANES), jnp.float32),
+            pltpu.VMEM((pad_to(STEPS, SUBS) * (vregs * SUBS + 1), LANES), jnp.float32),
             pltpu.VMEM((slot_count, 4 * pair_pad, LANES), jnp.float32),
             pltpu.SemaphoreType.DMA,
         ],
-        compiler_params=pltpu.CompilerParams(vmem_limit_bytes=VMEM_LIMIT),
+        compiler_params=pltpu.CompilerParams(vmem_limit_bytes=40 * MIB),
         name="coefficients",
     )(first_pair, jnp.transpose(spectra, (0, 2, 1, 3)))
 
@@ -322,7 +322,8 @@
     )()
 
 
-def grid_kernel(trig_ref, coeff_ref, out_ref, right_ref, *, lon_count, pair_count):
+def grid_kernel(lon_ref, trig_ref, coeff_ref, *refs, lon_count, pair_count):
+    flat_ref, right_ref = refs[lon_count:]
     share = coeff_ref.shape[1]
     width = coeff_ref.shape[2]
     rows = coeff_ref.shape[0] // lon_count * share
@@ -353,17 +354,27 @@
             preferred_element_type=jnp.float32,
         )
         total = part if total is None else total + part
+    quarter = total.shape[0]
     for turn in range(4):
-        out_ref[turn] = total[:, turn * rows : (turn + 1) * rows]
-
-
-def grid_field(trig, coeffs, pair_count):
+        flat_ref[pl.ds(turn * quarter, quarter), :] = total[:, turn * rows : (turn + 1) * rows]
+    cols = NLON // lon_count
+    for part in range(lon_count):
+        refs[part][...] = flat_ref[pl.ds((lon_ref[0] ^ part) * cols, cols), :]
+
+
+def grid_field(lon, trig, coeffs, pair_count):
     lon_count, quarter, width = trig.shape
     rows = coeffs.shape[0] // lon_count * coeffs.shape[1]
     return pl.pallas_call(
         functools.partial(grid_kernel, lon_count=lon_count, pair_count=pair_count),
-        out_shape=jax.ShapeDtypeStruct((4, quarter, rows), jnp.float32),
-        scratch_shapes=[pltpu.VMEM((lon_count * width, 4 * rows), jnp.bfloat16)],
+        out_shape=[jax.ShapeDtypeStruct((NLON // lon_count, rows), jnp.float32)] * lon_count,
+        in_specs=[pl.BlockSpec(memory_space=pltpu.SMEM)]
+        + [pl.BlockSpec(memory_space=pltpu.VMEM)] * 2,
+        out_specs=[pl.BlockSpec(memory_space=pltpu.VMEM)] * lon_count,
+        scratch_shapes=[
+            pltpu.VMEM((4 * quarter, rows), jnp.float32),
+            pltpu.VMEM((lon_count * width, 4 * rows), jnp.bfloat16),
+        ],
         compiler_params=pltpu.CompilerParams(vmem_limit_bytes=16 * MIB),
         cost_estimate=pl.CostEstimate(
             flops=2 * NLON * lon_count * width * rows,
@@ -371,7 +382,7 @@
             transcendentals=0,
         ),
         name="grid_field",
-    )(trig, coeffs)
+    )(lon, trig, coeffs)
 
 
 def gelu_parts(preact):
@@ -426,13 +437,15 @@
 
 
 def backward_kernel(
-    core_ref, grid_ref, scale_ref, place_ref, w_out_ref, slope_ref, hidden_t_ref, latents_t_ref,
-    preact_ref, keep_ref, send_ref, field_ref, hidden_acc, out_acc, bias_acc, sums_ref,
+    core_ref, scale_ref, place_ref, w_out_ref, slope_ref, hidden_t_ref, latents_t_ref, *refs,
+    blocks,
 ):
+    grid_refs = refs[:blocks]
+    preact_ref, keep_ref, send_ref = refs[blocks : blocks + 3]
+    field_ref, hidden_acc, out_acc, bias_acc, sums_ref = refs[blocks + 3 :]
     index = pl.program_id(0)
     total = pl.num_programs(0)
-    blocks = grid_ref.shape[0]
-    lon_cols = grid_ref.shape[1]
+    lon_cols = grid_refs[0].shape[0]
     width = hidden_acc.shape[0]
     cols = slope_ref.shape[0]
     sum_rows = sums_ref.shape[0]
@@ -441,7 +454,7 @@
     def _():
         field = None
         for block in range(blocks):
-            scaled = (grid_ref[block] * scale_ref[block]).astype(jnp.bfloat16)
+            scaled = (grid_refs[block][...] * scale_ref[block]).astype(jnp.bfloat16)
             part = jnp.dot(scaled, place_ref[block], preferred_element_type=jnp.float32)
             field = part if field is None else field + part
         for row in range(field.shape[1] // LANES):
@@ -484,14 +497,15 @@
         send_ref[...] = sums_ref[pl.ds(pl.multiple_of((1 - mine) * half, SUBS), half), :]
 
 
-def backward(core, grid, scale, place, w_out_t, slope, hidden_t, latents_t, sum_rows):
+def backward(core, grids, scale, place, w_out_t, slope, hidden_t, latents_t, sum_rows):
     cells, width = slope.shape
+    blocks = len(grids)
     parts, _, cols = hidden_t.shape
     half = (sum_rows // 2, LANES)
     whole3 = lambda i: (0, 0, 0)
     whole2 = lambda i: (0, 0)
     return pl.pallas_call(
-        backward_kernel,
+        functools.partial(backward_kernel, blocks=blocks),
         grid=(parts,),
         out_shape=(
             jax.ShapeDtypeStruct((cells, width), jnp.bfloat16),
@@ -500,14 +514,14 @@
         ),
         in_specs=[
             pl.BlockSpec(memory_space=pltpu.SMEM),
-            pl.BlockSpec(grid.shape, whole3),
             pl.BlockSpec(scale.shape, whole3),
             pl.BlockSpec(place.shape, whole3),
             pl.BlockSpec(w_out_t.shape, whole2),
             pl.BlockSpec((cols, width), lambda i: (i, 0)),
             pl.BlockSpec((None, width, cols), lambda i: (i, 0, 0)),
             pl.BlockSpec((None, width, cols), lambda i: (i, 0, 0)),
-        ],
+        ]
+        + [pl.BlockSpec(grids[0].shape, whole2)] * blocks,
         out_specs=(
             pl.BlockSpec((cols, width), lambda i: (i, 0)),
             pl.BlockSpec(half, whole2),
@@ -527,7 +541,7 @@
             transcendentals=0,
         ),
         name="backward",
-    )(core, grid, scale, place, w_out_t, slope, hidden_t, latents_t)
+    )(core, scale, place, w_out_t, slope, hidden_t, latents_t, *grids)
 
 
 def add_kernel(index_ref, *refs, inputs, outputs, factor):
@@ -635,7 +649,10 @@
     def spread(values):
         values = jnp.broadcast_to(values, (lat_count, slot_count, lat_rows))
         values = values.reshape(lat_count, lon_count, share)
-        return jnp.transpose(values, (1, 0, 2)).reshape(lon_count, lanes)
+        values = jnp.transpose(values, (1, 0, 2)).reshape(lon_count, lanes)
+        arrival = lon_index ^ jnp.arange(lon_count, dtype=jnp.int32)
+        chosen = arrival[:, None] == jnp.arange(lon_count, dtype=jnp.int32)
+        return jnp.sum(jnp.where(chosen[:, :, None], values[None], 0), axis=1)
 
     field_ids = spread(field_slot.reshape(lat_count, slot_count, 1))
     row_ids = spread(jnp.arange(lat_rows, dtype=jnp.int32).reshape(1, 1, lat_rows))
@@ -651,20 +668,15 @@
 
     core_index, deep_index = lat_index & 1, lat_index >> 1
     spots = jnp.stack([core_index, lon_index, deep_index])
-    coeffs, slope, hidden_t, latents_t, trig, scale, place, w_out_t, spots = (
-        lax.optimization_barrier(
-            (coeffs, slope, hidden_t, latents_t, trig, scale, place, w_out_t, spots)
-        )
-    )
-    grid = grid_field(trig, coeffs, pair_count).reshape(lon_count, lon_cols, lanes)
-    grid = lax.all_to_all(grid, "lon", split_axis=0, concat_axis=0, tiled=True)
+    grids = grid_field(lon_index.reshape(1), trig, coeffs, pair_count)
+    grids = [grids[0]] + [swap(grids[part], "lon", part) for part in range(1, lon_count)]
 
     device_count = lat_count * lon_count
     used_rows = (width + F + 1) * width // LANES
     chunk = pad_to(pad_to(used_rows, device_count) // device_count, SUBS)
     depth = lat_count // 2
     preact_back, keep, send = backward(
-        core_index.reshape(1), grid, scale, place, w_out_t, slope, hidden_t, latents_t,
+        core_index.reshape(1), grids, scale, place, w_out_t, slope, hidden_t, latents_t,
         chunk * device_count,
     )
     latent_grad = lax.dot_general(

time: 121 us -> 126 us (1.041)
  blocking collectives: 13.5 us -> 0 us
  waiting for transfers between devices: 20.9 us -> 29 us
  local copies, waits for them, and re-layouts: 13 us -> 18.5 us
  starting transfers between devices: 23.9 us -> 26.9 us
  matrix products: 3.43 us -> 5.16 us
    all_to_all x1 -> x0, blocking collectives: 13.5 us -> none  [local(): grid = lax.all_to_all(grid, 'lon', split_axis=0, concat_axis=0, tiled=True)]
    ppermute x17 -> x20, waiting for transfers between devices: 17.4 us -> 25.3 us  [swap(): return lax.ppermute(value, axis, [(i, i ^ bits) for i in range(count)])]
    unnamed x28 -> x32, local copies, waits for them, and re-layouts: 12.3 us -> 18 us
    ppermute x17 -> x20, starting transfers between devices: 16.6 us -> 19.6 us  [swap(): return lax.ppermute(value, axis, [(i, i ^ bits) for i in range(count)])]
    dot_general x1, matrix products: 3.43 us -> 5.16 us  [local(): lax.dot_general(preact_back, w_hidden, (((1,), (1,)), ((), ())), preferre...]
  transfers between devices with their start and end apart: 18 -> 21, of which waited for: 12 -> 14; matrix products, arithmetic and copies ran while one was open for 4% -> 5% of each run, Pallas kernels for 7% -> 7%
where the time goes in v5:
time: 126 us
  Pallas kernels  44.9 us (36%)
  waiting for transfers between devices  29 us (23%)
  starting transfers between devices  26.9 us (21%)
  local copies, waits for them, and re-layouts  18.5 us (15%)
  matrix products  5.16 us (4%)
    pallas_call x1, Pallas kernels, coefficients(): pl.pallas_call(kernel, out_shape=jax.ShapeDtypeStruct((lat_count, slot_co...  27.5 us
    ppermute x20, waiting for transfers between devices, swap(): return lax.ppermute(value, axis, [(i, i ^ bits) for i in range(count)])  25.3 us
    ppermute x20, starting transfers between devices, swap(): return lax.ppermute(value, axis, [(i, i ^ bits) for i in range(count)])  19.6 us
    unnamed x32, local copies, waits for them, and re-layouts  18 us
    all_to_all x1, starting transfers between devices, local(): lax.all_to_all(coeffs, ('lat', 'lon'), split_axis=0, concat_axis=0, tiled...  7.3 us
    pallas_call x1, Pallas kernels, forward(): pl.pallas_call(forward_kernel, grid=(parts,), out_shape=(jax.ShapeDtypeSt...  5.87 us
    pallas_call x1, Pallas kernels, backward(): pl.pallas_call(functools.partial(backward_kernel, blocks=blocks), grid=(p...  5.3 us
    dot_general x1, matrix products, local(): lax.dot_general(preact_back, w_hidden, (((1,), (1,)), ((), ())), preferre...  5.16 us
  transfers between devices with their start and end apart: 21, of which 14 were waited for; matrix products, arithmetic and copies ran while one was open for 5% of the time, Pallas kernels for 7%

profile of v5, /device:TPU:0, one launch (start us, length us, event | category | flops | bytes accessed | tf_op | source)
XLA Modules:
  0.0 125.9 jit_solution(2702120842620352016)
XLA Ops:
  0.6 2.2 %copy-done.2 = f32[8,2,90,721]{3,1,2,0:T(2,128)S(1)} copy-done((f32[8,2,90,721]{3,1,2,0:T(2,128)S(1)}, f32[8,2,90,721]{3,1,2,0:T(2,128)}, u32[]{:S(2)}) %copy-start.2) | copy-done | bytes 4152984
  2.9 27.5 %coefficients.1 = f32[8,64,384]{2,1,0:T(8,128)} custom-call(s32[1]{0:T(128)} %bitcast.7.first_ref, f32[8,90,2,721]{3,2,1,0:T(2,128)S(1)} %bitcast.16), custom_call_target="tpu_custom_call" | custom-call | tf_op jit(solution)/shard_map/coefficients/pallas_call | solution.py:248
  30.4 7.3 %all-to-all-start = ((f32[32,16,384]{2,1,0:T(8,128)}), f32[32,16,384]{2,1,0:T(8,128)S(1)}, u32[]{:S(2)}, u32[]{:S(2)}) async-start(f32[32,16,384]{2,1,0:T(8,128)} %bitcast.9), calls=%async_computation | async-start | bytes 1572864 | tf_op jit(solution)/shard_map/all_to_all | solution.py:640
  38.3 3.0 %trig_table.1.trig_ref = bf16[4,360,384]{2,1,0:T(8,128)(2,1)} custom-call(), custom_call_target="tpu_custom_call" | custom-call | flops 3317760 | bytes 1105920 | tf_op jit(solution)/shard_map/trig_table/pallas_call | solution.py:307
  41.6 1.8 %copy-done.8 = bf16[8,360,512]{2,1,0:T(8,128)(2,1)S(1)} copy-done((bf16[8,360,512]{2,1,0:T(8,128)(2,1)S(1)}, bf16[8,360,512]{2,1,0:T(8,128)(2,1)}, u32[]{:S(2)}) %copy-start.8) | copy-done | bytes 2949144
  43.5 5.9 %forward.1 = (f32[2880,512]{1,0:T(8,128)S(1)}, bf16[4,512,720]{2,1,0:T(8,128)(2,1)S(1)}, bf16[4,512,720]{2,1,0:T(8,128)(2,1)S(1)}) custom-call(bf16[2880,512]{1,0:T(8,128)(2,1)S(1)} %bitcast.18, bf16[512,512]{1,0:T(8,128)(2,1)S(1)} %copy-done.10, f32[1,512]{1,0:T(1,128)S(1)} %bitcast.19), custom_call_target="tpu_custom_call" | custom-call | flops 1509949440 | bytes 14745600 | tf_op jit(solution)/shard_map/forward/pallas_call | solution.py:411
  49.3 2.5 %copy-done = f32[2880,512]{1,0:T(8,128)} copy-done((f32[2880,512]{1,0:T(8,128)}, f32[2880,512]{1,0:T(8,128)S(1)}, u32[]{:S(2)}) %copy-start) | copy-done | bytes 5898264
  51.9 1.7 %copy-done.3 = bf16[4,512,720]{2,1,0:T(8,128)(2,1)} copy-done((bf16[4,512,720]{2,1,0:T(8,128)(2,1)}, bf16[4,512,720]{2,1,0:T(8,128)(2,1)S(1)}, u32[]{:S(2)}) %copy-start.3) | copy-done | bytes 2949144
  55.5 3.7 %all-to-all-done.coeff_ref = f32[32,16,384]{2,1,0:T(8,128)S(1)} async-done(((f32[32,16,384]{2,1,0:T(8,128)}), f32[32,16,384]{2,1,0:T(8,128)S(1)}, u32[]{:S(2)}, u32[]{:S(2)}) %all-to-all-start) | async-done | bytes 786464 | tf_op jit(solution)/shard_map/all_to_all | solution.py:640
  64.1 4.0 %collective-permute-done.refs_1_ = f32[360,128]{1,0:T(8,128)S(1)} collective-permute-done((f32[360,128]{1,0:T(8,128)S(1)}, f32[360,128]{1,0:T(8,128)S(1)}, u32[]{:S(2)}, u32[]{:S(2)}) %collective-permute-start) | collective-permute-done | bytes 184352 | tf_op jit(solution)/shard_map/ppermute | solution.py:622
  68.1 1.9 %collective-permute-done.1.refs_2_ = f32[360,128]{1,0:T(8,128)S(1)} collective-permute-done((f32[360,128]{1,0:T(8,128)S(1)}, f32[360,128]{1,0:T(8,128)S(1)}, u32[]{:S(2)}, u32[]{:S(2)}) %collective-permute-start.1) | collective-permute-done | bytes 184352 | tf_op jit(solution)/shard_map/ppermute | solution.py:622
  71.6 2.7 %copy-done.1 = f32[2880,512]{1,0:T(8,128)S(1)} copy-done((f32[2880,512]{1,0:T(8,128)S(1)}, f32[2880,512]{1,0:T(8,128)}, u32[]{:S(2)}) %copy-start.1) | copy-done | bytes 5898264
  74.3 1.9 %copy-done.4 = bf16[4,512,720]{2,1,0:T(8,128)(2,1)S(1)} copy-done((bf16[4,512,720]{2,1,0:T(8,128)(2,1)S(1)}, bf16[4,512,720]{2,1,0:T(8,128)(2,1)}, u32[]{:S(2)}) %copy-start.4) | copy-done | bytes 2949144
  76.2 1.9 %copy-done.6 = bf16[4,512,720]{2,1,0:T(8,128)(2,1)S(1)} copy-done((bf16[4,512,720]{2,1,0:T(8,128)(2,1)S(1)}, bf16[4,512,720]{2,1,0:T(8,128)(2,1)}, u32[]{:S(2)}) %copy-start.6) | copy-done | bytes 2949144
  78.1 5.3 %backward.1 = (bf16[2880,512]{1,0:T(8,128)(2,1)S(1)}, f32[1280,128]{1,0:T(8,128)S(1)}, f32[1280,128]{1,0:T(8,128)S(1)}) custom-call(s32[1]{0:T(128)} %bitcast.1.core_ref, f32[4,1,128]{2,1,0:T(1,128)S(1)} %bitcast.17, bf16[4,128,1024]{2,1,0:T(8,128)(2,1)S(1)} %fusion.place_ref, bf16[128,512]{1,0:T(8,128)(2,1)S(1)} %concatenate.6.w_out_ref, ...), custom_call_target="tpu_custom_call" | custom-call | flops 2264924160 | bytes 14745600 | tf_op jit(solution)/shard_map/backward/pallas_call | solution.py:507
  85.0 2.1 %collective-permute-done.3.refs_1_ = f32[1280,128]{1,0:T(8,128)S(1)} collective-permute-done((f32[1280,128]{1,0:T(8,128)S(1)}, f32[1280,128]{1,0:T(8,128)S(1)}, u32[]{:S(2)}, u32[]{:S(2)}) %collective-permute-start.3) | collective-permute-done | bytes 655392 | tf_op jit(solution)/shard_map/ppermute | solution.py:622
  90.7 5.2 %convolution_convert_fusion = bf16[2880,512]{1,0:T(8,128)(2,1)} fusion(bf16[2880,512]{1,0:T(8,128)(2,1)} %copy-done.9, bf16[512,512]{1,0:T(8,128)(2,1)S(1)} %copy-done.11), kind=kOutput, calls=%fused_computation | convolution fusion | flops 1511424000 | bytes 6422528 | tf_op jit(solution)/shard_map/dot_general | solution.py:682
  99.9 2.2 %collective-permute-start.9 = (f32[80,128]{1,0:T(8,128)S(1)}, f32[80,128]{1,0:T(8,128)S(1)}, u32[]{:S(2)}, u32[]{:S(2)}) collective-permute-start(f32[80,128]{1,0:T(8,128)S(1)} %get-tuple-element.50), channel_id=1, source_target_pairs={{0,24},{4,28},{8,16},{12,20},{16,8},{20,12},{24,0},{28,4},{1,25},{... | collective-permute-start | bytes 122888 | tf_op jit(solution)/shard_map/ppermute | solution.py:622
  102.1 2.2 %collective-permute-done.8.refs_2_ = f32[80,128]{1,0:T(8,128)S(1)} collective-permute-done((f32[80,128]{1,0:T(8,128)S(1)}, f32[80,128]{1,0:T(8,128)S(1)}, u32[]{:S(2)}, u32[]{:S(2)}) %collective-permute-start.8) | collective-permute-done | bytes 40992 | tf_op jit(solution)/shard_map/ppermute | solution.py:622
  105.8 2.7 %collective-permute-start.11 = (f32[80,128]{1,0:T(8,128)S(1)}, f32[80,128]{1,0:T(8,128)S(1)}, u32[]{:S(2)}, u32[]{:S(2)}) collective-permute-start(f32[80,128]{1,0:T(8,128)S(1)} %add_pieces.5), channel_id=1, source_target_pairs={{0,16},{4,20},{8,24},{12,28},{16,0},{20,4},{24,8},{28,12},{1,17},{... | collective-permute-start | bytes 122888 | tf_op jit(solution)/shard_map/ppermute | solution.py:622
  110.8 3.5 %collective-permute-done.12 = f32[80,128]{1,0:T(8,128)S(1)} collective-permute-done((f32[80,128]{1,0:T(8,128)S(1)}, f32[80,128]{1,0:T(8,128)S(1)}, u32[]{:S(2)}, u32[]{:S(2)}) %collective-permute-start.12) | collective-permute-done | bytes 40992 | tf_op jit(solution)/shard_map/ppermute | solution.py:622
  117.9 1.8 %collective-permute-done.13.refs_1_ = f32[320,128]{1,0:T(8,128)S(1)} collective-permute-done((f32[320,128]{1,0:T(8,128)S(1)}, f32[320,128]{1,0:T(8,128)S(1)}, u32[]{:S(2)}, u32[]{:S(2)}) %collective-permute-start.13) | collective-permute-done | bytes 163872 | tf_op jit(solution)/shard_map/ppermute | solution.py:622
  121.0 1.7 %collective-permute-done.15.refs_3_ = f32[320,128]{1,0:T(8,128)S(1)} collective-permute-done((f32[320,128]{1,0:T(8,128)S(1)}, f32[320,128]{1,0:T(8,128)S(1)}, u32[]{:S(2)}, u32[]{:S(2)}) %collective-permute-start.15) | collective-permute-done | bytes 163872 | tf_op jit(solution)/shard_map/ppermute | solution.py:622
  124.2 1.7 %finish.1 = (f32[512,512]{1,0:T(8,128)}, f32[1,512]{1,0:T(1,128)}, f32[64,512]{1,0:T(8,128)}) custom-call(s32[3]{0:T(128)S(1)} %pad_add_fusion.place_ref, f32[320,128]{1,0:T(8,128)S(1)} %pad_maximum_fusion.refs_0_, f32[320,128]{1,0:T(8,128)S(1)} %collective-permute-done.13.refs_1_, f32[320,128]{1,0:T(8,128)S(1)} %collective-permute-done.14.refs_2_, ...), custom_call_target="tpu_custom_call" | custom-call | tf_op jit(solution)/shard_map/finish/pallas_call | solution.py:604
  (79 shorter events, 28.6 us)
Async XLA Ops:
  2.9 38.6 %copy-start.15 = (f32[64]{0:T(128)S(1)}, f32[64]{0:T(128)}, u32[]{:S(2)}) copy-start(f32[64]{0:T(128)} %param.9) | copy-start | bytes 772
  2.9 38.7 %copy-start.10 = (bf16[512,512]{1,0:T(8,128)(2,1)S(1)}, bf16[512,512]{1,0:T(8,128)(2,1)}, u32[]{:S(2)}) copy-start(bf16[512,512]{1,0:T(8,128)(2,1)} %w_ref.1) | copy-start | bytes 1572868
  2.9 38.7 %copy-start.12 = (f32[512]{0:T(512)S(1)}, f32[512]{0:T(512)}, u32[]{:S(2)}) copy-start(f32[512]{0:T(512)} %param.12) | copy-start | bytes 6148
  30.4 28.7 %all-to-all-start = ((f32[32,16,384]{2,1,0:T(8,128)}), f32[32,16,384]{2,1,0:T(8,128)S(1)}, u32[]{:S(2)}, u32[]{:S(2)}) async-start(f32[32,16,384]{2,1,0:T(8,128)} %bitcast.9), calls=%async_computation | async-start | bytes 1572864 | tf_op jit(solution)/shard_map/all_to_all | solution.py:640
  60.5 7.6 %collective-permute-start = (f32[360,128]{1,0:T(8,128)S(1)}, f32[360,128]{1,0:T(8,128)S(1)}, u32[]{:S(2)}, u32[]{:S(2)}) collective-permute-start(f32[360,128]{1,0:T(8,128)S(1)} %get-tuple-element.33), channel_id=1, source_target_pairs={{0,1},{1,0},{2,3},{3,2},{4,5},{5,4},{6,7},{7,6},{8,9},{9,8},{10,11... | collective-permute-start | bytes 552968 | tf_op jit(solution)/shard_map/ppermute | solution.py:622
  61.3 8.8 %collective-permute-start.1 = (f32[360,128]{1,0:T(8,128)S(1)}, f32[360,128]{1,0:T(8,128)S(1)}, u32[]{:S(2)}, u32[]{:S(2)}) collective-permute-start(f32[360,128]{1,0:T(8,128)S(1)} %get-tuple-element.34), channel_id=1, source_target_pairs={{0,2},{1,3},{2,0},{3,1},{4,6},{5,7},{6,4},{7,5},{8,10},{9,11},{10,... | collective-permute-start | bytes 552968 | tf_op jit(solution)/shard_map/ppermute | solution.py:622
  62.8 8.9 %collective-permute-start.2 = (f32[360,128]{1,0:T(8,128)S(1)}, f32[360,128]{1,0:T(8,128)S(1)}, u32[]{:S(2)}, u32[]{:S(2)}) collective-permute-start(f32[360,128]{1,0:T(8,128)S(1)} %get-tuple-element.35), channel_id=1, source_target_pairs={{0,3},{1,2},{2,1},{3,0},{4,7},{5,6},{6,5},{7,4},{8,11},{9,10},{10,... | collective-permute-start | bytes 552968 | tf_op jit(solution)/shard_map/ppermute | solution.py:622
  85.0 2.1 %collective-permute-start.3 = (f32[1280,128]{1,0:T(8,128)S(1)}, f32[1280,128]{1,0:T(8,128)S(1)}, u32[]{:S(2)}, u32[]{:S(2)}) collective-permute-start(f32[1280,128]{1,0:T(8,128)S(1)} %get-tuple-element.37), channel_id=1, source_target_pairs={{0,4},{4,0},{8,12},{12,8},{16,20},{20,16},{24,28},{28,24},{1,5},{5... | collective-permute-start | bytes 1966088 | tf_op jit(solution)/shard_map/ppermute | solution.py:622
  87.2 8.7 %collective-permute-start.4 = (f32[320,128]{1,0:T(8,128)S(1)}, f32[320,128]{1,0:T(8,128)S(1)}, u32[]{:S(2)}, u32[]{:S(2)}) collective-permute-start(f32[320,128]{1,0:T(8,128)S(1)} %get-tuple-element.38), channel_id=1, source_target_pairs={{0,1},{1,0},{2,3},{3,2},{4,5},{5,4},{6,7},{7,6},{8,9},{9,8},{10,11... | collective-permute-start | bytes 491528 | tf_op jit(solution)/shard_map/ppermute | solution.py:622
  88.1 9.5 %collective-permute-start.5 = (f32[320,128]{1,0:T(8,128)S(1)}, f32[320,128]{1,0:T(8,128)S(1)}, u32[]{:S(2)}, u32[]{:S(2)}) collective-permute-start(f32[320,128]{1,0:T(8,128)S(1)} %get-tuple-element.39), channel_id=1, source_target_pairs={{0,2},{1,3},{2,0},{3,1},{4,6},{5,7},{6,4},{7,5},{8,10},{9,11},{10,... | collective-permute-start | bytes 491528 | tf_op jit(solution)/shard_map/ppermute | solution.py:622
  89.5 8.0 %collective-permute-start.6 = (f32[320,128]{1,0:T(8,128)S(1)}, f32[320,128]{1,0:T(8,128)S(1)}, u32[]{:S(2)}, u32[]{:S(2)}) collective-permute-start(f32[320,128]{1,0:T(8,128)S(1)} %get-tuple-element.40), channel_id=1, source_target_pairs={{0,3},{1,2},{2,1},{3,0},{4,7},{5,6},{6,5},{7,4},{8,11},{9,10},{10,... | collective-permute-start | bytes 491528 | tf_op jit(solution)/shard_map/ppermute | solution.py:622
  97.6 4.5 %collective-permute-start.7 = (f32[80,128]{1,0:T(8,128)S(1)}, f32[80,128]{1,0:T(8,128)S(1)}, u32[]{:S(2)}, u32[]{:S(2)}) collective-permute-start(f32[80,128]{1,0:T(8,128)S(1)} %get-tuple-element.48), channel_id=1, source_target_pairs={{0,8},{4,12},{8,0},{12,4},{16,24},{20,28},{24,16},{28,20},{1,9},{5... | collective-permute-start | bytes 122888 | tf_op jit(solution)/shard_map/ppermute | solution.py:622
  98.5 5.8 %collective-permute-start.8 = (f32[80,128]{1,0:T(8,128)S(1)}, f32[80,128]{1,0:T(8,128)S(1)}, u32[]{:S(2)}, u32[]{:S(2)}) collective-permute-start(f32[80,128]{1,0:T(8,128)S(1)} %get-tuple-element.49), channel_id=1, source_target_pairs={{0,16},{4,20},{8,24},{12,28},{16,0},{20,4},{24,8},{28,12},{1,17},{... | collective-permute-start | bytes 122888 | tf_op jit(solution)/shard_map/ppermute | solution.py:622
  99.9 5.8 %collective-permute-start.9 = (f32[80,128]{1,0:T(8,128)S(1)}, f32[80,128]{1,0:T(8,128)S(1)}, u32[]{:S(2)}, u32[]{:S(2)}) collective-permute-start(f32[80,128]{1,0:T(8,128)S(1)} %get-tuple-element.50), channel_id=1, source_target_pairs={{0,24},{4,28},{8,16},{12,20},{16,8},{20,12},{24,0},{28,4},{1,25},{... | collective-permute-start | bytes 122888 | tf_op jit(solution)/shard_map/ppermute | solution.py:622
  105.7 4.5 %collective-permute-start.10 = (f32[80,128]{1,0:T(8,128)S(1)}, f32[80,128]{1,0:T(8,128)S(1)}, u32[]{:S(2)}, u32[]{:S(2)}) collective-permute-start(f32[80,128]{1,0:T(8,128)S(1)} %add_pieces.5), channel_id=1, source_target_pairs={{0,8},{4,12},{8,0},{12,4},{16,24},{20,28},{24,16},{28,20},{1,9},{5... | collective-permute-start | bytes 122888 | tf_op jit(solution)/shard_map/ppermute | solution.py:622
  105.8 5.0 %collective-permute-start.11 = (f32[80,128]{1,0:T(8,128)S(1)}, f32[80,128]{1,0:T(8,128)S(1)}, u32[]{:S(2)}, u32[]{:S(2)}) collective-permute-start(f32[80,128]{1,0:T(8,128)S(1)} %add_pieces.5), channel_id=1, source_target_pairs={{0,16},{4,20},{8,24},{12,28},{16,0},{20,4},{24,8},{28,12},{1,17},{... | collective-permute-start | bytes 122888 | tf_op jit(solution)/shard_map/ppermute | solution.py:622
  108.5 5.8 %collective-permute-start.12 = (f32[80,128]{1,0:T(8,128)S(1)}, f32[80,128]{1,0:T(8,128)S(1)}, u32[]{:S(2)}, u32[]{:S(2)}) collective-permute-start(f32[80,128]{1,0:T(8,128)S(1)} %add_pieces.5), channel_id=1, source_target_pairs={{0,24},{4,28},{8,16},{12,20},{16,8},{20,12},{24,0},{28,4},{1,25},{... | collective-permute-start | bytes 122888 | tf_op jit(solution)/shard_map/ppermute | solution.py:622
  114.3 5.4 %collective-permute-start.13 = (f32[320,128]{1,0:T(8,128)S(1)}, f32[320,128]{1,0:T(8,128)S(1)}, u32[]{:S(2)}, u32[]{:S(2)}) collective-permute-start(f32[320,128]{1,0:T(8,128)S(1)} %pad_maximum_fusion.refs_0_), channel_id=1, source_target_pairs={{0,1},{1,0},{2,3},{3,2},{4,5},{5,4},{6,7},{7,6},{8,9},{9,8},{10,11... | collective-permute-start | bytes 491528 | tf_op jit(solution)/shard_map/ppermute | solution.py:622
  115.7 5.3 %collective-permute-start.14 = (f32[320,128]{1,0:T(8,128)S(1)}, f32[320,128]{1,0:T(8,128)S(1)}, u32[]{:S(2)}, u32[]{:S(2)}) collective-permute-start(f32[320,128]{1,0:T(8,128)S(1)} %pad_maximum_fusion.refs_0_), channel_id=1, source_target_pairs={{0,2},{1,3},{2,0},{3,1},{4,6},{5,7},{6,4},{7,5},{8,10},{9,11},{10,... | collective-permute-start | bytes 491528 | tf_op jit(solution)/shard_map/ppermute | solution.py:622
  116.4 6.3 %collective-permute-start.15 = (f32[320,128]{1,0:T(8,128)S(1)}, f32[320,128]{1,0:T(8,128)S(1)}, u32[]{:S(2)}, u32[]{:S(2)}) collective-permute-start(f32[320,128]{1,0:T(8,128)S(1)} %pad_maximum_fusion.refs_0_), channel_id=1, source_target_pairs={{0,3},{1,2},{2,1},{3,0},{4,7},{5,6},{6,5},{7,4},{8,11},{9,10},{10,... | collective-permute-start | bytes 491528 | tf_op jit(solution)/shard_map/ppermute | solution.py:622
  117.9 5.0 %collective-permute-start.16 = (f32[320,128]{1,0:T(8,128)S(1)}, f32[320,128]{1,0:T(8,128)S(1)}, u32[]{:S(2)}, u32[]{:S(2)}) collective-permute-start(f32[320,128]{1,0:T(8,128)S(1)} %pad_maximum_fusion.refs_0_), channel_id=1, source_target_pairs={{0,4},{4,0},{8,12},{12,8},{16,20},{20,16},{24,28},{28,24},{1,5},{5... | collective-permute-start | bytes 491528 | tf_op jit(solution)/shard_map/ppermute | solution.py:622
  119.7 3.2 %collective-permute-start.17 = (f32[320,128]{1,0:T(8,128)S(1)}, f32[320,128]{1,0:T(8,128)S(1)}, u32[]{:S(2)}, u32[]{:S(2)}) collective-permute-start(f32[320,128]{1,0:T(8,128)S(1)} %collective-permute-done.13.refs_1_), channel_id=1, source_target_pairs={{0,4},{4,0},{8,12},{12,8},{16,20},{20,16},{24,28},{28,24},{1,5},{5... | collective-permute-start | bytes 491528 | tf_op jit(solution)/shard_map/ppermute | solution.py:622
  121.0 1.8 %collective-permute-start.18 = (f32[320,128]{1,0:T(8,128)S(1)}, f32[320,128]{1,0:T(8,128)S(1)}, u32[]{:S(2)}, u32[]{:S(2)}) collective-permute-start(f32[320,128]{1,0:T(8,128)S(1)} %collective-permute-done.14.refs_2_), channel_id=1, source_target_pairs={{0,4},{4,0},{8,12},{12,8},{16,20},{20,16},{24,28},{28,24},{1,5},{5... | collective-permute-start | bytes 491528 | tf_op jit(solution)/shard_map/ppermute | solution.py:622
  122.8 1.4 %collective-permute-start.19 = (f32[320,128]{1,0:T(8,128)S(1)}, f32[320,128]{1,0:T(8,128)S(1)}, u32[]{:S(2)}, u32[]{:S(2)}) collective-permute-start(f32[320,128]{1,0:T(8,128)S(1)} %collective-permute-done.15.refs_3_), channel_id=1, source_target_pairs={{0,4},{4,0},{8,12},{12,8},{16,20},{20,16},{24,28},{28,24},{1,5},{5... | collective-permute-start | bytes 491528 | tf_op jit(solution)/shard_map/ppermute | solution.py:622
  (13 other events, 116.5 us)

commit v6 on v5

--- a/solution.py
+++ b/solution.py
@@ -182,7 +182,7 @@
         )
         values = values * scale[:, :STEPS]
         step = lax.broadcasted_iota(jnp.int32, (1, SUBS, STEPS), 2)
-        row_pair = lax.broadcasted_iota(jnp.int32, (1, SUBS, STEPS), 1) // 2
+        row_pair = lax.broadcasted_iota(jnp.int32, (1, SUBS, STEPS), 1) >> 1
         in_first = step < NM - (first_pair + start + row_pair)
         lower = jnp.where(in_first, values, 0.0)
         upper = jnp.where(in_first, 0.0, values)
@@ -202,12 +202,16 @@
             part = product(left.reshape(2 * rows_half, end - begin), table[begin:end])
             rest = part if rest is None else rest + part
         both = jnp.concatenate([rest[:rows_half] + base, rest[rows_half:]], axis=0)
-        row_id = lax.broadcasted_iota(jnp.int32, (2 * rows_half, LANES), 0) % SUBS // 2
-        lane_part = lax.broadcasted_iota(jnp.int32, (2 * rows_half, LANES), 1) // rows_all
-        total = jnp.zeros((2 * rows_half, LANES), jnp.float32)
+        both = both.reshape(2 * slot_count, SUBS, blocks * LANES)
+        row_id = lax.broadcasted_iota(jnp.int32, (1, SUBS, LANES), 1) >> 1
+        lane_part = lax.broadcasted_iota(jnp.int32, (1, SUBS, LANES), 2)
+        lane_part = jnp.where(lane_part < rows_all, 0, 1)
+        total = None
         for block in range(blocks):
+            part = both[:, :, block * LANES : (block + 1) * LANES]
             keep = row_id == block * per_block + lane_part
-            total = total + jnp.where(keep, both[:, block * LANES : (block + 1) * LANES], 0.0)
+            total = jnp.where(keep, part, 0.0 if total is None else total)
+        total = total.reshape(2 * rows_half, LANES)
         if per_block == 2:
             total = total + pltpu.roll(total, rows_all, 1)
         total = total.astype(jnp.bfloat16).astype(jnp.float32)
@@ -222,7 +226,7 @@
         group(index * PAIRS)
         return carry
 
-    lax.fori_loop(0, pair_count // PAIRS, group_body, 0)
+    lax.fori_loop(0, pair_count // PAIRS, group_body, 0, unroll=2 - pair_count // PAIRS % 2)
     if pair_count % PAIRS:
         group(pair_count - PAIRS)
 
@@ -264,7 +268,7 @@
             pltpu.VMEM((slot_count, 4 * pair_pad, LANES), jnp.float32),
             pltpu.SemaphoreType.DMA,
         ],
-        compiler_params=pltpu.CompilerParams(vmem_limit_bytes=40 * MIB),
+        compiler_params=pltpu.CompilerParams(vmem_limit_bytes=VMEM_LIMIT),
         name="coefficients",
     )(first_pair, jnp.transpose(spectra, (0, 2, 1, 3)))
 
@@ -396,7 +400,7 @@
     return preact * half, slope
 
 
-def forward_kernel(latents_ref, w_ref, b_ref, slope_ref, hidden_t_ref, latents_t_ref):
+def forward_kernel(latents_ref, w_ref, b_ref, _, slope_ref, hidden_t_ref, latents_t_ref):
     latents = latents_ref[...]
     preact = jnp.dot(latents, w_ref[...], preferred_element_type=jnp.float32) + b_ref[...]
     hidden, slope = gelu_parts(preact)
@@ -405,7 +409,7 @@
     latents_t_ref[...] = latents.T
 
 
-def forward(latents, w_hidden, b_hidden, parts):
+def forward(latents, w_hidden, b_hidden, after, parts):
     cells, width = latents.shape
     cols = cells // parts
     return pl.pallas_call(
@@ -420,6 +424,7 @@
             pl.BlockSpec((cols, width), lambda i: (i, 0)),
             pl.BlockSpec((width, width), lambda i: (0, 0)),
             pl.BlockSpec((1, width), lambda i: (0, 0)),
+            pl.BlockSpec(memory_space=pl.ANY),
         ],
         out_specs=(
             pl.BlockSpec((cols, width), lambda i: (i, 0)),
@@ -433,7 +438,7 @@
             transcendentals=cells * width,
         ),
         name="forward",
-    )(latents, w_hidden, b_hidden.reshape(1, width))
+    )(latents, w_hidden, b_hidden.reshape(1, width), after)
 
 
 def backward_kernel(
@@ -639,9 +644,6 @@
     coeffs = coeffs.reshape(lat_count * lon_count, share, 4 * pair_pad)
     coeffs = lax.all_to_all(coeffs, ("lat", "lon"), split_axis=0, concat_axis=0, tiled=True)
 
-    slope, hidden_t, latents_t = forward(
-        latents.reshape(cells, width), w_hidden, b_hidden, parts
-    )
     trig = trig_table(pair_count, lon_count)
 
     lanes = lat_count * share
@@ -666,15 +668,20 @@
     ).astype(jnp.bfloat16)
     w_out_t = jnp.concatenate([w_out.T, jnp.zeros((LANES - F, width), w_out.dtype)], axis=0)
 
-    core_index, deep_index = lat_index & 1, lat_index >> 1
+    depth = lat_count // 2
+    bits = depth.bit_length() - 1
+    core_index = lat_index & 1
+    deep_index = sum(((lat_index >> (bit + 1)) & 1) << (bits - 1 - bit) for bit in range(bits))
     spots = jnp.stack([core_index, lon_index, deep_index])
     grids = grid_field(lon_index.reshape(1), trig, coeffs, pair_count)
+    slope, hidden_t, latents_t = forward(
+        latents.reshape(cells, width), w_hidden, b_hidden, grids[0], parts
+    )
     grids = [grids[0]] + [swap(grids[part], "lon", part) for part in range(1, lon_count)]
 
     device_count = lat_count * lon_count
     used_rows = (width + F + 1) * width // LANES
     chunk = pad_to(pad_to(used_rows, device_count) // device_count, SUBS)
-    depth = lat_count // 2
     preact_back, keep, send = backward(
         core_index.reshape(1), grids, scale, place, w_out_t, slope, hidden_t, latents_t,
         chunk * device_count,
@@ -688,11 +695,15 @@
     )
     arrived = [swap(pieces[part], "lon", part) for part in range(1, lon_count)]
     arrived, latent_grad = lax.optimization_barrier((arrived, latent_grad))
-    pieces = add_pieces(deep_index.reshape(1), [pieces[0]] + arrived, depth)
-    arrived = [swap(pieces[part], "lat", 2 * part) for part in range(1, depth)]
+    pieces = [pieces[0]] + arrived
+    for bit in range(bits):
+        side = (lat_index >> (bit + 1)) & 1
+        pieces = add_pieces(side.reshape(1), pieces, 2)
+        pieces = [pieces[0], swap(pieces[1], "lat", 2 << bit)]
     norm = 1.0 / math.sqrt(rows_all * NLON)
-    total = add_pieces(deep_index.reshape(1), [pieces[0]] + arrived, 1, norm)[0]
-    total = jnp.concatenate([total] + [swap(total, "lat", 2 * part) for part in range(1, depth)])
+    total = add_pieces(deep_index.reshape(1), pieces, 1, norm)[0]
+    for bit in reversed(range(bits)):
+        total = jnp.concatenate([total, swap(total, "lat", 2 << bit)])
     totals = [total] + [swap(total, "lon", part) for part in range(1, lon_count)]
     totals = totals + [swap(piece, "lat", 1) for piece in totals]
     hidden_grad, bias_grad, out_grad = finish(spots, totals, width, depth)

time: 126 us -> 119 us (0.944)
  local copies, waits for them, and re-layouts: 18.5 us -> 5.17 us
  waiting for transfers between devices: 29 us -> 41.7 us
  starting transfers between devices: 26.9 us -> 22.5 us
  Pallas kernels: 44.9 us -> 42.7 us
    all_to_all x1, waiting for transfers between devices: 3.67 us -> 17.3 us  [local(): lax.all_to_all(coeffs, ('lat', 'lon'), split_axis=0, concat_axis=0, tiled...]
    unnamed x32 -> x16, local copies, waits for them, and re-layouts: 18 us -> 4.68 us
    ppermute x20 -> x18, starting transfers between devices: 19.6 us -> 15.2 us  [swap(): return lax.ppermute(value, axis, [(i, i ^ bits) for i in range(count)])]
    pallas_call x1, Pallas kernels: 27.5 us -> 25.3 us  [coefficients(): pl.pallas_call(kernel, out_shape=jax.ShapeDtypeStruct((lat_count, slot_co...]
    ppermute x20 -> x18, waiting for transfers between devices: 25.3 us -> 24.4 us  [swap(): return lax.ppermute(value, axis, [(i, i ^ bits) for i in range(count)])]
  transfers between devices with their start and end apart: 21 -> 19, of which waited for: 14 -> 11; matrix products, arithmetic and copies ran while one was open for 5% -> 5% of each run, Pallas kernels for 7% -> 8%
where the time goes in v6:
time: 119 us
  Pallas kernels  42.7 us (36%)
  waiting for transfers between devices  41.7 us (35%)
  starting transfers between devices  22.5 us (19%)
  matrix products  5.26 us (4%)
  local copies, waits for them, and re-layouts  5.17 us (4%)
    pallas_call x1, Pallas kernels, coefficients(): pl.pallas_call(kernel, out_shape=jax.ShapeDtypeStruct((lat_count, slot_co...  25.3 us
    ppermute x18, waiting for transfers between devices, swap(): return lax.ppermute(value, axis, [(i, i ^ bits) for i in range(count)])  24.4 us
    all_to_all x1, waiting for transfers between devices, local(): lax.all_to_all(coeffs, ('lat', 'lon'), split_axis=0, concat_axis=0, tiled...  17.3 us
    ppermute x18, starting transfers between devices, swap(): return lax.ppermute(value, axis, [(i, i ^ bits) for i in range(count)])  15.2 us
    all_to_all x1, starting transfers between devices, local(): lax.all_to_all(coeffs, ('lat', 'lon'), split_axis=0, concat_axis=0, tiled...  7.3 us
    pallas_call x1, Pallas kernels, forward(): pl.pallas_call(forward_kernel, grid=(parts,), out_shape=(jax.ShapeDtypeSt...  5.89 us
    pallas_call x1, Pallas kernels, backward(): pl.pallas_call(functools.partial(backward_kernel, blocks=blocks), grid=(p...  5.27 us
    dot_general x1, matrix products, local(): lax.dot_general(preact_back, w_hidden, (((1,), (1,)), ((), ())), preferre...  5.26 us
  transfers between devices with their start and end apart: 19, of which 11 were waited for; matrix products, arithmetic and copies ran while one was open for 5% of the time, Pallas kernels for 8%

profile of v6, /device:TPU:0, one launch (start us, length us, event | category | flops | bytes accessed | tf_op | source)
XLA Modules:
  0.0 118.8 jit_solution(9281980386443007816)
XLA Ops:
  0.7 25.3 %coefficients.1 = f32[8,64,384]{2,1,0:T(8,128)} custom-call(s32[1]{0:T(128)} %bitcast.7.first_ref, f32[8,90,2,721]{3,2,1,0:T(2,128)} %bitcast.21), custom_call_target="tpu_custom_call" | custom-call | tf_op jit(solution)/shard_map/coefficients/pallas_call | solution.py:252
  26.0 7.3 %all-to-all-start = ((f32[32,16,384]{2,1,0:T(8,128)}), f32[32,16,384]{2,1,0:T(8,128)S(1)}, u32[]{:S(2)}, u32[]{:S(2)}) async-start(f32[32,16,384]{2,1,0:T(8,128)} %bitcast.22), calls=%async_computation | async-start | bytes 1572864 | tf_op jit(solution)/shard_map/all_to_all | solution.py:645
  33.8 3.0 %trig_table.1.trig_ref = bf16[4,360,384]{2,1,0:T(8,128)(2,1)} custom-call(), custom_call_target="tpu_custom_call" | custom-call | flops 3317760 | bytes 1105920 | tf_op jit(solution)/shard_map/trig_table/pallas_call | solution.py:311
  37.4 17.3 %all-to-all-done.coeff_ref = f32[32,16,384]{2,1,0:T(8,128)S(1)} async-done(((f32[32,16,384]{2,1,0:T(8,128)}), f32[32,16,384]{2,1,0:T(8,128)S(1)}, u32[]{:S(2)}, u32[]{:S(2)}) %all-to-all-start) | async-done | bytes 786464 | tf_op jit(solution)/shard_map/all_to_all | solution.py:645
  55.9 1.3 %grid_field.1 = (f32[360,128]{1,0:T(8,128)S(1)}, f32[360,128]{1,0:T(8,128)S(1)}, f32[360,128]{1,0:T(8,128)S(1)}, f32[360,128]{1,0:T(8,128)S(1)}) custom-call(s32[1]{0:T(128)} %bitcast.lon_ref.index_ref, bf16[4,360,384]{2,1,0:T(8,128)(2,1)S(1)} %copy-done, f32[32,16,384]{2,1,0:T(8,128)S(1)} %all-to-all-done.coeff_ref), custom_call_target="tpu_custom_call" | custom-call | flops 566231040 | bytes 2678784 | tf_op jit(solution)/shard_map/grid_field/pallas_call | solution.py:372
  58.1 1.5 %collective-permute-start.1 = (f32[360,128]{1,0:T(8,128)S(1)}, f32[360,128]{1,0:T(8,128)S(1)}, u32[]{:S(2)}, u32[]{:S(2)}) collective-permute-start(f32[360,128]{1,0:T(8,128)S(1)} %get-tuple-element.34), channel_id=1, source_target_pairs={{0,2},{1,3},{2,0},{3,1},{4,6},{5,7},{6,4},{7,5},{8,10},{9,11},{10,... | collective-permute-start | bytes 552968 | tf_op jit(solution)/shard_map/ppermute | solution.py:627
  59.6 1.3 %collective-permute-start.2 = (f32[360,128]{1,0:T(8,128)S(1)}, f32[360,128]{1,0:T(8,128)S(1)}, u32[]{:S(2)}, u32[]{:S(2)}) collective-permute-start(f32[360,128]{1,0:T(8,128)S(1)} %get-tuple-element.35), channel_id=1, source_target_pairs={{0,3},{1,2},{2,1},{3,0},{4,7},{5,6},{6,5},{7,4},{8,11},{9,10},{10,... | collective-permute-start | bytes 552968 | tf_op jit(solution)/shard_map/ppermute | solution.py:627
  60.9 1.8 %copy-done.1 = bf16[8,360,512]{2,1,0:T(8,128)(2,1)S(1)} copy-done((bf16[8,360,512]{2,1,0:T(8,128)(2,1)S(1)}, bf16[8,360,512]{2,1,0:T(8,128)(2,1)}, u32[]{:S(2)}) %copy-start.1) | copy-done | bytes 2949144
  62.8 5.9 %forward.1 = (f32[2880,512]{1,0:T(8,128)S(1)}, bf16[4,512,720]{2,1,0:T(8,128)(2,1)S(1)}, bf16[4,512,720]{2,1,0:T(8,128)(2,1)S(1)}) custom-call(bf16[2880,512]{1,0:T(8,128)(2,1)S(1)} %bitcast.19, bf16[512,512]{1,0:T(8,128)(2,1)S(1)} %copy-done.3, f32[1,512]{1,0:T(1,128)S(1)} %bitcast.20, f32[360,128]{1,0:T(8,128)S(1)} %get-tuple-element.29._.refs_0_), custom_call_target="tpu_custom_call" | custom-call | flops 1509949440 | bytes 14745600 | tf_op jit(solution)/shard_map/forward/pallas_call | solution.py:415
  68.7 5.3 %backward.1 = (bf16[2880,512]{1,0:T(8,128)(2,1)S(1)}, f32[1280,128]{1,0:T(8,128)S(1)}, f32[1280,128]{1,0:T(8,128)S(1)}) custom-call(s32[1]{0:T(128)} %bitcast.1.core_ref, f32[4,1,128]{2,1,0:T(1,128)S(1)} %bitcast.18, bf16[4,128,1024]{2,1,0:T(8,128)(2,1)S(1)} %fusion.place_ref, bf16[128,512]{1,0:T(8,128)(2,1)S(1)} %concatenate.10.w_out_ref, ...), custom_call_target="tpu_custom_call" | custom-call | flops 2264924160 | bytes 14745600 | tf_op jit(solution)/shard_map/backward/pallas_call | solution.py:512
  74.0 1.6 %copy-done.2 = bf16[2880,512]{1,0:T(8,128)(2,1)} copy-done((bf16[2880,512]{1,0:T(8,128)(2,1)}, bf16[2880,512]{1,0:T(8,128)(2,1)S(1)}, u32[]{:S(2)}) %copy-start.2) | copy-done | bytes 2949144
  75.6 2.1 %collective-permute-done.3.refs_1_ = f32[1280,128]{1,0:T(8,128)S(1)} collective-permute-done((f32[1280,128]{1,0:T(8,128)S(1)}, f32[1280,128]{1,0:T(8,128)S(1)}, u32[]{:S(2)}, u32[]{:S(2)}) %collective-permute-start.3) | collective-permute-done | bytes 655392 | tf_op jit(solution)/shard_map/ppermute | solution.py:627
  78.5 1.5 %collective-permute-start.5 = (f32[320,128]{1,0:T(8,128)S(1)}, f32[320,128]{1,0:T(8,128)S(1)}, u32[]{:S(2)}, u32[]{:S(2)}) collective-permute-start(f32[320,128]{1,0:T(8,128)S(1)} %get-tuple-element.39), channel_id=1, source_target_pairs={{0,2},{1,3},{2,0},{3,1},{4,6},{5,7},{6,4},{7,5},{8,10},{9,11},{10,... | collective-permute-start | bytes 491528 | tf_op jit(solution)/shard_map/ppermute | solution.py:627
  81.3 5.3 %convolution_convert_fusion = bf16[2880,512]{1,0:T(8,128)(2,1)} fusion(bf16[2880,512]{1,0:T(8,128)(2,1)} %copy-done.2, bf16[512,512]{1,0:T(8,128)(2,1)} %w_ref.1), kind=kOutput, calls=%fused_computation | convolution fusion | flops 1511424000 | bytes 6422528 | tf_op jit(solution)/shard_map/dot_general | solution.py:689
  86.6 1.4 %collective-permute-done.5.refs_2_ = f32[320,128]{1,0:T(8,128)S(1)} collective-permute-done((f32[320,128]{1,0:T(8,128)S(1)}, f32[320,128]{1,0:T(8,128)S(1)}, u32[]{:S(2)}, u32[]{:S(2)}) %collective-permute-start.5) | collective-permute-done | bytes 163872 | tf_op jit(solution)/shard_map/ppermute | solution.py:627
  89.2 3.4 %collective-permute-done.7.refs_1_ = f32[160,128]{1,0:T(8,128)S(1)} collective-permute-done((f32[160,128]{1,0:T(8,128)S(1)}, f32[160,128]{1,0:T(8,128)S(1)}, u32[]{:S(2)}, u32[]{:S(2)}) %collective-permute-start.7) | collective-permute-done | bytes 81952 | tf_op jit(solution)/shard_map/ppermute | solution.py:627
  93.5 4.0 %collective-permute-done.8.refs_1_ = f32[80,128]{1,0:T(8,128)S(1)} collective-permute-done((f32[80,128]{1,0:T(8,128)S(1)}, f32[80,128]{1,0:T(8,128)S(1)}, u32[]{:S(2)}, u32[]{:S(2)}) %collective-permute-start.8) | collective-permute-done | bytes 40992 | tf_op jit(solution)/shard_map/ppermute | solution.py:627
  98.6 4.0 %collective-permute-done.9 = f32[80,128]{1,0:T(8,128)S(1)} collective-permute-done((f32[80,128]{1,0:T(8,128)S(1)}, f32[80,128]{1,0:T(8,128)S(1)}, u32[]{:S(2)}, u32[]{:S(2)}) %collective-permute-start.9) | collective-permute-done | bytes 40992 | tf_op jit(solution)/shard_map/ppermute | solution.py:627
  103.6 3.5 %collective-permute-done.10 = f32[160,128]{1,0:T(8,128)S(1)} collective-permute-done((f32[160,128]{1,0:T(8,128)S(1)}, f32[160,128]{1,0:T(8,128)S(1)}, u32[]{:S(2)}, u32[]{:S(2)}) %collective-permute-start.10) | collective-permute-done | bytes 81952 | tf_op jit(solution)/shard_map/ppermute | solution.py:627
  107.1 1.4 %collective-permute-start.11 = (f32[320,128]{1,0:T(8,128)S(1)}, f32[320,128]{1,0:T(8,128)S(1)}, u32[]{:S(2)}, u32[]{:S(2)}) collective-permute-start(f32[320,128]{1,0:T(8,128)S(1)} %pad_maximum_fusion.refs_0_), channel_id=1, source_target_pairs={{0,1},{1,0},{2,3},{3,2},{4,5},{5,4},{6,7},{7,6},{8,9},{9,8},{10,11... | collective-permute-start | bytes 491528 | tf_op jit(solution)/shard_map/ppermute | solution.py:627
  109.1 1.5 %collective-permute-start.13 = (f32[320,128]{1,0:T(8,128)S(1)}, f32[320,128]{1,0:T(8,128)S(1)}, u32[]{:S(2)}, u32[]{:S(2)}) collective-permute-start(f32[320,128]{1,0:T(8,128)S(1)} %pad_maximum_fusion.refs_0_), channel_id=1, source_target_pairs={{0,3},{1,2},{2,1},{3,0},{4,7},{5,6},{6,5},{7,4},{8,11},{9,10},{10,... | collective-permute-start | bytes 491528 | tf_op jit(solution)/shard_map/ppermute | solution.py:627
  110.6 1.8 %collective-permute-done.11.refs_1_ = f32[320,128]{1,0:T(8,128)S(1)} collective-permute-done((f32[320,128]{1,0:T(8,128)S(1)}, f32[320,128]{1,0:T(8,128)S(1)}, u32[]{:S(2)}, u32[]{:S(2)}) %collective-permute-start.11) | collective-permute-done | bytes 163872 | tf_op jit(solution)/shard_map/ppermute | solution.py:627
  112.4 3.1 %collective-permute-done.12.refs_2_ = f32[320,128]{1,0:T(8,128)S(1)} collective-permute-done((f32[320,128]{1,0:T(8,128)S(1)}, f32[320,128]{1,0:T(8,128)S(1)}, u32[]{:S(2)}, u32[]{:S(2)}) %collective-permute-start.12) | collective-permute-done | bytes 163872 | tf_op jit(solution)/shard_map/ppermute | solution.py:627
  117.1 1.7 %finish.1 = (f32[512,512]{1,0:T(8,128)}, f32[1,512]{1,0:T(1,128)}, f32[64,512]{1,0:T(8,128)}) custom-call(s32[3]{0:T(128)S(1)} %pad_add_fusion.place_ref, f32[320,128]{1,0:T(8,128)S(1)} %pad_maximum_fusion.refs_0_, f32[320,128]{1,0:T(8,128)S(1)} %collective-permute-done.11.refs_1_, f32[320,128]{1,0:T(8,128)S(1)} %collective-permute-done.12.refs_2_, ...), custom_call_target="tpu_custom_call" | custom-call | tf_op jit(solution)/shard_map/finish/pallas_call | solution.py:609
  (61 shorter events, 11.6 us)
Async XLA Ops:
  0.6 32.7 %copy-start.6 = (s32[64]{0:T(128)S(1)}, s32[64]{0:T(128)}, u32[]{:S(2)}) copy-start(s32[64]{0:T(128)} %param.8) | copy-start | bytes 772
  0.6 36.4 %copy-start.7 = (f32[64]{0:T(128)S(1)}, f32[64]{0:T(128)}, u32[]{:S(2)}) copy-start(f32[64]{0:T(128)} %param.9) | copy-start | bytes 772
  26.0 34.9 %copy-start.5 = (bf16[512,64]{0,1:T(8,128)(2,1)S(1)}, bf16[512,64]{0,1:T(8,128)(2,1)}, u32[]{:S(2)}) copy-start(bf16[512,64]{0,1:T(8,128)(2,1)} %param.13) | copy-start | bytes 196612
  26.0 35.0 %copy-start.3 = (bf16[512,512]{1,0:T(8,128)(2,1)S(1)}, bf16[512,512]{1,0:T(8,128)(2,1)}, u32[]{:S(2)}) copy-start(bf16[512,512]{1,0:T(8,128)(2,1)} %w_ref.1) | copy-start | bytes 1572868
  26.0 35.0 %copy-start.4 = (f32[512]{0:T(512)S(1)}, f32[512]{0:T(512)}, u32[]{:S(2)}) copy-start(f32[512]{0:T(512)} %param.12) | copy-start | bytes 6148
  26.0 28.7 %all-to-all-start = ((f32[32,16,384]{2,1,0:T(8,128)}), f32[32,16,384]{2,1,0:T(8,128)S(1)}, u32[]{:S(2)}, u32[]{:S(2)}) async-start(f32[32,16,384]{2,1,0:T(8,128)} %bitcast.22), calls=%async_computation | async-start | bytes 1572864 | tf_op jit(solution)/shard_map/all_to_all | solution.py:645
  57.3 11.4 %collective-permute-start = (f32[360,128]{1,0:T(8,128)S(1)}, f32[360,128]{1,0:T(8,128)S(1)}, u32[]{:S(2)}, u32[]{:S(2)}) collective-permute-start(f32[360,128]{1,0:T(8,128)S(1)} %get-tuple-element.33), channel_id=1, source_target_pairs={{0,1},{1,0},{2,3},{3,2},{4,5},{5,4},{6,7},{7,6},{8,9},{9,8},{10,11... | collective-permute-start | bytes 552968 | tf_op jit(solution)/shard_map/ppermute | solution.py:627
  58.1 10.6 %collective-permute-start.1 = (f32[360,128]{1,0:T(8,128)S(1)}, f32[360,128]{1,0:T(8,128)S(1)}, u32[]{:S(2)}, u32[]{:S(2)}) collective-permute-start(f32[360,128]{1,0:T(8,128)S(1)} %get-tuple-element.34), channel_id=1, source_target_pairs={{0,2},{1,3},{2,0},{3,1},{4,6},{5,7},{6,4},{7,5},{8,10},{9,11},{10,... | collective-permute-start | bytes 552968 | tf_op jit(solution)/shard_map/ppermute | solution.py:627
  59.6 9.1 %collective-permute-start.2 = (f32[360,128]{1,0:T(8,128)S(1)}, f32[360,128]{1,0:T(8,128)S(1)}, u32[]{:S(2)}, u32[]{:S(2)}) collective-permute-start(f32[360,128]{1,0:T(8,128)S(1)} %get-tuple-element.35), channel_id=1, source_target_pairs={{0,3},{1,2},{2,1},{3,0},{4,7},{5,6},{6,5},{7,4},{8,11},{9,10},{10,... | collective-permute-start | bytes 552968 | tf_op jit(solution)/shard_map/ppermute | solution.py:627
  75.6 2.1 %collective-permute-start.3 = (f32[1280,128]{1,0:T(8,128)S(1)}, f32[1280,128]{1,0:T(8,128)S(1)}, u32[]{:S(2)}, u32[]{:S(2)}) collective-permute-start(f32[1280,128]{1,0:T(8,128)S(1)} %get-tuple-element.37), channel_id=1, source_target_pairs={{0,4},{4,0},{8,12},{12,8},{16,20},{20,16},{24,28},{28,24},{1,5},{5... | collective-permute-start | bytes 1966088 | tf_op jit(solution)/shard_map/ppermute | solution.py:627
  77.7 8.8 %collective-permute-start.4 = (f32[320,128]{1,0:T(8,128)S(1)}, f32[320,128]{1,0:T(8,128)S(1)}, u32[]{:S(2)}, u32[]{:S(2)}) collective-permute-start(f32[320,128]{1,0:T(8,128)S(1)} %get-tuple-element.38), channel_id=1, source_target_pairs={{0,1},{1,0},{2,3},{3,2},{4,5},{5,4},{6,7},{7,6},{8,9},{9,8},{10,11... | collective-permute-start | bytes 491528 | tf_op jit(solution)/shard_map/ppermute | solution.py:627
  78.5 9.5 %collective-permute-start.5 = (f32[320,128]{1,0:T(8,128)S(1)}, f32[320,128]{1,0:T(8,128)S(1)}, u32[]{:S(2)}, u32[]{:S(2)}) collective-permute-start(f32[320,128]{1,0:T(8,128)S(1)} %get-tuple-element.39), channel_id=1, source_target_pairs={{0,2},{1,3},{2,0},{3,1},{4,6},{5,7},{6,4},{7,5},{8,10},{9,11},{10,... | collective-permute-start | bytes 491528 | tf_op jit(solution)/shard_map/ppermute | solution.py:627
  80.0 7.9 %collective-permute-start.6 = (f32[320,128]{1,0:T(8,128)S(1)}, f32[320,128]{1,0:T(8,128)S(1)}, u32[]{:S(2)}, u32[]{:S(2)}) collective-permute-start(f32[320,128]{1,0:T(8,128)S(1)} %get-tuple-element.40), channel_id=1, source_target_pairs={{0,3},{1,2},{2,1},{3,0},{4,7},{5,6},{6,5},{7,4},{8,11},{9,10},{10,... | collective-permute-start | bytes 491528 | tf_op jit(solution)/shard_map/ppermute | solution.py:627
  88.0 4.5 %collective-permute-start.7 = (f32[160,128]{1,0:T(8,128)S(1)}, f32[160,128]{1,0:T(8,128)S(1)}, u32[]{:S(2)}, u32[]{:S(2)}) collective-permute-start(f32[160,128]{1,0:T(8,128)S(1)} %get-tuple-element.48), channel_id=1, source_target_pairs={{0,8},{4,12},{8,0},{12,4},{16,24},{20,28},{24,16},{28,20},{1,9},{5... | collective-permute-start | bytes 245768 | tf_op jit(solution)/shard_map/ppermute | solution.py:627
  92.5 5.0 %collective-permute-start.8 = (f32[80,128]{1,0:T(8,128)S(1)}, f32[80,128]{1,0:T(8,128)S(1)}, u32[]{:S(2)}, u32[]{:S(2)}) collective-permute-start(f32[80,128]{1,0:T(8,128)S(1)} %get-tuple-element.50), channel_id=1, source_target_pairs={{0,16},{4,20},{8,24},{12,28},{16,0},{20,4},{24,8},{28,12},{1,17},{... | collective-permute-start | bytes 122888 | tf_op jit(solution)/shard_map/ppermute | solution.py:627
  97.5 5.1 %collective-permute-start.9 = (f32[80,128]{1,0:T(8,128)S(1)}, f32[80,128]{1,0:T(8,128)S(1)}, u32[]{:S(2)}, u32[]{:S(2)}) collective-permute-start(f32[80,128]{1,0:T(8,128)S(1)} %add_pieces.7), channel_id=1, source_target_pairs={{0,16},{4,20},{8,24},{12,28},{16,0},{20,4},{24,8},{28,12},{1,17},{... | collective-permute-start | bytes 122888 | tf_op jit(solution)/shard_map/ppermute | solution.py:627
  102.6 4.4 %collective-permute-start.10 = (f32[160,128]{1,0:T(8,128)S(1)}, f32[160,128]{1,0:T(8,128)S(1)}, u32[]{:S(2)}, u32[]{:S(2)}) collective-permute-start(f32[160,128]{1,0:T(8,128)S(1)} %pad_maximum_fusion.1), channel_id=1, source_target_pairs={{0,8},{4,12},{8,0},{12,4},{16,24},{20,28},{24,16},{28,20},{1,9},{5... | collective-permute-start | bytes 245768 | tf_op jit(solution)/shard_map/ppermute | solution.py:627
  107.1 5.4 %collective-permute-start.11 = (f32[320,128]{1,0:T(8,128)S(1)}, f32[320,128]{1,0:T(8,128)S(1)}, u32[]{:S(2)}, u32[]{:S(2)}) collective-permute-start(f32[320,128]{1,0:T(8,128)S(1)} %pad_maximum_fusion.refs_0_), channel_id=1, source_target_pairs={{0,1},{1,0},{2,3},{3,2},{4,5},{5,4},{6,7},{7,6},{8,9},{9,8},{10,11... | collective-permute-start | bytes 491528 | tf_op jit(solution)/shard_map/ppermute | solution.py:627
  108.4 7.1 %collective-permute-start.12 = (f32[320,128]{1,0:T(8,128)S(1)}, f32[320,128]{1,0:T(8,128)S(1)}, u32[]{:S(2)}, u32[]{:S(2)}) collective-permute-start(f32[320,128]{1,0:T(8,128)S(1)} %pad_maximum_fusion.refs_0_), channel_id=1, source_target_pairs={{0,2},{1,3},{2,0},{3,1},{4,6},{5,7},{6,4},{7,5},{8,10},{9,11},{10,... | collective-permute-start | bytes 491528 | tf_op jit(solution)/shard_map/ppermute | solution.py:627
  109.1 6.5 %collective-permute-start.13 = (f32[320,128]{1,0:T(8,128)S(1)}, f32[320,128]{1,0:T(8,128)S(1)}, u32[]{:S(2)}, u32[]{:S(2)}) collective-permute-start(f32[320,128]{1,0:T(8,128)S(1)} %pad_maximum_fusion.refs_0_), channel_id=1, source_target_pairs={{0,3},{1,2},{2,1},{3,0},{4,7},{5,6},{6,5},{7,4},{8,11},{9,10},{10,... | collective-permute-start | bytes 491528 | tf_op jit(solution)/shard_map/ppermute | solution.py:627
  110.6 5.5 %collective-permute-start.14 = (f32[320,128]{1,0:T(8,128)S(1)}, f32[320,128]{1,0:T(8,128)S(1)}, u32[]{:S(2)}, u32[]{:S(2)}) collective-permute-start(f32[320,128]{1,0:T(8,128)S(1)} %pad_maximum_fusion.refs_0_), channel_id=1, source_target_pairs={{0,4},{4,0},{8,12},{12,8},{16,20},{20,16},{24,28},{28,24},{1,5},{5... | collective-permute-start | bytes 491528 | tf_op jit(solution)/shard_map/ppermute | solution.py:627
  112.4 3.7 %collective-permute-start.15 = (f32[320,128]{1,0:T(8,128)S(1)}, f32[320,128]{1,0:T(8,128)S(1)}, u32[]{:S(2)}, u32[]{:S(2)}) collective-permute-start(f32[320,128]{1,0:T(8,128)S(1)} %collective-permute-done.11.refs_1_), channel_id=1, source_target_pairs={{0,4},{4,0},{8,12},{12,8},{16,20},{20,16},{24,28},{28,24},{1,5},{5... | collective-permute-start | bytes 491528 | tf_op jit(solution)/shard_map/ppermute | solution.py:627
  115.5 1.4 %collective-permute-start.16 = (f32[320,128]{1,0:T(8,128)S(1)}, f32[320,128]{1,0:T(8,128)S(1)}, u32[]{:S(2)}, u32[]{:S(2)}) collective-permute-start(f32[320,128]{1,0:T(8,128)S(1)} %collective-permute-done.12.refs_2_), channel_id=1, source_target_pairs={{0,4},{4,0},{8,12},{12,8},{16,20},{20,16},{24,28},{28,24},{1,5},{5... | collective-permute-start | bytes 491528 | tf_op jit(solution)/shard_map/ppermute | solution.py:627
  115.5 1.6 %collective-permute-start.17 = (f32[320,128]{1,0:T(8,128)S(1)}, f32[320,128]{1,0:T(8,128)S(1)}, u32[]{:S(2)}, u32[]{:S(2)}) collective-permute-start(f32[320,128]{1,0:T(8,128)S(1)} %collective-permute-done.13.refs_3_), channel_id=1, source_target_pairs={{0,4},{4,0},{8,12},{12,8},{16,20},{20,16},{24,28},{28,24},{1,5},{5... | collective-permute-start | bytes 491528 | tf_op jit(solution)/shard_map/ppermute | solution.py:627
  (3 other events, 4.7 us)

commit v7 on v6

--- a/solution.py
+++ b/solution.py
@@ -119,7 +119,7 @@
                     low, pltpu.roll(even, rows_all, 1), odd
                 )
 
-    def advance(tile, offset, state, grows):
+    def advance(tile, offset, state, grows, plain):
         previous, before = state
         index = which * rows_all + offset
         step = tile * step_tile + offset
@@ -127,26 +127,33 @@
         for v in range(vregs):
             grow = jnp.take_along_axis(grows[v], index, axis=1)
             value = (grow * cosine) * previous[v] - before[v]
-            restart = switches[v] == step
-            value = jnp.where(restart, seconds[v], value)
+            older = previous[v]
+            if not plain:
+                restart = switches[v] == step
+                value = jnp.where(restart, seconds[v], value)
+                older = jnp.where(restart, 0.0, older)
             table_ref[pl.ds(step * stride + v * SUBS, SUBS), :] = value
             produced.append(value)
-            kept.append(jnp.where(restart, 0.0, previous[v]))
+            kept.append(older)
         return (tuple(produced), tuple(kept))
 
-    def run_tile(tile, state, count, unroll):
+    def run_tile(tile, state, count, unroll, plain=False):
         grows = [grow_ref[tile, pl.ds(v * SUBS, SUBS), :] for v in range(vregs)]
 
         def body(offset, carry):
-            return advance(tile, offset, carry, grows)
+            return advance(tile, offset, carry, grows, plain)
 
         return lax.fori_loop(0, count, body, state, unroll=unroll)
 
     zeros = tuple(jnp.zeros((SUBS, LANES), jnp.float32) for _ in range(vregs))
     state = (zeros, tuple(-value for value in firsts))
     whole_tiles = STEPS // step_tile
+    plain_tiles = (NM // 2 + 1) // step_tile
     state = lax.fori_loop(
-        0, whole_tiles, lambda tile, carry: run_tile(tile, carry, step_tile, 8), state
+        0, plain_tiles, lambda tile, carry: run_tile(tile, carry, step_tile, 16, True), state
+    )
+    state = lax.fori_loop(
+        plain_tiles, whole_tiles, lambda tile, carry: run_tile(tile, carry, step_tile, 16), state
     )
     if STEPS % step_tile:
         run_tile(whole_tiles, state, STEPS % step_tile, STEPS % step_tile % 16)
@@ -174,35 +181,38 @@
         both = dot(jnp.concatenate([left_high, left_low], axis=0), right_high)
         return both[:rows] + both[rows:] + dot(left_high, right_low)
 
-    def group(start):
+    def group(start, kinds):
         values = spectra_ref[:, pl.ds(start, PAIRS), :, :].reshape(slot_count, SUBS, STEPS)
         scale = jnp.concatenate(
             [scale_ref[tile, pl.ds(2 * start, SUBS), :] for tile in range(scale_ref.shape[0])],
             axis=1,
         )
         values = values * scale[:, :STEPS]
+        row_pair = lax.broadcasted_iota(jnp.int32, (1, SUBS, STEPS), 1) >> 1
         step = lax.broadcasted_iota(jnp.int32, (1, SUBS, STEPS), 2)
-        row_pair = lax.broadcasted_iota(jnp.int32, (1, SUBS, STEPS), 1) >> 1
         in_first = step < NM - (first_pair + start + row_pair)
-        lower = jnp.where(in_first, values, 0.0)
-        upper = jnp.where(in_first, 0.0, values)
         first_block = start // per_block
         blocks = PAIRS // per_block
         table = jnp.concatenate(
             [table_ref[pl.ds(first_block + n, STEPS, stride=stride), :] for n in range(blocks)],
             axis=1,
         )
-        begin, end = edges[0], edges[1]
-        base = product(
-            values[:, :, begin:end].reshape(rows_half, end - begin), table[begin:end]
-        )
-        rest = None
-        for begin, end in zip(edges[1:-1], edges[2:]):
-            left = jnp.concatenate([lower[:, :, begin:end], upper[:, :, begin:end]], axis=0)
-            part = product(left.reshape(2 * rows_half, end - begin), table[begin:end])
-            rest = part if rest is None else rest + part
-        both = jnp.concatenate([rest[:rows_half] + base, rest[rows_half:]], axis=0)
-        both = both.reshape(2 * slot_count, SUBS, blocks * LANES)
+        sums = [None, None]
+        for begin, end, kind in zip(edges[:-1], edges[1:], ("low",) + kinds):
+            piece = values[:, :, begin:end]
+            if kind == "both":
+                first = in_first[:, :, begin:end]
+                piece = jnp.concatenate(
+                    [jnp.where(first, piece, 0.0), jnp.where(first, 0.0, piece)], axis=0
+                )
+            part = product(piece.reshape(-1, end - begin), table[begin:end])
+            if kind == "both":
+                halves = ((0, part[:rows_half]), (1, part[rows_half:]))
+            else:
+                halves = ((0 if kind == "low" else 1, part),)
+            for half, value in halves:
+                sums[half] = value if sums[half] is None else sums[half] + value
+        both = jnp.concatenate(sums, axis=0).reshape(2 * slot_count, SUBS, blocks * LANES)
         row_id = lax.broadcasted_iota(jnp.int32, (1, SUBS, LANES), 1) >> 1
         lane_part = lax.broadcasted_iota(jnp.int32, (1, SUBS, LANES), 2)
         lane_part = jnp.where(lane_part < rows_all, 0, 1)
@@ -222,13 +232,25 @@
                     source : source + SUBS
                 ]
 
-    def group_body(index, carry):
-        group(index * PAIRS)
-        return carry
-
-    lax.fori_loop(0, pair_count // PAIRS, group_body, 0, unroll=2 - pair_count // PAIRS % 2)
-    if pair_count % PAIRS:
-        group(pair_count - PAIRS)
+    def twice(kinds):
+        def body(index, carry):
+            group(index * 2 * PAIRS, kinds)
+            group(index * 2 * PAIRS + PAIRS, kinds)
+            return carry
+
+        return body
+
+    turns = pair_count // (2 * PAIRS)
+    border = NM - edges[2]
+    low_turns = jnp.clip((border + 1 - first_pair) // (2 * PAIRS), 0, turns)
+    high_turn = jnp.clip((border - first_pair + 2 * PAIRS - 1) // (2 * PAIRS), low_turns, turns)
+    lax.fori_loop(0, low_turns, twice(("low", "both")), 0)
+    lax.fori_loop(low_turns, high_turn, twice(("both", "both")), 0)
+    lax.fori_loop(high_turn, turns, twice(("both", "high")), 0)
+    start = turns * 2 * PAIRS
+    while start < pair_count:
+        group(min(start, pair_count - PAIRS), ("both", "both"))
+        start = start + PAIRS
 
     for row in range(slot_count):
         flipped = stage_ref[row].T
@@ -316,7 +338,7 @@
         grid=(lon_count,),
         out_shape=jax.ShapeDtypeStruct((lon_count, quarter, 4 * pair_pad), jnp.bfloat16),
         out_specs=pl.BlockSpec((None, quarter, 4 * pair_pad), lambda b: (b, 0, 0)),
-        compiler_params=pltpu.CompilerParams(vmem_limit_bytes=VMEM_LIMIT),
+        compiler_params=pltpu.CompilerParams(vmem_limit_bytes=12 * MIB),
         cost_estimate=pl.CostEstimate(
             flops=24 * lon_count * quarter * pair_pad,
             bytes_accessed=lon_count * quarter * 8 * pair_pad,
@@ -668,10 +690,8 @@
     ).astype(jnp.bfloat16)
     w_out_t = jnp.concatenate([w_out.T, jnp.zeros((LANES - F, width), w_out.dtype)], axis=0)
 
+    core_index, deep_index = lat_index & 1, lat_index >> 1
     depth = lat_count // 2
-    bits = depth.bit_length() - 1
-    core_index = lat_index & 1
-    deep_index = sum(((lat_index >> (bit + 1)) & 1) << (bits - 1 - bit) for bit in range(bits))
     spots = jnp.stack([core_index, lon_index, deep_index])
     grids = grid_field(lon_index.reshape(1), trig, coeffs, pair_count)
     slope, hidden_t, latents_t = forward(
@@ -695,15 +715,11 @@
     )
     arrived = [swap(pieces[part], "lon", part) for part in range(1, lon_count)]
     arrived, latent_grad = lax.optimization_barrier((arrived, latent_grad))
-    pieces = [pieces[0]] + arrived
-    for bit in range(bits):
-        side = (lat_index >> (bit + 1)) & 1
-        pieces = add_pieces(side.reshape(1), pieces, 2)
-        pieces = [pieces[0], swap(pieces[1], "lat", 2 << bit)]
+    pieces = add_pieces(deep_index.reshape(1), [pieces[0]] + arrived, depth)
+    arrived = [swap(pieces[part], "lat", 2 * part) for part in range(1, depth)]
     norm = 1.0 / math.sqrt(rows_all * NLON)
-    total = add_pieces(deep_index.reshape(1), pieces, 1, norm)[0]
-    for bit in reversed(range(bits)):
-        total = jnp.concatenate([total, swap(total, "lat", 2 << bit)])
+    total = add_pieces(deep_index.reshape(1), [pieces[0]] + arrived, 1, norm)[0]
+    total = jnp.concatenate([total] + [swap(total, "lat", 2 * part) for part in range(1, depth)])
     totals = [total] + [swap(total, "lon", part) for part in range(1, lon_count)]
     totals = totals + [swap(piece, "lat", 1) for piece in totals]
     hidden_grad, bias_grad, out_grad = finish(spots, totals, width, depth)

time: 119 us -> 115 us (0.966)
  waiting for transfers between devices: 41.7 us -> 35.6 us
  starting transfers between devices: 22.5 us -> 26.7 us
  Pallas kernels: 42.7 us -> 39.5 us
    ppermute x18 -> x20, waiting for transfers between devices: 24.4 us -> 17.6 us  [swap(): return lax.ppermute(value, axis, [(i, i ^ bits) for i in range(count)])]
    ppermute x18 -> x20, starting transfers between devices: 15.2 us -> 19.5 us  [swap(): return lax.ppermute(value, axis, [(i, i ^ bits) for i in range(count)])]
    pallas_call x1, Pallas kernels: 25.3 us -> 22.3 us  [coefficients(): pl.pallas_call(kernel, out_shape=jax.ShapeDtypeStruct((lat_count, slot_co...]
    unnamed x16 -> x12, local copies, waits for them, and re-layouts: 4.68 us -> 4.45 us
  transfers between devices with their start and end apart: 19 -> 21, of which waited for: 11 -> 11; matrix products, arithmetic and copies ran while one was open for 5% -> 6% of each run, Pallas kernels for 8% -> 7%
where the time goes in v7:
time: 115 us; the launch traced here: 114 us
  Pallas kernels  39.5 us (34%)
  waiting for transfers between devices  35.6 us (31%)
  starting transfers between devices  26.7 us (23%)
  local copies, waits for them, and re-layouts  5.79 us (5%)
  matrix products  5.26 us (5%)
    pallas_call x1, Pallas kernels, coefficients(): pl.pallas_call(kernel, out_shape=jax.ShapeDtypeStruct((lat_count, slot_co...  22.3 us
    ppermute x20, starting transfers between devices, swap(): return lax.ppermute(value, axis, [(i, i ^ bits) for i in range(count)])  19.5 us
    all_to_all x1, waiting for transfers between devices, local(): lax.all_to_all(coeffs, ('lat', 'lon'), split_axis=0, concat_axis=0, tiled...  18 us
    ppermute x20, waiting for transfers between devices, swap(): return lax.ppermute(value, axis, [(i, i ^ bits) for i in range(count)])  17.6 us
    all_to_all x1, starting transfers between devices, local(): lax.all_to_all(coeffs, ('lat', 'lon'), split_axis=0, concat_axis=0, tiled...  7.22 us
    pallas_call x1, Pallas kernels, forward(): pl.pallas_call(forward_kernel, grid=(parts,), out_shape=(jax.ShapeDtypeSt...  5.87 us
    pallas_call x1, Pallas kernels, backward(): pl.pallas_call(functools.partial(backward_kernel, blocks=blocks), grid=(p...  5.29 us
    dot_general x1, matrix products, local(): lax.dot_general(preact_back, w_hidden, (((1,), (1,)), ((), ())), preferre...  5.26 us
  transfers between devices with their start and end apart: 21, of which 11 were waited for; matrix products, arithmetic and copies ran while one was open for 6% of the time, Pallas kernels for 7%

profile of v7, /device:TPU:0, one launch (start us, length us, event | category | flops | bytes accessed | tf_op | source)
XLA Modules:
  0.0 114.3 jit_solution(16514553882508091773)
XLA Ops:
  0.7 22.3 %coefficients.1 = f32[8,64,384]{2,1,0:T(8,128)} custom-call(s32[1]{0:T(128)} %bitcast.7.first_ref, f32[8,90,2,721]{3,2,1,0:T(2,128)} %bitcast.19), custom_call_target="tpu_custom_call" | custom-call | tf_op jit(solution)/shard_map/coefficients/pallas_call | solution.py:274
  22.9 7.2 %all-to-all-start = ((f32[32,16,384]{2,1,0:T(8,128)}), f32[32,16,384]{2,1,0:T(8,128)S(1)}, u32[]{:S(2)}, u32[]{:S(2)}) async-start(f32[32,16,384]{2,1,0:T(8,128)} %bitcast.20), calls=%async_computation | async-start | bytes 1572864 | tf_op jit(solution)/shard_map/all_to_all | solution.py:667
  30.7 2.2 %trig_table.1.trig_ref = bf16[4,360,384]{2,1,0:T(8,128)(2,1)S(1)} custom-call(), custom_call_target="tpu_custom_call" | custom-call | flops 3317760 | bytes 1105920 | tf_op jit(solution)/shard_map/trig_table/pallas_call | solution.py:333
  33.4 18.0 %all-to-all-done.coeff_ref = f32[32,16,384]{2,1,0:T(8,128)S(1)} async-done(((f32[32,16,384]{2,1,0:T(8,128)}), f32[32,16,384]{2,1,0:T(8,128)S(1)}, u32[]{:S(2)}, u32[]{:S(2)}) %all-to-all-start) | async-done | bytes 786464 | tf_op jit(solution)/shard_map/all_to_all | solution.py:667
  51.4 2.0 %grid_field.1 = (f32[360,128]{1,0:T(8,128)S(1)}, f32[360,128]{1,0:T(8,128)}, f32[360,128]{1,0:T(8,128)S(1)}, f32[360,128]{1,0:T(8,128)S(1)}) custom-call(s32[1]{0:T(128)} %bitcast.lon_ref.index_ref, bf16[4,360,384]{2,1,0:T(8,128)(2,1)S(1)} %trig_table.1.trig_ref, f32[32,16,384]{2,1,0:T(8,128)S(1)} %all-to-all-done.coeff_ref), custom_call_target="tpu_custom_call" | custom-call | flops 566231040 | bytes 2678784 | tf_op jit(solution)/shard_map/grid_field/pallas_call | solution.py:394
  54.1 1.5 %collective-permute-start.1 = (f32[360,128]{1,0:T(8,128)S(1)}, f32[360,128]{1,0:T(8,128)S(1)}, u32[]{:S(2)}, u32[]{:S(2)}) collective-permute-start(f32[360,128]{1,0:T(8,128)S(1)} %get-tuple-element.34), channel_id=1, source_target_pairs={{0,2},{1,3},{2,0},{3,1},{4,6},{5,7},{6,4},{7,5},{8,10},{9,11},{10,... | collective-permute-start | bytes 552968 | tf_op jit(solution)/shard_map/ppermute | solution.py:649
  57.8 1.8 %copy-done = bf16[8,360,512]{2,1,0:T(8,128)(2,1)S(1)} copy-done((bf16[8,360,512]{2,1,0:T(8,128)(2,1)S(1)}, bf16[8,360,512]{2,1,0:T(8,128)(2,1)}, u32[]{:S(2)}) %copy-start) | copy-done | bytes 2949144
  60.7 5.9 %forward.1 = (f32[2880,512]{1,0:T(8,128)S(1)}, bf16[4,512,720]{2,1,0:T(8,128)(2,1)S(1)}, bf16[4,512,720]{2,1,0:T(8,128)(2,1)S(1)}) custom-call(bf16[2880,512]{1,0:T(8,128)(2,1)S(1)} %bitcast.17, bf16[512,512]{1,0:T(8,128)(2,1)S(1)} %copy-done.2, f32[1,512]{1,0:T(1,128)S(1)} %bitcast.18, f32[360,128]{1,0:T(8,128)S(1)} %get-tuple-element.29._.refs_0_), custom_call_target="tpu_custom_call" | custom-call | flops 1509949440 | bytes 14745600 | tf_op jit(solution)/shard_map/forward/pallas_call | solution.py:437
  66.6 5.3 %backward.1 = (bf16[2880,512]{1,0:T(8,128)(2,1)S(1)}, f32[1280,128]{1,0:T(8,128)S(1)}, f32[1280,128]{1,0:T(8,128)S(1)}) custom-call(s32[1]{0:T(128)} %bitcast.1.core_ref, f32[4,1,128]{2,1,0:T(1,128)S(1)} %bitcast.16, bf16[4,128,1024]{2,1,0:T(8,128)(2,1)S(1)} %fusion.place_ref, bf16[128,512]{1,0:T(8,128)(2,1)S(1)} %concatenate.6.w_out_ref, ...), custom_call_target="tpu_custom_call" | custom-call | flops 2264924160 | bytes 14745600 | tf_op jit(solution)/shard_map/backward/pallas_call | solution.py:534
  71.9 1.6 %copy-done.1 = bf16[2880,512]{1,0:T(8,128)(2,1)} copy-done((bf16[2880,512]{1,0:T(8,128)(2,1)}, bf16[2880,512]{1,0:T(8,128)(2,1)S(1)}, u32[]{:S(2)}) %copy-start.1) | copy-done | bytes 2949144
  73.5 2.1 %collective-permute-done.3.refs_1_ = f32[1280,128]{1,0:T(8,128)S(1)} collective-permute-done((f32[1280,128]{1,0:T(8,128)S(1)}, f32[1280,128]{1,0:T(8,128)S(1)}, u32[]{:S(2)}, u32[]{:S(2)}) %collective-permute-start.3) | collective-permute-done | bytes 655392 | tf_op jit(solution)/shard_map/ppermute | solution.py:649
  76.4 1.5 %collective-permute-start.5 = (f32[320,128]{1,0:T(8,128)S(1)}, f32[320,128]{1,0:T(8,128)S(1)}, u32[]{:S(2)}, u32[]{:S(2)}) collective-permute-start(f32[320,128]{1,0:T(8,128)S(1)} %get-tuple-element.39), channel_id=1, source_target_pairs={{0,2},{1,3},{2,0},{3,1},{4,6},{5,7},{6,4},{7,5},{8,10},{9,11},{10,... | collective-permute-start | bytes 491528 | tf_op jit(solution)/shard_map/ppermute | solution.py:649
  79.2 5.3 %convolution_convert_fusion = bf16[2880,512]{1,0:T(8,128)(2,1)} fusion(bf16[2880,512]{1,0:T(8,128)(2,1)} %copy-done.1, bf16[512,512]{1,0:T(8,128)(2,1)} %w_ref.1), kind=kOutput, calls=%fused_computation | convolution fusion | flops 1511424000 | bytes 6422528 | tf_op jit(solution)/shard_map/dot_general | solution.py:709
  84.5 1.4 %collective-permute-done.5.refs_2_ = f32[320,128]{1,0:T(8,128)S(1)} collective-permute-done((f32[320,128]{1,0:T(8,128)S(1)}, f32[320,128]{1,0:T(8,128)S(1)}, u32[]{:S(2)}, u32[]{:S(2)}) %collective-permute-start.5) | collective-permute-done | bytes 163872 | tf_op jit(solution)/shard_map/ppermute | solution.py:649
  88.0 2.4 %collective-permute-start.9 = (f32[80,128]{1,0:T(8,128)S(1)}, f32[80,128]{1,0:T(8,128)S(1)}, u32[]{:S(2)}, u32[]{:S(2)}) collective-permute-start(f32[80,128]{1,0:T(8,128)S(1)} %get-tuple-element.50), channel_id=1, source_target_pairs={{0,24},{4,28},{8,16},{12,20},{16,8},{20,12},{24,0},{28,4},{1,25},{... | collective-permute-start | bytes 122888 | tf_op jit(solution)/shard_map/ppermute | solution.py:649
  90.4 1.6 %collective-permute-done.8.refs_2_ = f32[80,128]{1,0:T(8,128)S(1)} collective-permute-done((f32[80,128]{1,0:T(8,128)S(1)}, f32[80,128]{1,0:T(8,128)S(1)}, u32[]{:S(2)}, u32[]{:S(2)}) %collective-permute-start.8) | collective-permute-done | bytes 40992 | tf_op jit(solution)/shard_map/ppermute | solution.py:649
  92.0 1.8 %collective-permute-done.9.refs_3_ = f32[80,128]{1,0:T(8,128)S(1)} collective-permute-done((f32[80,128]{1,0:T(8,128)S(1)}, f32[80,128]{1,0:T(8,128)S(1)}, u32[]{:S(2)}, u32[]{:S(2)}) %collective-permute-start.9) | collective-permute-done | bytes 40992 | tf_op jit(solution)/shard_map/ppermute | solution.py:649
  93.9 3.2 %collective-permute-start.11 = (f32[80,128]{1,0:T(8,128)S(1)}, f32[80,128]{1,0:T(8,128)S(1)}, u32[]{:S(2)}, u32[]{:S(2)}) collective-permute-start(f32[80,128]{1,0:T(8,128)S(1)} %add_pieces.5), channel_id=1, source_target_pairs={{0,16},{4,20},{8,24},{12,28},{16,0},{20,4},{24,8},{28,12},{1,17},{... | collective-permute-start | bytes 122888 | tf_op jit(solution)/shard_map/ppermute | solution.py:649
  99.4 3.5 %collective-permute-done.12 = f32[80,128]{1,0:T(8,128)S(1)} collective-permute-done((f32[80,128]{1,0:T(8,128)S(1)}, f32[80,128]{1,0:T(8,128)S(1)}, u32[]{:S(2)}, u32[]{:S(2)}) %collective-permute-start.12) | collective-permute-done | bytes 40992 | tf_op jit(solution)/shard_map/ppermute | solution.py:649
  105.0 1.5 %collective-permute-start.15 = (f32[320,128]{1,0:T(8,128)S(1)}, f32[320,128]{1,0:T(8,128)S(1)}, u32[]{:S(2)}, u32[]{:S(2)}) collective-permute-start(f32[320,128]{1,0:T(8,128)S(1)} %pad_maximum_fusion.refs_0_), channel_id=1, source_target_pairs={{0,3},{1,2},{2,1},{3,0},{4,7},{5,6},{6,5},{7,4},{8,11},{9,10},{10,... | collective-permute-start | bytes 491528 | tf_op jit(solution)/shard_map/ppermute | solution.py:649
  106.5 1.8 %collective-permute-done.13.refs_1_ = f32[320,128]{1,0:T(8,128)S(1)} collective-permute-done((f32[320,128]{1,0:T(8,128)S(1)}, f32[320,128]{1,0:T(8,128)S(1)}, u32[]{:S(2)}, u32[]{:S(2)}) %collective-permute-start.13) | collective-permute-done | bytes 163872 | tf_op jit(solution)/shard_map/ppermute | solution.py:649
  109.5 1.8 %collective-permute-done.15.refs_3_ = f32[320,128]{1,0:T(8,128)S(1)} collective-permute-done((f32[320,128]{1,0:T(8,128)S(1)}, f32[320,128]{1,0:T(8,128)S(1)}, u32[]{:S(2)}, u32[]{:S(2)}) %collective-permute-start.15) | collective-permute-done | bytes 163872 | tf_op jit(solution)/shard_map/ppermute | solution.py:649
  111.3 1.3 %collective-permute-done.19.refs_7_ = f32[320,128]{1,0:T(8,128)S(1)} collective-permute-done((f32[320,128]{1,0:T(8,128)S(1)}, f32[320,128]{1,0:T(8,128)S(1)}, u32[]{:S(2)}, u32[]{:S(2)}) %collective-permute-start.19) | collective-permute-done | bytes 163872 | tf_op jit(solution)/shard_map/ppermute | solution.py:649
  112.6 1.7 %finish.1 = (f32[512,512]{1,0:T(8,128)}, f32[1,512]{1,0:T(1,128)}, f32[64,512]{1,0:T(8,128)}) custom-call(s32[3]{0:T(128)S(1)} %pad_add_fusion.place_ref, f32[320,128]{1,0:T(8,128)S(1)} %pad_maximum_fusion.refs_0_, f32[320,128]{1,0:T(8,128)S(1)} %collective-permute-done.13.refs_1_, f32[320,128]{1,0:T(8,128)S(1)} %collective-permute-done.14.refs_2_, ...), custom_call_target="tpu_custom_call" | custom-call | tf_op jit(solution)/shard_map/finish/pallas_call | solution.py:631
  (59 shorter events, 14.9 us)
Async XLA Ops:
  0.6 29.5 %copy-start.4 = (s32[64]{0:T(128)S(1)}, s32[64]{0:T(128)}, u32[]{:S(2)}) copy-start(s32[64]{0:T(128)} %param.8) | copy-start | bytes 772
  0.6 32.4 %copy-start.5 = (f32[64]{0:T(128)S(1)}, f32[64]{0:T(128)}, u32[]{:S(2)}) copy-start(f32[64]{0:T(128)} %param.9) | copy-start | bytes 772
  22.9 34.9 %copy-start.3 = (f32[512]{0:T(512)S(1)}, f32[512]{0:T(512)}, u32[]{:S(2)}) copy-start(f32[512]{0:T(512)} %param.12) | copy-start | bytes 6148
  22.9 28.4 %all-to-all-start = ((f32[32,16,384]{2,1,0:T(8,128)}), f32[32,16,384]{2,1,0:T(8,128)S(1)}, u32[]{:S(2)}, u32[]{:S(2)}) async-start(f32[32,16,384]{2,1,0:T(8,128)} %bitcast.20), calls=%async_computation | async-start | bytes 1572864 | tf_op jit(solution)/shard_map/all_to_all | solution.py:667
  53.4 13.2 %collective-permute-start = (f32[360,128]{1,0:T(8,128)}, f32[360,128]{1,0:T(8,128)S(1)}, u32[]{:S(2)}, u32[]{:S(2)}) collective-permute-start(f32[360,128]{1,0:T(8,128)} %get-tuple-element.33), channel_id=1, source_target_pairs={{0,1},{1,0},{2,3},{3,2},{4,5},{5,4},{6,7},{7,6},{8,9},{9,8},{10,11... | collective-permute-start | bytes 552968 | tf_op jit(solution)/shard_map/ppermute | solution.py:649
  54.1 12.5 %collective-permute-start.1 = (f32[360,128]{1,0:T(8,128)S(1)}, f32[360,128]{1,0:T(8,128)S(1)}, u32[]{:S(2)}, u32[]{:S(2)}) collective-permute-start(f32[360,128]{1,0:T(8,128)S(1)} %get-tuple-element.34), channel_id=1, source_target_pairs={{0,2},{1,3},{2,0},{3,1},{4,6},{5,7},{6,4},{7,5},{8,10},{9,11},{10,... | collective-permute-start | bytes 552968 | tf_op jit(solution)/shard_map/ppermute | solution.py:649
  55.7 10.9 %collective-permute-start.2 = (f32[360,128]{1,0:T(8,128)S(1)}, f32[360,128]{1,0:T(8,128)S(1)}, u32[]{:S(2)}, u32[]{:S(2)}) collective-permute-start(f32[360,128]{1,0:T(8,128)S(1)} %get-tuple-element.35), channel_id=1, source_target_pairs={{0,3},{1,2},{2,1},{3,0},{4,7},{5,6},{6,5},{7,4},{8,11},{9,10},{10,... | collective-permute-start | bytes 552968 | tf_op jit(solution)/shard_map/ppermute | solution.py:649
  73.5 2.1 %collective-permute-start.3 = (f32[1280,128]{1,0:T(8,128)S(1)}, f32[1280,128]{1,0:T(8,128)S(1)}, u32[]{:S(2)}, u32[]{:S(2)}) collective-permute-start(f32[1280,128]{1,0:T(8,128)S(1)} %get-tuple-element.37), channel_id=1, source_target_pairs={{0,4},{4,0},{8,12},{12,8},{16,20},{20,16},{24,28},{28,24},{1,5},{5... | collective-permute-start | bytes 1966088 | tf_op jit(solution)/shard_map/ppermute | solution.py:649
  75.7 8.8 %collective-permute-start.4 = (f32[320,128]{1,0:T(8,128)S(1)}, f32[320,128]{1,0:T(8,128)S(1)}, u32[]{:S(2)}, u32[]{:S(2)}) collective-permute-start(f32[320,128]{1,0:T(8,128)S(1)} %get-tuple-element.38), channel_id=1, source_target_pairs={{0,1},{1,0},{2,3},{3,2},{4,5},{5,4},{6,7},{7,6},{8,9},{9,8},{10,11... | collective-permute-start | bytes 491528 | tf_op jit(solution)/shard_map/ppermute | solution.py:649
  76.4 9.5 %collective-permute-start.5 = (f32[320,128]{1,0:T(8,128)S(1)}, f32[320,128]{1,0:T(8,128)S(1)}, u32[]{:S(2)}, u32[]{:S(2)}) collective-permute-start(f32[320,128]{1,0:T(8,128)S(1)} %get-tuple-element.39), channel_id=1, source_target_pairs={{0,2},{1,3},{2,0},{3,1},{4,6},{5,7},{6,4},{7,5},{8,10},{9,11},{10,... | collective-permute-start | bytes 491528 | tf_op jit(solution)/shard_map/ppermute | solution.py:649
  78.0 7.9 %collective-permute-start.6 = (f32[320,128]{1,0:T(8,128)S(1)}, f32[320,128]{1,0:T(8,128)S(1)}, u32[]{:S(2)}, u32[]{:S(2)}) collective-permute-start(f32[320,128]{1,0:T(8,128)S(1)} %get-tuple-element.40), channel_id=1, source_target_pairs={{0,3},{1,2},{2,1},{3,0},{4,7},{5,6},{6,5},{7,4},{8,11},{9,10},{10,... | collective-permute-start | bytes 491528 | tf_op jit(solution)/shard_map/ppermute | solution.py:649
  86.0 4.5 %collective-permute-start.7 = (f32[80,128]{1,0:T(8,128)S(1)}, f32[80,128]{1,0:T(8,128)S(1)}, u32[]{:S(2)}, u32[]{:S(2)}) collective-permute-start(f32[80,128]{1,0:T(8,128)S(1)} %get-tuple-element.48), channel_id=1, source_target_pairs={{0,8},{4,12},{8,0},{12,4},{16,24},{20,28},{24,16},{28,20},{1,9},{5... | collective-permute-start | bytes 122888 | tf_op jit(solution)/shard_map/ppermute | solution.py:649
  87.1 4.9 %collective-permute-start.8 = (f32[80,128]{1,0:T(8,128)S(1)}, f32[80,128]{1,0:T(8,128)S(1)}, u32[]{:S(2)}, u32[]{:S(2)}) collective-permute-start(f32[80,128]{1,0:T(8,128)S(1)} %get-tuple-element.49), channel_id=1, source_target_pairs={{0,16},{4,20},{8,24},{12,28},{16,0},{20,4},{24,8},{28,12},{1,17},{... | collective-permute-start | bytes 122888 | tf_op jit(solution)/shard_map/ppermute | solution.py:649
  88.0 5.8 %collective-permute-start.9 = (f32[80,128]{1,0:T(8,128)S(1)}, f32[80,128]{1,0:T(8,128)S(1)}, u32[]{:S(2)}, u32[]{:S(2)}) collective-permute-start(f32[80,128]{1,0:T(8,128)S(1)} %get-tuple-element.50), channel_id=1, source_target_pairs={{0,24},{4,28},{8,16},{12,20},{16,8},{20,12},{24,0},{28,4},{1,25},{... | collective-permute-start | bytes 122888 | tf_op jit(solution)/shard_map/ppermute | solution.py:649
  93.9 4.5 %collective-permute-start.10 = (f32[80,128]{1,0:T(8,128)S(1)}, f32[80,128]{1,0:T(8,128)S(1)}, u32[]{:S(2)}, u32[]{:S(2)}) collective-permute-start(f32[80,128]{1,0:T(8,128)S(1)} %add_pieces.5), channel_id=1, source_target_pairs={{0,8},{4,12},{8,0},{12,4},{16,24},{20,28},{24,16},{28,20},{1,9},{5... | collective-permute-start | bytes 122888 | tf_op jit(solution)/shard_map/ppermute | solution.py:649
  93.9 5.5 %collective-permute-start.11 = (f32[80,128]{1,0:T(8,128)S(1)}, f32[80,128]{1,0:T(8,128)S(1)}, u32[]{:S(2)}, u32[]{:S(2)}) collective-permute-start(f32[80,128]{1,0:T(8,128)S(1)} %add_pieces.5), channel_id=1, source_target_pairs={{0,16},{4,20},{8,24},{12,28},{16,0},{20,4},{24,8},{28,12},{1,17},{... | collective-permute-start | bytes 122888 | tf_op jit(solution)/shard_map/ppermute | solution.py:649
  97.1 5.8 %collective-permute-start.12 = (f32[80,128]{1,0:T(8,128)S(1)}, f32[80,128]{1,0:T(8,128)S(1)}, u32[]{:S(2)}, u32[]{:S(2)}) collective-permute-start(f32[80,128]{1,0:T(8,128)S(1)} %add_pieces.5), channel_id=1, source_target_pairs={{0,24},{4,28},{8,16},{12,20},{16,8},{20,12},{24,0},{28,4},{1,25},{... | collective-permute-start | bytes 122888 | tf_op jit(solution)/shard_map/ppermute | solution.py:649
  102.9 5.4 %collective-permute-start.13 = (f32[320,128]{1,0:T(8,128)S(1)}, f32[320,128]{1,0:T(8,128)S(1)}, u32[]{:S(2)}, u32[]{:S(2)}) collective-permute-start(f32[320,128]{1,0:T(8,128)S(1)} %pad_maximum_fusion.refs_0_), channel_id=1, source_target_pairs={{0,1},{1,0},{2,3},{3,2},{4,5},{5,4},{6,7},{7,6},{8,9},{9,8},{10,11... | collective-permute-start | bytes 491528 | tf_op jit(solution)/shard_map/ppermute | solution.py:649
  104.1 5.3 %collective-permute-start.14 = (f32[320,128]{1,0:T(8,128)S(1)}, f32[320,128]{1,0:T(8,128)S(1)}, u32[]{:S(2)}, u32[]{:S(2)}) collective-permute-start(f32[320,128]{1,0:T(8,128)S(1)} %pad_maximum_fusion.refs_0_), channel_id=1, source_target_pairs={{0,2},{1,3},{2,0},{3,1},{4,6},{5,7},{6,4},{7,5},{8,10},{9,11},{10,... | collective-permute-start | bytes 491528 | tf_op jit(solution)/shard_map/ppermute | solution.py:649
  105.0 6.2 %collective-permute-start.15 = (f32[320,128]{1,0:T(8,128)S(1)}, f32[320,128]{1,0:T(8,128)S(1)}, u32[]{:S(2)}, u32[]{:S(2)}) collective-permute-start(f32[320,128]{1,0:T(8,128)S(1)} %pad_maximum_fusion.refs_0_), channel_id=1, source_target_pairs={{0,3},{1,2},{2,1},{3,0},{4,7},{5,6},{6,5},{7,4},{8,11},{9,10},{10,... | collective-permute-start | bytes 491528 | tf_op jit(solution)/shard_map/ppermute | solution.py:649
  106.5 4.8 %collective-permute-start.16 = (f32[320,128]{1,0:T(8,128)S(1)}, f32[320,128]{1,0:T(8,128)S(1)}, u32[]{:S(2)}, u32[]{:S(2)}) collective-permute-start(f32[320,128]{1,0:T(8,128)S(1)} %pad_maximum_fusion.refs_0_), channel_id=1, source_target_pairs={{0,4},{4,0},{8,12},{12,8},{16,20},{20,16},{24,28},{28,24},{1,5},{5... | collective-permute-start | bytes 491528 | tf_op jit(solution)/shard_map/ppermute | solution.py:649
  108.3 3.0 %collective-permute-start.17 = (f32[320,128]{1,0:T(8,128)S(1)}, f32[320,128]{1,0:T(8,128)S(1)}, u32[]{:S(2)}, u32[]{:S(2)}) collective-permute-start(f32[320,128]{1,0:T(8,128)S(1)} %collective-permute-done.13.refs_1_), channel_id=1, source_target_pairs={{0,4},{4,0},{8,12},{12,8},{16,20},{20,16},{24,28},{28,24},{1,5},{5... | collective-permute-start | bytes 491528 | tf_op jit(solution)/shard_map/ppermute | solution.py:649
  109.5 1.9 %collective-permute-start.18 = (f32[320,128]{1,0:T(8,128)S(1)}, f32[320,128]{1,0:T(8,128)S(1)}, u32[]{:S(2)}, u32[]{:S(2)}) collective-permute-start(f32[320,128]{1,0:T(8,128)S(1)} %collective-permute-done.14.refs_2_), channel_id=1, source_target_pairs={{0,4},{4,0},{8,12},{12,8},{16,20},{20,16},{24,28},{28,24},{1,5},{5... | collective-permute-start | bytes 491528 | tf_op jit(solution)/shard_map/ppermute | solution.py:649
  111.2 1.4 %collective-permute-start.19 = (f32[320,128]{1,0:T(8,128)S(1)}, f32[320,128]{1,0:T(8,128)S(1)}, u32[]{:S(2)}, u32[]{:S(2)}) collective-permute-start(f32[320,128]{1,0:T(8,128)S(1)} %collective-permute-done.15.refs_3_), channel_id=1, source_target_pairs={{0,4},{4,0},{8,12},{12,8},{16,20},{20,16},{24,28},{28,24},{1,5},{5... | collective-permute-start | bytes 491528 | tf_op jit(solution)/shard_map/ppermute | solution.py:649
  (3 other events, 4.5 us)

commit v8 on v7

--- a/solution.py
+++ b/solution.py
@@ -453,7 +453,7 @@
             pl.BlockSpec((None, width, cols), lambda i: (i, 0, 0)),
             pl.BlockSpec((None, width, cols), lambda i: (i, 0, 0)),
         ),
-        compiler_params=pltpu.CompilerParams(vmem_limit_bytes=32 * MIB),
+        compiler_params=pltpu.CompilerParams(vmem_limit_bytes=46 * MIB),
         cost_estimate=pl.CostEstimate(
             flops=2 * cells * width * width,
             bytes_accessed=cells * width * 10,

time: 115 us -> 121 us (1.052)
  local copies, waits for them, and re-layouts: 5.79 us -> 10.4 us
  Pallas kernels: 39.5 us -> 40.8 us
    unnamed x12 -> x16, local copies, waits for them, and re-layouts: 4.45 us -> 9.03 us
    pallas_call x1, Pallas kernels: 5.87 us -> 7.25 us  [forward(): pl.pallas_call(forward_kernel, grid=(parts,), out_shape=(jax.ShapeDtypeSt...]
  transfers between devices with their start and end apart: 21 -> 21, of which waited for: 11 -> 11; matrix products, arithmetic and copies ran while one was open for 6% -> 6% of each run, Pallas kernels for 7% -> 8%
where the time goes in v8:
time: 121 us; the launch traced here: 120 us
  Pallas kernels  40.8 us (34%)
  waiting for transfers between devices  35.6 us (29%)
  starting transfers between devices  26.7 us (22%)
  local copies, waits for them, and re-layouts  10.4 us (9%)
  matrix products  5.26 us (4%)
    pallas_call x1, Pallas kernels, coefficients(): pl.pallas_call(kernel, out_shape=jax.ShapeDtypeStruct((lat_count, slot_co...  22.3 us
    ppermute x20, starting transfers between devices, swap(): return lax.ppermute(value, axis, [(i, i ^ bits) for i in range(count)])  19.5 us
    all_to_all x1, waiting for transfers between devices, local(): lax.all_to_all(coeffs, ('lat', 'lon'), split_axis=0, concat_axis=0, tiled...  18 us
    ppermute x20, waiting for transfers between devices, swap(): return lax.ppermute(value, axis, [(i, i ^ bits) for i in range(count)])  17.6 us
    unnamed x16, local copies, waits for them, and re-layouts  9.03 us
    pallas_call x1, Pallas kernels, forward(): pl.pallas_call(forward_kernel, grid=(parts,), out_shape=(jax.ShapeDtypeSt...  7.25 us
    all_to_all x1, starting transfers between devices, local(): lax.all_to_all(coeffs, ('lat', 'lon'), split_axis=0, concat_axis=0, tiled...  7.22 us
    pallas_call x1, Pallas kernels, backward(): pl.pallas_call(functools.partial(backward_kernel, blocks=blocks), grid=(p...  5.27 us
  transfers between devices with their start and end apart: 21, of which 11 were waited for; matrix products, arithmetic and copies ran while one was open for 6% of the time, Pallas kernels for 8%

profile of v8, /device:TPU:0, one launch (start us, length us, event | category | flops | bytes accessed | tf_op | source)
XLA Modules:
  0.0 120.3 jit_solution(4878004459189884696)
XLA Ops:
  0.7 22.3 %coefficients.1 = f32[8,64,384]{2,1,0:T(8,128)} custom-call(s32[1]{0:T(128)} %bitcast.7.first_ref, f32[8,90,2,721]{3,2,1,0:T(2,128)} %bitcast.19), custom_call_target="tpu_custom_call" | custom-call | tf_op jit(solution)/shard_map/coefficients/pallas_call | solution.py:274
  22.9 7.2 %all-to-all-start = ((f32[32,16,384]{2,1,0:T(8,128)}), f32[32,16,384]{2,1,0:T(8,128)S(1)}, u32[]{:S(2)}, u32[]{:S(2)}) async-start(f32[32,16,384]{2,1,0:T(8,128)} %bitcast.20), calls=%async_computation | async-start | bytes 1572864 | tf_op jit(solution)/shard_map/all_to_all | solution.py:667
  30.7 2.2 %trig_table.1.trig_ref = bf16[4,360,384]{2,1,0:T(8,128)(2,1)S(1)} custom-call(), custom_call_target="tpu_custom_call" | custom-call | flops 3317760 | bytes 1105920 | tf_op jit(solution)/shard_map/trig_table/pallas_call | solution.py:333
  33.4 18.0 %all-to-all-done.coeff_ref = f32[32,16,384]{2,1,0:T(8,128)S(1)} async-done(((f32[32,16,384]{2,1,0:T(8,128)}), f32[32,16,384]{2,1,0:T(8,128)S(1)}, u32[]{:S(2)}, u32[]{:S(2)}) %all-to-all-start) | async-done | bytes 786464 | tf_op jit(solution)/shard_map/all_to_all | solution.py:667
  51.4 2.0 %grid_field.1 = (f32[360,128]{1,0:T(8,128)S(1)}, f32[360,128]{1,0:T(8,128)}, f32[360,128]{1,0:T(8,128)S(1)}, f32[360,128]{1,0:T(8,128)S(1)}) custom-call(s32[1]{0:T(128)} %bitcast.lon_ref.index_ref, bf16[4,360,384]{2,1,0:T(8,128)(2,1)S(1)} %trig_table.1.trig_ref, f32[32,16,384]{2,1,0:T(8,128)S(1)} %all-to-all-done.coeff_ref), custom_call_target="tpu_custom_call" | custom-call | flops 566231040 | bytes 2678784 | tf_op jit(solution)/shard_map/grid_field/pallas_call | solution.py:394
  54.1 1.5 %collective-permute-start.1 = (f32[360,128]{1,0:T(8,128)S(1)}, f32[360,128]{1,0:T(8,128)S(1)}, u32[]{:S(2)}, u32[]{:S(2)}) collective-permute-start(f32[360,128]{1,0:T(8,128)S(1)} %get-tuple-element.34), channel_id=1, source_target_pairs={{0,2},{1,3},{2,0},{3,1},{4,6},{5,7},{6,4},{7,5},{8,10},{9,11},{10,... | collective-permute-start | bytes 552968 | tf_op jit(solution)/shard_map/ppermute | solution.py:649
  57.8 1.8 %copy-done.2 = bf16[8,360,512]{2,1,0:T(8,128)(2,1)S(1)} copy-done((bf16[8,360,512]{2,1,0:T(8,128)(2,1)S(1)}, bf16[8,360,512]{2,1,0:T(8,128)(2,1)}, u32[]{:S(2)}) %copy-start.2) | copy-done | bytes 2949144
  60.7 7.3 %forward.1 = (f32[2880,512]{1,0:T(8,128)}, bf16[4,512,720]{2,1,0:T(8,128)(2,1)S(1)}, bf16[4,512,720]{2,1,0:T(8,128)(2,1)}) custom-call(bf16[2880,512]{1,0:T(8,128)(2,1)S(1)} %bitcast.17, bf16[512,512]{1,0:T(8,128)(2,1)S(1)} %copy-done.4, f32[1,512]{1,0:T(1,128)S(1)} %bitcast.18, f32[360,128]{1,0:T(8,128)S(1)} %get-tuple-element.29._.refs_0_), custom_call_target="tpu_custom_call" | custom-call | flops 1509949440 | bytes 14745600 | tf_op jit(solution)/shard_map/forward/pallas_call | solution.py:437
  68.0 2.7 %copy-done = f32[2880,512]{1,0:T(8,128)S(1)} copy-done((f32[2880,512]{1,0:T(8,128)S(1)}, f32[2880,512]{1,0:T(8,128)}, u32[]{:S(2)}) %copy-start) | copy-done | bytes 5898264
  70.6 1.9 %copy-done.1 = bf16[4,512,720]{2,1,0:T(8,128)(2,1)S(1)} copy-done((bf16[4,512,720]{2,1,0:T(8,128)(2,1)S(1)}, bf16[4,512,720]{2,1,0:T(8,128)(2,1)}, u32[]{:S(2)}) %copy-start.1) | copy-done | bytes 2949144
  72.5 5.3 %backward.1 = (bf16[2880,512]{1,0:T(8,128)(2,1)S(1)}, f32[1280,128]{1,0:T(8,128)S(1)}, f32[1280,128]{1,0:T(8,128)S(1)}) custom-call(s32[1]{0:T(128)} %bitcast.1.core_ref, f32[4,1,128]{2,1,0:T(1,128)S(1)} %bitcast.16, bf16[4,128,1024]{2,1,0:T(8,128)(2,1)S(1)} %fusion.place_ref, bf16[128,512]{1,0:T(8,128)(2,1)S(1)} %concatenate.6.w_out_ref, ...), custom_call_target="tpu_custom_call" | custom-call | flops 2264924160 | bytes 14745600 | tf_op jit(solution)/shard_map/backward/pallas_call | solution.py:534
  77.8 1.6 %copy-done.3 = bf16[2880,512]{1,0:T(8,128)(2,1)} copy-done((bf16[2880,512]{1,0:T(8,128)(2,1)}, bf16[2880,512]{1,0:T(8,128)(2,1)S(1)}, u32[]{:S(2)}) %copy-start.3) | copy-done | bytes 2949144
  79.4 2.1 %collective-permute-done.3.refs_1_ = f32[1280,128]{1,0:T(8,128)S(1)} collective-permute-done((f32[1280,128]{1,0:T(8,128)S(1)}, f32[1280,128]{1,0:T(8,128)S(1)}, u32[]{:S(2)}, u32[]{:S(2)}) %collective-permute-start.3) | collective-permute-done | bytes 655392 | tf_op jit(solution)/shard_map/ppermute | solution.py:649
  82.4 1.5 %collective-permute-start.5 = (f32[320,128]{1,0:T(8,128)S(1)}, f32[320,128]{1,0:T(8,128)S(1)}, u32[]{:S(2)}, u32[]{:S(2)}) collective-permute-start(f32[320,128]{1,0:T(8,128)S(1)} %get-tuple-element.39), channel_id=1, source_target_pairs={{0,2},{1,3},{2,0},{3,1},{4,6},{5,7},{6,4},{7,5},{8,10},{9,11},{10,... | collective-permute-start | bytes 491528 | tf_op jit(solution)/shard_map/ppermute | solution.py:649
  85.1 5.3 %convolution_convert_fusion = bf16[2880,512]{1,0:T(8,128)(2,1)} fusion(bf16[2880,512]{1,0:T(8,128)(2,1)} %copy-done.3, bf16[512,512]{1,0:T(8,128)(2,1)} %w_ref.1), kind=kOutput, calls=%fused_computation | convolution fusion | flops 1511424000 | bytes 6422528 | tf_op jit(solution)/shard_map/dot_general | solution.py:709
  94.0 2.4 %collective-permute-start.9 = (f32[80,128]{1,0:T(8,128)S(1)}, f32[80,128]{1,0:T(8,128)S(1)}, u32[]{:S(2)}, u32[]{:S(2)}) collective-permute-start(f32[80,128]{1,0:T(8,128)S(1)} %get-tuple-element.50), channel_id=1, source_target_pairs={{0,24},{4,28},{8,16},{12,20},{16,8},{20,12},{24,0},{28,4},{1,25},{... | collective-permute-start | bytes 122888 | tf_op jit(solution)/shard_map/ppermute | solution.py:649
  96.3 1.6 %collective-permute-done.8.refs_2_ = f32[80,128]{1,0:T(8,128)S(1)} collective-permute-done((f32[80,128]{1,0:T(8,128)S(1)}, f32[80,128]{1,0:T(8,128)S(1)}, u32[]{:S(2)}, u32[]{:S(2)}) %collective-permute-start.8) | collective-permute-done | bytes 40992 | tf_op jit(solution)/shard_map/ppermute | solution.py:649
  97.9 1.8 %collective-permute-done.9.refs_3_ = f32[80,128]{1,0:T(8,128)S(1)} collective-permute-done((f32[80,128]{1,0:T(8,128)S(1)}, f32[80,128]{1,0:T(8,128)S(1)}, u32[]{:S(2)}, u32[]{:S(2)}) %collective-permute-start.9) | collective-permute-done | bytes 40992 | tf_op jit(solution)/shard_map/ppermute | solution.py:649
  99.8 3.2 %collective-permute-start.11 = (f32[80,128]{1,0:T(8,128)S(1)}, f32[80,128]{1,0:T(8,128)S(1)}, u32[]{:S(2)}, u32[]{:S(2)}) collective-permute-start(f32[80,128]{1,0:T(8,128)S(1)} %add_pieces.5), channel_id=1, source_target_pairs={{0,16},{4,20},{8,24},{12,28},{16,0},{20,4},{24,8},{28,12},{1,17},{... | collective-permute-start | bytes 122888 | tf_op jit(solution)/shard_map/ppermute | solution.py:649
  105.3 3.5 %collective-permute-done.12 = f32[80,128]{1,0:T(8,128)S(1)} collective-permute-done((f32[80,128]{1,0:T(8,128)S(1)}, f32[80,128]{1,0:T(8,128)S(1)}, u32[]{:S(2)}, u32[]{:S(2)}) %collective-permute-start.12) | collective-permute-done | bytes 40992 | tf_op jit(solution)/shard_map/ppermute | solution.py:649
  111.0 1.4 %collective-permute-start.15 = (f32[320,128]{1,0:T(8,128)S(1)}, f32[320,128]{1,0:T(8,128)S(1)}, u32[]{:S(2)}, u32[]{:S(2)}) collective-permute-start(f32[320,128]{1,0:T(8,128)S(1)} %pad_maximum_fusion.refs_0_), channel_id=1, source_target_pairs={{0,3},{1,2},{2,1},{3,0},{4,7},{5,6},{6,5},{7,4},{8,11},{9,10},{10,... | collective-permute-start | bytes 491528 | tf_op jit(solution)/shard_map/ppermute | solution.py:649
  112.4 1.8 %collective-permute-done.13.refs_1_ = f32[320,128]{1,0:T(8,128)S(1)} collective-permute-done((f32[320,128]{1,0:T(8,128)S(1)}, f32[320,128]{1,0:T(8,128)S(1)}, u32[]{:S(2)}, u32[]{:S(2)}) %collective-permute-start.13) | collective-permute-done | bytes 163872 | tf_op jit(solution)/shard_map/ppermute | solution.py:649
  115.4 1.8 %collective-permute-done.15.refs_3_ = f32[320,128]{1,0:T(8,128)S(1)} collective-permute-done((f32[320,128]{1,0:T(8,128)S(1)}, f32[320,128]{1,0:T(8,128)S(1)}, u32[]{:S(2)}, u32[]{:S(2)}) %collective-permute-start.15) | collective-permute-done | bytes 163872 | tf_op jit(solution)/shard_map/ppermute | solution.py:649
  118.6 1.7 %finish.1 = (f32[512,512]{1,0:T(8,128)}, f32[1,512]{1,0:T(1,128)}, f32[64,512]{1,0:T(8,128)}) custom-call(s32[3]{0:T(128)S(1)} %pad_add_fusion.place_ref, f32[320,128]{1,0:T(8,128)S(1)} %pad_maximum_fusion.refs_0_, f32[320,128]{1,0:T(8,128)S(1)} %collective-permute-done.13.refs_1_, f32[320,128]{1,0:T(8,128)S(1)} %collective-permute-done.14.refs_2_, ...), custom_call_target="tpu_custom_call" | custom-call | tf_op jit(solution)/shard_map/finish/pallas_call | solution.py:631
  (63 shorter events, 17.7 us)
Async XLA Ops:
  0.6 29.5 %copy-start.6 = (s32[64]{0:T(128)S(1)}, s32[64]{0:T(128)}, u32[]{:S(2)}) copy-start(s32[64]{0:T(128)} %param.8) | copy-start | bytes 772
  0.6 32.4 %copy-start.7 = (f32[64]{0:T(128)S(1)}, f32[64]{0:T(128)}, u32[]{:S(2)}) copy-start(f32[64]{0:T(128)} %param.9) | copy-start | bytes 772
  22.9 34.9 %copy-start.5 = (f32[512]{0:T(512)S(1)}, f32[512]{0:T(512)}, u32[]{:S(2)}) copy-start(f32[512]{0:T(512)} %param.12) | copy-start | bytes 6148
  22.9 28.4 %all-to-all-start = ((f32[32,16,384]{2,1,0:T(8,128)}), f32[32,16,384]{2,1,0:T(8,128)S(1)}, u32[]{:S(2)}, u32[]{:S(2)}) async-start(f32[32,16,384]{2,1,0:T(8,128)} %bitcast.20), calls=%async_computation | async-start | bytes 1572864 | tf_op jit(solution)/shard_map/all_to_all | solution.py:667
  53.4 14.5 %collective-permute-start = (f32[360,128]{1,0:T(8,128)}, f32[360,128]{1,0:T(8,128)S(1)}, u32[]{:S(2)}, u32[]{:S(2)}) collective-permute-start(f32[360,128]{1,0:T(8,128)} %get-tuple-element.33), channel_id=1, source_target_pairs={{0,1},{1,0},{2,3},{3,2},{4,5},{5,4},{6,7},{7,6},{8,9},{9,8},{10,11... | collective-permute-start | bytes 552968 | tf_op jit(solution)/shard_map/ppermute | solution.py:649
  54.1 13.8 %collective-permute-start.1 = (f32[360,128]{1,0:T(8,128)S(1)}, f32[360,128]{1,0:T(8,128)S(1)}, u32[]{:S(2)}, u32[]{:S(2)}) collective-permute-start(f32[360,128]{1,0:T(8,128)S(1)} %get-tuple-element.34), channel_id=1, source_target_pairs={{0,2},{1,3},{2,0},{3,1},{4,6},{5,7},{6,4},{7,5},{8,10},{9,11},{10,... | collective-permute-start | bytes 552968 | tf_op jit(solution)/shard_map/ppermute | solution.py:649
  55.7 12.3 %collective-permute-start.2 = (f32[360,128]{1,0:T(8,128)S(1)}, f32[360,128]{1,0:T(8,128)S(1)}, u32[]{:S(2)}, u32[]{:S(2)}) collective-permute-start(f32[360,128]{1,0:T(8,128)S(1)} %get-tuple-element.35), channel_id=1, source_target_pairs={{0,3},{1,2},{2,1},{3,0},{4,7},{5,6},{6,5},{7,4},{8,11},{9,10},{10,... | collective-permute-start | bytes 552968 | tf_op jit(solution)/shard_map/ppermute | solution.py:649
  79.4 2.1 %collective-permute-start.3 = (f32[1280,128]{1,0:T(8,128)S(1)}, f32[1280,128]{1,0:T(8,128)S(1)}, u32[]{:S(2)}, u32[]{:S(2)}) collective-permute-start(f32[1280,128]{1,0:T(8,128)S(1)} %get-tuple-element.37), channel_id=1, source_target_pairs={{0,4},{4,0},{8,12},{12,8},{16,20},{20,16},{24,28},{28,24},{1,5},{5... | collective-permute-start | bytes 1966088 | tf_op jit(solution)/shard_map/ppermute | solution.py:649
  81.6 8.8 %collective-permute-start.4 = (f32[320,128]{1,0:T(8,128)S(1)}, f32[320,128]{1,0:T(8,128)S(1)}, u32[]{:S(2)}, u32[]{:S(2)}) collective-permute-start(f32[320,128]{1,0:T(8,128)S(1)} %get-tuple-element.38), channel_id=1, source_target_pairs={{0,1},{1,0},{2,3},{3,2},{4,5},{5,4},{6,7},{7,6},{8,9},{9,8},{10,11... | collective-permute-start | bytes 491528 | tf_op jit(solution)/shard_map/ppermute | solution.py:649
  82.4 9.5 %collective-permute-start.5 = (f32[320,128]{1,0:T(8,128)S(1)}, f32[320,128]{1,0:T(8,128)S(1)}, u32[]{:S(2)}, u32[]{:S(2)}) collective-permute-start(f32[320,128]{1,0:T(8,128)S(1)} %get-tuple-element.39), channel_id=1, source_target_pairs={{0,2},{1,3},{2,0},{3,1},{4,6},{5,7},{6,4},{7,5},{8,10},{9,11},{10,... | collective-permute-start | bytes 491528 | tf_op jit(solution)/shard_map/ppermute | solution.py:649
  83.9 7.9 %collective-permute-start.6 = (f32[320,128]{1,0:T(8,128)S(1)}, f32[320,128]{1,0:T(8,128)S(1)}, u32[]{:S(2)}, u32[]{:S(2)}) collective-permute-start(f32[320,128]{1,0:T(8,128)S(1)} %get-tuple-element.40), channel_id=1, source_target_pairs={{0,3},{1,2},{2,1},{3,0},{4,7},{5,6},{6,5},{7,4},{8,11},{9,10},{10,... | collective-permute-start | bytes 491528 | tf_op jit(solution)/shard_map/ppermute | solution.py:649
  91.9 4.5 %collective-permute-start.7 = (f32[80,128]{1,0:T(8,128)S(1)}, f32[80,128]{1,0:T(8,128)S(1)}, u32[]{:S(2)}, u32[]{:S(2)}) collective-permute-start(f32[80,128]{1,0:T(8,128)S(1)} %get-tuple-element.48), channel_id=1, source_target_pairs={{0,8},{4,12},{8,0},{12,4},{16,24},{20,28},{24,16},{28,20},{1,9},{5... | collective-permute-start | bytes 122888 | tf_op jit(solution)/shard_map/ppermute | solution.py:649
  93.0 4.9 %collective-permute-start.8 = (f32[80,128]{1,0:T(8,128)S(1)}, f32[80,128]{1,0:T(8,128)S(1)}, u32[]{:S(2)}, u32[]{:S(2)}) collective-permute-start(f32[80,128]{1,0:T(8,128)S(1)} %get-tuple-element.49), channel_id=1, source_target_pairs={{0,16},{4,20},{8,24},{12,28},{16,0},{20,4},{24,8},{28,12},{1,17},{... | collective-permute-start | bytes 122888 | tf_op jit(solution)/shard_map/ppermute | solution.py:649
  94.0 5.8 %collective-permute-start.9 = (f32[80,128]{1,0:T(8,128)S(1)}, f32[80,128]{1,0:T(8,128)S(1)}, u32[]{:S(2)}, u32[]{:S(2)}) collective-permute-start(f32[80,128]{1,0:T(8,128)S(1)} %get-tuple-element.50), channel_id=1, source_target_pairs={{0,24},{4,28},{8,16},{12,20},{16,8},{20,12},{24,0},{28,4},{1,25},{... | collective-permute-start | bytes 122888 | tf_op jit(solution)/shard_map/ppermute | solution.py:649
  99.8 4.5 %collective-permute-start.10 = (f32[80,128]{1,0:T(8,128)S(1)}, f32[80,128]{1,0:T(8,128)S(1)}, u32[]{:S(2)}, u32[]{:S(2)}) collective-permute-start(f32[80,128]{1,0:T(8,128)S(1)} %add_pieces.5), channel_id=1, source_target_pairs={{0,8},{4,12},{8,0},{12,4},{16,24},{20,28},{24,16},{28,20},{1,9},{5... | collective-permute-start | bytes 122888 | tf_op jit(solution)/shard_map/ppermute | solution.py:649
  99.8 5.4 %collective-permute-start.11 = (f32[80,128]{1,0:T(8,128)S(1)}, f32[80,128]{1,0:T(8,128)S(1)}, u32[]{:S(2)}, u32[]{:S(2)}) collective-permute-start(f32[80,128]{1,0:T(8,128)S(1)} %add_pieces.5), channel_id=1, source_target_pairs={{0,16},{4,20},{8,24},{12,28},{16,0},{20,4},{24,8},{28,12},{1,17},{... | collective-permute-start | bytes 122888 | tf_op jit(solution)/shard_map/ppermute | solution.py:649
  103.0 5.8 %collective-permute-start.12 = (f32[80,128]{1,0:T(8,128)S(1)}, f32[80,128]{1,0:T(8,128)S(1)}, u32[]{:S(2)}, u32[]{:S(2)}) collective-permute-start(f32[80,128]{1,0:T(8,128)S(1)} %add_pieces.5), channel_id=1, source_target_pairs={{0,24},{4,28},{8,16},{12,20},{16,8},{20,12},{24,0},{28,4},{1,25},{... | collective-permute-start | bytes 122888 | tf_op jit(solution)/shard_map/ppermute | solution.py:649
  108.8 5.4 %collective-permute-start.13 = (f32[320,128]{1,0:T(8,128)S(1)}, f32[320,128]{1,0:T(8,128)S(1)}, u32[]{:S(2)}, u32[]{:S(2)}) collective-permute-start(f32[320,128]{1,0:T(8,128)S(1)} %pad_maximum_fusion.refs_0_), channel_id=1, source_target_pairs={{0,1},{1,0},{2,3},{3,2},{4,5},{5,4},{6,7},{7,6},{8,9},{9,8},{10,11... | collective-permute-start | bytes 491528 | tf_op jit(solution)/shard_map/ppermute | solution.py:649
  110.1 5.3 %collective-permute-start.14 = (f32[320,128]{1,0:T(8,128)S(1)}, f32[320,128]{1,0:T(8,128)S(1)}, u32[]{:S(2)}, u32[]{:S(2)}) collective-permute-start(f32[320,128]{1,0:T(8,128)S(1)} %pad_maximum_fusion.refs_0_), channel_id=1, source_target_pairs={{0,2},{1,3},{2,0},{3,1},{4,6},{5,7},{6,4},{7,5},{8,10},{9,11},{10,... | collective-permute-start | bytes 491528 | tf_op jit(solution)/shard_map/ppermute | solution.py:649
  111.0 6.2 %collective-permute-start.15 = (f32[320,128]{1,0:T(8,128)S(1)}, f32[320,128]{1,0:T(8,128)S(1)}, u32[]{:S(2)}, u32[]{:S(2)}) collective-permute-start(f32[320,128]{1,0:T(8,128)S(1)} %pad_maximum_fusion.refs_0_), channel_id=1, source_target_pairs={{0,3},{1,2},{2,1},{3,0},{4,7},{5,6},{6,5},{7,4},{8,11},{9,10},{10,... | collective-permute-start | bytes 491528 | tf_op jit(solution)/shard_map/ppermute | solution.py:649
  112.4 4.9 %collective-permute-start.16 = (f32[320,128]{1,0:T(8,128)S(1)}, f32[320,128]{1,0:T(8,128)S(1)}, u32[]{:S(2)}, u32[]{:S(2)}) collective-permute-start(f32[320,128]{1,0:T(8,128)S(1)} %pad_maximum_fusion.refs_0_), channel_id=1, source_target_pairs={{0,4},{4,0},{8,12},{12,8},{16,20},{20,16},{24,28},{28,24},{1,5},{5... | collective-permute-start | bytes 491528 | tf_op jit(solution)/shard_map/ppermute | solution.py:649
  114.2 3.1 %collective-permute-start.17 = (f32[320,128]{1,0:T(8,128)S(1)}, f32[320,128]{1,0:T(8,128)S(1)}, u32[]{:S(2)}, u32[]{:S(2)}) collective-permute-start(f32[320,128]{1,0:T(8,128)S(1)} %collective-permute-done.13.refs_1_), channel_id=1, source_target_pairs={{0,4},{4,0},{8,12},{12,8},{16,20},{20,16},{24,28},{28,24},{1,5},{5... | collective-permute-start | bytes 491528 | tf_op jit(solution)/shard_map/ppermute | solution.py:649
  115.4 1.9 %collective-permute-start.18 = (f32[320,128]{1,0:T(8,128)S(1)}, f32[320,128]{1,0:T(8,128)S(1)}, u32[]{:S(2)}, u32[]{:S(2)}) collective-permute-start(f32[320,128]{1,0:T(8,128)S(1)} %collective-permute-done.14.refs_2_), channel_id=1, source_target_pairs={{0,4},{4,0},{8,12},{12,8},{16,20},{20,16},{24,28},{28,24},{1,5},{5... | collective-permute-start | bytes 491528 | tf_op jit(solution)/shard_map/ppermute | solution.py:649
  117.2 1.4 %collective-permute-start.19 = (f32[320,128]{1,0:T(8,128)S(1)}, f32[320,128]{1,0:T(8,128)S(1)}, u32[]{:S(2)}, u32[]{:S(2)}) collective-permute-start(f32[320,128]{1,0:T(8,128)S(1)} %collective-permute-done.15.refs_3_), channel_id=1, source_target_pairs={{0,4},{4,0},{8,12},{12,8},{16,20},{20,16},{24,28},{28,24},{1,5},{5... | collective-permute-start | bytes 491528 | tf_op jit(solution)/shard_map/ppermute | solution.py:649
  (5 other events, 9.0 us)

commit v9 on v7

--- a/solution.py
+++ b/solution.py
@@ -427,7 +427,7 @@
     preact = jnp.dot(latents, w_ref[...], preferred_element_type=jnp.float32) + b_ref[...]
     hidden, slope = gelu_parts(preact)
     slope_ref[...] = slope
-    hidden_t_ref[...] = hidden.T.astype(jnp.bfloat16)
+    hidden_t_ref[...] = hidden.astype(jnp.bfloat16).T
     latents_t_ref[...] = latents.T
 
 
@@ -493,7 +493,7 @@
         bias_acc[...] = jnp.zeros_like(bias_acc)
 
     field = field_ref[pl.ds(pl.multiple_of(index * cols, SUBS), cols), :].astype(jnp.bfloat16)
-    back = jnp.dot(field, w_out_ref[...], preferred_element_type=jnp.float32)
+    back = jnp.dot(field[:, :F], w_out_ref[...], preferred_element_type=jnp.float32)
     preact_back = (back * slope_ref[...]).astype(jnp.bfloat16)
     preact_ref[...] = preact_back
     hidden_acc[...] += jnp.dot(
@@ -569,6 +569,41 @@
         ),
         name="backward",
     )(core, scale, place, w_out_t, slope, hidden_t, latents_t, *grids)
+
+
+def latent_kernel(preact_hbm, w_ref, _, out_ref, preact_ref, copy_sem, *, parts):
+    fetch = pltpu.make_async_copy(preact_hbm, preact_ref, copy_sem)
+    fetch.start()
+    fetch.wait()
+    cols = preact_ref.shape[0] // parts
+    for part in range(parts):
+        rows = pl.ds(part * cols, cols)
+        out_ref[rows, :] = lax.dot_general(
+            preact_ref[rows, :],
+            w_ref[...],
+            (((1,), (1,)), ((), ())),
+            preferred_element_type=jnp.float32,
+        ).astype(jnp.bfloat16)
+
+
+def latent_gradient(preact_back, w_hidden, after, parts):
+    cells, width = preact_back.shape
+    return pl.pallas_call(
+        functools.partial(latent_kernel, parts=parts),
+        out_shape=jax.ShapeDtypeStruct((cells, width), jnp.bfloat16),
+        in_specs=[
+            pl.BlockSpec(memory_space=pltpu.HBM),
+            pl.BlockSpec(memory_space=pltpu.VMEM),
+            pl.BlockSpec(memory_space=pl.ANY),
+        ],
+        out_specs=pl.BlockSpec(memory_space=pltpu.VMEM),
+        scratch_shapes=[pltpu.VMEM((cells, width), jnp.bfloat16), pltpu.SemaphoreType.DMA],
+        compiler_params=pltpu.CompilerParams(vmem_limit_bytes=16 * MIB),
+        cost_estimate=pl.CostEstimate(
+            flops=2 * cells * width * width, bytes_accessed=4 * cells * width, transcendentals=0
+        ),
+        name="latent_gradient",
+    )(preact_back, w_hidden, after)
 
 
 def add_kernel(index_ref, *refs, inputs, outputs, factor):
@@ -688,7 +723,7 @@
     place = (
         target[:, :, None] == jnp.arange(lat_rows * LANES, dtype=jnp.int32)[None, None, :]
     ).astype(jnp.bfloat16)
-    w_out_t = jnp.concatenate([w_out.T, jnp.zeros((LANES - F, width), w_out.dtype)], axis=0)
+    w_out_t = w_out.T
 
     core_index, deep_index = lat_index & 1, lat_index >> 1
     depth = lat_count // 2
@@ -706,14 +741,11 @@
         core_index.reshape(1), grids, scale, place, w_out_t, slope, hidden_t, latents_t,
         chunk * device_count,
     )
-    latent_grad = lax.dot_general(
-        preact_back, w_hidden, (((1,), (1,)), ((), ())), preferred_element_type=jnp.float32
-    ).astype(jnp.bfloat16)
-
     pieces = add_pieces(
         lon_index.reshape(1), [keep, swap(send, "lat", 1)], lon_count
     )
     arrived = [swap(pieces[part], "lon", part) for part in range(1, lon_count)]
+    latent_grad = latent_gradient(preact_back, w_hidden, pieces[0], parts)
     arrived, latent_grad = lax.optimization_barrier((arrived, latent_grad))
     pieces = add_pieces(deep_index.reshape(1), [pieces[0]] + arrived, depth)
     arrived = [swap(pieces[part], "lat", 2 * part) for part in range(1, depth)]

time: 115 us -> 114 us (level)
  matrix products: 5.26 us -> 0 us
  Pallas kernels: 39.5 us -> 43 us
  local copies, waits for them, and re-layouts: 5.79 us -> 7.36 us
    dot_general x1 -> x0, matrix products: 5.26 us -> none  [local(): lax.dot_general(preact_back, w_hidden, (((1,), (1,)), ((), ())), preferre...]
    pallas_call x0 -> x1, Pallas kernels: none -> 3.61 us  [latent_gradient(): pl.pallas_call(functools.partial(latent_kernel, parts=parts), out_shape=j...]
    unnamed x12 -> x20, local copies, waits for them, and re-layouts: 4.45 us -> 6.87 us
  transfers between devices with their start and end apart: 21 -> 21, of which waited for: 11 -> 11; matrix products, arithmetic and copies ran while one was open for 6% -> 1% of each run, Pallas kernels for 7% -> 10%
where the time goes in v9:
time: 114 us
  Pallas kernels  43 us (38%)
  waiting for transfers between devices  35.4 us (31%)
  starting transfers between devices  26.7 us (23%)
  local copies, waits for them, and re-layouts  7.36 us (6%)
    pallas_call x1, Pallas kernels, coefficients(): pl.pallas_call(kernel, out_shape=jax.ShapeDtypeStruct((lat_count, slot_co...  22.3 us
    ppermute x20, starting transfers between devices, swap(): return lax.ppermute(value, axis, [(i, i ^ bits) for i in range(count)])  19.5 us
    all_to_all x1, waiting for transfers between devices, local(): lax.all_to_all(coeffs, ('lat', 'lon'), split_axis=0, concat_axis=0, tiled...  18 us
    ppermute x20, waiting for transfers between devices, swap(): return lax.ppermute(value, axis, [(i, i ^ bits) for i in range(count)])  17.4 us
    all_to_all x1, starting transfers between devices, local(): lax.all_to_all(coeffs, ('lat', 'lon'), split_axis=0, concat_axis=0, tiled...  7.22 us
    unnamed x20, local copies, waits for them, and re-layouts  6.87 us
    pallas_call x1, Pallas kernels, forward(): pl.pallas_call(forward_kernel, grid=(parts,), out_shape=(jax.ShapeDtypeSt...  5.73 us
    pallas_call x1, Pallas kernels, backward(): pl.pallas_call(functools.partial(backward_kernel, blocks=blocks), grid=(p...  5.25 us
  transfers between devices with their start and end apart: 21, of which 11 were waited for; matrix products, arithmetic and copies ran while one was open for 1% of the time, Pallas kernels for 10%

profile of v9, /device:TPU:0, one launch (start us, length us, event | category | flops | bytes accessed | tf_op | source)
XLA Modules:
  0.0 114.0 jit_solution(16217494263228917357)
XLA Ops:
  0.7 22.3 %coefficients.1 = f32[8,64,384]{2,1,0:T(8,128)} custom-call(s32[1]{0:T(128)} %bitcast.7.first_ref, f32[8,90,2,721]{3,2,1,0:T(2,128)} %bitcast.18), custom_call_target="tpu_custom_call" | custom-call | tf_op jit(solution)/shard_map/coefficients/pallas_call | solution.py:274
  22.9 7.2 %all-to-all-start = ((f32[32,16,384]{2,1,0:T(8,128)}), f32[32,16,384]{2,1,0:T(8,128)S(1)}, u32[]{:S(2)}, u32[]{:S(2)}) async-start(f32[32,16,384]{2,1,0:T(8,128)} %bitcast.19), calls=%async_computation | async-start | bytes 1572864 | tf_op jit(solution)/shard_map/all_to_all | solution.py:702
  30.7 2.2 %trig_table.1.trig_ref = bf16[4,360,384]{2,1,0:T(8,128)(2,1)S(1)} custom-call(), custom_call_target="tpu_custom_call" | custom-call | flops 3317760 | bytes 1105920 | tf_op jit(solution)/shard_map/trig_table/pallas_call | solution.py:333
  33.4 18.0 %all-to-all-done.coeff_ref = f32[32,16,384]{2,1,0:T(8,128)S(1)} async-done(((f32[32,16,384]{2,1,0:T(8,128)}), f32[32,16,384]{2,1,0:T(8,128)S(1)}, u32[]{:S(2)}, u32[]{:S(2)}) %all-to-all-start) | async-done | bytes 786464 | tf_op jit(solution)/shard_map/all_to_all | solution.py:702
  51.4 2.1 %grid_field.1 = (f32[360,128]{1,0:T(8,128)S(1)}, f32[360,128]{1,0:T(8,128)}, f32[360,128]{1,0:T(8,128)}, f32[360,128]{1,0:T(8,128)}) custom-call(s32[1]{0:T(128)} %bitcast.lon_ref.index_ref, bf16[4,360,384]{2,1,0:T(8,128)(2,1)S(1)} %trig_table.1.trig_ref, f32[32,16,384]{2,1,0:T(8,128)S(1)} %all-to-all-done.coeff_ref), custom_call_target="tpu_custom_call" | custom-call | flops 566231040 | bytes 2678784 | tf_op jit(solution)/shard_map/grid_field/pallas_call | solution.py:394
  54.9 1.5 %collective-permute-start.1 = (f32[360,128]{1,0:T(8,128)}, f32[360,128]{1,0:T(8,128)S(1)}, u32[]{:S(2)}, u32[]{:S(2)}) collective-permute-start(f32[360,128]{1,0:T(8,128)} %get-tuple-element.34), channel_id=1, source_target_pairs={{0,2},{1,3},{2,0},{3,1},{4,6},{5,7},{6,4},{7,5},{8,10},{9,11},{10,... | collective-permute-start | bytes 552968 | tf_op jit(solution)/shard_map/ppermute | solution.py:684
  58.7 1.8 %copy-done.6 = bf16[8,360,512]{2,1,0:T(8,128)(2,1)S(1)} copy-done((bf16[8,360,512]{2,1,0:T(8,128)(2,1)S(1)}, bf16[8,360,512]{2,1,0:T(8,128)(2,1)}, u32[]{:S(2)}) %copy-start.6) | copy-done | bytes 2949144
  60.5 5.7 %forward.1 = (f32[2880,512]{1,0:T(8,128)S(1)}, bf16[4,512,720]{2,1,0:T(8,128)(2,1)S(1)}, bf16[4,512,720]{2,1,0:T(8,128)(2,1)S(1)}) custom-call(bf16[2880,512]{1,0:T(8,128)(2,1)S(1)} %bitcast.16, bf16[512,512]{1,0:T(8,128)(2,1)S(1)} %copy-done.2, f32[1,512]{1,0:T(1,128)S(1)} %bitcast.17, f32[360,128]{1,0:T(8,128)S(1)} %copy-done.4), custom_call_target="tpu_custom_call" | custom-call | flops 1509949440 | bytes 14745600 | tf_op jit(solution)/shard_map/forward/pallas_call | solution.py:437
  66.3 5.3 %backward.1 = (bf16[2880,512]{1,0:T(8,128)(2,1)S(1)}, f32[1280,128]{1,0:T(8,128)S(1)}, f32[1280,128]{1,0:T(8,128)S(1)}) custom-call(s32[1]{0:T(128)} %bitcast.1.core_ref, f32[4,1,128]{2,1,0:T(1,128)S(1)} %bitcast.15, bf16[4,128,1024]{2,1,0:T(8,128)(2,1)S(1)} %fusion.place_ref, bf16[64,512]{1,0:T(8,128)(2,1)S(1)} %bitcast.14, ...), custom_call_target="tpu_custom_call" | custom-call | flops 2264924160 | bytes 14745600 | tf_op jit(solution)/shard_map/backward/pallas_call | solution.py:534
  71.6 1.6 %copy-done = bf16[2880,512]{1,0:T(8,128)(2,1)} copy-done((bf16[2880,512]{1,0:T(8,128)(2,1)}, bf16[2880,512]{1,0:T(8,128)(2,1)S(1)}, u32[]{:S(2)}) %copy-start) | copy-done | bytes 2949144
  73.2 2.1 %collective-permute-done.3.refs_1_ = f32[1280,128]{1,0:T(8,128)S(1)} collective-permute-done((f32[1280,128]{1,0:T(8,128)S(1)}, f32[1280,128]{1,0:T(8,128)S(1)}, u32[]{:S(2)}, u32[]{:S(2)}) %collective-permute-start.3) | collective-permute-done | bytes 655392 | tf_op jit(solution)/shard_map/ppermute | solution.py:684
  76.1 1.5 %collective-permute-start.5 = (f32[320,128]{1,0:T(8,128)S(1)}, f32[320,128]{1,0:T(8,128)S(1)}, u32[]{:S(2)}, u32[]{:S(2)}) collective-permute-start(f32[320,128]{1,0:T(8,128)S(1)} %get-tuple-element.39), channel_id=1, source_target_pairs={{0,2},{1,3},{2,0},{3,1},{4,6},{5,7},{6,4},{7,5},{8,10},{9,11},{10,... | collective-permute-start | bytes 491528 | tf_op jit(solution)/shard_map/ppermute | solution.py:684
  78.9 1.8 %copy-done.1 = bf16[2880,512]{1,0:T(8,128)(2,1)S(1)} copy-done((bf16[2880,512]{1,0:T(8,128)(2,1)S(1)}, bf16[2880,512]{1,0:T(8,128)(2,1)}, u32[]{:S(2)}) %copy-start.1) | copy-done | bytes 2949144
  80.7 3.6 %latent_gradient.1 = bf16[2880,512]{1,0:T(8,128)(2,1)} custom-call(bf16[2880,512]{1,0:T(8,128)(2,1)S(1)} %copy-done.1, bf16[512,512]{1,0:T(8,128)(2,1)S(1)} %copy-done.2, f32[320,128]{1,0:T(8,128)S(1)} %get-tuple-element.42._.refs_0_), custom_call_target="tpu_custom_call" | custom-call | flops 1509949440 | bytes 5898240 | tf_op jit(solution)/shard_map/latent_gradient/pallas_call | solution.py:591
  87.7 2.4 %collective-permute-start.9 = (f32[80,128]{1,0:T(8,128)S(1)}, f32[80,128]{1,0:T(8,128)S(1)}, u32[]{:S(2)}, u32[]{:S(2)}) collective-permute-start(f32[80,128]{1,0:T(8,128)S(1)} %get-tuple-element.50), channel_id=1, source_target_pairs={{0,24},{4,28},{8,16},{12,20},{16,8},{20,12},{24,0},{28,4},{1,25},{... | collective-permute-start | bytes 122888 | tf_op jit(solution)/shard_map/ppermute | solution.py:684
  90.1 1.6 %collective-permute-done.8.refs_2_ = f32[80,128]{1,0:T(8,128)S(1)} collective-permute-done((f32[80,128]{1,0:T(8,128)S(1)}, f32[80,128]{1,0:T(8,128)S(1)}, u32[]{:S(2)}, u32[]{:S(2)}) %collective-permute-start.8) | collective-permute-done | bytes 40992 | tf_op jit(solution)/shard_map/ppermute | solution.py:684
  91.7 1.8 %collective-permute-done.9.refs_3_ = f32[80,128]{1,0:T(8,128)S(1)} collective-permute-done((f32[80,128]{1,0:T(8,128)S(1)}, f32[80,128]{1,0:T(8,128)S(1)}, u32[]{:S(2)}, u32[]{:S(2)}) %collective-permute-start.9) | collective-permute-done | bytes 40992 | tf_op jit(solution)/shard_map/ppermute | solution.py:684
  93.6 3.2 %collective-permute-start.11 = (f32[80,128]{1,0:T(8,128)S(1)}, f32[80,128]{1,0:T(8,128)S(1)}, u32[]{:S(2)}, u32[]{:S(2)}) collective-permute-start(f32[80,128]{1,0:T(8,128)S(1)} %add_pieces.5), channel_id=1, source_target_pairs={{0,16},{4,20},{8,24},{12,28},{16,0},{20,4},{24,8},{28,12},{1,17},{... | collective-permute-start | bytes 122888 | tf_op jit(solution)/shard_map/ppermute | solution.py:684
  99.1 3.5 %collective-permute-done.12 = f32[80,128]{1,0:T(8,128)S(1)} collective-permute-done((f32[80,128]{1,0:T(8,128)S(1)}, f32[80,128]{1,0:T(8,128)S(1)}, u32[]{:S(2)}, u32[]{:S(2)}) %collective-permute-start.12) | collective-permute-done | bytes 40992 | tf_op jit(solution)/shard_map/ppermute | solution.py:684
  104.7 1.4 %collective-permute-start.15 = (f32[320,128]{1,0:T(8,128)S(1)}, f32[320,128]{1,0:T(8,128)S(1)}, u32[]{:S(2)}, u32[]{:S(2)}) collective-permute-start(f32[320,128]{1,0:T(8,128)S(1)} %pad_maximum_fusion.refs_0_), channel_id=1, source_target_pairs={{0,3},{1,2},{2,1},{3,0},{4,7},{5,6},{6,5},{7,4},{8,11},{9,10},{10,... | collective-permute-start | bytes 491528 | tf_op jit(solution)/shard_map/ppermute | solution.py:684
  106.1 1.8 %collective-permute-done.13.refs_1_ = f32[320,128]{1,0:T(8,128)S(1)} collective-permute-done((f32[320,128]{1,0:T(8,128)S(1)}, f32[320,128]{1,0:T(8,128)S(1)}, u32[]{:S(2)}, u32[]{:S(2)}) %collective-permute-start.13) | collective-permute-done | bytes 163872 | tf_op jit(solution)/shard_map/ppermute | solution.py:684
  109.1 1.8 %collective-permute-done.15.refs_3_ = f32[320,128]{1,0:T(8,128)S(1)} collective-permute-done((f32[320,128]{1,0:T(8,128)S(1)}, f32[320,128]{1,0:T(8,128)S(1)}, u32[]{:S(2)}, u32[]{:S(2)}) %collective-permute-start.15) | collective-permute-done | bytes 163872 | tf_op jit(solution)/shard_map/ppermute | solution.py:684
  111.0 1.3 %collective-permute-done.19.refs_7_ = f32[320,128]{1,0:T(8,128)S(1)} collective-permute-done((f32[320,128]{1,0:T(8,128)S(1)}, f32[320,128]{1,0:T(8,128)S(1)}, u32[]{:S(2)}, u32[]{:S(2)}) %collective-permute-start.19) | collective-permute-done | bytes 163872 | tf_op jit(solution)/shard_map/ppermute | solution.py:684
  112.3 1.7 %finish.1 = (f32[512,512]{1,0:T(8,128)}, f32[1,512]{1,0:T(1,128)}, f32[64,512]{1,0:T(8,128)}) custom-call(s32[3]{0:T(128)S(1)} %pad_add_fusion.place_ref, f32[320,128]{1,0:T(8,128)S(1)} %pad_maximum_fusion.refs_0_, f32[320,128]{1,0:T(8,128)S(1)} %collective-permute-done.13.refs_1_, f32[320,128]{1,0:T(8,128)S(1)} %collective-permute-done.14.refs_2_, ...), custom_call_target="tpu_custom_call" | custom-call | tf_op jit(solution)/shard_map/finish/pallas_call | solution.py:666
  (66 shorter events, 15.8 us)
Async XLA Ops:
  0.6 32.4 %copy-start.9 = (f32[64]{0:T(128)S(1)}, f32[64]{0:T(128)}, u32[]{:S(2)}) copy-start(f32[64]{0:T(128)} %param.9) | copy-start | bytes 772
  22.9 34.8 %copy-start.2 = (bf16[512,512]{1,0:T(8,128)(2,1)S(1)}, bf16[512,512]{1,0:T(8,128)(2,1)}, u32[]{:S(2)}) copy-start(bf16[512,512]{1,0:T(8,128)(2,1)} %w_ref.3) | copy-start | bytes 1572868
  22.9 34.8 %copy-start.7 = (f32[512]{0:T(512)S(1)}, f32[512]{0:T(512)}, u32[]{:S(2)}) copy-start(f32[512]{0:T(512)} %param.12) | copy-start | bytes 6148
  22.9 28.4 %all-to-all-start = ((f32[32,16,384]{2,1,0:T(8,128)}), f32[32,16,384]{2,1,0:T(8,128)S(1)}, u32[]{:S(2)}, u32[]{:S(2)}) async-start(f32[32,16,384]{2,1,0:T(8,128)} %bitcast.19), calls=%async_computation | async-start | bytes 1572864 | tf_op jit(solution)/shard_map/all_to_all | solution.py:702
  54.2 12.1 %collective-permute-start = (f32[360,128]{1,0:T(8,128)}, f32[360,128]{1,0:T(8,128)S(1)}, u32[]{:S(2)}, u32[]{:S(2)}) collective-permute-start(f32[360,128]{1,0:T(8,128)} %get-tuple-element.33), channel_id=1, source_target_pairs={{0,1},{1,0},{2,3},{3,2},{4,5},{5,4},{6,7},{7,6},{8,9},{9,8},{10,11... | collective-permute-start | bytes 552968 | tf_op jit(solution)/shard_map/ppermute | solution.py:684
  54.9 11.4 %collective-permute-start.1 = (f32[360,128]{1,0:T(8,128)}, f32[360,128]{1,0:T(8,128)S(1)}, u32[]{:S(2)}, u32[]{:S(2)}) collective-permute-start(f32[360,128]{1,0:T(8,128)} %get-tuple-element.34), channel_id=1, source_target_pairs={{0,2},{1,3},{2,0},{3,1},{4,6},{5,7},{6,4},{7,5},{8,10},{9,11},{10,... | collective-permute-start | bytes 552968 | tf_op jit(solution)/shard_map/ppermute | solution.py:684
  56.4 9.8 %collective-permute-start.2 = (f32[360,128]{1,0:T(8,128)}, f32[360,128]{1,0:T(8,128)S(1)}, u32[]{:S(2)}, u32[]{:S(2)}) collective-permute-start(f32[360,128]{1,0:T(8,128)} %get-tuple-element.35), channel_id=1, source_target_pairs={{0,3},{1,2},{2,1},{3,0},{4,7},{5,6},{6,5},{7,4},{8,11},{9,10},{10,... | collective-permute-start | bytes 552968 | tf_op jit(solution)/shard_map/ppermute | solution.py:684
  73.2 2.1 %collective-permute-start.3 = (f32[1280,128]{1,0:T(8,128)S(1)}, f32[1280,128]{1,0:T(8,128)S(1)}, u32[]{:S(2)}, u32[]{:S(2)}) collective-permute-start(f32[1280,128]{1,0:T(8,128)S(1)} %get-tuple-element.37), channel_id=1, source_target_pairs={{0,4},{4,0},{8,12},{12,8},{16,20},{20,16},{24,28},{28,24},{1,5},{5... | collective-permute-start | bytes 1966088 | tf_op jit(solution)/shard_map/ppermute | solution.py:684
  75.3 9.0 %collective-permute-start.4 = (f32[320,128]{1,0:T(8,128)S(1)}, f32[320,128]{1,0:T(8,128)S(1)}, u32[]{:S(2)}, u32[]{:S(2)}) collective-permute-start(f32[320,128]{1,0:T(8,128)S(1)} %get-tuple-element.38), channel_id=1, source_target_pairs={{0,1},{1,0},{2,3},{3,2},{4,5},{5,4},{6,7},{7,6},{8,9},{9,8},{10,11... | collective-permute-start | bytes 491528 | tf_op jit(solution)/shard_map/ppermute | solution.py:684
  76.1 9.5 %collective-permute-start.5 = (f32[320,128]{1,0:T(8,128)S(1)}, f32[320,128]{1,0:T(8,128)S(1)}, u32[]{:S(2)}, u32[]{:S(2)}) collective-permute-start(f32[320,128]{1,0:T(8,128)S(1)} %get-tuple-element.39), channel_id=1, source_target_pairs={{0,2},{1,3},{2,0},{3,1},{4,6},{5,7},{6,4},{7,5},{8,10},{9,11},{10,... | collective-permute-start | bytes 491528 | tf_op jit(solution)/shard_map/ppermute | solution.py:684
  77.6 7.9 %collective-permute-start.6 = (f32[320,128]{1,0:T(8,128)S(1)}, f32[320,128]{1,0:T(8,128)S(1)}, u32[]{:S(2)}, u32[]{:S(2)}) collective-permute-start(f32[320,128]{1,0:T(8,128)S(1)} %get-tuple-element.40), channel_id=1, source_target_pairs={{0,3},{1,2},{2,1},{3,0},{4,7},{5,6},{6,5},{7,4},{8,11},{9,10},{10,... | collective-permute-start | bytes 491528 | tf_op jit(solution)/shard_map/ppermute | solution.py:684
  85.6 4.5 %collective-permute-start.7 = (f32[80,128]{1,0:T(8,128)S(1)}, f32[80,128]{1,0:T(8,128)S(1)}, u32[]{:S(2)}, u32[]{:S(2)}) collective-permute-start(f32[80,128]{1,0:T(8,128)S(1)} %get-tuple-element.48), channel_id=1, source_target_pairs={{0,8},{4,12},{8,0},{12,4},{16,24},{20,28},{24,16},{28,20},{1,9},{5... | collective-permute-start | bytes 122888 | tf_op jit(solution)/shard_map/ppermute | solution.py:684
  86.8 4.9 %collective-permute-start.8 = (f32[80,128]{1,0:T(8,128)S(1)}, f32[80,128]{1,0:T(8,128)S(1)}, u32[]{:S(2)}, u32[]{:S(2)}) collective-permute-start(f32[80,128]{1,0:T(8,128)S(1)} %get-tuple-element.49), channel_id=1, source_target_pairs={{0,16},{4,20},{8,24},{12,28},{16,0},{20,4},{24,8},{28,12},{1,17},{... | collective-permute-start | bytes 122888 | tf_op jit(solution)/shard_map/ppermute | solution.py:684
  87.7 5.8 %collective-permute-start.9 = (f32[80,128]{1,0:T(8,128)S(1)}, f32[80,128]{1,0:T(8,128)S(1)}, u32[]{:S(2)}, u32[]{:S(2)}) collective-permute-start(f32[80,128]{1,0:T(8,128)S(1)} %get-tuple-element.50), channel_id=1, source_target_pairs={{0,24},{4,28},{8,16},{12,20},{16,8},{20,12},{24,0},{28,4},{1,25},{... | collective-permute-start | bytes 122888 | tf_op jit(solution)/shard_map/ppermute | solution.py:684
  93.5 4.5 %collective-permute-start.10 = (f32[80,128]{1,0:T(8,128)S(1)}, f32[80,128]{1,0:T(8,128)S(1)}, u32[]{:S(2)}, u32[]{:S(2)}) collective-permute-start(f32[80,128]{1,0:T(8,128)S(1)} %add_pieces.5), channel_id=1, source_target_pairs={{0,8},{4,12},{8,0},{12,4},{16,24},{20,28},{24,16},{28,20},{1,9},{5... | collective-permute-start | bytes 122888 | tf_op jit(solution)/shard_map/ppermute | solution.py:684
  93.6 5.5 %collective-permute-start.11 = (f32[80,128]{1,0:T(8,128)S(1)}, f32[80,128]{1,0:T(8,128)S(1)}, u32[]{:S(2)}, u32[]{:S(2)}) collective-permute-start(f32[80,128]{1,0:T(8,128)S(1)} %add_pieces.5), channel_id=1, source_target_pairs={{0,16},{4,20},{8,24},{12,28},{16,0},{20,4},{24,8},{28,12},{1,17},{... | collective-permute-start | bytes 122888 | tf_op jit(solution)/shard_map/ppermute | solution.py:684
  96.8 5.8 %collective-permute-start.12 = (f32[80,128]{1,0:T(8,128)S(1)}, f32[80,128]{1,0:T(8,128)S(1)}, u32[]{:S(2)}, u32[]{:S(2)}) collective-permute-start(f32[80,128]{1,0:T(8,128)S(1)} %add_pieces.5), channel_id=1, source_target_pairs={{0,24},{4,28},{8,16},{12,20},{16,8},{20,12},{24,0},{28,4},{1,25},{... | collective-permute-start | bytes 122888 | tf_op jit(solution)/shard_map/ppermute | solution.py:684
  102.6 5.4 %collective-permute-start.13 = (f32[320,128]{1,0:T(8,128)S(1)}, f32[320,128]{1,0:T(8,128)S(1)}, u32[]{:S(2)}, u32[]{:S(2)}) collective-permute-start(f32[320,128]{1,0:T(8,128)S(1)} %pad_maximum_fusion.refs_0_), channel_id=1, source_target_pairs={{0,1},{1,0},{2,3},{3,2},{4,5},{5,4},{6,7},{7,6},{8,9},{9,8},{10,11... | collective-permute-start | bytes 491528 | tf_op jit(solution)/shard_map/ppermute | solution.py:684
  103.8 5.3 %collective-permute-start.14 = (f32[320,128]{1,0:T(8,128)S(1)}, f32[320,128]{1,0:T(8,128)S(1)}, u32[]{:S(2)}, u32[]{:S(2)}) collective-permute-start(f32[320,128]{1,0:T(8,128)S(1)} %pad_maximum_fusion.refs_0_), channel_id=1, source_target_pairs={{0,2},{1,3},{2,0},{3,1},{4,6},{5,7},{6,4},{7,5},{8,10},{9,11},{10,... | collective-permute-start | bytes 491528 | tf_op jit(solution)/shard_map/ppermute | solution.py:684
  104.7 6.2 %collective-permute-start.15 = (f32[320,128]{1,0:T(8,128)S(1)}, f32[320,128]{1,0:T(8,128)S(1)}, u32[]{:S(2)}, u32[]{:S(2)}) collective-permute-start(f32[320,128]{1,0:T(8,128)S(1)} %pad_maximum_fusion.refs_0_), channel_id=1, source_target_pairs={{0,3},{1,2},{2,1},{3,0},{4,7},{5,6},{6,5},{7,4},{8,11},{9,10},{10,... | collective-permute-start | bytes 491528 | tf_op jit(solution)/shard_map/ppermute | solution.py:684
  106.1 4.9 %collective-permute-start.16 = (f32[320,128]{1,0:T(8,128)S(1)}, f32[320,128]{1,0:T(8,128)S(1)}, u32[]{:S(2)}, u32[]{:S(2)}) collective-permute-start(f32[320,128]{1,0:T(8,128)S(1)} %pad_maximum_fusion.refs_0_), channel_id=1, source_target_pairs={{0,4},{4,0},{8,12},{12,8},{16,20},{20,16},{24,28},{28,24},{1,5},{5... | collective-permute-start | bytes 491528 | tf_op jit(solution)/shard_map/ppermute | solution.py:684
  108.0 3.1 %collective-permute-start.17 = (f32[320,128]{1,0:T(8,128)S(1)}, f32[320,128]{1,0:T(8,128)S(1)}, u32[]{:S(2)}, u32[]{:S(2)}) collective-permute-start(f32[320,128]{1,0:T(8,128)S(1)} %collective-permute-done.13.refs_1_), channel_id=1, source_target_pairs={{0,4},{4,0},{8,12},{12,8},{16,20},{20,16},{24,28},{28,24},{1,5},{5... | collective-permute-start | bytes 491528 | tf_op jit(solution)/shard_map/ppermute | solution.py:684
  109.1 1.9 %collective-permute-start.18 = (f32[320,128]{1,0:T(8,128)S(1)}, f32[320,128]{1,0:T(8,128)S(1)}, u32[]{:S(2)}, u32[]{:S(2)}) collective-permute-start(f32[320,128]{1,0:T(8,128)S(1)} %collective-permute-done.14.refs_2_), channel_id=1, source_target_pairs={{0,4},{4,0},{8,12},{12,8},{16,20},{20,16},{24,28},{28,24},{1,5},{5... | collective-permute-start | bytes 491528 | tf_op jit(solution)/shard_map/ppermute | solution.py:684
  110.9 1.4 %collective-permute-start.19 = (f32[320,128]{1,0:T(8,128)S(1)}, f32[320,128]{1,0:T(8,128)S(1)}, u32[]{:S(2)}, u32[]{:S(2)}) collective-permute-start(f32[320,128]{1,0:T(8,128)S(1)} %collective-permute-done.15.refs_3_), channel_id=1, source_target_pairs={{0,4},{4,0},{8,12},{12,8},{16,20},{20,16},{24,28},{28,24},{1,5},{5... | collective-permute-start | bytes 491528 | tf_op jit(solution)/shard_map/ppermute | solution.py:684
  (7 other events, 51.3 us)

commit v10 on v7

--- a/solution.py
+++ b/solution.py
@@ -150,10 +150,10 @@
     whole_tiles = STEPS // step_tile
     plain_tiles = (NM // 2 + 1) // step_tile
     state = lax.fori_loop(
-        0, plain_tiles, lambda tile, carry: run_tile(tile, carry, step_tile, 16, True), state
+        0, plain_tiles, lambda tile, carry: run_tile(tile, carry, step_tile, 32, True), state
     )
     state = lax.fori_loop(
-        plain_tiles, whole_tiles, lambda tile, carry: run_tile(tile, carry, step_tile, 16), state
+        plain_tiles, whole_tiles, lambda tile, carry: run_tile(tile, carry, step_tile, 32), state
     )
     if STEPS % step_tile:
         run_tile(whole_tiles, state, STEPS % step_tile, STEPS % step_tile % 16)
@@ -232,22 +232,24 @@
                     source : source + SUBS
                 ]
 
-    def twice(kinds):
+    span = 4 * PAIRS
+
+    def several(kinds):
         def body(index, carry):
-            group(index * 2 * PAIRS, kinds)
-            group(index * 2 * PAIRS + PAIRS, kinds)
+            for part in range(0, span, PAIRS):
+                group(index * span + part, kinds)
             return carry
 
         return body
 
-    turns = pair_count // (2 * PAIRS)
+    turns = pair_count // span
     border = NM - edges[2]
-    low_turns = jnp.clip((border + 1 - first_pair) // (2 * PAIRS), 0, turns)
-    high_turn = jnp.clip((border - first_pair + 2 * PAIRS - 1) // (2 * PAIRS), low_turns, turns)
-    lax.fori_loop(0, low_turns, twice(("low", "both")), 0)
-    lax.fori_loop(low_turns, high_turn, twice(("both", "both")), 0)
-    lax.fori_loop(high_turn, turns, twice(("both", "high")), 0)
-    start = turns * 2 * PAIRS
+    low_turns = jnp.clip((border + 1 - first_pair) // span, 0, turns)
+    high_turn = jnp.clip((border - first_pair + span - 1) // span, low_turns, turns)
+    lax.fori_loop(0, low_turns, several(("low", "both")), 0)
+    lax.fori_loop(low_turns, high_turn, several(("both", "both")), 0)
+    lax.fori_loop(high_turn, turns, several(("both", "high")), 0)
+    start = turns * span
     while start < pair_count:
         group(min(start, pair_count - PAIRS), ("both", "both"))
         start = start + PAIRS
@@ -349,7 +351,8 @@
 
 
 def grid_kernel(lon_ref, trig_ref, coeff_ref, *refs, lon_count, pair_count):
-    flat_ref, right_ref = refs[lon_count:]
+    token_ref, flat_ref, right_ref = refs[lon_count:]
+    token_ref[...] = jnp.zeros_like(token_ref)
     share = coeff_ref.shape[1]
     width = coeff_ref.shape[2]
     rows = coeff_ref.shape[0] // lon_count * share
@@ -393,10 +396,11 @@
     rows = coeffs.shape[0] // lon_count * coeffs.shape[1]
     return pl.pallas_call(
         functools.partial(grid_kernel, lon_count=lon_count, pair_count=pair_count),
-        out_shape=[jax.ShapeDtypeStruct((NLON // lon_count, rows), jnp.float32)] * lon_count,
+        out_shape=[jax.ShapeDtypeStruct((NLON // lon_count, rows), jnp.float32)] * lon_count
+        + [jax.ShapeDtypeStruct((SUBS, LANES), jnp.float32)],
         in_specs=[pl.BlockSpec(memory_space=pltpu.SMEM)]
         + [pl.BlockSpec(memory_space=pltpu.VMEM)] * 2,
-        out_specs=[pl.BlockSpec(memory_space=pltpu.VMEM)] * lon_count,
+        out_specs=[pl.BlockSpec(memory_space=pltpu.VMEM)] * (lon_count + 1),
         scratch_shapes=[
             pltpu.VMEM((4 * quarter, rows), jnp.float32),
             pltpu.VMEM((lon_count * width, 4 * rows), jnp.bfloat16),
@@ -427,7 +431,7 @@
     preact = jnp.dot(latents, w_ref[...], preferred_element_type=jnp.float32) + b_ref[...]
     hidden, slope = gelu_parts(preact)
     slope_ref[...] = slope
-    hidden_t_ref[...] = hidden.T.astype(jnp.bfloat16)
+    hidden_t_ref[...] = hidden.astype(jnp.bfloat16).T
     latents_t_ref[...] = latents.T
 
 
@@ -446,7 +450,7 @@
             pl.BlockSpec((cols, width), lambda i: (i, 0)),
             pl.BlockSpec((width, width), lambda i: (0, 0)),
             pl.BlockSpec((1, width), lambda i: (0, 0)),
-            pl.BlockSpec(memory_space=pl.ANY),
+            pl.BlockSpec((SUBS, LANES), lambda i: (0, 0)),
         ],
         out_specs=(
             pl.BlockSpec((cols, width), lambda i: (i, 0)),
@@ -493,7 +497,7 @@
         bias_acc[...] = jnp.zeros_like(bias_acc)
 
     field = field_ref[pl.ds(pl.multiple_of(index * cols, SUBS), cols), :].astype(jnp.bfloat16)
-    back = jnp.dot(field, w_out_ref[...], preferred_element_type=jnp.float32)
+    back = jnp.dot(field[:, :F], w_out_ref[...], preferred_element_type=jnp.float32)
     preact_back = (back * slope_ref[...]).astype(jnp.bfloat16)
     preact_ref[...] = preact_back
     hidden_acc[...] += jnp.dot(
@@ -688,14 +692,14 @@
     place = (
         target[:, :, None] == jnp.arange(lat_rows * LANES, dtype=jnp.int32)[None, None, :]
     ).astype(jnp.bfloat16)
-    w_out_t = jnp.concatenate([w_out.T, jnp.zeros((LANES - F, width), w_out.dtype)], axis=0)
+    w_out_t = w_out.T
 
     core_index, deep_index = lat_index & 1, lat_index >> 1
     depth = lat_count // 2
     spots = jnp.stack([core_index, lon_index, deep_index])
-    grids = grid_field(lon_index.reshape(1), trig, coeffs, pair_count)
+    *grids, token = grid_field(lon_index.reshape(1), trig, coeffs, pair_count)
     slope, hidden_t, latents_t = forward(
-        latents.reshape(cells, width), w_hidden, b_hidden, grids[0], parts
+        latents.reshape(cells, width), w_hidden, b_hidden, token, parts
     )
     grids = [grids[0]] + [swap(grids[part], "lon", part) for part in range(1, lon_count)]
 
@@ -706,14 +710,13 @@
         core_index.reshape(1), grids, scale, place, w_out_t, slope, hidden_t, latents_t,
         chunk * device_count,
     )
+    pieces = add_pieces(
+        lon_index.reshape(1), [keep, swap(send, "lat", 1)], lon_count
+    )
+    arrived = [swap(pieces[part], "lon", part) for part in range(1, lon_count)]
     latent_grad = lax.dot_general(
         preact_back, w_hidden, (((1,), (1,)), ((), ())), preferred_element_type=jnp.float32
     ).astype(jnp.bfloat16)
-
-    pieces = add_pieces(
-        lon_index.reshape(1), [keep, swap(send, "lat", 1)], lon_count
-    )
-    arrived = [swap(pieces[part], "lon", part) for part in range(1, lon_count)]
     arrived, latent_grad = lax.optimization_barrier((arrived, latent_grad))
     pieces = add_pieces(deep_index.reshape(1), [pieces[0]] + arrived, depth)
     arrived = [swap(pieces[part], "lat", 2 * part) for part in range(1, depth)]

time: 115 us -> 111 us (0.965)
  Pallas kernels: 39.5 us -> 36.6 us
    pallas_call x1, Pallas kernels: 22.3 us -> 19.6 us  [coefficients(): pl.pallas_call(kernel, out_shape=jax.ShapeDtypeStruct((lat_count, slot_co...]
    unnamed x12 -> x14, local copies, waits for them, and re-layouts: 4.45 us -> 4.46 us
where the time goes in v10:
time: 111 us
  Pallas kernels  36.6 us (33%)
  waiting for transfers between devices  35.6 us (32%)
  starting transfers between devices  26.7 us (24%)
  matrix products  5.26 us (5%)
  local copies, waits for them, and re-layouts  4.95 us (4%)
    pallas_call x1, Pallas kernels, coefficients(): pl.pallas_call(kernel, out_shape=jax.ShapeDtypeStruct((lat_count, slot_co...  19.6 us
    ppermute x20, starting transfers between devices, swap(): return lax.ppermute(value, axis, [(i, i ^ bits) for i in range(count)])  19.5 us
    all_to_all x1, waiting for transfers between devices, local(): lax.all_to_all(coeffs, ('lat', 'lon'), split_axis=0, concat_axis=0, tiled...  18 us
    ppermute x20, waiting for transfers between devices, swap(): return lax.ppermute(value, axis, [(i, i ^ bits) for i in range(count)])  17.6 us
    all_to_all x1, starting transfers between devices, local(): lax.all_to_all(coeffs, ('lat', 'lon'), split_axis=0, concat_axis=0, tiled...  7.19 us
    pallas_call x1, Pallas kernels, forward(): pl.pallas_call(forward_kernel, grid=(parts,), out_shape=(jax.ShapeDtypeSt...  5.73 us
    dot_general x1, matrix products, local(): lax.dot_general(preact_back, w_hidden, (((1,), (1,)), ((), ())), preferre...  5.26 us
    pallas_call x1, Pallas kernels, backward(): pl.pallas_call(functools.partial(backward_kernel, blocks=blocks), grid=(p...  5.25 us
  transfers between devices with their start and end apart: 21, of which 11 were waited for; matrix products, arithmetic and copies ran while one was open for 6% of the time, Pallas kernels for 7%

profile of v10, /device:TPU:0, one launch (start us, length us, event | category | flops | bytes accessed | tf_op | source)
XLA Modules:
  0.0 110.6 jit_solution(10075539172849338753)
XLA Ops:
  0.7 19.6 %coefficients.1 = f32[8,64,384]{2,1,0:T(8,128)} custom-call(s32[1]{0:T(128)} %bitcast.7.first_ref, f32[8,90,2,721]{3,2,1,0:T(2,128)} %bitcast.20), custom_call_target="tpu_custom_call" | custom-call | tf_op jit(solution)/shard_map/coefficients/pallas_call | solution.py:276
  20.2 7.2 %all-to-all-start = ((f32[32,16,384]{2,1,0:T(8,128)}), f32[32,16,384]{2,1,0:T(8,128)S(1)}, u32[]{:S(2)}, u32[]{:S(2)}) async-start(f32[32,16,384]{2,1,0:T(8,128)} %bitcast.21), calls=%async_computation | async-start | bytes 1572864 | tf_op jit(solution)/shard_map/all_to_all | solution.py:671
  27.9 2.2 %trig_table.1.trig_ref = bf16[4,360,384]{2,1,0:T(8,128)(2,1)S(1)} custom-call(), custom_call_target="tpu_custom_call" | custom-call | flops 3317760 | bytes 1105920 | tf_op jit(solution)/shard_map/trig_table/pallas_call | solution.py:335
  30.7 18.0 %all-to-all-done.coeff_ref = f32[32,16,384]{2,1,0:T(8,128)S(1)} async-done(((f32[32,16,384]{2,1,0:T(8,128)}), f32[32,16,384]{2,1,0:T(8,128)S(1)}, u32[]{:S(2)}, u32[]{:S(2)}) %all-to-all-start) | async-done | bytes 786464 | tf_op jit(solution)/shard_map/all_to_all | solution.py:671
  48.6 2.1 %grid_field.1 = (f32[360,128]{1,0:T(8,128)S(1)}, f32[360,128]{1,0:T(8,128)}, f32[360,128]{1,0:T(8,128)S(1)}, f32[360,128]{1,0:T(8,128)S(1)}, f32[8,128]{1,0:T(8,128)S(1)}) custom-call(s32[1]{0:T(128)} %bitcast.lon_ref.index_ref, bf16[4,360,384]{2,1,0:T(8,128)(2,1)S(1)} %trig_table.1.trig_ref, f32[32,16,384]{2,1,0:T(8,128)S(1)} %all-to-all-done.coeff_ref), custom_call_target="tpu_custom_call" | custom-call | flops 566231040 | bytes 2678784 | tf_op jit(solution)/shard_map/grid_field/pallas_call | solution.py:397
  51.4 1.5 %collective-permute-start.1 = (f32[360,128]{1,0:T(8,128)S(1)}, f32[360,128]{1,0:T(8,128)S(1)}, u32[]{:S(2)}, u32[]{:S(2)}) collective-permute-start(f32[360,128]{1,0:T(8,128)S(1)} %get-tuple-element.36), channel_id=1, source_target_pairs={{0,2},{1,3},{2,0},{3,1},{4,6},{5,7},{6,4},{7,5},{8,10},{9,11},{10,... | collective-permute-start | bytes 552968 | tf_op jit(solution)/shard_map/ppermute | solution.py:653
  54.3 1.8 %copy-done.1 = bf16[8,360,512]{2,1,0:T(8,128)(2,1)S(1)} copy-done((bf16[8,360,512]{2,1,0:T(8,128)(2,1)S(1)}, bf16[8,360,512]{2,1,0:T(8,128)(2,1)}, u32[]{:S(2)}) %copy-start.1) | copy-done | bytes 2949144
  57.1 5.7 %forward.1 = (f32[2880,512]{1,0:T(8,128)S(1)}, bf16[4,512,720]{2,1,0:T(8,128)(2,1)S(1)}, bf16[4,512,720]{2,1,0:T(8,128)(2,1)S(1)}) custom-call(bf16[2880,512]{1,0:T(8,128)(2,1)S(1)} %bitcast.18, bf16[512,512]{1,0:T(8,128)(2,1)S(1)} %copy-done.3, f32[1,512]{1,0:T(1,128)S(1)} %bitcast.19, f32[8,128]{1,0:T(8,128)S(1)} %get-tuple-element.30._), custom_call_target="tpu_custom_call" | custom-call | flops 1509949440 | bytes 14745600 | tf_op jit(solution)/shard_map/forward/pallas_call | solution.py:441
  62.9 5.2 %backward.1 = (bf16[2880,512]{1,0:T(8,128)(2,1)S(1)}, f32[1280,128]{1,0:T(8,128)S(1)}, f32[1280,128]{1,0:T(8,128)S(1)}) custom-call(s32[1]{0:T(128)} %bitcast.1.core_ref, f32[4,1,128]{2,1,0:T(1,128)S(1)} %bitcast.17, bf16[4,128,1024]{2,1,0:T(8,128)(2,1)S(1)} %fusion.place_ref, bf16[64,512]{1,0:T(8,128)(2,1)S(1)} %bitcast.16, ...), custom_call_target="tpu_custom_call" | custom-call | flops 2264924160 | bytes 14745600 | tf_op jit(solution)/shard_map/backward/pallas_call | solution.py:538
  68.2 1.6 %copy-done.2 = bf16[2880,512]{1,0:T(8,128)(2,1)} copy-done((bf16[2880,512]{1,0:T(8,128)(2,1)}, bf16[2880,512]{1,0:T(8,128)(2,1)S(1)}, u32[]{:S(2)}) %copy-start.2) | copy-done | bytes 2949144
  69.8 2.1 %collective-permute-done.3.refs_1_ = f32[1280,128]{1,0:T(8,128)S(1)} collective-permute-done((f32[1280,128]{1,0:T(8,128)S(1)}, f32[1280,128]{1,0:T(8,128)S(1)}, u32[]{:S(2)}, u32[]{:S(2)}) %collective-permute-start.3) | collective-permute-done | bytes 655392 | tf_op jit(solution)/shard_map/ppermute | solution.py:653
  72.7 1.5 %collective-permute-start.5 = (f32[320,128]{1,0:T(8,128)S(1)}, f32[320,128]{1,0:T(8,128)S(1)}, u32[]{:S(2)}, u32[]{:S(2)}) collective-permute-start(f32[320,128]{1,0:T(8,128)S(1)} %get-tuple-element.41), channel_id=1, source_target_pairs={{0,2},{1,3},{2,0},{3,1},{4,6},{5,7},{6,4},{7,5},{8,10},{9,11},{10,... | collective-permute-start | bytes 491528 | tf_op jit(solution)/shard_map/ppermute | solution.py:653
  75.5 5.3 %convolution_convert_fusion = bf16[2880,512]{1,0:T(8,128)(2,1)} fusion(bf16[2880,512]{1,0:T(8,128)(2,1)} %copy-done.2, bf16[512,512]{1,0:T(8,128)(2,1)} %w_ref.1), kind=kOutput, calls=%fused_computation | convolution fusion | flops 1511424000 | bytes 6422528 | tf_op jit(solution)/shard_map/dot_general | solution.py:717
  80.8 1.4 %collective-permute-done.5.refs_2_ = f32[320,128]{1,0:T(8,128)S(1)} collective-permute-done((f32[320,128]{1,0:T(8,128)S(1)}, f32[320,128]{1,0:T(8,128)S(1)}, u32[]{:S(2)}, u32[]{:S(2)}) %collective-permute-start.5) | collective-permute-done | bytes 163872 | tf_op jit(solution)/shard_map/ppermute | solution.py:653
  84.3 2.4 %collective-permute-start.9 = (f32[80,128]{1,0:T(8,128)S(1)}, f32[80,128]{1,0:T(8,128)S(1)}, u32[]{:S(2)}, u32[]{:S(2)}) collective-permute-start(f32[80,128]{1,0:T(8,128)S(1)} %get-tuple-element.52), channel_id=1, source_target_pairs={{0,24},{4,28},{8,16},{12,20},{16,8},{20,12},{24,0},{28,4},{1,25},{... | collective-permute-start | bytes 122888 | tf_op jit(solution)/shard_map/ppermute | solution.py:653
  86.7 1.6 %collective-permute-done.8.refs_2_ = f32[80,128]{1,0:T(8,128)S(1)} collective-permute-done((f32[80,128]{1,0:T(8,128)S(1)}, f32[80,128]{1,0:T(8,128)S(1)}, u32[]{:S(2)}, u32[]{:S(2)}) %collective-permute-start.8) | collective-permute-done | bytes 40992 | tf_op jit(solution)/shard_map/ppermute | solution.py:653
  88.3 1.8 %collective-permute-done.9.refs_3_ = f32[80,128]{1,0:T(8,128)S(1)} collective-permute-done((f32[80,128]{1,0:T(8,128)S(1)}, f32[80,128]{1,0:T(8,128)S(1)}, u32[]{:S(2)}, u32[]{:S(2)}) %collective-permute-start.9) | collective-permute-done | bytes 40992 | tf_op jit(solution)/shard_map/ppermute | solution.py:653
  90.2 3.2 %collective-permute-start.11 = (f32[80,128]{1,0:T(8,128)S(1)}, f32[80,128]{1,0:T(8,128)S(1)}, u32[]{:S(2)}, u32[]{:S(2)}) collective-permute-start(f32[80,128]{1,0:T(8,128)S(1)} %add_pieces.5), channel_id=1, source_target_pairs={{0,16},{4,20},{8,24},{12,28},{16,0},{20,4},{24,8},{28,12},{1,17},{... | collective-permute-start | bytes 122888 | tf_op jit(solution)/shard_map/ppermute | solution.py:653
  95.7 3.5 %collective-permute-done.12 = f32[80,128]{1,0:T(8,128)S(1)} collective-permute-done((f32[80,128]{1,0:T(8,128)S(1)}, f32[80,128]{1,0:T(8,128)S(1)}, u32[]{:S(2)}, u32[]{:S(2)}) %collective-permute-start.12) | collective-permute-done | bytes 40992 | tf_op jit(solution)/shard_map/ppermute | solution.py:653
  101.3 1.4 %collective-permute-start.15 = (f32[320,128]{1,0:T(8,128)S(1)}, f32[320,128]{1,0:T(8,128)S(1)}, u32[]{:S(2)}, u32[]{:S(2)}) collective-permute-start(f32[320,128]{1,0:T(8,128)S(1)} %pad_maximum_fusion.refs_0_), channel_id=1, source_target_pairs={{0,3},{1,2},{2,1},{3,0},{4,7},{5,6},{6,5},{7,4},{8,11},{9,10},{10,... | collective-permute-start | bytes 491528 | tf_op jit(solution)/shard_map/ppermute | solution.py:653
  102.8 1.8 %collective-permute-done.13.refs_1_ = f32[320,128]{1,0:T(8,128)S(1)} collective-permute-done((f32[320,128]{1,0:T(8,128)S(1)}, f32[320,128]{1,0:T(8,128)S(1)}, u32[]{:S(2)}, u32[]{:S(2)}) %collective-permute-start.13) | collective-permute-done | bytes 163872 | tf_op jit(solution)/shard_map/ppermute | solution.py:653
  105.8 1.8 %collective-permute-done.15.refs_3_ = f32[320,128]{1,0:T(8,128)S(1)} collective-permute-done((f32[320,128]{1,0:T(8,128)S(1)}, f32[320,128]{1,0:T(8,128)S(1)}, u32[]{:S(2)}, u32[]{:S(2)}) %collective-permute-start.15) | collective-permute-done | bytes 163872 | tf_op jit(solution)/shard_map/ppermute | solution.py:653
  107.6 1.3 %collective-permute-done.19.refs_7_ = f32[320,128]{1,0:T(8,128)S(1)} collective-permute-done((f32[320,128]{1,0:T(8,128)S(1)}, f32[320,128]{1,0:T(8,128)S(1)}, u32[]{:S(2)}, u32[]{:S(2)}) %collective-permute-start.19) | collective-permute-done | bytes 163872 | tf_op jit(solution)/shard_map/ppermute | solution.py:653
  108.9 1.7 %finish.1 = (f32[512,512]{1,0:T(8,128)}, f32[1,512]{1,0:T(1,128)}, f32[64,512]{1,0:T(8,128)}) custom-call(s32[3]{0:T(128)S(1)} %pad_add_fusion.place_ref, f32[320,128]{1,0:T(8,128)S(1)} %pad_maximum_fusion.refs_0_, f32[320,128]{1,0:T(8,128)S(1)} %collective-permute-done.13.refs_1_, f32[320,128]{1,0:T(8,128)S(1)} %collective-permute-done.14.refs_2_, ...), custom_call_target="tpu_custom_call" | custom-call | tf_op jit(solution)/shard_map/finish/pallas_call | solution.py:635
  (60 shorter events, 14.0 us)
Async XLA Ops:
  0.6 26.8 %copy-start.5 = (s32[64]{0:T(128)S(1)}, s32[64]{0:T(128)}, u32[]{:S(2)}) copy-start(s32[64]{0:T(128)} %param.8) | copy-start | bytes 772
  0.6 29.7 %copy-start.6 = (f32[64]{0:T(128)S(1)}, f32[64]{0:T(128)}, u32[]{:S(2)}) copy-start(f32[64]{0:T(128)} %param.9) | copy-start | bytes 772
  20.2 34.0 %copy-start.4 = (f32[512]{0:T(512)S(1)}, f32[512]{0:T(512)}, u32[]{:S(2)}) copy-start(f32[512]{0:T(512)} %param.12) | copy-start | bytes 6148
  20.2 28.4 %all-to-all-start = ((f32[32,16,384]{2,1,0:T(8,128)}), f32[32,16,384]{2,1,0:T(8,128)S(1)}, u32[]{:S(2)}, u32[]{:S(2)}) async-start(f32[32,16,384]{2,1,0:T(8,128)} %bitcast.21), calls=%async_computation | async-start | bytes 1572864 | tf_op jit(solution)/shard_map/all_to_all | solution.py:671
  50.7 12.2 %collective-permute-start = (f32[360,128]{1,0:T(8,128)}, f32[360,128]{1,0:T(8,128)S(1)}, u32[]{:S(2)}, u32[]{:S(2)}) collective-permute-start(f32[360,128]{1,0:T(8,128)} %get-tuple-element.35), channel_id=1, source_target_pairs={{0,1},{1,0},{2,3},{3,2},{4,5},{5,4},{6,7},{7,6},{8,9},{9,8},{10,11... | collective-permute-start | bytes 552968 | tf_op jit(solution)/shard_map/ppermute | solution.py:653
  51.4 11.5 %collective-permute-start.1 = (f32[360,128]{1,0:T(8,128)S(1)}, f32[360,128]{1,0:T(8,128)S(1)}, u32[]{:S(2)}, u32[]{:S(2)}) collective-permute-start(f32[360,128]{1,0:T(8,128)S(1)} %get-tuple-element.36), channel_id=1, source_target_pairs={{0,2},{1,3},{2,0},{3,1},{4,6},{5,7},{6,4},{7,5},{8,10},{9,11},{10,... | collective-permute-start | bytes 552968 | tf_op jit(solution)/shard_map/ppermute | solution.py:653
  53.0 10.0 %collective-permute-start.2 = (f32[360,128]{1,0:T(8,128)S(1)}, f32[360,128]{1,0:T(8,128)S(1)}, u32[]{:S(2)}, u32[]{:S(2)}) collective-permute-start(f32[360,128]{1,0:T(8,128)S(1)} %get-tuple-element.37), channel_id=1, source_target_pairs={{0,3},{1,2},{2,1},{3,0},{4,7},{5,6},{6,5},{7,4},{8,11},{9,10},{10,... | collective-permute-start | bytes 552968 | tf_op jit(solution)/shard_map/ppermute | solution.py:653
  69.8 2.1 %collective-permute-start.3 = (f32[1280,128]{1,0:T(8,128)S(1)}, f32[1280,128]{1,0:T(8,128)S(1)}, u32[]{:S(2)}, u32[]{:S(2)}) collective-permute-start(f32[1280,128]{1,0:T(8,128)S(1)} %get-tuple-element.39), channel_id=1, source_target_pairs={{0,4},{4,0},{8,12},{12,8},{16,20},{20,16},{24,28},{28,24},{1,5},{5... | collective-permute-start | bytes 1966088 | tf_op jit(solution)/shard_map/ppermute | solution.py:653
  72.0 8.8 %collective-permute-start.4 = (f32[320,128]{1,0:T(8,128)S(1)}, f32[320,128]{1,0:T(8,128)S(1)}, u32[]{:S(2)}, u32[]{:S(2)}) collective-permute-start(f32[320,128]{1,0:T(8,128)S(1)} %get-tuple-element.40), channel_id=1, source_target_pairs={{0,1},{1,0},{2,3},{3,2},{4,5},{5,4},{6,7},{7,6},{8,9},{9,8},{10,11... | collective-permute-start | bytes 491528 | tf_op jit(solution)/shard_map/ppermute | solution.py:653
  72.7 9.5 %collective-permute-start.5 = (f32[320,128]{1,0:T(8,128)S(1)}, f32[320,128]{1,0:T(8,128)S(1)}, u32[]{:S(2)}, u32[]{:S(2)}) collective-permute-start(f32[320,128]{1,0:T(8,128)S(1)} %get-tuple-element.41), channel_id=1, source_target_pairs={{0,2},{1,3},{2,0},{3,1},{4,6},{5,7},{6,4},{7,5},{8,10},{9,11},{10,... | collective-permute-start | bytes 491528 | tf_op jit(solution)/shard_map/ppermute | solution.py:653
  74.3 7.9 %collective-permute-start.6 = (f32[320,128]{1,0:T(8,128)S(1)}, f32[320,128]{1,0:T(8,128)S(1)}, u32[]{:S(2)}, u32[]{:S(2)}) collective-permute-start(f32[320,128]{1,0:T(8,128)S(1)} %get-tuple-element.42), channel_id=1, source_target_pairs={{0,3},{1,2},{2,1},{3,0},{4,7},{5,6},{6,5},{7,4},{8,11},{9,10},{10,... | collective-permute-start | bytes 491528 | tf_op jit(solution)/shard_map/ppermute | solution.py:653
  82.2 4.5 %collective-permute-start.7 = (f32[80,128]{1,0:T(8,128)S(1)}, f32[80,128]{1,0:T(8,128)S(1)}, u32[]{:S(2)}, u32[]{:S(2)}) collective-permute-start(f32[80,128]{1,0:T(8,128)S(1)} %get-tuple-element.50), channel_id=1, source_target_pairs={{0,8},{4,12},{8,0},{12,4},{16,24},{20,28},{24,16},{28,20},{1,9},{5... | collective-permute-start | bytes 122888 | tf_op jit(solution)/shard_map/ppermute | solution.py:653
  83.4 4.9 %collective-permute-start.8 = (f32[80,128]{1,0:T(8,128)S(1)}, f32[80,128]{1,0:T(8,128)S(1)}, u32[]{:S(2)}, u32[]{:S(2)}) collective-permute-start(f32[80,128]{1,0:T(8,128)S(1)} %get-tuple-element.51), channel_id=1, source_target_pairs={{0,16},{4,20},{8,24},{12,28},{16,0},{20,4},{24,8},{28,12},{1,17},{... | collective-permute-start | bytes 122888 | tf_op jit(solution)/shard_map/ppermute | solution.py:653
  84.3 5.8 %collective-permute-start.9 = (f32[80,128]{1,0:T(8,128)S(1)}, f32[80,128]{1,0:T(8,128)S(1)}, u32[]{:S(2)}, u32[]{:S(2)}) collective-permute-start(f32[80,128]{1,0:T(8,128)S(1)} %get-tuple-element.52), channel_id=1, source_target_pairs={{0,24},{4,28},{8,16},{12,20},{16,8},{20,12},{24,0},{28,4},{1,25},{... | collective-permute-start | bytes 122888 | tf_op jit(solution)/shard_map/ppermute | solution.py:653
  90.1 4.5 %collective-permute-start.10 = (f32[80,128]{1,0:T(8,128)S(1)}, f32[80,128]{1,0:T(8,128)S(1)}, u32[]{:S(2)}, u32[]{:S(2)}) collective-permute-start(f32[80,128]{1,0:T(8,128)S(1)} %add_pieces.5), channel_id=1, source_target_pairs={{0,8},{4,12},{8,0},{12,4},{16,24},{20,28},{24,16},{28,20},{1,9},{5... | collective-permute-start | bytes 122888 | tf_op jit(solution)/shard_map/ppermute | solution.py:653
  90.2 5.5 %collective-permute-start.11 = (f32[80,128]{1,0:T(8,128)S(1)}, f32[80,128]{1,0:T(8,128)S(1)}, u32[]{:S(2)}, u32[]{:S(2)}) collective-permute-start(f32[80,128]{1,0:T(8,128)S(1)} %add_pieces.5), channel_id=1, source_target_pairs={{0,16},{4,20},{8,24},{12,28},{16,0},{20,4},{24,8},{28,12},{1,17},{... | collective-permute-start | bytes 122888 | tf_op jit(solution)/shard_map/ppermute | solution.py:653
  93.4 5.8 %collective-permute-start.12 = (f32[80,128]{1,0:T(8,128)S(1)}, f32[80,128]{1,0:T(8,128)S(1)}, u32[]{:S(2)}, u32[]{:S(2)}) collective-permute-start(f32[80,128]{1,0:T(8,128)S(1)} %add_pieces.5), channel_id=1, source_target_pairs={{0,24},{4,28},{8,16},{12,20},{16,8},{20,12},{24,0},{28,4},{1,25},{... | collective-permute-start | bytes 122888 | tf_op jit(solution)/shard_map/ppermute | solution.py:653
  99.2 5.4 %collective-permute-start.13 = (f32[320,128]{1,0:T(8,128)S(1)}, f32[320,128]{1,0:T(8,128)S(1)}, u32[]{:S(2)}, u32[]{:S(2)}) collective-permute-start(f32[320,128]{1,0:T(8,128)S(1)} %pad_maximum_fusion.refs_0_), channel_id=1, source_target_pairs={{0,1},{1,0},{2,3},{3,2},{4,5},{5,4},{6,7},{7,6},{8,9},{9,8},{10,11... | collective-permute-start | bytes 491528 | tf_op jit(solution)/shard_map/ppermute | solution.py:653
  100.4 5.3 %collective-permute-start.14 = (f32[320,128]{1,0:T(8,128)S(1)}, f32[320,128]{1,0:T(8,128)S(1)}, u32[]{:S(2)}, u32[]{:S(2)}) collective-permute-start(f32[320,128]{1,0:T(8,128)S(1)} %pad_maximum_fusion.refs_0_), channel_id=1, source_target_pairs={{0,2},{1,3},{2,0},{3,1},{4,6},{5,7},{6,4},{7,5},{8,10},{9,11},{10,... | collective-permute-start | bytes 491528 | tf_op jit(solution)/shard_map/ppermute | solution.py:653
  101.3 6.2 %collective-permute-start.15 = (f32[320,128]{1,0:T(8,128)S(1)}, f32[320,128]{1,0:T(8,128)S(1)}, u32[]{:S(2)}, u32[]{:S(2)}) collective-permute-start(f32[320,128]{1,0:T(8,128)S(1)} %pad_maximum_fusion.refs_0_), channel_id=1, source_target_pairs={{0,3},{1,2},{2,1},{3,0},{4,7},{5,6},{6,5},{7,4},{8,11},{9,10},{10,... | collective-permute-start | bytes 491528 | tf_op jit(solution)/shard_map/ppermute | solution.py:653
  102.8 4.9 %collective-permute-start.16 = (f32[320,128]{1,0:T(8,128)S(1)}, f32[320,128]{1,0:T(8,128)S(1)}, u32[]{:S(2)}, u32[]{:S(2)}) collective-permute-start(f32[320,128]{1,0:T(8,128)S(1)} %pad_maximum_fusion.refs_0_), channel_id=1, source_target_pairs={{0,4},{4,0},{8,12},{12,8},{16,20},{20,16},{24,28},{28,24},{1,5},{5... | collective-permute-start | bytes 491528 | tf_op jit(solution)/shard_map/ppermute | solution.py:653
  104.6 3.0 %collective-permute-start.17 = (f32[320,128]{1,0:T(8,128)S(1)}, f32[320,128]{1,0:T(8,128)S(1)}, u32[]{:S(2)}, u32[]{:S(2)}) collective-permute-start(f32[320,128]{1,0:T(8,128)S(1)} %collective-permute-done.13.refs_1_), channel_id=1, source_target_pairs={{0,4},{4,0},{8,12},{12,8},{16,20},{20,16},{24,28},{28,24},{1,5},{5... | collective-permute-start | bytes 491528 | tf_op jit(solution)/shard_map/ppermute | solution.py:653
  105.8 1.9 %collective-permute-start.18 = (f32[320,128]{1,0:T(8,128)S(1)}, f32[320,128]{1,0:T(8,128)S(1)}, u32[]{:S(2)}, u32[]{:S(2)}) collective-permute-start(f32[320,128]{1,0:T(8,128)S(1)} %collective-permute-done.14.refs_2_), channel_id=1, source_target_pairs={{0,4},{4,0},{8,12},{12,8},{16,20},{20,16},{24,28},{28,24},{1,5},{5... | collective-permute-start | bytes 491528 | tf_op jit(solution)/shard_map/ppermute | solution.py:653
  107.5 1.4 %collective-permute-start.19 = (f32[320,128]{1,0:T(8,128)S(1)}, f32[320,128]{1,0:T(8,128)S(1)}, u32[]{:S(2)}, u32[]{:S(2)}) collective-permute-start(f32[320,128]{1,0:T(8,128)S(1)} %collective-permute-done.15.refs_3_), channel_id=1, source_target_pairs={{0,4},{4,0},{8,12},{12,8},{16,20},{20,16},{24,28},{28,24},{1,5},{5... | collective-permute-start | bytes 491528 | tf_op jit(solution)/shard_map/ppermute | solution.py:653
  (4 other events, 16.7 us)

commit v11 on v10

--- a/solution.py
+++ b/solution.py
@@ -150,10 +150,10 @@
     whole_tiles = STEPS // step_tile
     plain_tiles = (NM // 2 + 1) // step_tile
     state = lax.fori_loop(
-        0, plain_tiles, lambda tile, carry: run_tile(tile, carry, step_tile, 32, True), state
+        0, plain_tiles, lambda tile, carry: run_tile(tile, carry, step_tile, 64, True), state
     )
     state = lax.fori_loop(
-        plain_tiles, whole_tiles, lambda tile, carry: run_tile(tile, carry, step_tile, 32), state
+        plain_tiles, whole_tiles, lambda tile, carry: run_tile(tile, carry, step_tile, 64), state
     )
     if STEPS % step_tile:
         run_tile(whole_tiles, state, STEPS % step_tile, STEPS % step_tile % 16)
@@ -232,7 +232,7 @@
                     source : source + SUBS
                 ]
 
-    span = 4 * PAIRS
+    span = 7 * PAIRS
 
     def several(kinds):
         def body(index, carry):

time: 111 us -> 109 us (0.982)
  Pallas kernels: 36.6 us -> 35.1 us
    pallas_call x1, Pallas kernels: 19.6 us -> 18 us  [coefficients(): pl.pallas_call(kernel, out_shape=jax.ShapeDtypeStruct((lat_count, slot_co...]
where the time goes in v11:
time: 109 us
  waiting for transfers between devices  35.6 us (33%)
  Pallas kernels  35.1 us (32%)
  starting transfers between devices  26.7 us (24%)
  matrix products  5.26 us (5%)
  local copies, waits for them, and re-layouts  4.95 us (5%)
    ppermute x20, starting transfers between devices, swap(): return lax.ppermute(value, axis, [(i, i ^ bits) for i in range(count)])  19.5 us
    pallas_call x1, Pallas kernels, coefficients(): pl.pallas_call(kernel, out_shape=jax.ShapeDtypeStruct((lat_count, slot_co...  18 us
    all_to_all x1, waiting for transfers between devices, local(): lax.all_to_all(coeffs, ('lat', 'lon'), split_axis=0, concat_axis=0, tiled...  18 us
    ppermute x20, waiting for transfers between devices, swap(): return lax.ppermute(value, axis, [(i, i ^ bits) for i in range(count)])  17.6 us
    all_to_all x1, starting transfers between devices, local(): lax.all_to_all(coeffs, ('lat', 'lon'), split_axis=0, concat_axis=0, tiled...  7.16 us
    pallas_call x1, Pallas kernels, forward(): pl.pallas_call(forward_kernel, grid=(parts,), out_shape=(jax.ShapeDtypeSt...  5.74 us
    dot_general x1, matrix products, local(): lax.dot_general(preact_back, w_hidden, (((1,), (1,)), ((), ())), preferre...  5.26 us
    pallas_call x1, Pallas kernels, backward(): pl.pallas_call(functools.partial(backward_kernel, blocks=blocks), grid=(p...  5.25 us
  transfers between devices with their start and end apart: 21, of which 11 were waited for; matrix products, arithmetic and copies ran while one was open for 6% of the time, Pallas kernels for 7%

profile of v11, /device:TPU:0, one launch (start us, length us, event | category | flops | bytes accessed | tf_op | source)
XLA Modules:
  0.0 109.0 jit_solution(17878254606642243686)
XLA Ops:
  0.7 18.0 %coefficients.1 = f32[8,64,384]{2,1,0:T(8,128)} custom-call(s32[1]{0:T(128)} %bitcast.7.first_ref, f32[8,90,2,721]{3,2,1,0:T(2,128)} %bitcast.20), custom_call_target="tpu_custom_call" | custom-call | tf_op jit(solution)/shard_map/coefficients/pallas_call | solution.py:276
  18.7 7.2 %all-to-all-start = ((f32[32,16,384]{2,1,0:T(8,128)}), f32[32,16,384]{2,1,0:T(8,128)S(1)}, u32[]{:S(2)}, u32[]{:S(2)}) async-start(f32[32,16,384]{2,1,0:T(8,128)} %bitcast.21), calls=%async_computation | async-start | bytes 1572864 | tf_op jit(solution)/shard_map/all_to_all | solution.py:671
  26.3 2.2 %trig_table.1.trig_ref = bf16[4,360,384]{2,1,0:T(8,128)(2,1)S(1)} custom-call(), custom_call_target="tpu_custom_call" | custom-call | flops 3317760 | bytes 1105920 | tf_op jit(solution)/shard_map/trig_table/pallas_call | solution.py:335
  29.1 18.0 %all-to-all-done.coeff_ref = f32[32,16,384]{2,1,0:T(8,128)S(1)} async-done(((f32[32,16,384]{2,1,0:T(8,128)}), f32[32,16,384]{2,1,0:T(8,128)S(1)}, u32[]{:S(2)}, u32[]{:S(2)}) %all-to-all-start) | async-done | bytes 786464 | tf_op jit(solution)/shard_map/all_to_all | solution.py:671
  47.0 2.1 %grid_field.1 = (f32[360,128]{1,0:T(8,128)S(1)}, f32[360,128]{1,0:T(8,128)}, f32[360,128]{1,0:T(8,128)S(1)}, f32[360,128]{1,0:T(8,128)S(1)}, f32[8,128]{1,0:T(8,128)S(1)}) custom-call(s32[1]{0:T(128)} %bitcast.lon_ref.index_ref, bf16[4,360,384]{2,1,0:T(8,128)(2,1)S(1)} %trig_table.1.trig_ref, f32[32,16,384]{2,1,0:T(8,128)S(1)} %all-to-all-done.coeff_ref), custom_call_target="tpu_custom_call" | custom-call | flops 566231040 | bytes 2678784 | tf_op jit(solution)/shard_map/grid_field/pallas_call | solution.py:397
  49.8 1.5 %collective-permute-start.1 = (f32[360,128]{1,0:T(8,128)S(1)}, f32[360,128]{1,0:T(8,128)S(1)}, u32[]{:S(2)}, u32[]{:S(2)}) collective-permute-start(f32[360,128]{1,0:T(8,128)S(1)} %get-tuple-element.36), channel_id=1, source_target_pairs={{0,2},{1,3},{2,0},{3,1},{4,6},{5,7},{6,4},{7,5},{8,10},{9,11},{10,... | collective-permute-start | bytes 552968 | tf_op jit(solution)/shard_map/ppermute | solution.py:653
  52.7 1.8 %copy-done.1 = bf16[8,360,512]{2,1,0:T(8,128)(2,1)S(1)} copy-done((bf16[8,360,512]{2,1,0:T(8,128)(2,1)S(1)}, bf16[8,360,512]{2,1,0:T(8,128)(2,1)}, u32[]{:S(2)}) %copy-start.1) | copy-done | bytes 2949144
  55.5 5.7 %forward.1 = (f32[2880,512]{1,0:T(8,128)S(1)}, bf16[4,512,720]{2,1,0:T(8,128)(2,1)S(1)}, bf16[4,512,720]{2,1,0:T(8,128)(2,1)S(1)}) custom-call(bf16[2880,512]{1,0:T(8,128)(2,1)S(1)} %bitcast.18, bf16[512,512]{1,0:T(8,128)(2,1)S(1)} %copy-done.3, f32[1,512]{1,0:T(1,128)S(1)} %bitcast.19, f32[8,128]{1,0:T(8,128)S(1)} %get-tuple-element.30._), custom_call_target="tpu_custom_call" | custom-call | flops 1509949440 | bytes 14745600 | tf_op jit(solution)/shard_map/forward/pallas_call | solution.py:441
  61.3 5.2 %backward.1 = (bf16[2880,512]{1,0:T(8,128)(2,1)S(1)}, f32[1280,128]{1,0:T(8,128)S(1)}, f32[1280,128]{1,0:T(8,128)S(1)}) custom-call(s32[1]{0:T(128)} %bitcast.1.core_ref, f32[4,1,128]{2,1,0:T(1,128)S(1)} %bitcast.17, bf16[4,128,1024]{2,1,0:T(8,128)(2,1)S(1)} %fusion.place_ref, bf16[64,512]{1,0:T(8,128)(2,1)S(1)} %bitcast.16, ...), custom_call_target="tpu_custom_call" | custom-call | flops 2264924160 | bytes 14745600 | tf_op jit(solution)/shard_map/backward/pallas_call | solution.py:538
  66.6 1.6 %copy-done.2 = bf16[2880,512]{1,0:T(8,128)(2,1)} copy-done((bf16[2880,512]{1,0:T(8,128)(2,1)}, bf16[2880,512]{1,0:T(8,128)(2,1)S(1)}, u32[]{:S(2)}) %copy-start.2) | copy-done | bytes 2949144
  68.2 2.1 %collective-permute-done.3.refs_1_ = f32[1280,128]{1,0:T(8,128)S(1)} collective-permute-done((f32[1280,128]{1,0:T(8,128)S(1)}, f32[1280,128]{1,0:T(8,128)S(1)}, u32[]{:S(2)}, u32[]{:S(2)}) %collective-permute-start.3) | collective-permute-done | bytes 655392 | tf_op jit(solution)/shard_map/ppermute | solution.py:653
  71.1 1.5 %collective-permute-start.5 = (f32[320,128]{1,0:T(8,128)S(1)}, f32[320,128]{1,0:T(8,128)S(1)}, u32[]{:S(2)}, u32[]{:S(2)}) collective-permute-start(f32[320,128]{1,0:T(8,128)S(1)} %get-tuple-element.41), channel_id=1, source_target_pairs={{0,2},{1,3},{2,0},{3,1},{4,6},{5,7},{6,4},{7,5},{8,10},{9,11},{10,... | collective-permute-start | bytes 491528 | tf_op jit(solution)/shard_map/ppermute | solution.py:653
  73.9 5.3 %convolution_convert_fusion = bf16[2880,512]{1,0:T(8,128)(2,1)} fusion(bf16[2880,512]{1,0:T(8,128)(2,1)} %copy-done.2, bf16[512,512]{1,0:T(8,128)(2,1)} %w_ref.1), kind=kOutput, calls=%fused_computation | convolution fusion | flops 1511424000 | bytes 6422528 | tf_op jit(solution)/shard_map/dot_general | solution.py:717
  79.2 1.4 %collective-permute-done.5.refs_2_ = f32[320,128]{1,0:T(8,128)S(1)} collective-permute-done((f32[320,128]{1,0:T(8,128)S(1)}, f32[320,128]{1,0:T(8,128)S(1)}, u32[]{:S(2)}, u32[]{:S(2)}) %collective-permute-start.5) | collective-permute-done | bytes 163872 | tf_op jit(solution)/shard_map/ppermute | solution.py:653
  82.7 2.4 %collective-permute-start.9 = (f32[80,128]{1,0:T(8,128)S(1)}, f32[80,128]{1,0:T(8,128)S(1)}, u32[]{:S(2)}, u32[]{:S(2)}) collective-permute-start(f32[80,128]{1,0:T(8,128)S(1)} %get-tuple-element.52), channel_id=1, source_target_pairs={{0,24},{4,28},{8,16},{12,20},{16,8},{20,12},{24,0},{28,4},{1,25},{... | collective-permute-start | bytes 122888 | tf_op jit(solution)/shard_map/ppermute | solution.py:653
  85.1 1.6 %collective-permute-done.8.refs_2_ = f32[80,128]{1,0:T(8,128)S(1)} collective-permute-done((f32[80,128]{1,0:T(8,128)S(1)}, f32[80,128]{1,0:T(8,128)S(1)}, u32[]{:S(2)}, u32[]{:S(2)}) %collective-permute-start.8) | collective-permute-done | bytes 40992 | tf_op jit(solution)/shard_map/ppermute | solution.py:653
  86.7 1.8 %collective-permute-done.9.refs_3_ = f32[80,128]{1,0:T(8,128)S(1)} collective-permute-done((f32[80,128]{1,0:T(8,128)S(1)}, f32[80,128]{1,0:T(8,128)S(1)}, u32[]{:S(2)}, u32[]{:S(2)}) %collective-permute-start.9) | collective-permute-done | bytes 40992 | tf_op jit(solution)/shard_map/ppermute | solution.py:653
  88.6 3.2 %collective-permute-start.11 = (f32[80,128]{1,0:T(8,128)S(1)}, f32[80,128]{1,0:T(8,128)S(1)}, u32[]{:S(2)}, u32[]{:S(2)}) collective-permute-start(f32[80,128]{1,0:T(8,128)S(1)} %add_pieces.5), channel_id=1, source_target_pairs={{0,16},{4,20},{8,24},{12,28},{16,0},{20,4},{24,8},{28,12},{1,17},{... | collective-permute-start | bytes 122888 | tf_op jit(solution)/shard_map/ppermute | solution.py:653
  94.1 3.5 %collective-permute-done.12 = f32[80,128]{1,0:T(8,128)S(1)} collective-permute-done((f32[80,128]{1,0:T(8,128)S(1)}, f32[80,128]{1,0:T(8,128)S(1)}, u32[]{:S(2)}, u32[]{:S(2)}) %collective-permute-start.12) | collective-permute-done | bytes 40992 | tf_op jit(solution)/shard_map/ppermute | solution.py:653
  99.7 1.4 %collective-permute-start.15 = (f32[320,128]{1,0:T(8,128)S(1)}, f32[320,128]{1,0:T(8,128)S(1)}, u32[]{:S(2)}, u32[]{:S(2)}) collective-permute-start(f32[320,128]{1,0:T(8,128)S(1)} %pad_maximum_fusion.refs_0_), channel_id=1, source_target_pairs={{0,3},{1,2},{2,1},{3,0},{4,7},{5,6},{6,5},{7,4},{8,11},{9,10},{10,... | collective-permute-start | bytes 491528 | tf_op jit(solution)/shard_map/ppermute | solution.py:653
  101.2 1.8 %collective-permute-done.13.refs_1_ = f32[320,128]{1,0:T(8,128)S(1)} collective-permute-done((f32[320,128]{1,0:T(8,128)S(1)}, f32[320,128]{1,0:T(8,128)S(1)}, u32[]{:S(2)}, u32[]{:S(2)}) %collective-permute-start.13) | collective-permute-done | bytes 163872 | tf_op jit(solution)/shard_map/ppermute | solution.py:653
  104.2 1.8 %collective-permute-done.15.refs_3_ = f32[320,128]{1,0:T(8,128)S(1)} collective-permute-done((f32[320,128]{1,0:T(8,128)S(1)}, f32[320,128]{1,0:T(8,128)S(1)}, u32[]{:S(2)}, u32[]{:S(2)}) %collective-permute-start.15) | collective-permute-done | bytes 163872 | tf_op jit(solution)/shard_map/ppermute | solution.py:653
  106.0 1.3 %collective-permute-done.19.refs_7_ = f32[320,128]{1,0:T(8,128)S(1)} collective-permute-done((f32[320,128]{1,0:T(8,128)S(1)}, f32[320,128]{1,0:T(8,128)S(1)}, u32[]{:S(2)}, u32[]{:S(2)}) %collective-permute-start.19) | collective-permute-done | bytes 163872 | tf_op jit(solution)/shard_map/ppermute | solution.py:653
  107.3 1.7 %finish.1 = (f32[512,512]{1,0:T(8,128)}, f32[1,512]{1,0:T(1,128)}, f32[64,512]{1,0:T(8,128)}) custom-call(s32[3]{0:T(128)S(1)} %pad_add_fusion.place_ref, f32[320,128]{1,0:T(8,128)S(1)} %pad_maximum_fusion.refs_0_, f32[320,128]{1,0:T(8,128)S(1)} %collective-permute-done.13.refs_1_, f32[320,128]{1,0:T(8,128)S(1)} %collective-permute-done.14.refs_2_, ...), custom_call_target="tpu_custom_call" | custom-call | tf_op jit(solution)/shard_map/finish/pallas_call | solution.py:635
  (60 shorter events, 14.1 us)
Async XLA Ops:
  0.6 25.2 %copy-start.5 = (s32[64]{0:T(128)S(1)}, s32[64]{0:T(128)}, u32[]{:S(2)}) copy-start(s32[64]{0:T(128)} %param.8) | copy-start | bytes 772
  0.6 28.1 %copy-start.6 = (f32[64]{0:T(128)S(1)}, f32[64]{0:T(128)}, u32[]{:S(2)}) copy-start(f32[64]{0:T(128)} %param.9) | copy-start | bytes 772
  18.6 34.0 %copy-start.4 = (f32[512]{0:T(512)S(1)}, f32[512]{0:T(512)}, u32[]{:S(2)}) copy-start(f32[512]{0:T(512)} %param.12) | copy-start | bytes 6148
  18.7 28.4 %all-to-all-start = ((f32[32,16,384]{2,1,0:T(8,128)}), f32[32,16,384]{2,1,0:T(8,128)S(1)}, u32[]{:S(2)}, u32[]{:S(2)}) async-start(f32[32,16,384]{2,1,0:T(8,128)} %bitcast.21), calls=%async_computation | async-start | bytes 1572864 | tf_op jit(solution)/shard_map/all_to_all | solution.py:671
  49.1 12.2 %collective-permute-start = (f32[360,128]{1,0:T(8,128)}, f32[360,128]{1,0:T(8,128)S(1)}, u32[]{:S(2)}, u32[]{:S(2)}) collective-permute-start(f32[360,128]{1,0:T(8,128)} %get-tuple-element.35), channel_id=1, source_target_pairs={{0,1},{1,0},{2,3},{3,2},{4,5},{5,4},{6,7},{7,6},{8,9},{9,8},{10,11... | collective-permute-start | bytes 552968 | tf_op jit(solution)/shard_map/ppermute | solution.py:653
  49.8 11.5 %collective-permute-start.1 = (f32[360,128]{1,0:T(8,128)S(1)}, f32[360,128]{1,0:T(8,128)S(1)}, u32[]{:S(2)}, u32[]{:S(2)}) collective-permute-start(f32[360,128]{1,0:T(8,128)S(1)} %get-tuple-element.36), channel_id=1, source_target_pairs={{0,2},{1,3},{2,0},{3,1},{4,6},{5,7},{6,4},{7,5},{8,10},{9,11},{10,... | collective-permute-start | bytes 552968 | tf_op jit(solution)/shard_map/ppermute | solution.py:653
  51.4 10.0 %collective-permute-start.2 = (f32[360,128]{1,0:T(8,128)S(1)}, f32[360,128]{1,0:T(8,128)S(1)}, u32[]{:S(2)}, u32[]{:S(2)}) collective-permute-start(f32[360,128]{1,0:T(8,128)S(1)} %get-tuple-element.37), channel_id=1, source_target_pairs={{0,3},{1,2},{2,1},{3,0},{4,7},{5,6},{6,5},{7,4},{8,11},{9,10},{10,... | collective-permute-start | bytes 552968 | tf_op jit(solution)/shard_map/ppermute | solution.py:653
  68.2 2.1 %collective-permute-start.3 = (f32[1280,128]{1,0:T(8,128)S(1)}, f32[1280,128]{1,0:T(8,128)S(1)}, u32[]{:S(2)}, u32[]{:S(2)}) collective-permute-start(f32[1280,128]{1,0:T(8,128)S(1)} %get-tuple-element.39), channel_id=1, source_target_pairs={{0,4},{4,0},{8,12},{12,8},{16,20},{20,16},{24,28},{28,24},{1,5},{5... | collective-permute-start | bytes 1966088 | tf_op jit(solution)/shard_map/ppermute | solution.py:653
  70.4 8.8 %collective-permute-start.4 = (f32[320,128]{1,0:T(8,128)S(1)}, f32[320,128]{1,0:T(8,128)S(1)}, u32[]{:S(2)}, u32[]{:S(2)}) collective-permute-start(f32[320,128]{1,0:T(8,128)S(1)} %get-tuple-element.40), channel_id=1, source_target_pairs={{0,1},{1,0},{2,3},{3,2},{4,5},{5,4},{6,7},{7,6},{8,9},{9,8},{10,11... | collective-permute-start | bytes 491528 | tf_op jit(solution)/shard_map/ppermute | solution.py:653
  71.1 9.5 %collective-permute-start.5 = (f32[320,128]{1,0:T(8,128)S(1)}, f32[320,128]{1,0:T(8,128)S(1)}, u32[]{:S(2)}, u32[]{:S(2)}) collective-permute-start(f32[320,128]{1,0:T(8,128)S(1)} %get-tuple-element.41), channel_id=1, source_target_pairs={{0,2},{1,3},{2,0},{3,1},{4,6},{5,7},{6,4},{7,5},{8,10},{9,11},{10,... | collective-permute-start | bytes 491528 | tf_op jit(solution)/shard_map/ppermute | solution.py:653
  72.7 7.9 %collective-permute-start.6 = (f32[320,128]{1,0:T(8,128)S(1)}, f32[320,128]{1,0:T(8,128)S(1)}, u32[]{:S(2)}, u32[]{:S(2)}) collective-permute-start(f32[320,128]{1,0:T(8,128)S(1)} %get-tuple-element.42), channel_id=1, source_target_pairs={{0,3},{1,2},{2,1},{3,0},{4,7},{5,6},{6,5},{7,4},{8,11},{9,10},{10,... | collective-permute-start | bytes 491528 | tf_op jit(solution)/shard_map/ppermute | solution.py:653
  80.6 4.5 %collective-permute-start.7 = (f32[80,128]{1,0:T(8,128)S(1)}, f32[80,128]{1,0:T(8,128)S(1)}, u32[]{:S(2)}, u32[]{:S(2)}) collective-permute-start(f32[80,128]{1,0:T(8,128)S(1)} %get-tuple-element.50), channel_id=1, source_target_pairs={{0,8},{4,12},{8,0},{12,4},{16,24},{20,28},{24,16},{28,20},{1,9},{5... | collective-permute-start | bytes 122888 | tf_op jit(solution)/shard_map/ppermute | solution.py:653
  81.8 4.9 %collective-permute-start.8 = (f32[80,128]{1,0:T(8,128)S(1)}, f32[80,128]{1,0:T(8,128)S(1)}, u32[]{:S(2)}, u32[]{:S(2)}) collective-permute-start(f32[80,128]{1,0:T(8,128)S(1)} %get-tuple-element.51), channel_id=1, source_target_pairs={{0,16},{4,20},{8,24},{12,28},{16,0},{20,4},{24,8},{28,12},{1,17},{... | collective-permute-start | bytes 122888 | tf_op jit(solution)/shard_map/ppermute | solution.py:653
  82.7 5.8 %collective-permute-start.9 = (f32[80,128]{1,0:T(8,128)S(1)}, f32[80,128]{1,0:T(8,128)S(1)}, u32[]{:S(2)}, u32[]{:S(2)}) collective-permute-start(f32[80,128]{1,0:T(8,128)S(1)} %get-tuple-element.52), channel_id=1, source_target_pairs={{0,24},{4,28},{8,16},{12,20},{16,8},{20,12},{24,0},{28,4},{1,25},{... | collective-permute-start | bytes 122888 | tf_op jit(solution)/shard_map/ppermute | solution.py:653
  88.5 4.5 %collective-permute-start.10 = (f32[80,128]{1,0:T(8,128)S(1)}, f32[80,128]{1,0:T(8,128)S(1)}, u32[]{:S(2)}, u32[]{:S(2)}) collective-permute-start(f32[80,128]{1,0:T(8,128)S(1)} %add_pieces.5), channel_id=1, source_target_pairs={{0,8},{4,12},{8,0},{12,4},{16,24},{20,28},{24,16},{28,20},{1,9},{5... | collective-permute-start | bytes 122888 | tf_op jit(solution)/shard_map/ppermute | solution.py:653
  88.6 5.5 %collective-permute-start.11 = (f32[80,128]{1,0:T(8,128)S(1)}, f32[80,128]{1,0:T(8,128)S(1)}, u32[]{:S(2)}, u32[]{:S(2)}) collective-permute-start(f32[80,128]{1,0:T(8,128)S(1)} %add_pieces.5), channel_id=1, source_target_pairs={{0,16},{4,20},{8,24},{12,28},{16,0},{20,4},{24,8},{28,12},{1,17},{... | collective-permute-start | bytes 122888 | tf_op jit(solution)/shard_map/ppermute | solution.py:653
  91.8 5.8 %collective-permute-start.12 = (f32[80,128]{1,0:T(8,128)S(1)}, f32[80,128]{1,0:T(8,128)S(1)}, u32[]{:S(2)}, u32[]{:S(2)}) collective-permute-start(f32[80,128]{1,0:T(8,128)S(1)} %add_pieces.5), channel_id=1, source_target_pairs={{0,24},{4,28},{8,16},{12,20},{16,8},{20,12},{24,0},{28,4},{1,25},{... | collective-permute-start | bytes 122888 | tf_op jit(solution)/shard_map/ppermute | solution.py:653
  97.6 5.4 %collective-permute-start.13 = (f32[320,128]{1,0:T(8,128)S(1)}, f32[320,128]{1,0:T(8,128)S(1)}, u32[]{:S(2)}, u32[]{:S(2)}) collective-permute-start(f32[320,128]{1,0:T(8,128)S(1)} %pad_maximum_fusion.refs_0_), channel_id=1, source_target_pairs={{0,1},{1,0},{2,3},{3,2},{4,5},{5,4},{6,7},{7,6},{8,9},{9,8},{10,11... | collective-permute-start | bytes 491528 | tf_op jit(solution)/shard_map/ppermute | solution.py:653
  98.8 5.3 %collective-permute-start.14 = (f32[320,128]{1,0:T(8,128)S(1)}, f32[320,128]{1,0:T(8,128)S(1)}, u32[]{:S(2)}, u32[]{:S(2)}) collective-permute-start(f32[320,128]{1,0:T(8,128)S(1)} %pad_maximum_fusion.refs_0_), channel_id=1, source_target_pairs={{0,2},{1,3},{2,0},{3,1},{4,6},{5,7},{6,4},{7,5},{8,10},{9,11},{10,... | collective-permute-start | bytes 491528 | tf_op jit(solution)/shard_map/ppermute | solution.py:653
  99.7 6.2 %collective-permute-start.15 = (f32[320,128]{1,0:T(8,128)S(1)}, f32[320,128]{1,0:T(8,128)S(1)}, u32[]{:S(2)}, u32[]{:S(2)}) collective-permute-start(f32[320,128]{1,0:T(8,128)S(1)} %pad_maximum_fusion.refs_0_), channel_id=1, source_target_pairs={{0,3},{1,2},{2,1},{3,0},{4,7},{5,6},{6,5},{7,4},{8,11},{9,10},{10,... | collective-permute-start | bytes 491528 | tf_op jit(solution)/shard_map/ppermute | solution.py:653
  101.2 4.9 %collective-permute-start.16 = (f32[320,128]{1,0:T(8,128)S(1)}, f32[320,128]{1,0:T(8,128)S(1)}, u32[]{:S(2)}, u32[]{:S(2)}) collective-permute-start(f32[320,128]{1,0:T(8,128)S(1)} %pad_maximum_fusion.refs_0_), channel_id=1, source_target_pairs={{0,4},{4,0},{8,12},{12,8},{16,20},{20,16},{24,28},{28,24},{1,5},{5... | collective-permute-start | bytes 491528 | tf_op jit(solution)/shard_map/ppermute | solution.py:653
  103.0 3.0 %collective-permute-start.17 = (f32[320,128]{1,0:T(8,128)S(1)}, f32[320,128]{1,0:T(8,128)S(1)}, u32[]{:S(2)}, u32[]{:S(2)}) collective-permute-start(f32[320,128]{1,0:T(8,128)S(1)} %collective-permute-done.13.refs_1_), channel_id=1, source_target_pairs={{0,4},{4,0},{8,12},{12,8},{16,20},{20,16},{24,28},{28,24},{1,5},{5... | collective-permute-start | bytes 491528 | tf_op jit(solution)/shard_map/ppermute | solution.py:653
  104.2 1.9 %collective-permute-start.18 = (f32[320,128]{1,0:T(8,128)S(1)}, f32[320,128]{1,0:T(8,128)S(1)}, u32[]{:S(2)}, u32[]{:S(2)}) collective-permute-start(f32[320,128]{1,0:T(8,128)S(1)} %collective-permute-done.14.refs_2_), channel_id=1, source_target_pairs={{0,4},{4,0},{8,12},{12,8},{16,20},{20,16},{24,28},{28,24},{1,5},{5... | collective-permute-start | bytes 491528 | tf_op jit(solution)/shard_map/ppermute | solution.py:653
  105.9 1.4 %collective-permute-start.19 = (f32[320,128]{1,0:T(8,128)S(1)}, f32[320,128]{1,0:T(8,128)S(1)}, u32[]{:S(2)}, u32[]{:S(2)}) collective-permute-start(f32[320,128]{1,0:T(8,128)S(1)} %collective-permute-done.15.refs_3_), channel_id=1, source_target_pairs={{0,4},{4,0},{8,12},{12,8},{16,20},{20,16},{24,28},{28,24},{1,5},{5... | collective-permute-start | bytes 491528 | tf_op jit(solution)/shard_map/ppermute | solution.py:653
  (4 other events, 16.7 us)
